TPU v7x, 32 devices: a whole 2x2x4 slice. The times are simulated.
32 devices in a mesh: blk: 8 (over z, y), grp: 4 (over x, core).
Axes of the slice: x: 2, y: 2, z: 4, core: 2. Of those that a mesh axis runs over, the one named last changes fastest.
Arguments:
- tiles: bfloat16 [128, 20, 128, 128], P(('blk', 'grp')), may hold values from -1 to 3.5
- columns: int32 [128, 20], P(('blk', 'grp')), may hold values from -1 to 127, as said below
Outputs:
- square: bfloat16 [128, 20, 128, 128], P(('blk', 'grp'))
- trace_mean: float32 [], replicated
Inputs may be any that keep to these rules, and one draw needn't show every extreme that they name: Slot 0 of row i holds i. The filled slots of a row come first, then -1. The filled columns of a row are distinct and lie within 12 block rows of i, counted periodically modulo 128. Every device has a row with all 20 slots filled that reaches i - 12 and one that reaches i + 12.
All inputs are finite; a program needn't handle non-finite values.
Results may differ from a plain program's by a relative error of at most 0.001.
Values may be sent and summed in bfloat16 or wider, within the bound.
No kernel may reach another device: no remote copies, remote signals or barrier semaphores. Data moves between devices by JAX's collectives and lax.ppermute only.
A program may use at most 192 MiB of HBM per device.

v0:
```python
import jax
import jax.numpy as jnp
from jax import lax
from jax.sharding import PartitionSpec as P

REACH = 12


def shifted(shard, axis, by):
    size = lax.axis_size(axis)
    return lax.ppermute(shard, axis, [(i, (i + by) % size) for i in range(size)])


def shards(tiles, columns):
    shard_rows = tiles.shape[0]
    slots_count = tiles.shape[1]
    block_size = tiles.shape[2]
    devices = lax.axis_size(("blk", "grp"))
    all_rows = shard_rows * devices
    device = lax.axis_index(("blk", "grp"))
    hop_count = (REACH + shard_rows - 1) // shard_rows
    window_count = 2 * hop_count + 1
    tile_buf = jnp.zeros((window_count,) + tiles.shape, tiles.dtype).at[hop_count].set(tiles)
    col_buf = jnp.zeros((window_count,) + columns.shape, jnp.int32).at[hop_count].set(columns)

    def advance(hop_step, loop_state):
        lower_piece, upper_piece, tile_acc, col_acc = loop_state
        lower_piece = shifted((lower_piece[0], lower_piece[1]), ("blk", "grp"), 1)
        upper_piece = shifted((upper_piece[0], upper_piece[1]), ("blk", "grp"), -1)
        below_slot = hop_count - 1 - hop_step
        above_slot = hop_count + 1 + hop_step
        tile_acc = lax.dynamic_update_index_in_dim(tile_acc, lower_piece[0], below_slot, 0)
        col_acc = lax.dynamic_update_index_in_dim(col_acc, lower_piece[1], below_slot, 0)
        tile_acc = lax.dynamic_update_index_in_dim(tile_acc, upper_piece[0], above_slot, 0)
        col_acc = lax.dynamic_update_index_in_dim(col_acc, upper_piece[1], above_slot, 0)
        return (lower_piece, upper_piece, tile_acc, col_acc)

    start_state = ((tiles, columns), (tiles, columns), tile_buf, col_buf)
    final_state = lax.fori_loop(0, hop_count, advance, start_state)
    window_tiles = final_state[2]
    window_cols = final_state[3]
    row_tiles = window_tiles.reshape(window_count * shard_rows, slots_count, block_size, block_size)
    row_cols = window_cols.reshape(window_count * shard_rows, slots_count)
    first_row = (device - hop_count) * shard_rows

    def one_row(inputs):
        own_tiles, own_cols = inputs
        filled = own_cols >= 0
        position = jnp.where(filled, jnp.mod(own_cols - first_row, all_rows), 0)
        far_tiles = row_tiles[position]
        far_cols = row_cols[position]
        routing = (
            (far_cols[:, :, None] == own_cols[None, None, :])
            & filled[None, None, :]
            & filled[:, None, None]
        ).astype(jnp.bfloat16)
        panel = jnp.einsum(
            "tus,tubc->tsbc", routing, far_tiles, preferred_element_type=jnp.float32
        ).astype(jnp.bfloat16)
        product = jnp.einsum("tab,tsbc->sac", own_tiles, panel, preferred_element_type=jnp.float32)
        return (product.astype(jnp.bfloat16), jnp.trace(product[0]))

    square, traces = lax.map(one_row, (tiles, columns))
    total_trace = lax.psum(jnp.sum(traces), ("blk", "grp"))
    trace_mean = total_trace / (all_rows * block_size)
    return (square, trace_mean)


def solution(mesh):
    return jax.shard_map(
        shards,
        mesh=mesh,
        in_specs=(P(("blk", "grp"), None, None, None), P(("blk", "grp"), None)),
        out_specs=(P(("blk", "grp"), None, None, None), P()),
        check_vma=False,
    )
```

profile of v0, /device:TPU:0, one launch (start us, length us, event | category | flops | bytes accessed | tf_op | source)
XLA Modules:
  0.0 539.9 jit_solution(2088846072396987717)
XLA Ops:
  0.6 0.7 scatter.9
  1.3 8.1 %scatter.6 = bf16[7,4,20,128,128]{4,3,2,1,0:T(8,128)(2,1)} pad(bf16[1,4,20,128,128]{4,3,2,1,0:T(8,128)(2,1)} %bitcast.77, bf16[]{:T(256)} %constant.169.clone.1), padding=3_3x0_0x0_0x0_0x0_0 | pad | bytes 20971522 | tf_op jit(solution)/shard_map/scatter | solution.py:23
  9.4 1.5 copy.28
  10.9 1.5 copy.30
  12.3 185.6 %while.39 = (s32[]{:T(128)}, bf16[4,20,128,128]{3,2,1,0:T(8,128)(2,1)}, s32[4,20]{1,0:T(4,128)S(1)}, bf16[4,20,128,128]{3,2,1,0:T(8,128)(2,1)}, s32[4,20]{1,0:T(...) while((s32[]{:T(128)}, ...), condition=%wide.region_1.0_spmd, body=%wide.region_0.0_spmd.sunk | while | flops 10 | bytes 41955460 | solution.py:39
  12.3 0.5 collective-permute-start
  12.8 6.0 %collective-permute-start.2 = (bf16[4,20,128,128]{3,2,1,0:T(8,128)(2,1)}, bf16[4,20,128,128]{3,2,1,0:T(8,128)(2,1)S(1)}, u32[]{:S(2)}, u32[]{:S(2)}) collective-permute-start(bf16[4,20,128,128]{3,2,1,0:T(8,128)(2,1)} %get-tuple-element.406), channel_id=1, source_target_pairs={{0,31},{1,0},{2,1},{3,2},{4,3},{5,4},{6,5},{7,6},{8,7},{9,8},{10,9... | collective-permute-start | bytes 7864328 | tf_op jit(solution)/shard_map/while/body/eval_jaxpr/ppermute | solution.py:11
  18.8 5.3 collective-permute-start.3
  24.1 24.3 %collective-permute-done.1 = s32[4,20]{1,0:T(4,128)S(1)} collective-permute-done((s32[4,20]{1,0:T(4,128)S(1)}, s32[4,20]{1,0:T(4,128)S(1)}, u32[]{:S(2)}, u32[]{:S(2)}) %collective-permute-start.1) | collective-permute-done | bytes 352 | tf_op jit(solution)/shard_map/while/body/eval_jaxpr/ppermute | solution.py:11
  48.5 3.6 copy.42
  52.1 3.6 bitcast_dynamic-update-slice_fusion.8
  55.7 1.5 copy.44
  57.1 1.7 bitcast_dynamic-update-slice_fusion.9
  58.8 25.9 %collective-permute-start = (bf16[4,20,128,128]{3,2,1,0:T(8,128)(2,1)}, bf16[4,20,128,128]{3,2,1,0:T(8,128)(2,1)}, u32[]{:S(2)}, u32[]{:S(2)}) collective-permute-start(bf16[4,20,128,128]{3,2,1,0:T(8,128)(2,1)} %get-tuple-element.404), channel_id=1, source_target_pairs={{0,1},{1,2},{2,3},{3,4},{4,5},{5,6},{6,7},{7,8},{8,9},{9,10},{10,1... | collective-permute-start | bytes 7864328 | tf_op jit(solution)/shard_map/while/body/eval_jaxpr/ppermute | solution.py:11
  84.7 0.5 collective-permute-start.1
  85.3 31.0 %collective-permute-start.3 = (s32[4,20]{1,0:T(4,128)S(1)}, s32[4,20]{1,0:T(4,128)S(1)}, u32[]{:S(2)}, u32[]{:S(2)}) collective-permute-start(s32[4,20]{1,0:T(4,128)S(1)} %get-tuple-element.407), channel_id=1, source_target_pairs={{0,31},{1,0},{2,1},{3,2},{4,3},{5,4},{6,5},{7,6},{8,7},{9,8},{10,9... | collective-permute-start | bytes 968 | tf_op jit(solution)/shard_map/while/body/eval_jaxpr/ppermute | solution.py:11
  116.2 1.3 collective-permute-done.1
  117.5 3.6 copy.42
  121.1 3.6 bitcast_dynamic-update-slice_fusion.8
  124.7 1.5 copy.44
  126.2 1.7 bitcast_dynamic-update-slice_fusion.9
  127.8 26.8 %collective-permute-start = (bf16[4,20,128,128]{3,2,1,0:T(8,128)(2,1)}, bf16[4,20,128,128]{3,2,1,0:T(8,128)(2,1)}, u32[]{:S(2)}, u32[]{:S(2)}) collective-permute-start(bf16[4,20,128,128]{3,2,1,0:T(8,128)(2,1)} %get-tuple-element.404), channel_id=1, source_target_pairs={{0,1},{1,2},{2,3},{3,4},{4,5},{5,6},{6,7},{7,8},{8,9},{9,10},{10,1... | collective-permute-start | bytes 7864328 | tf_op jit(solution)/shard_map/while/body/eval_jaxpr/ppermute | solution.py:11
  154.6 0.5 collective-permute-start.1
  155.1 31.2 %collective-permute-start.3 = (s32[4,20]{1,0:T(4,128)S(1)}, s32[4,20]{1,0:T(4,128)S(1)}, u32[]{:S(2)}, u32[]{:S(2)}) collective-permute-start(s32[4,20]{1,0:T(4,128)S(1)} %get-tuple-element.407), channel_id=1, source_target_pairs={{0,31},{1,0},{2,1},{3,2},{4,3},{5,4},{6,5},{7,6},{8,7},{9,8},{10,9... | collective-permute-start | bytes 968 | tf_op jit(solution)/shard_map/while/body/eval_jaxpr/ppermute | solution.py:11
  186.3 1.3 collective-permute-done.1
  187.6 3.6 copy.42
  191.2 3.6 bitcast_dynamic-update-slice_fusion.8
  194.8 1.5 copy.44
  196.3 1.7 bitcast_dynamic-update-slice_fusion.9
  197.9 247.0 %while.40 = (s32[]{:T(128)}, bf16[4,20,128,128]{3,2,1,0:T(8,128)(2,1)}, f32[4]{0:T(128)S(1)}, s32[4,20]{1,0:T(4,128)S(1)}, s32[]{:T(128)}, /*index=5*/s32[28,20]...) while((s32[]{:T(128)}, bf16[4,20,128,128]{3,2,1,0:T(8,128)(2,1)}, ...), condition=%wide.region_4.5_spmd, body=%wide.region_2.4_spmd.sunk | while | flops 1940267776 | bytes 98380256 | solution.py:63
  198.0 12.7 %gather_fusion = bf16[20,20,128,128]{3,2,1,0:T(8,128)(2,1)} fusion(bf16[28,20,128,128]{3,2,1,0:T(8,128)(2,1)} %get-tuple-element.453, s32[1024]{0:T(1024)S(1)} %pad_clamp_fusion.2), kind=kCustom, calls=%fused_computation.1.clone.1 | custom fusion | bytes 26214480 | tf_op jit(solution)/shard_map/while/body/eval_jaxpr/gather | solution.py:50
  210.7 0.6 gather_fusion.1
  211.2 19.4 %fusion.38 = bf16[20,20,128,128]{3,1,2,0:T(8,128)(2,1)} fusion(bf16[20,20,128,128]{3,2,1,0:T(8,128)(2,1)} %gather_fusion, s32[20]{0:T(128)S(1)} %get-tuple-element.388, s32[20,20]{1,0:T(8,128)S(1)} %gather_fusion.1, pred[20]{0:T(512)(128)(4,1)S(1)} %get-tuple-element.389), kind=kOutput, calls=%fused_computation.6.clone.1 | convolution fusion | flops 262168000 | bytes 26216100 | tf_op jit(solution)/shard_map/while/body/eval_jaxpr/tus,tubc->tsbc/dot_general | solution.py:57
  230.6 19.5 %copy.19 = bf16[20,20,128,128]{2,3,0,1:T(8,128)(2,1)} copy(bf16[20,20,128,128]{3,1,2,0:T(8,128)(2,1)} %fusion.38) | data formatting | bytes 26214400 | tf_op jit(solution)/shard_map/while/body/eval_jaxpr/tus,tubc->tsbc/dot_general | solution.py:57
  250.2 6.9 %fusion.39 = f32[20,128,128]{1,2,0:T(8,128)S(1)} fusion(bf16[20,20,128,128]{2,3,0,1:T(8,128)(2,1)} %copy.19, bf16[4,20,128,128]{3,2,1,0:T(8,128)(2,1)} %get-tuple-element.454, s32[]{:T(128)} %get-tuple-element.438), kind=kOutput, calls=%fused_computation.10.clone.1 | convolution fusion | flops 1677721600 | bytes 15073792 | tf_op jit(solution)/shard_map/while/body/eval_jaxpr/tab,tsbc->sac/dot_general | solution.py:60
  257.5 0.9 constant_dynamic-update-slice_fusion.2
  258.4 0.6 fusion.40
  259.0 0.7 dynamic_update_slice.60
  259.7 12.7 %gather_fusion = bf16[20,20,128,128]{3,2,1,0:T(8,128)(2,1)} fusion(bf16[28,20,128,128]{3,2,1,0:T(8,128)(2,1)} %get-tuple-element.453, s32[1024]{0:T(1024)S(1)} %pad_clamp_fusion.2), kind=kCustom, calls=%fused_computation.1.clone.1 | custom fusion | bytes 26214480 | tf_op jit(solution)/shard_map/while/body/eval_jaxpr/gather | solution.py:50
  272.4 0.6 gather_fusion.1
  273.0 19.4 %fusion.38 = bf16[20,20,128,128]{3,1,2,0:T(8,128)(2,1)} fusion(bf16[20,20,128,128]{3,2,1,0:T(8,128)(2,1)} %gather_fusion, s32[20]{0:T(128)S(1)} %get-tuple-element.388, s32[20,20]{1,0:T(8,128)S(1)} %gather_fusion.1, pred[20]{0:T(512)(128)(4,1)S(1)} %get-tuple-element.389), kind=kOutput, calls=%fused_computation.6.clone.1 | convolution fusion | flops 262168000 | bytes 26216100 | tf_op jit(solution)/shard_map/while/body/eval_jaxpr/tus,tubc->tsbc/dot_general | solution.py:57
  292.4 19.5 %copy.19 = bf16[20,20,128,128]{2,3,0,1:T(8,128)(2,1)} copy(bf16[20,20,128,128]{3,1,2,0:T(8,128)(2,1)} %fusion.38) | data formatting | bytes 26214400 | tf_op jit(solution)/shard_map/while/body/eval_jaxpr/tus,tubc->tsbc/dot_general | solution.py:57
  311.9 6.9 %fusion.39 = f32[20,128,128]{1,2,0:T(8,128)S(1)} fusion(bf16[20,20,128,128]{2,3,0,1:T(8,128)(2,1)} %copy.19, bf16[4,20,128,128]{3,2,1,0:T(8,128)(2,1)} %get-tuple-element.454, s32[]{:T(128)} %get-tuple-element.438), kind=kOutput, calls=%fused_computation.10.clone.1 | convolution fusion | flops 1677721600 | bytes 15073792 | tf_op jit(solution)/shard_map/while/body/eval_jaxpr/tab,tsbc->sac/dot_general | solution.py:60
  319.2 0.9 constant_dynamic-update-slice_fusion.2
  320.1 0.6 fusion.40
  320.8 0.7 dynamic_update_slice.60
  321.5 12.7 %gather_fusion = bf16[20,20,128,128]{3,2,1,0:T(8,128)(2,1)} fusion(bf16[28,20,128,128]{3,2,1,0:T(8,128)(2,1)} %get-tuple-element.453, s32[1024]{0:T(1024)S(1)} %pad_clamp_fusion.2), kind=kCustom, calls=%fused_computation.1.clone.1 | custom fusion | bytes 26214480 | tf_op jit(solution)/shard_map/while/body/eval_jaxpr/gather | solution.py:50
  334.2 0.6 gather_fusion.1
  334.8 19.4 %fusion.38 = bf16[20,20,128,128]{3,1,2,0:T(8,128)(2,1)} fusion(bf16[20,20,128,128]{3,2,1,0:T(8,128)(2,1)} %gather_fusion, s32[20]{0:T(128)S(1)} %get-tuple-element.388, s32[20,20]{1,0:T(8,128)S(1)} %gather_fusion.1, pred[20]{0:T(512)(128)(4,1)S(1)} %get-tuple-element.389), kind=kOutput, calls=%fused_computation.6.clone.1 | convolution fusion | flops 262168000 | bytes 26216100 | tf_op jit(solution)/shard_map/while/body/eval_jaxpr/tus,tubc->tsbc/dot_general | solution.py:57
  354.1 19.5 %copy.19 = bf16[20,20,128,128]{2,3,0,1:T(8,128)(2,1)} copy(bf16[20,20,128,128]{3,1,2,0:T(8,128)(2,1)} %fusion.38) | data formatting | bytes 26214400 | tf_op jit(solution)/shard_map/while/body/eval_jaxpr/tus,tubc->tsbc/dot_general | solution.py:57
  373.7 6.9 %fusion.39 = f32[20,128,128]{1,2,0:T(8,128)S(1)} fusion(bf16[20,20,128,128]{2,3,0,1:T(8,128)(2,1)} %copy.19, bf16[4,20,128,128]{3,2,1,0:T(8,128)(2,1)} %get-tuple-element.454, s32[]{:T(128)} %get-tuple-element.438), kind=kOutput, calls=%fused_computation.10.clone.1 | convolution fusion | flops 1677721600 | bytes 15073792 | tf_op jit(solution)/shard_map/while/body/eval_jaxpr/tab,tsbc->sac/dot_general | solution.py:60
  381.0 0.9 constant_dynamic-update-slice_fusion.2
  381.9 0.6 fusion.40
  382.5 0.7 dynamic_update_slice.60
  383.2 12.7 %gather_fusion = bf16[20,20,128,128]{3,2,1,0:T(8,128)(2,1)} fusion(bf16[28,20,128,128]{3,2,1,0:T(8,128)(2,1)} %get-tuple-element.453, s32[1024]{0:T(1024)S(1)} %pad_clamp_fusion.2), kind=kCustom, calls=%fused_computation.1.clone.1 | custom fusion | bytes 26214480 | tf_op jit(solution)/shard_map/while/body/eval_jaxpr/gather | solution.py:50
  395.9 0.6 gather_fusion.1
  396.5 19.4 %fusion.38 = bf16[20,20,128,128]{3,1,2,0:T(8,128)(2,1)} fusion(bf16[20,20,128,128]{3,2,1,0:T(8,128)(2,1)} %gather_fusion, s32[20]{0:T(128)S(1)} %get-tuple-element.388, s32[20,20]{1,0:T(8,128)S(1)} %gather_fusion.1, pred[20]{0:T(512)(128)(4,1)S(1)} %get-tuple-element.389), kind=kOutput, calls=%fused_computation.6.clone.1 | convolution fusion | flops 262168000 | bytes 26216100 | tf_op jit(solution)/shard_map/while/body/eval_jaxpr/tus,tubc->tsbc/dot_general | solution.py:57
  415.9 19.5 %copy.19 = bf16[20,20,128,128]{2,3,0,1:T(8,128)(2,1)} copy(bf16[20,20,128,128]{3,1,2,0:T(8,128)(2,1)} %fusion.38) | data formatting | bytes 26214400 | tf_op jit(solution)/shard_map/while/body/eval_jaxpr/tus,tubc->tsbc/dot_general | solution.py:57
  435.4 6.9 %fusion.39 = f32[20,128,128]{1,2,0:T(8,128)S(1)} fusion(bf16[20,20,128,128]{2,3,0,1:T(8,128)(2,1)} %copy.19, bf16[4,20,128,128]{3,2,1,0:T(8,128)(2,1)} %get-tuple-element.454, s32[]{:T(128)} %get-tuple-element.438), kind=kOutput, calls=%fused_computation.10.clone.1 | convolution fusion | flops 1677721600 | bytes 15073792 | tf_op jit(solution)/shard_map/while/body/eval_jaxpr/tab,tsbc->sac/dot_general | solution.py:60
  442.7 0.9 constant_dynamic-update-slice_fusion.2
  443.6 0.6 fusion.40
  444.3 0.7 dynamic_update_slice.60
  445.0 0.6 reduce_sum.22
  445.6 92.6 %psum.7 = f32[]{:T(128)} all-reduce(f32[]{:T(128)} %reduce_sum.22), channel_id=1, replica_groups=mesh['blk'=8,'grp'=4] {'blk','grp'}, use_global_device_ids=true, to_apply=%region_6.7 | all-reduce | flops 1 | bytes 8 | tf_op jit(solution)/shard_map/psum | solution.py:64
  (53 shorter events, 2.1 us)
Async XLA Ops:
  1.3 8.1 %copy-start = (bf16[4,20,128,128]{3,2,1,0:T(8,128)(2,1)S(1)}, bf16[4,20,128,128]{3,2,1,0:T(8,128)(2,1)}, u32[]{:S(2)}) copy-start(bf16[4,20,128,128]{3,2,1,0:T(8,128)(2,1)} %param.10) | copy-start | bytes 7864324
  10.9 1.5 copy-start.1
  12.3 36.2 %collective-permute-start = (bf16[4,20,128,128]{3,2,1,0:T(8,128)(2,1)}, bf16[4,20,128,128]{3,2,1,0:T(8,128)(2,1)}, u32[]{:S(2)}, u32[]{:S(2)}) collective-permute-start(bf16[4,20,128,128]{3,2,1,0:T(8,128)(2,1)} %get-tuple-element.404), channel_id=1, source_target_pairs={{0,1},{1,2},{2,3},{3,4},{4,5},{5,6},{6,7},{7,8},{8,9},{9,10},{10,1... | collective-permute-start | bytes 7864328 | tf_op jit(solution)/shard_map/while/body/eval_jaxpr/ppermute | solution.py:11
  12.8 42.9 %collective-permute-start.2 = (bf16[4,20,128,128]{3,2,1,0:T(8,128)(2,1)}, bf16[4,20,128,128]{3,2,1,0:T(8,128)(2,1)S(1)}, u32[]{:S(2)}, u32[]{:S(2)}) collective-permute-start(bf16[4,20,128,128]{3,2,1,0:T(8,128)(2,1)} %get-tuple-element.406), channel_id=1, source_target_pairs={{0,31},{1,0},{2,1},{3,2},{4,3},{5,4},{6,5},{7,6},{8,7},{9,8},{10,9... | collective-permute-start | bytes 7864328 | tf_op jit(solution)/shard_map/while/body/eval_jaxpr/ppermute | solution.py:11
  18.8 29.7 %collective-permute-start.1 = (s32[4,20]{1,0:T(4,128)S(1)}, s32[4,20]{1,0:T(4,128)S(1)}, u32[]{:S(2)}, u32[]{:S(2)}) collective-permute-start(s32[4,20]{1,0:T(4,128)S(1)} %get-tuple-element.405), channel_id=1, source_target_pairs={{0,1},{1,2},{2,3},{3,4},{4,5},{5,6},{6,7},{7,8},{8,9},{9,10},{10,1... | collective-permute-start | bytes 968 | tf_op jit(solution)/shard_map/while/body/eval_jaxpr/ppermute | solution.py:11
  18.8 29.7 %collective-permute-start.3 = (s32[4,20]{1,0:T(4,128)S(1)}, s32[4,20]{1,0:T(4,128)S(1)}, u32[]{:S(2)}, u32[]{:S(2)}) collective-permute-start(s32[4,20]{1,0:T(4,128)S(1)} %get-tuple-element.407), channel_id=1, source_target_pairs={{0,31},{1,0},{2,1},{3,2},{4,3},{5,4},{6,5},{7,6},{8,7},{9,8},{10,9... | collective-permute-start | bytes 968 | tf_op jit(solution)/shard_map/while/body/eval_jaxpr/ppermute | solution.py:11
  58.8 58.7 %collective-permute-start = (bf16[4,20,128,128]{3,2,1,0:T(8,128)(2,1)}, bf16[4,20,128,128]{3,2,1,0:T(8,128)(2,1)}, u32[]{:S(2)}, u32[]{:S(2)}) collective-permute-start(bf16[4,20,128,128]{3,2,1,0:T(8,128)(2,1)} %get-tuple-element.404), channel_id=1, source_target_pairs={{0,1},{1,2},{2,3},{3,4},{4,5},{5,6},{6,7},{7,8},{8,9},{9,10},{10,1... | collective-permute-start | bytes 7864328 | tf_op jit(solution)/shard_map/while/body/eval_jaxpr/ppermute | solution.py:11
  84.7 40.0 %collective-permute-start.2 = (bf16[4,20,128,128]{3,2,1,0:T(8,128)(2,1)}, bf16[4,20,128,128]{3,2,1,0:T(8,128)(2,1)S(1)}, u32[]{:S(2)}, u32[]{:S(2)}) collective-permute-start(bf16[4,20,128,128]{3,2,1,0:T(8,128)(2,1)} %get-tuple-element.406), channel_id=1, source_target_pairs={{0,31},{1,0},{2,1},{3,2},{4,3},{5,4},{6,5},{7,6},{8,7},{9,8},{10,9... | collective-permute-start | bytes 7864328 | tf_op jit(solution)/shard_map/while/body/eval_jaxpr/ppermute | solution.py:11
  84.7 32.8 %collective-permute-start.1 = (s32[4,20]{1,0:T(4,128)S(1)}, s32[4,20]{1,0:T(4,128)S(1)}, u32[]{:S(2)}, u32[]{:S(2)}) collective-permute-start(s32[4,20]{1,0:T(4,128)S(1)} %get-tuple-element.405), channel_id=1, source_target_pairs={{0,1},{1,2},{2,3},{3,4},{4,5},{5,6},{6,7},{7,8},{8,9},{9,10},{10,1... | collective-permute-start | bytes 968 | tf_op jit(solution)/shard_map/while/body/eval_jaxpr/ppermute | solution.py:11
  85.3 32.3 %collective-permute-start.3 = (s32[4,20]{1,0:T(4,128)S(1)}, s32[4,20]{1,0:T(4,128)S(1)}, u32[]{:S(2)}, u32[]{:S(2)}) collective-permute-start(s32[4,20]{1,0:T(4,128)S(1)} %get-tuple-element.407), channel_id=1, source_target_pairs={{0,31},{1,0},{2,1},{3,2},{4,3},{5,4},{6,5},{7,6},{8,7},{9,8},{10,9... | collective-permute-start | bytes 968 | tf_op jit(solution)/shard_map/while/body/eval_jaxpr/ppermute | solution.py:11
  127.8 59.8 %collective-permute-start = (bf16[4,20,128,128]{3,2,1,0:T(8,128)(2,1)}, bf16[4,20,128,128]{3,2,1,0:T(8,128)(2,1)}, u32[]{:S(2)}, u32[]{:S(2)}) collective-permute-start(bf16[4,20,128,128]{3,2,1,0:T(8,128)(2,1)} %get-tuple-element.404), channel_id=1, source_target_pairs={{0,1},{1,2},{2,3},{3,4},{4,5},{5,6},{6,7},{7,8},{8,9},{9,10},{10,1... | collective-permute-start | bytes 7864328 | tf_op jit(solution)/shard_map/while/body/eval_jaxpr/ppermute | solution.py:11
  154.6 40.2 %collective-permute-start.2 = (bf16[4,20,128,128]{3,2,1,0:T(8,128)(2,1)}, bf16[4,20,128,128]{3,2,1,0:T(8,128)(2,1)S(1)}, u32[]{:S(2)}, u32[]{:S(2)}) collective-permute-start(bf16[4,20,128,128]{3,2,1,0:T(8,128)(2,1)} %get-tuple-element.406), channel_id=1, source_target_pairs={{0,31},{1,0},{2,1},{3,2},{4,3},{5,4},{6,5},{7,6},{8,7},{9,8},{10,9... | collective-permute-start | bytes 7864328 | tf_op jit(solution)/shard_map/while/body/eval_jaxpr/ppermute | solution.py:11
  154.6 33.0 %collective-permute-start.1 = (s32[4,20]{1,0:T(4,128)S(1)}, s32[4,20]{1,0:T(4,128)S(1)}, u32[]{:S(2)}, u32[]{:S(2)}) collective-permute-start(s32[4,20]{1,0:T(4,128)S(1)} %get-tuple-element.405), channel_id=1, source_target_pairs={{0,1},{1,2},{2,3},{3,4},{4,5},{5,6},{6,7},{7,8},{8,9},{9,10},{10,1... | collective-permute-start | bytes 968 | tf_op jit(solution)/shard_map/while/body/eval_jaxpr/ppermute | solution.py:11
  155.1 32.5 %collective-permute-start.3 = (s32[4,20]{1,0:T(4,128)S(1)}, s32[4,20]{1,0:T(4,128)S(1)}, u32[]{:S(2)}, u32[]{:S(2)}) collective-permute-start(s32[4,20]{1,0:T(4,128)S(1)} %get-tuple-element.407), channel_id=1, source_target_pairs={{0,31},{1,0},{2,1},{3,2},{4,3},{5,4},{6,5},{7,6},{8,7},{9,8},{10,9... | collective-permute-start | bytes 968 | tf_op jit(solution)/shard_map/while/body/eval_jaxpr/ppermute | solution.py:11
where the time goes:
time: 542 us; the launch traced here: 540 us
  local copies, waits for them, and re-layouts  181 us (33%)
  starting transfers between devices  128 us (24%)
  matrix products  105 us (19%)
  blocking collectives  92.6 us (17%)
  waiting for transfers between devices  27 us (5%)
    ppermute x12, starting transfers between devices, shifted(): lax.ppermute(shard, axis, [(i, (i + by) % size) for i in range(size)])  128 us
    psum x1, blocking collectives, shards(): total_trace = lax.psum(jnp.sum(traces), ('blk', 'grp'))  92.6 us
    dot_general x4, local copies, waits for them, and re-layouts, one_row(): jnp.einsum('tus,tubc->tsbc', routing, far_tiles, preferred_element_type=j...  78.1 us
    dot_general x4, matrix products, one_row(): jnp.einsum('tus,tubc->tsbc', routing, far_tiles, preferred_element_type=j...  77.5 us
    gather x4, local copies, waits for them, and re-layouts, one_row(): far_tiles = row_tiles[position]  50.7 us
    dot_general x4, matrix products, one_row(): jnp.einsum('tab,tsbc->sac', own_tiles, panel, preferred_element_type=jnp....  27.4 us
    ppermute x12, waiting for transfers between devices, shifted(): lax.ppermute(shard, axis, [(i, (i + by) % size) for i in range(size)])  27 us
    while x12, local copies, waits for them, and re-layouts  15.1 us
  transfers between devices with their start and end apart: 12, of which 3 were waited for; matrix products, arithmetic and copies ran while one was open for 4% of the time, Pallas kernels for 0%

commit v1 on v0

v1 whole, which is shorter than its diff:
```python
import functools

import jax
import jax.numpy as jnp
from jax import lax
from jax.experimental import pallas as pl
from jax.experimental.pallas import tpu as pltpu
from jax.sharding import PartitionSpec as P

REACH = 12
AXES = ("blk", "grp")

FIRST = (2, 3, -3, -2)
SECOND = (-3, 2, -2, 3)
RELAY_FROM = (2, -5, 5, -2)
PARTNER = (1, -1, 1, -1)


def receive(shard, offsets):
    size = lax.axis_size(AXES)
    pairs = [((d + offsets[d % 4]) % size, d) for d in range(size)]
    return lax.ppermute(shard, AXES, pairs)


def body(rows, slots, block, window, piece_ids, final, has_prev, info, pos, *refs):
    refs = list(refs)
    take = lambda count: [refs.pop(0) for _ in range(count)]
    (own,) = take(1)
    sources = []
    for piece in piece_ids:
        sources.append(take({0: 0, 4: 2}.get(piece, 1)))
    prev = take(1)[0] if has_prev else None
    out = take(1)[0]
    trace_out = take(1)[0] if final else None
    own_stage, left, stage, right, total, out_stage = take(6)
    prev_stage = take(1)[0] if has_prev else None
    in_sem, own_sem, prev_sem, out_sem = take(4)
    span = rows * block
    chunks = window // rows

    def fetch(index, start):
        piece = piece_ids[index]
        source = sources[index]
        slot = index % 2
        if piece == 0:
            return
        if piece == 4:
            @pl.when(info[7] == 0)
            def _():
                copy = pltpu.make_async_copy(source[0], stage.at[slot], in_sem.at[slot])
                copy.start() if start else copy.wait()

            @pl.when(info[7] != 0)
            def _():
                copy = pltpu.make_async_copy(source[1], stage.at[slot], in_sem.at[slot])
                copy.start() if start else copy.wait()
        else:
            copy = pltpu.make_async_copy(source[0], stage.at[slot], in_sem.at[slot])
            copy.start() if start else copy.wait()

    own_copy = pltpu.make_async_copy(own, own_stage, own_sem)
    own_copy.start()
    fetch(0, True)
    if len(piece_ids) > 1:
        fetch(1, True)
    if has_prev:
        prev_copy = pltpu.make_async_copy(prev, prev_stage, prev_sem)
        prev_copy.start()

    def scatter(dense, source, place):
        dense[...] = jnp.zeros_like(dense)
        for r in range(rows):
            def one(u, carry):
                column = pl.multiple_of(pos[place * rows + r, u] * block, block)
                dense[r * block:(r + 1) * block, pl.ds(column, block)] = source[r, u]
                return carry
            lax.fori_loop(0, slots, one, 0, unroll=4)

    total[...] = jnp.zeros_like(total)
    own_copy.wait()
    scatter(left, own_stage, chunks // 2)

    for index, piece in enumerate(piece_ids):
        place = info[piece]
        fetch(index, False)
        if piece == 0:
            dense = left
        else:
            dense = right
            scatter(right, stage.at[index % 2], place)
            if index + 2 < len(piece_ids):
                fetch(index + 2, True)

        def multiply(n, carry):
            columns = pl.ds(pl.multiple_of(n * span, span), span)
            inner = pl.ds(pl.multiple_of(place * span, span), span)
            total[:, columns] += jnp.dot(
                left[:, inner], dense[:, columns], preferred_element_type=jnp.float32
            )
            return carry

        half = chunks // 2
        lax.fori_loop(jnp.maximum(0, place - half), jnp.minimum(chunks, place + half + 1), multiply, 0)

    if has_prev:
        prev_copy.wait()
    diagonal = jnp.zeros((block, block), jnp.float32)
    for r in range(rows):
        def emit(s, carry):
            column = pl.multiple_of(pos[rows * (chunks // 2) + r, s] * block, block)
            value = total[r * block:(r + 1) * block, pl.ds(column, block)]
            if has_prev:
                value = value + prev_stage[r, s]
            out_stage[r, s] = value.astype(out_stage.dtype)
            return carry
        lax.fori_loop(0, slots, emit, 0, unroll=2)
        copy = pltpu.make_async_copy(out_stage.at[r], out.at[r], out_sem.at[r])
        copy.start()
        if final:
            column = pl.multiple_of(pos[rows * (chunks // 2) + r, 0] * block, block)
            value = total[r * block:(r + 1) * block, pl.ds(column, block)]
            if has_prev:
                value = value + prev_stage[r, 0]
            diagonal = diagonal + value
    if final:
        on = lax.broadcasted_iota(jnp.int32, (block, block), 0) == lax.broadcasted_iota(
            jnp.int32, (block, block), 1
        )
        trace_out[...] = jnp.sum(jnp.where(on, diagonal, 0.0), axis=0, keepdims=True)
    for r in range(rows):
        pltpu.make_async_copy(out_stage.at[r], out.at[r], out_sem.at[r]).wait()


def partial_square(info, pos, own, pieces, prev, final):
    rows, slots, block, _ = own.shape
    window = pos.shape[0]
    span = rows * block
    piece_ids = tuple(p[0] for p in pieces)
    operands = [own]
    for _, arrays in pieces:
        operands.extend(arrays)
    if prev is not None:
        operands.append(prev)
    wide = (window + 1) * block
    scratch = [
        pltpu.VMEM(own.shape, own.dtype),
        pltpu.VMEM((span, wide), own.dtype),
        pltpu.VMEM((2,) + own.shape, own.dtype),
        pltpu.VMEM((span, wide), own.dtype),
        pltpu.VMEM((span, wide), jnp.float32),
        pltpu.VMEM(own.shape, own.dtype if final else jnp.float32),
    ]
    if prev is not None:
        scratch.append(pltpu.VMEM(own.shape, jnp.float32))
    scratch += [
        pltpu.SemaphoreType.DMA((2,)),
        pltpu.SemaphoreType.DMA,
        pltpu.SemaphoreType.DMA,
        pltpu.SemaphoreType.DMA((rows,)),
    ]
    any_spec = pl.BlockSpec(memory_space=pl.ANY)
    out_shape = [jax.ShapeDtypeStruct(own.shape, own.dtype if final else jnp.float32)]
    out_specs = [any_spec]
    if final:
        out_shape.append(jax.ShapeDtypeStruct((1, block), jnp.float32))
        out_specs.append(pl.BlockSpec(memory_space=pltpu.VMEM))
    count = len(piece_ids)
    return pl.pallas_call(
        functools.partial(body, rows, slots, block, window, piece_ids, final, prev is not None),
        out_shape=out_shape,
        grid_spec=pltpu.PrefetchScalarGridSpec(
            num_scalar_prefetch=2,
            grid=(),
            in_specs=[any_spec] * len(operands),
            out_specs=out_specs,
            scratch_shapes=scratch,
        ),
        compiler_params=pltpu.CompilerParams(vmem_limit_bytes=48 * 1024 * 1024),
        cost_estimate=pl.CostEstimate(
            flops=2 * span * span * window * block * count,
            bytes_accessed=own.size * 2 * (count + 2),
            transcendentals=0,
        ),
    )(info, pos, *operands)


def shards(tiles, columns):
    rows = tiles.shape[0]
    block = tiles.shape[2]
    devices = lax.axis_size(AXES)
    all_rows = rows * devices
    device = lax.axis_index(AXES)
    hops = (REACH + rows - 1) // rows
    assert hops == 3 and devices % 4 == 0 and devices > 8
    window = (2 * hops + 1) * rows

    first = receive(tiles, FIRST)
    second = receive(tiles, SECOND)
    beside = receive(tiles, PARTNER)
    all_cols = lax.all_gather(columns, AXES, tiled=True)
    start = jnp.mod((device - hops) * rows, all_rows)
    window_cols = lax.dynamic_slice_in_dim(jnp.concatenate([all_cols, all_cols]), start, window)
    pos = jnp.where(window_cols >= 0, jnp.mod(window_cols - start, all_rows), window)
    pos = jnp.minimum(pos, window).astype(jnp.int32)

    kind = device % 4
    other = kind ^ 1
    pick = lambda table: jnp.asarray(table, jnp.int32)
    first_off, second_off = pick(FIRST), pick(SECOND)
    relay_off = pick(tuple(RELAY_FROM[m] + FIRST[(m + RELAY_FROM[m]) % 4] for m in range(4)))
    beside_off = pick(PARTNER)[kind]
    use_second = jnp.abs(beside_off + first_off[other]) > hops
    beside_one = beside_off + jnp.where(use_second, second_off[other], first_off[other])
    info = jnp.stack([
        jnp.int32(0),
        beside_off,
        first_off[kind],
        second_off[kind],
        beside_one,
        relay_off[kind],
        beside_off + relay_off[other],
        use_second.astype(jnp.int32) - hops,
    ]) + hops

    acc = partial_square(info, pos, tiles, [(0, []), (1, [beside])], None, False)[0]
    relay = receive(first, RELAY_FROM)
    beside_first = receive(first, PARTNER)
    beside_second = receive(second, PARTNER)
    acc = partial_square(
        info, pos, tiles,
        [(2, [first]), (3, [second]), (4, [beside_first, beside_second])], acc, False,
    )[0]
    beside_relay = receive(relay, PARTNER)
    square, traces = partial_square(
        info, pos, tiles, [(5, [relay]), (6, [beside_relay])], acc, True
    )
    total_trace = lax.psum(jnp.sum(traces), AXES)
    return square, total_trace / (all_rows * block)


def solution(mesh):
    return jax.shard_map(
        shards,
        mesh=mesh,
        in_specs=(P(AXES, None, None, None), P(AXES, None)),
        out_specs=(P(AXES, None, None, None), P()),
        check_vma=False,
    )
```

time: 542 us -> 228 us (0.42)
  local copies, waits for them, and re-layouts: 181 us -> 8.38 us
  starting transfers between devices: 128 us -> 11.2 us
  matrix products: 105 us -> 0 us
  waiting for transfers between devices: 27 us -> 84.3 us
  Pallas kernels: 0 us -> 36.3 us
  blocking collectives: 92.6 us -> 78.5 us
    ppermute x12 -> x7, starting transfers between devices: 128 us -> 11.2 us  [receive(): return lax.ppermute(shard, AXES, pairs)]
    dot_general x8 -> x0, matrix products: 105 us -> none  [the longest x4 77.5 us: one_row(): jnp.einsum('tus,tubc->tsbc', routing, far_tiles, preferred_element_type=j...]
    dot_general x4 -> x0, local copies, waits for them, and re-layouts: 78.1 us -> none  [one_row(): jnp.einsum('tus,tubc->tsbc', routing, far_tiles, preferred_element_type=j...]
    ppermute x12 -> x7, waiting for transfers between devices: 27 us -> 84.3 us  [receive(): return lax.ppermute(shard, AXES, pairs)]
    psum x1, blocking collectives: 92.6 us -> 37.1 us  [shards(): total_trace = lax.psum(jnp.sum(traces), AXES)]
    gather x8 -> x0, local copies, waits for them, and re-layouts: 52.9 us -> none  [the longest x4 50.7 us: one_row(): far_tiles = row_tiles[position]]
    all_gather x0 -> x1, blocking collectives: none -> 41.4 us  [shards(): all_cols = lax.all_gather(columns, AXES, tiled=True)]
    pallas_call x0 -> x3, Pallas kernels: none -> 36.3 us  [partial_square(): pl.pallas_call(functools.partial(body, rows, slots, block, window, piece_...]
  transfers between devices with their start and end apart: 12 -> 7, of which waited for: 3 -> 2; matrix products, arithmetic and copies ran while one was open for 4% -> 3% of each run, Pallas kernels for 0% -> 11%
where the time goes in v1:
time: 228 us; the launch traced here: 226 us
  waiting for transfers between devices  84.3 us (37%)
  blocking collectives  78.5 us (34%)
  Pallas kernels  36.3 us (16%)
  starting transfers between devices  11.2 us (5%)
  local copies, waits for them, and re-layouts  8.38 us (4%)
  between operations  7.01 us (3%)
    ppermute x7, waiting for transfers between devices, receive(): return lax.ppermute(shard, AXES, pairs)  84.3 us
    all_gather x1, blocking collectives, shards(): all_cols = lax.all_gather(columns, AXES, tiled=True)  41.4 us
    psum x1, blocking collectives, shards(): total_trace = lax.psum(jnp.sum(traces), AXES)  37.1 us
    pallas_call x3, Pallas kernels, partial_square(): pl.pallas_call(functools.partial(body, rows, slots, block, window, piece_...  36.3 us
    ppermute x7, starting transfers between devices, receive(): return lax.ppermute(shard, AXES, pairs)  11.2 us
  transfers between devices with their start and end apart: 7, of which 2 were waited for; matrix products, arithmetic and copies ran while one was open for 3% of the time, Pallas kernels for 11%

profile of v1, /device:TPU:0, one launch (start us, length us, event | category | flops | bytes accessed | tf_op | source)
XLA Modules:
  0.0 226.3 jit_solution(629686963408933719)
XLA Ops:
  0.6 5.5 %collective-permute-start = (bf16[4,20,128,128]{3,2,1,0:T(8,128)(2,1)}, bf16[4,20,128,128]{3,2,1,0:T(8,128)(2,1)S(1)}, u32[]{:S(2)}, u32[]{:S(2)}) collective-permute-start(bf16[4,20,128,128]{3,2,1,0:T(8,128)(2,1)} %refs_0_.5), channel_id=1, source_target_pairs={{2,0},{4,1},{31,2},{1,3},{6,4},{8,5},{3,6},{5,7},{10,8},{12,9},{7,... | collective-permute-start | bytes 7864328 | tf_op jit(solution)/shard_map/ppermute | solution.py:22
  6.1 0.0 collective-permute-start.3
  6.1 54.5 %collective-permute-done.refs_1_ = bf16[4,20,128,128]{3,2,1,0:T(8,128)(2,1)S(1)} collective-permute-done((bf16[4,20,128,128]{3,2,1,0:T(8,128)(2,1)}, bf16[4,20,128,128]{3,2,1,0:T(8,128)(2,1)S(1)}, u32[]{:S(2)}, u32[]{:S(2)}) %collective-permute-start) | collective-permute-done | bytes 2621472 | tf_op jit(solution)/shard_map/ppermute | solution.py:22
  60.6 0.0 collective-permute-start.1
  60.6 1.4 collective-permute-start.6
  62.0 0.0 collective-permute-done.3.refs_2_
  62.0 0.0 collective-permute-start.5
  62.0 0.5 collective-permute-start.4
  62.5 29.8 %collective-permute-done.1.refs_1_ = bf16[4,20,128,128]{3,2,1,0:T(8,128)(2,1)} collective-permute-done((bf16[4,20,128,128]{3,2,1,0:T(8,128)(2,1)S(1)}, bf16[4,20,128,128]{3,2,1,0:T(8,128)(2,1)}, u32[]{:S(2)}, u32[]{:S(2)}) %collective-permute-start.1) | collective-permute-done | bytes 2621472 | tf_op jit(solution)/shard_map/ppermute | solution.py:22
  92.3 3.8 %collective-permute-start.2 = (bf16[4,20,128,128]{3,2,1,0:T(8,128)(2,1)}, bf16[4,20,128,128]{3,2,1,0:T(8,128)(2,1)}, u32[]{:S(2)}, u32[]{:S(2)}) collective-permute-start(bf16[4,20,128,128]{3,2,1,0:T(8,128)(2,1)} %collective-permute-done.1.refs_1_), channel_id=1, source_target_pairs={{1,0},{0,1},{3,2},{2,3},{5,4},{4,5},{7,6},{6,7},{9,8},{8,9},{11,10... | collective-permute-start | bytes 7864328 | tf_op jit(solution)/shard_map/ppermute | solution.py:22
  96.1 1.2 dynamic_slice.25
  97.4 1.4 fusion.6
  100.0 1.4 fusion.4
  104.7 2.6 %stack.15 = s32[8]{0:T(128)S(1)} concatenate(s32[1]{0:T(128)} %constant.54.clone.1, s32[1]{0:T(128)} %dynamic_slice.25, s32[1]{0:T(128)} %get-tuple-element.11, s32[1]{0:T(128)} %get-tuple-element.12, s32[1]{0:T(128)} %bitcast.3, s32[1]{0:T(128)} %get-tuple-element.7, s32[1]{0:T(128)} %bitcast.5, s32[1]{0:T(128)} %bitcast.6), dimensions={0} | concatenate | bytes 64 | tf_op jit(solution)/shard_map/stack | solution.py:214
  107.3 41.4 %all-gather = s32[32,4,20]{2,1,0:T(4,128)S(1)} all-gather(s32[1,4,20]{2,1,0:T(4,128)} %bitcast.10), channel_id=1, replica_groups=mesh['blk'=8,'grp'=4] {'blk','grp'}, dimensions={0}, use_global_device_ids=true | all-gather | bytes 10560 | tf_op jit(solution)/shard_map/all_gather | solution.py:200
  148.8 0.0 collective-permute-done.6.refs_1_
  148.8 0.0 copy-start
  148.8 1.7 copy-done
  150.5 11.6 %shard_map.77.refs_5_ = f32[4,20,128,128]{3,2,1,0:T(8,128)} custom-call(s32[8]{0:T(128)S(1)} %broadcast_add_fusion.info, s32[28,20]{1,0:T(8,128)S(1)} %fusion.2.pos, bf16[4,20,128,128]{3,2,1,0:T(8,128)(2,1)S(1)} %copy-done, bf16[4,20,128,128]{3,2,1,0:T(8,128)(2,1)} %collective-permute-done.6.refs_1_), custom_call_target="tpu_custom_call" | custom-call | flops 3758096384 | bytes 10485760 | tf_op jit(solution)/shard_map/pallas_call | solution.py:168
  162.1 0.0 collective-permute-done.5.refs_4_
  162.2 0.0 collective-permute-done.4.refs_3_
  162.2 13.6 %shard_map.78.refs_3_ = f32[4,20,128,128]{3,2,1,0:T(8,128)} custom-call(s32[8]{0:T(128)S(1)} %broadcast_add_fusion.info, s32[28,20]{1,0:T(8,128)S(1)} %fusion.2.pos, bf16[4,20,128,128]{3,2,1,0:T(8,128)(2,1)S(1)} %copy-done, bf16[4,20,128,128]{3,2,1,0:T(8,128)(2,1)S(1)} %collective-permute-done.refs_1_, ...), custom_call_target="tpu_custom_call" | custom-call | flops 5637144576 | bytes 13107200 | tf_op jit(solution)/shard_map/pallas_call | solution.py:168
  175.8 0.0 collective-permute-done.2.refs_2_
  175.8 11.1 %shard_map.79 = (bf16[4,20,128,128]{3,2,1,0:T(8,128)(2,1)}, f32[1,128]{1,0:T(1,128)S(1)}) custom-call(s32[8]{0:T(128)S(1)} %broadcast_add_fusion.info, s32[28,20]{1,0:T(8,128)S(1)} %fusion.2.pos, bf16[4,20,128,128]{3,2,1,0:T(8,128)(2,1)S(1)} %copy-done, bf16[4,20,128,128]{3,2,1,0:T(8,128)(2,1)} %collective-permute-done.1.refs_1_, ...), custom_call_target="tpu_custom_call" | custom-call | flops 3758096384 | bytes 10485760 | tf_op jit(solution)/shard_map/pallas_call | solution.py:168
  186.9 0.6 reduce_sum.9
  187.5 37.1 %psum.7 = f32[]{:T(128)} all-reduce(f32[]{:T(128)} %reduce_sum.9), channel_id=1, replica_groups=mesh['blk'=8,'grp'=4] {'blk','grp'}, use_global_device_ids=true, to_apply=%region_1.2 | all-reduce | flops 1 | bytes 8 | tf_op jit(solution)/shard_map/psum | solution.py:237
  (2 shorter events, 0.0 us)
Async XLA Ops:
  0.6 60.0 %collective-permute-start = (bf16[4,20,128,128]{3,2,1,0:T(8,128)(2,1)}, bf16[4,20,128,128]{3,2,1,0:T(8,128)(2,1)S(1)}, u32[]{:S(2)}, u32[]{:S(2)}) collective-permute-start(bf16[4,20,128,128]{3,2,1,0:T(8,128)(2,1)} %refs_0_.5), channel_id=1, source_target_pairs={{2,0},{4,1},{31,2},{1,3},{6,4},{8,5},{3,6},{5,7},{10,8},{12,9},{7,... | collective-permute-start | bytes 7864328 | tf_op jit(solution)/shard_map/ppermute | solution.py:22
  6.1 55.9 %collective-permute-start.3 = (bf16[4,20,128,128]{3,2,1,0:T(8,128)(2,1)}, bf16[4,20,128,128]{3,2,1,0:T(8,128)(2,1)}, u32[]{:S(2)}, u32[]{:S(2)}) collective-permute-start(bf16[4,20,128,128]{3,2,1,0:T(8,128)(2,1)} %refs_0_.5), channel_id=1, source_target_pairs={{29,0},{3,1},{0,2},{6,3},{1,4},{7,5},{4,6},{10,7},{5,8},{11,9},{8,... | collective-permute-start | bytes 7864328 | tf_op jit(solution)/shard_map/ppermute | solution.py:22
  60.6 31.8 %collective-permute-start.1 = (bf16[4,20,128,128]{3,2,1,0:T(8,128)(2,1)S(1)}, bf16[4,20,128,128]{3,2,1,0:T(8,128)(2,1)}, u32[]{:S(2)}, u32[]{:S(2)}) collective-permute-start(bf16[4,20,128,128]{3,2,1,0:T(8,128)(2,1)S(1)} %collective-permute-done.refs_1_), channel_id=1, source_target_pairs={{2,0},{28,1},{7,2},{1,3},{6,4},{0,5},{11,6},{5,7},{10,8},{4,9},{15... | collective-permute-start | bytes 7864328 | tf_op jit(solution)/shard_map/ppermute | solution.py:22
  60.6 88.2 %collective-permute-start.6 = (bf16[4,20,128,128]{3,2,1,0:T(8,128)(2,1)}, bf16[4,20,128,128]{3,2,1,0:T(8,128)(2,1)}, u32[]{:S(2)}, u32[]{:S(2)}) collective-permute-start(bf16[4,20,128,128]{3,2,1,0:T(8,128)(2,1)} %refs_0_.5), channel_id=1, source_target_pairs={{1,0},{0,1},{3,2},{2,3},{5,4},{4,5},{7,6},{6,7},{9,8},{8,9},{11,10... | collective-permute-start | bytes 7864328 | tf_op jit(solution)/shard_map/ppermute | solution.py:22
  62.0 100.2 %collective-permute-start.5 = (bf16[4,20,128,128]{3,2,1,0:T(8,128)(2,1)}, bf16[4,20,128,128]{3,2,1,0:T(8,128)(2,1)}, u32[]{:S(2)}, u32[]{:S(2)}) collective-permute-start(bf16[4,20,128,128]{3,2,1,0:T(8,128)(2,1)} %collective-permute-done.3.refs_2_), channel_id=1, source_target_pairs={{1,0},{0,1},{3,2},{2,3},{5,4},{4,5},{7,6},{6,7},{9,8},{8,9},{11,10... | collective-permute-start | bytes 7864328 | tf_op jit(solution)/shard_map/ppermute | solution.py:22
  62.0 100.2 %collective-permute-start.4 = (bf16[4,20,128,128]{3,2,1,0:T(8,128)(2,1)S(1)}, bf16[4,20,128,128]{3,2,1,0:T(8,128)(2,1)}, u32[]{:S(2)}, u32[]{:S(2)}) collective-permute-start(bf16[4,20,128,128]{3,2,1,0:T(8,128)(2,1)S(1)} %collective-permute-done.refs_1_), channel_id=1, source_target_pairs={{1,0},{0,1},{3,2},{2,3},{5,4},{4,5},{7,6},{6,7},{9,8},{8,9},{11,10... | collective-permute-start | bytes 7864328 | tf_op jit(solution)/shard_map/ppermute | solution.py:22
  92.3 83.4 %collective-permute-start.2 = (bf16[4,20,128,128]{3,2,1,0:T(8,128)(2,1)}, bf16[4,20,128,128]{3,2,1,0:T(8,128)(2,1)}, u32[]{:S(2)}, u32[]{:S(2)}) collective-permute-start(bf16[4,20,128,128]{3,2,1,0:T(8,128)(2,1)} %collective-permute-done.1.refs_1_), channel_id=1, source_target_pairs={{1,0},{0,1},{3,2},{2,3},{5,4},{4,5},{7,6},{6,7},{9,8},{8,9},{11,10... | collective-permute-start | bytes 7864328 | tf_op jit(solution)/shard_map/ppermute | solution.py:22
  148.8 1.7 copy-start

commit v2 on v0

v2 whole, which is shorter than its diff:
```python
import functools

import jax
import jax.numpy as jnp
from jax import lax
from jax.experimental import pallas as pl
from jax.experimental.pallas import tpu as pltpu
from jax.sharding import PartitionSpec as P

REACH = 12
AXES = ("blk", "grp")
EMPTY = 64
VMEM_LIMIT = 48 * 1024 * 1024

FIRST = (2, 3, -3, -2)
SECOND = (-3, 2, -2, 3)
RELAY_FROM = (2, -5, 5, -2)
PARTNER = (1, -1, 1, -1)
RELAY = tuple(RELAY_FROM[m] + FIRST[(m + RELAY_FROM[m]) % 4] for m in range(4))


def across(table):
    return tuple(PARTNER[m] + table[m ^ 1] for m in range(4))


USE_SECOND = tuple(int(abs(offset) > 3) for offset in across(FIRST))
MIXED = tuple(
    second if use else first
    for first, second, use in zip(across(FIRST), across(SECOND), USE_SECOND)
)
OFFSETS = {
    "own": (0, 0, 0, 0),
    "beside": PARTNER,
    "first": FIRST,
    "second": SECOND,
    "mixed": MIXED,
    "relay": RELAY,
    "relay_beside": across(RELAY),
}


def receive(shard, offsets):
    size = lax.axis_size(AXES)
    pairs = [((d + offsets[d % 4]) % size, d) for d in range(size)]
    return lax.ppermute(shard, AXES, pairs)


def total_over_devices(value):
    size = lax.axis_size(AXES)
    assert size & (size - 1) == 0
    step = 1
    while step < size:
        value = value + lax.ppermute(value, AXES, [(d, d ^ step) for d in range(size)])
        step *= 2
    return value


def pick(table, kind):
    value = jnp.int32(table[3])
    for m in range(3):
        value = jnp.where(kind == m, jnp.int32(table[m]), value)
    return value


def swapped(kind):
    return kind // 2


def pack_body(rows, slots, devices, tiles, columns, out, meta, sems):
    device = lax.axis_index(AXES)
    swap = swapped(device % 4)
    half = rows // 2
    copies = []
    for h in range(2):
        for r in range(half):
            source = tiles.at[half * (h ^ swap) + r]
            copies.append(pltpu.make_async_copy(
                source, out.at[h, pl.ds(r * slots, slots)], sems.at[h * half + r]
            ))
    for copy in copies:
        copy.start()
    cols = columns[...]
    row = device * rows + lax.broadcasted_iota(jnp.int32, cols.shape, 0)
    offset = cols - row
    size = rows * devices
    offset = jnp.where(offset > size // 2, offset - size, offset)
    offset = jnp.where(offset < -(size // 2), offset + size, offset)
    offset = jnp.where(cols < 0, EMPTY, offset)
    meta[...] = jnp.zeros_like(meta)
    meta[0:16, :] = offset.astype(jnp.float32).astype(meta.dtype)
    for h in range(2):
        copy = pltpu.make_async_copy(meta, out.at[h, half * slots], sems.at[rows + h])
        copy.start()
        copies.append(copy)
    for copy in copies:
        copy.wait()


def pack(tiles, columns, devices):
    rows, slots, block, _ = tiles.shape
    columns = jnp.pad(columns, ((0, 16 - rows), (0, block - slots)), constant_values=-1)
    return pl.pallas_call(
        functools.partial(pack_body, rows, slots, devices),
        out_shape=jax.ShapeDtypeStruct((2, rows // 2 * slots + 1, block, block), tiles.dtype),
        in_specs=[pl.BlockSpec(memory_space=pl.ANY), pl.BlockSpec(memory_space=pltpu.VMEM)],
        out_specs=pl.BlockSpec(memory_space=pl.ANY),
        scratch_shapes=[
            pltpu.VMEM((block, block), tiles.dtype),
            pltpu.SemaphoreType.DMA((rows + 2,)),
        ],
        cost_estimate=pl.CostEstimate(flops=0, bytes_accessed=4 * tiles.size, transcendentals=0),
    )(tiles, columns)


def body(rows, slots, block, window, names, half_index, begin, final, *refs):
    refs = list(refs)
    take = lambda count: [refs.pop(0) for _ in range(count)]
    if begin:
        own = take(1)[0]
    else:
        left_in, own_pos, prev = take(3)
    sources = {name: take(2 if name == "mixed" else 1) for name in names}
    out = take(1)[0]
    if begin:
        left_out, own_pos = take(2)
    if final:
        trace_out = take(1)[0]
    left, stage, right, total, out_stage, pos_vmem, pos = take(7)
    if not begin:
        prev_stage = take(1)[0]
    in_sem, left_sem, prev_sem, pos_sem, out_sem = take(5)

    device = lax.axis_index(AXES)
    kind = device % 4
    half = rows // 2
    span = rows * block
    part = half * block
    chunks = window // rows
    middle = chunks // 2
    whole = half_index is None
    place = {name: pick(OFFSETS[name], kind) + middle for name in names}
    base = {
        name: half * swapped((kind + pick(OFFSETS[name], kind) + 8) % 4)
        for name in names
    }

    def fetch(index, start):
        name = names[index]
        refs_in = sources[name]
        target = stage.at[index % 2]
        def go(source):
            copy = pltpu.make_async_copy(source, target, in_sem.at[index % 2])
            copy.start() if start else copy.wait()
        if len(refs_in) == 1:
            go(refs_in[0])
        else:
            use_second = pick(USE_SECOND, kind)
            pl.when(use_second == 0)(lambda: go(refs_in[0]))
            pl.when(use_second != 0)(lambda: go(refs_in[1]))

    def start_decode(offsets, spot, where):
        value = offsets.astype(jnp.float32).astype(jnp.int32)
        value = value + spot * rows + lax.broadcasted_iota(jnp.int32, value.shape, 0)
        value = jnp.where((value < 0) | (value > window), window, value)
        pos_vmem[where] = value
        copy = pltpu.make_async_copy(pos_vmem.at[where], pos.at[where], pos_sem.at[where])
        copy.start()
        return copy

    def scatter(dense, source, where, first_row):
        for r in range(half):
            def one(u, carry):
                column = pl.multiple_of(pos[where, first_row + r, u] * block, block)
                dense[r * block:(r + 1) * block, pl.ds(column, block)] = source[r * slots + u]
                return carry
            lax.fori_loop(0, slots, one, 0, unroll=4)

    if begin:
        own_copy = pltpu.make_async_copy(own, stage.at[1], left_sem)
        own_copy.start()
        fetch(0, True)
        total[...] = jnp.zeros_like(total)
        left[...] = jnp.zeros_like(left)
        own_copy.wait()
        start_decode(stage[1, 0, half * slots, 0:16, :], jnp.int32(middle), 2).wait()
        own_base = half * swapped(kind)
        for h in range(2):
            first_row = half - own_base if h else own_base
            top = pl.multiple_of(first_row * block, block)
            for r in range(half):
                def one(u, carry):
                    column = pl.multiple_of(pos[2, first_row + r, u] * block, block)
                    left[pl.ds(top + r * block, block), pl.ds(column, block)] = stage[1, h, r * slots + u]
                    return carry
                lax.fori_loop(0, slots, one, 0, unroll=4)
        left_copy = pltpu.make_async_copy(left, left_out, left_sem)
        left_copy.start()
        def save(index, carry):
            r, s = index // slots, index % slots
            own_pos[r, s] = pos[2, r, s]
            return carry
        lax.fori_loop(0, rows * slots, save, 0)
    else:
        left_copy = pltpu.make_async_copy(left_in, left, left_sem)
        left_copy.start()
        for index in range(min(2, len(names))):
            fetch(index, True)
        prev_copy = pltpu.make_async_copy(prev, prev_stage, prev_sem)
        prev_copy.start()
        total[...] = jnp.zeros_like(total)
        left_copy.wait()

    def multiply(spot, parts):
        def one(n, carry):
            columns = pl.ds(pl.multiple_of(n * span, span), span)
            value = total[:, columns]
            for first_row, dense in parts:
                inner = pl.ds(pl.multiple_of(first_row * block, part), part)
                value = value + jnp.dot(
                    left[:, inner], dense[:, columns], preferred_element_type=jnp.float32
                )
            total[:, columns] = value
            return carry
        lax.fori_loop(
            jnp.maximum(0, spot - middle), jnp.minimum(chunks, spot + middle + 1), one, 0
        )

    if begin:
        def own_product(n, carry):
            columns = pl.ds(pl.multiple_of(n * span, span), span)
            total[:, columns] += jnp.dot(
                left[:, middle * span:(middle + 1) * span], left[:, columns],
                preferred_element_type=jnp.float32,
            )
            return carry
        lax.fori_loop(0, chunks, own_product, 0)

    for index, name in enumerate(names):
        slot = index % 2
        spot = place[name]
        first_base = base[name]
        if whole:
            right[...] = jnp.zeros_like(right)
            fetch(index, False)
            start_decode(stage[slot, 0, half * slots, 0:16, :], spot, slot).wait()
            parts = []
            for h in range(2):
                first_row = half - first_base if h else first_base
                scatter(right.at[h], stage.at[slot, h], slot, first_row)
                parts.append((spot * rows + first_row, right.at[h]))
            if index + 2 < len(names):
                fetch(index + 2, True)
            multiply(spot, parts)
        else:
            dense = right.at[slot]
            dense[...] = jnp.zeros_like(dense)
            fetch(index, False)
            start_decode(stage[slot, half * slots, 0:16, :], spot, slot).wait()
            first_row = half - first_base if half_index else first_base
            scatter(dense, stage.at[slot], slot, first_row)
            multiply(spot, [(spot * rows + first_row, dense)])

    if not begin:
        prev_copy.wait()
    diagonal = jnp.zeros((block, block), jnp.float32)
    for r in range(rows):
        def block_at(s):
            column = pl.multiple_of(own_pos[r, s] * block, block)
            value = total[r * block:(r + 1) * block, pl.ds(column, block)]
            return value if begin else value + prev_stage[r, s]
        def emit(s, carry):
            out_stage[r, s] = block_at(s).astype(out_stage.dtype)
            return carry
        lax.fori_loop(0, slots, emit, 0, unroll=2)
        pltpu.make_async_copy(out_stage.at[r], out.at[r], out_sem.at[r]).start()
        if final:
            diagonal = diagonal + block_at(0)
    if final:
        on = lax.broadcasted_iota(jnp.int32, (block, block), 0) == lax.broadcasted_iota(
            jnp.int32, (block, block), 1
        )
        trace_out[...] = jnp.sum(jnp.where(on, diagonal, 0.0), axis=0, keepdims=True)
    if begin:
        left_copy.wait()
    for r in range(rows):
        pltpu.make_async_copy(out_stage.at[r], out.at[r], out_sem.at[r]).wait()


def product(shape, dtype, window, names, arrays, carried=None, own=None, half_index=None, final=False):
    rows, slots, block = shape
    span = rows * block
    begin = carried is None
    wide = (window + 1) * block
    any_spec = pl.BlockSpec(memory_space=pl.ANY)
    smem_spec = pl.BlockSpec(memory_space=pltpu.SMEM)
    if begin:
        operands, in_specs = [own], [any_spec]
    else:
        operands, in_specs = list(carried), [any_spec, smem_spec, any_spec]
    operands += arrays
    in_specs += [any_spec] * len(arrays)
    tile_shape = (rows, slots, block, block)
    out_shape = [jax.ShapeDtypeStruct(tile_shape, dtype if final else jnp.float32)]
    out_specs = [any_spec]
    if begin:
        out_shape += [
            jax.ShapeDtypeStruct((span, wide), dtype),
            jax.ShapeDtypeStruct((rows, slots), jnp.int32),
        ]
        out_specs += [any_spec, smem_spec]
    if final:
        out_shape.append(jax.ShapeDtypeStruct((1, block), jnp.float32))
        out_specs.append(pl.BlockSpec(memory_space=pltpu.VMEM))
    half_shape = (rows // 2 * slots + 1, block, block)
    scratch = [
        pltpu.VMEM((span, wide), dtype),
        pltpu.VMEM((2, 2) + half_shape if half_index is None else (2,) + half_shape, dtype),
        pltpu.VMEM((2, span // 2, wide), dtype),
        pltpu.VMEM((span, wide), jnp.float32),
        pltpu.VMEM(tile_shape, dtype if final else jnp.float32),
        pltpu.VMEM((3, 16, block), jnp.int32),
        pltpu.SMEM((3, 16, block), jnp.int32),
    ]
    if not begin:
        scratch.append(pltpu.VMEM(tile_shape, jnp.float32))
    scratch += [
        pltpu.SemaphoreType.DMA((2,)),
        pltpu.SemaphoreType.DMA,
        pltpu.SemaphoreType.DMA,
        pltpu.SemaphoreType.DMA((3,)),
        pltpu.SemaphoreType.DMA((rows,)),
    ]
    count = len(names) * (1 if half_index is None else 0.5) + begin
    return pl.pallas_call(
        functools.partial(body, rows, slots, block, window, names, half_index, begin, final),
        out_shape=out_shape,
        in_specs=in_specs,
        out_specs=out_specs,
        scratch_shapes=scratch,
        compiler_params=pltpu.CompilerParams(vmem_limit_bytes=VMEM_LIMIT),
        cost_estimate=pl.CostEstimate(
            flops=int(2 * span * span * window * block * count),
            bytes_accessed=int(2 * span * slots * block * (count + 4)),
            transcendentals=0,
        ),
    )(*operands)


def shards(tiles, columns):
    rows, slots, block, _ = tiles.shape
    devices = lax.axis_size(AXES)
    hops = (REACH + rows - 1) // rows
    assert hops == 3 and rows == 4 and devices % 4 == 0 and devices > 8
    window = (2 * hops + 1) * rows
    multiply = functools.partial(product, (rows, slots, block), tiles.dtype, window)

    payload = pack(tiles, columns, devices)
    first = receive(payload, FIRST)
    beside = receive(payload, PARTNER)
    later, beside = lax.optimization_barrier((payload, beside))
    second = receive(later, SECOND)
    total, left, own_pos = multiply(("beside",), [beside], own=payload)
    relays = [receive(first[h], RELAY_FROM) for h in range(2)]
    first_beside = receive(first, PARTNER)
    second_beside = receive(second, PARTNER)
    total = multiply(
        ("first", "second", "mixed"), [first, second, first_beside, second_beside],
        (left, own_pos, total),
    )[0]
    for h in range(2):
        relay_beside = receive(relays[h], PARTNER)
        result = multiply(
            ("relay", "relay_beside"), [relays[h], relay_beside], (left, own_pos, total),
            half_index=h, final=h == 1,
        )
        total = result[0]
    trace = jnp.sum(total_over_devices(result[1]))
    return total, trace / (rows * devices * block)


def solution(mesh):
    return jax.shard_map(
        shards,
        mesh=mesh,
        in_specs=(P(AXES, None, None, None), P(AXES, None)),
        out_specs=(P(AXES, None, None, None), P()),
        check_vma=False,
    )
```

time: 542 us -> 253 us (0.47)
  local copies, waits for them, and re-layouts: 181 us -> 3.13 us
  Pallas kernels: 0 us -> 132 us
  matrix products: 105 us -> 0 us
  starting transfers between devices: 128 us -> 25.4 us
  blocking collectives: 92.6 us -> 0 us
  waiting for transfers between devices: 27 us -> 89.7 us
    pallas_call x0 -> x5, Pallas kernels: none -> 132 us  [the longest x1 81.3 us: pack(): pl.pallas_call(functools.partial(pack_body, rows, slots, devices), out_sh...]
    dot_general x8 -> x0, matrix products: 105 us -> none  [the longest x4 77.5 us: one_row(): jnp.einsum('tus,tubc->tsbc', routing, far_tiles, preferred_element_type=j...]
    ppermute x12 -> x14, starting transfers between devices: 128 us -> 25.4 us  [the longest x9 25.4 us: receive(): return lax.ppermute(shard, AXES, pairs)]
    psum x1 -> x0, blocking collectives: 92.6 us -> none  [shards(): total_trace = lax.psum(jnp.sum(traces), ('blk', 'grp'))]
    dot_general x4 -> x0, local copies, waits for them, and re-layouts: 78.1 us -> none  [one_row(): jnp.einsum('tus,tubc->tsbc', routing, far_tiles, preferred_element_type=j...]
    ppermute x12 -> x14, waiting for transfers between devices: 27 us -> 89.7 us  [the longest x9 73.5 us: receive(): return lax.ppermute(shard, AXES, pairs)]
    gather x8 -> x0, local copies, waits for them, and re-layouts: 52.9 us -> none  [the longest x4 50.7 us: one_row(): far_tiles = row_tiles[position]]
    dynamic_update_slice x24 -> x0, local copies, waits for them, and re-layouts: 23.6 us -> none  [the longest x3 10.7 us: advance(): lax.dynamic_update_index_in_dim(tile_acc, lower_piece[0], below_slot, 0)]
  transfers between devices with their start and end apart: 12 -> 14, of which waited for: 3 -> 8; matrix products, arithmetic and copies ran while one was open for 4% -> 0% of each run, Pallas kernels for 0% -> 16%
where the time goes in v2:
time: 253 us
  Pallas kernels  132 us (52%)
  waiting for transfers between devices  89.7 us (35%)
  starting transfers between devices  25.4 us (10%)
  local copies, waits for them, and re-layouts  3.13 us (1%)
    pallas_call x1, Pallas kernels, pack(): pl.pallas_call(functools.partial(pack_body, rows, slots, devices), out_sh...  81.3 us
    ppermute x9, waiting for transfers between devices, receive(): return lax.ppermute(shard, AXES, pairs)  73.5 us
    pallas_call x4, Pallas kernels, product(): pl.pallas_call(functools.partial(body, rows, slots, block, window, names,...  50.4 us
    ppermute x9, starting transfers between devices, receive(): return lax.ppermute(shard, AXES, pairs)  25.4 us
    ppermute x5, waiting for transfers between devices, total_over_devices(): lax.ppermute(value, AXES, [(d, d ^ step) for d in range(size)])  16.2 us
  transfers between devices with their start and end apart: 14, of which 8 were waited for; matrix products, arithmetic and copies ran while one was open for 0% of the time, Pallas kernels for 16%

profile of v2, /device:TPU:0, one launch (start us, length us, event | category | flops | bytes accessed | tf_op | source)
XLA Modules:
  0.0 253.0 jit_solution(6384082973162980592)
XLA Ops:
  0.6 1.3 pad.4.columns
  1.9 81.3 %shard_map.41.refs_0_ = bf16[2,41,128,128]{3,2,1,0:T(8,128)(2,1)} custom-call(bf16[4,20,128,128]{3,2,1,0:T(8,128)(2,1)} %tiles.1, s32[16,128]{1,0:T(8,128)} %pad.4.columns), custom_call_target="tpu_custom_call" | custom-call | bytes 5242880 | tf_op jit(solution)/shard_map/pallas_call | solution.py:102
  83.2 0.0 copy-start
  83.2 0.5 collective-permute-start
  83.7 5.7 %collective-permute-start.1 = (bf16[2,41,128,128]{3,2,1,0:T(8,128)(2,1)}, bf16[2,41,128,128]{3,2,1,0:T(8,128)(2,1)S(1)}, u32[]{:S(2)}, u32[]{:S(2)}) collective-permute-start(bf16[2,41,128,128]{3,2,1,0:T(8,128)(2,1)} %shard_map.41.refs_0_), channel_id=1, source_target_pairs={{2,0},{4,1},{31,2},{1,3},{6,4},{8,5},{3,6},{5,7},{10,8},{12,9},{7,... | collective-permute-start | bytes 8060936 | tf_op jit(solution)/shard_map/ppermute | solution.py:45
  89.4 0.0 collective-permute-done.refs_1_
  89.4 0.0 copy-start.1
  89.4 1.6 copy-done.1
  91.0 2.0 collective-permute-start.2
  93.0 0.0 copy-start.2
  93.0 46.4 %collective-permute-done.1.refs_3_ = bf16[2,41,128,128]{3,2,1,0:T(8,128)(2,1)S(1)} collective-permute-done((bf16[2,41,128,128]{3,2,1,0:T(8,128)(2,1)}, bf16[2,41,128,128]{3,2,1,0:T(8,128)(2,1)S(1)}, u32[]{:S(2)}, u32[]{:S(2)}) %collective-permute-start.1) | collective-permute-done | bytes 2687008 | tf_op jit(solution)/shard_map/ppermute | solution.py:45
  139.4 6.1 %collective-permute-start.3 = (bf16[2,41,128,128]{3,2,1,0:T(8,128)(2,1)S(1)}, bf16[2,41,128,128]{3,2,1,0:T(8,128)(2,1)}, u32[]{:S(2)}, u32[]{:S(2)}) collective-permute-start(bf16[2,41,128,128]{3,2,1,0:T(8,128)(2,1)S(1)} %collective-permute-done.1.refs_3_), channel_id=1, source_target_pairs={{1,0},{0,1},{3,2},{2,3},{5,4},{4,5},{7,6},{6,7},{9,8},{8,9},{11,10... | collective-permute-start | bytes 8060936 | tf_op jit(solution)/shard_map/ppermute | solution.py:45
  145.5 0.0 collective-permute-done.2.refs_4_
  145.5 0.9 collective-permute-start.4
  146.3 0.3 slice_bitcast_fusion
  146.6 2.4 collective-permute-start.5
  149.0 0.7 collective-permute-start.7
  149.7 16.3 %collective-permute-done.5.refs_3_ = bf16[41,128,128]{2,1,0:T(8,128)(2,1)S(1)} collective-permute-done((bf16[41,128,128]{2,1,0:T(8,128)(2,1)S(1)}, bf16[41,128,128]{2,1,0:T(8,128)(2,1)S(1)}, u32[]{:S(2)}, u32[]{:S(2)}) %collective-permute-start.5) | collective-permute-done | bytes 1343520 | tf_op jit(solution)/shard_map/ppermute | solution.py:45
  166.0 3.5 %collective-permute-start.6 = (bf16[41,128,128]{2,1,0:T(8,128)(2,1)S(1)}, bf16[41,128,128]{2,1,0:T(8,128)(2,1)S(1)}, u32[]{:S(2)}, u32[]{:S(2)}) collective-permute-start(bf16[41,128,128]{2,1,0:T(8,128)(2,1)S(1)} %collective-permute-done.5.refs_3_), channel_id=1, source_target_pairs={{1,0},{0,1},{3,2},{2,3},{5,4},{4,5},{7,6},{6,7},{9,8},{8,9},{11,10... | collective-permute-start | bytes 4030472 | tf_op jit(solution)/shard_map/ppermute | solution.py:45
  169.5 10.9 %collective-permute-done.7.refs_3_ = bf16[41,128,128]{2,1,0:T(8,128)(2,1)S(1)} collective-permute-done((bf16[41,128,128]{2,1,0:T(8,128)(2,1)S(1)}, bf16[41,128,128]{2,1,0:T(8,128)(2,1)S(1)}, u32[]{:S(2)}, u32[]{:S(2)}) %collective-permute-start.7) | collective-permute-done | bytes 1343520 | tf_op jit(solution)/shard_map/ppermute | solution.py:45
  180.4 3.5 %collective-permute-start.8 = (bf16[41,128,128]{2,1,0:T(8,128)(2,1)S(1)}, bf16[41,128,128]{2,1,0:T(8,128)(2,1)S(1)}, u32[]{:S(2)}, u32[]{:S(2)}) collective-permute-start(bf16[41,128,128]{2,1,0:T(8,128)(2,1)S(1)} %collective-permute-done.7.refs_3_), channel_id=1, source_target_pairs={{1,0},{0,1},{3,2},{2,3},{5,4},{4,5},{7,6},{6,7},{9,8},{8,9},{11,10... | collective-permute-start | bytes 4030472 | tf_op jit(solution)/shard_map/ppermute | solution.py:45
  183.9 0.0 copy-done
  183.9 0.0 copy-done.2
  183.9 14.3 %shard_map.42 = (f32[4,20,128,128]{3,2,1,0:T(8,128)}, bf16[512,3712]{1,0:T(8,128)(2,1)}, s32[4,20]{1,0:T(4,128)S(1)}) custom-call(bf16[2,41,128,128]{3,2,1,0:T(8,128)(2,1)S(1)} %copy-done, bf16[2,41,128,128]{3,2,1,0:T(8,128)(2,1)S(1)} %copy-done.2), custom_call_target="tpu_custom_call" | custom-call | flops 3758096384 | bytes 15728640 | tf_op jit(solution)/shard_map/pallas_call | solution.py:334
  198.2 0.0 collective-permute-done.3.refs_5_
  198.2 0.0 collective-permute-done.4.refs_6_
  198.2 15.6 %shard_map.43.refs_2_ = f32[4,20,128,128]{3,2,1,0:T(8,128)} custom-call(bf16[512,3712]{1,0:T(8,128)(2,1)} %get-tuple-element.10.refs_0_, s32[4,20]{1,0:T(4,128)S(1)} %get-tuple-element.11.refs_1_, f32[4,20,128,128]{3,2,1,0:T(8,128)} %get-tuple-element.12.refs_2_, bf16[2,41,128,128]{3,2,1,0:T(8,128)(2,1)S(1)} %collective-permute-done.1.refs_3_, ...), custom_call_target="tpu_custom_call" | custom-call | flops 5637144576 | bytes 18350080 | tf_op jit(solution)/shard_map/pallas_call | solution.py:334
  213.8 0.0 collective-permute-done.6.refs_4_
  213.8 10.7 %shard_map.44.refs_2_ = f32[4,20,128,128]{3,2,1,0:T(8,128)} custom-call(bf16[512,3712]{1,0:T(8,128)(2,1)} %get-tuple-element.10.refs_0_, s32[4,20]{1,0:T(4,128)S(1)} %get-tuple-element.11.refs_1_, f32[4,20,128,128]{3,2,1,0:T(8,128)} %shard_map.43.refs_2_, bf16[41,128,128]{2,1,0:T(8,128)(2,1)S(1)} %collective-permute-done.5.refs_3_, ...), custom_call_target="tpu_custom_call" | custom-call | flops 1879048192 | bytes 13107200 | tf_op jit(solution)/shard_map/pallas_call | solution.py:334
  224.5 0.0 collective-permute-done.8.refs_4_
  224.5 9.9 %shard_map.45 = (bf16[4,20,128,128]{3,2,1,0:T(8,128)(2,1)}, f32[1,128]{1,0:T(1,128)S(1)}) custom-call(bf16[512,3712]{1,0:T(8,128)(2,1)} %get-tuple-element.10.refs_0_, s32[4,20]{1,0:T(4,128)S(1)} %get-tuple-element.11.refs_1_, f32[4,20,128,128]{3,2,1,0:T(8,128)} %shard_map.44.refs_2_, bf16[41,128,128]{2,1,0:T(8,128)(2,1)S(1)} %collective-permute-done.7.refs_3_, ...), custom_call_target="tpu_custom_call" | custom-call | flops 1879048192 | bytes 13107200 | tf_op jit(solution)/shard_map/pallas_call | solution.py:334
  234.4 0.1 collective-permute-start.9
  234.5 1.1 collective-permute-done.9
  235.6 0.0 collective-permute-start.10
  235.6 3.5 %collective-permute-done.10 = f32[1,128]{1,0:T(1,128)S(1)} collective-permute-done((f32[1,128]{1,0:T(1,128)S(1)}, f32[1,128]{1,0:T(1,128)S(1)}, u32[]{:S(2)}, u32[]{:S(2)}) %collective-permute-start.10) | collective-permute-done | bytes 544 | tf_op jit(solution)/shard_map/ppermute | solution.py:53
  239.1 0.0 collective-permute-start.11
  239.1 3.5 %collective-permute-done.11 = f32[1,128]{1,0:T(1,128)S(1)} collective-permute-done((f32[1,128]{1,0:T(1,128)S(1)}, f32[1,128]{1,0:T(1,128)S(1)}, u32[]{:S(2)}, u32[]{:S(2)}) %collective-permute-start.11) | collective-permute-done | bytes 544 | tf_op jit(solution)/shard_map/ppermute | solution.py:53
  242.7 0.0 collective-permute-start.12
  242.7 3.5 %collective-permute-done.12 = f32[1,128]{1,0:T(1,128)S(1)} collective-permute-done((f32[1,128]{1,0:T(1,128)S(1)}, f32[1,128]{1,0:T(1,128)S(1)}, u32[]{:S(2)}, u32[]{:S(2)}) %collective-permute-start.12) | collective-permute-done | bytes 544 | tf_op jit(solution)/shard_map/ppermute | solution.py:53
  246.2 0.0 collective-permute-start.13
  246.2 4.4 %collective-permute-done.13 = f32[1,128]{1,0:T(1,128)S(1)} collective-permute-done((f32[1,128]{1,0:T(1,128)S(1)}, f32[1,128]{1,0:T(1,128)S(1)}, u32[]{:S(2)}, u32[]{:S(2)}) %collective-permute-start.13) | collective-permute-done | bytes 544 | tf_op jit(solution)/shard_map/ppermute | solution.py:53
  250.6 0.6 add_reduce_fusion
  (4 shorter events, 0.0 us)
Async XLA Ops:
  83.2 100.7 %copy-start = (bf16[2,41,128,128]{3,2,1,0:T(8,128)(2,1)S(1)}, bf16[2,41,128,128]{3,2,1,0:T(8,128)(2,1)}, u32[]{:S(2)}) copy-start(bf16[2,41,128,128]{3,2,1,0:T(8,128)(2,1)} %shard_map.41.refs_0_) | copy-start | bytes 8060932
  83.2 6.2 %collective-permute-start = (bf16[2,41,128,128]{3,2,1,0:T(8,128)(2,1)}, bf16[2,41,128,128]{3,2,1,0:T(8,128)(2,1)S(1)}, u32[]{:S(2)}, u32[]{:S(2)}) collective-permute-start(bf16[2,41,128,128]{3,2,1,0:T(8,128)(2,1)} %shard_map.41.refs_0_), channel_id=1, source_target_pairs={{1,0},{0,1},{3,2},{2,3},{5,4},{4,5},{7,6},{6,7},{9,8},{8,9},{11,10... | collective-permute-start | bytes 8060936 | tf_op jit(solution)/shard_map/ppermute | solution.py:45
  83.7 55.7 %collective-permute-start.1 = (bf16[2,41,128,128]{3,2,1,0:T(8,128)(2,1)}, bf16[2,41,128,128]{3,2,1,0:T(8,128)(2,1)S(1)}, u32[]{:S(2)}, u32[]{:S(2)}) collective-permute-start(bf16[2,41,128,128]{3,2,1,0:T(8,128)(2,1)} %shard_map.41.refs_0_), channel_id=1, source_target_pairs={{2,0},{4,1},{31,2},{1,3},{6,4},{8,5},{3,6},{5,7},{10,8},{12,9},{7,... | collective-permute-start | bytes 8060936 | tf_op jit(solution)/shard_map/ppermute | solution.py:45
  89.4 1.6 copy-start.1
  91.0 54.5 %collective-permute-start.2 = (bf16[2,41,128,128]{3,2,1,0:T(8,128)(2,1)}, bf16[2,41,128,128]{3,2,1,0:T(8,128)(2,1)S(1)}, u32[]{:S(2)}, u32[]{:S(2)}) collective-permute-start(bf16[2,41,128,128]{3,2,1,0:T(8,128)(2,1)} %shard_map.41.refs_0_), channel_id=1, source_target_pairs={{29,0},{3,1},{0,2},{6,3},{1,4},{7,5},{4,6},{10,7},{5,8},{11,9},{8,... | collective-permute-start | bytes 8060936 | tf_op jit(solution)/shard_map/ppermute | solution.py:45
  93.0 90.9 %copy-start.2 = (bf16[2,41,128,128]{3,2,1,0:T(8,128)(2,1)S(1)}, bf16[2,41,128,128]{3,2,1,0:T(8,128)(2,1)}, u32[]{:S(2)}) copy-start(bf16[2,41,128,128]{3,2,1,0:T(8,128)(2,1)} %copy-done.1) | copy-start | bytes 8060932
  139.4 58.8 %collective-permute-start.3 = (bf16[2,41,128,128]{3,2,1,0:T(8,128)(2,1)S(1)}, bf16[2,41,128,128]{3,2,1,0:T(8,128)(2,1)}, u32[]{:S(2)}, u32[]{:S(2)}) collective-permute-start(bf16[2,41,128,128]{3,2,1,0:T(8,128)(2,1)S(1)} %collective-permute-done.1.refs_3_), channel_id=1, source_target_pairs={{1,0},{0,1},{3,2},{2,3},{5,4},{4,5},{7,6},{6,7},{9,8},{8,9},{11,10... | collective-permute-start | bytes 8060936 | tf_op jit(solution)/shard_map/ppermute | solution.py:45
  145.5 52.8 %collective-permute-start.4 = (bf16[2,41,128,128]{3,2,1,0:T(8,128)(2,1)S(1)}, bf16[2,41,128,128]{3,2,1,0:T(8,128)(2,1)}, u32[]{:S(2)}, u32[]{:S(2)}) collective-permute-start(bf16[2,41,128,128]{3,2,1,0:T(8,128)(2,1)S(1)} %collective-permute-done.2.refs_4_), channel_id=1, source_target_pairs={{1,0},{0,1},{3,2},{2,3},{5,4},{4,5},{7,6},{6,7},{9,8},{8,9},{11,10... | collective-permute-start | bytes 8060936 | tf_op jit(solution)/shard_map/ppermute | solution.py:45
  146.6 19.4 %collective-permute-start.5 = (bf16[41,128,128]{2,1,0:T(8,128)(2,1)S(1)}, bf16[41,128,128]{2,1,0:T(8,128)(2,1)S(1)}, u32[]{:S(2)}, u32[]{:S(2)}) collective-permute-start(bf16[41,128,128]{2,1,0:T(8,128)(2,1)S(1)} %get-tuple-element.17), channel_id=1, source_target_pairs={{2,0},{28,1},{7,2},{1,3},{6,4},{0,5},{11,6},{5,7},{10,8},{4,9},{15... | collective-permute-start | bytes 4030472 | tf_op jit(solution)/shard_map/ppermute | solution.py:45
  149.0 31.4 %collective-permute-start.7 = (bf16[41,128,128]{2,1,0:T(8,128)(2,1)S(1)}, bf16[41,128,128]{2,1,0:T(8,128)(2,1)S(1)}, u32[]{:S(2)}, u32[]{:S(2)}) collective-permute-start(bf16[41,128,128]{2,1,0:T(8,128)(2,1)S(1)} %get-tuple-element.16), channel_id=1, source_target_pairs={{2,0},{28,1},{7,2},{1,3},{6,4},{0,5},{11,6},{5,7},{10,8},{4,9},{15... | collective-permute-start | bytes 4030472 | tf_op jit(solution)/shard_map/ppermute | solution.py:45
  166.0 47.8 %collective-permute-start.6 = (bf16[41,128,128]{2,1,0:T(8,128)(2,1)S(1)}, bf16[41,128,128]{2,1,0:T(8,128)(2,1)S(1)}, u32[]{:S(2)}, u32[]{:S(2)}) collective-permute-start(bf16[41,128,128]{2,1,0:T(8,128)(2,1)S(1)} %collective-permute-done.5.refs_3_), channel_id=1, source_target_pairs={{1,0},{0,1},{3,2},{2,3},{5,4},{4,5},{7,6},{6,7},{9,8},{8,9},{11,10... | collective-permute-start | bytes 4030472 | tf_op jit(solution)/shard_map/ppermute | solution.py:45
  180.4 44.1 %collective-permute-start.8 = (bf16[41,128,128]{2,1,0:T(8,128)(2,1)S(1)}, bf16[41,128,128]{2,1,0:T(8,128)(2,1)S(1)}, u32[]{:S(2)}, u32[]{:S(2)}) collective-permute-start(bf16[41,128,128]{2,1,0:T(8,128)(2,1)S(1)} %collective-permute-done.7.refs_3_), channel_id=1, source_target_pairs={{1,0},{0,1},{3,2},{2,3},{5,4},{4,5},{7,6},{6,7},{9,8},{8,9},{11,10... | collective-permute-start | bytes 4030472 | tf_op jit(solution)/shard_map/ppermute | solution.py:45
  234.4 1.2 collective-permute-start.9
  235.6 3.5 %collective-permute-start.10 = (f32[1,128]{1,0:T(1,128)S(1)}, f32[1,128]{1,0:T(1,128)S(1)}, u32[]{:S(2)}, u32[]{:S(2)}) collective-permute-start(f32[1,128]{1,0:T(1,128)S(1)} %add.17), channel_id=1, source_target_pairs={{0,2},{1,3},{2,0},{3,1},{4,6},{5,7},{6,4},{7,5},{8,10},{9,11},{10,... | collective-permute-start | bytes 1544 | tf_op jit(solution)/shard_map/ppermute | solution.py:53
  239.1 3.5 %collective-permute-start.11 = (f32[1,128]{1,0:T(1,128)S(1)}, f32[1,128]{1,0:T(1,128)S(1)}, u32[]{:S(2)}, u32[]{:S(2)}) collective-permute-start(f32[1,128]{1,0:T(1,128)S(1)} %add.18), channel_id=1, source_target_pairs={{0,4},{1,5},{2,6},{3,7},{4,0},{5,1},{6,2},{7,3},{8,12},{9,13},{10,... | collective-permute-start | bytes 1544 | tf_op jit(solution)/shard_map/ppermute | solution.py:53
  242.7 3.5 %collective-permute-start.12 = (f32[1,128]{1,0:T(1,128)S(1)}, f32[1,128]{1,0:T(1,128)S(1)}, u32[]{:S(2)}, u32[]{:S(2)}) collective-permute-start(f32[1,128]{1,0:T(1,128)S(1)} %add.19), channel_id=1, source_target_pairs={{0,8},{1,9},{2,10},{3,11},{4,12},{5,13},{6,14},{7,15},{8,0},{9,1},... | collective-permute-start | bytes 1544 | tf_op jit(solution)/shard_map/ppermute | solution.py:53
  246.2 4.4 %collective-permute-start.13 = (f32[1,128]{1,0:T(1,128)S(1)}, f32[1,128]{1,0:T(1,128)S(1)}, u32[]{:S(2)}, u32[]{:S(2)}) collective-permute-start(f32[1,128]{1,0:T(1,128)S(1)} %add.20), channel_id=1, source_target_pairs={{0,16},{1,17},{2,18},{3,19},{4,20},{5,21},{6,22},{7,23},{8,24},{9,... | collective-permute-start | bytes 1544 | tf_op jit(solution)/shard_map/ppermute | solution.py:53

commit v3 on v0

v3 whole, which is shorter than its diff:
```python
import functools

import jax
import jax.numpy as jnp
from jax import lax
from jax.experimental import pallas as pl
from jax.experimental.pallas import tpu as pltpu
from jax.sharding import PartitionSpec as P

REACH = 12
AXES = ("blk", "grp")
VMEM_LIMIT = 48 * 1024 * 1024

FIRST = (2, 3, -3, -2)
SECOND = (-3, 2, -2, 3)
RELAY_FROM = (2, -5, 5, -2)
PARTNER = (1, -1, 1, -1)
RELAY = tuple(RELAY_FROM[m] + FIRST[(m + RELAY_FROM[m]) % 4] for m in range(4))


def across(table):
    return tuple(PARTNER[m] + table[m ^ 1] for m in range(4))


USE_SECOND = tuple(int(abs(offset) > 3) for offset in across(FIRST))
MIXED = tuple(
    second if use else first
    for first, second, use in zip(across(FIRST), across(SECOND), USE_SECOND)
)
OFFSETS = {
    "beside": PARTNER,
    "first": FIRST,
    "second": SECOND,
    "mixed": MIXED,
    "relay": RELAY,
    "relay_beside": across(RELAY),
}
COUNTS = {"beside": (2, 0, 2, 0), "first": (2, 0, 2, 0), "second": (2, 2, 0, 0), "mixed": (2, 2, 0, 0)}
OUTSIDE = {("first", "mixed"): (0, 2, 2, 0), ("first", "second"): (0, 2, 0, 0)}
CORNER = {1: -3, 2: 3}


def receive(shard, offsets, kinds=range(4)):
    size = lax.axis_size(AXES)
    pairs = [((d + offsets[d % 4]) % size, d) for d in range(size) if d % 4 in kinds]
    return lax.ppermute(shard, AXES, pairs)


def total_over_devices(value):
    size = lax.axis_size(AXES)
    assert size & (size - 1) == 0
    step = 1
    while step < size:
        value = value + lax.ppermute(value, AXES, [(d, d ^ step) for d in range(size)])
        step *= 2
    return value


def pick(table, kind):
    value = jnp.int32(table[3])
    for m in range(3):
        value = jnp.where(kind == m, jnp.int32(table[m]), value)
    return value


def aligned(index, unit):
    return pl.multiple_of(index * unit, unit)


class Sizes:
    def __init__(self, shape, devices):
        self.rows, self.slots, self.block, _ = shape
        self.hops = (REACH + self.rows - 1) // self.rows
        self.chunks = 2 * self.hops + 1
        self.window = self.chunks * self.rows
        self.span = self.rows * self.block
        self.wide = (self.window + 1) * self.block
        self.all_rows = self.rows * devices

    def start(self, device):
        start = (device - self.hops) * self.rows
        return jnp.where(start < 0, start + self.all_rows, start)

    def position(self, column, start):
        place = column - start
        place = jnp.where(place < 0, place + self.all_rows, place)
        place = jnp.where(column < 0, self.window, place)
        return jnp.minimum(place, self.window)


def scatter(z, dense, top, source, columns, start, save=None):
    for r in range(z.rows):
        def one(u, carry):
            place = z.position(columns[r, u], start)
            if save is not None:
                save[r, u] = place
            dense[top + r * z.block:top + (r + 1) * z.block, pl.ds(aligned(place, z.block), z.block)] = source[r, u]
            return carry
        lax.fori_loop(0, z.slots, one, 0, unroll=4)


def emit(z, total, positions, stage, out, sems, prev=None):
    for r in range(z.rows):
        def one(s, carry):
            value = total[r * z.block:(r + 1) * z.block, pl.ds(aligned(positions[r, s], z.block), z.block)]
            if prev is not None:
                value = value + prev[r, s]
            stage[r, s] = value.astype(stage.dtype)
            return carry
        lax.fori_loop(0, z.slots, one, 0, unroll=4)
        pltpu.make_async_copy(stage.at[r], out.at[r], sems.at[r]).start()
    for r in range(z.rows):
        pltpu.make_async_copy(stage.at[r], out.at[r], sems.at[r]).wait()


def add_trace(trace, weight, one, other):
    value = jnp.dot(one, other, preferred_element_type=jnp.float32)
    on = lax.broadcasted_iota(jnp.int32, value.shape, 0) == lax.broadcasted_iota(jnp.int32, value.shape, 1)
    diagonal = jnp.sum(jnp.where(on, value, 0.0), axis=0, keepdims=True)
    trace[:, :value.shape[1]] += weight.astype(jnp.float32) * diagonal


def own_body(z, own, columns, out, left_out, corner_out, positions, trace, stage, left, total, out_stage,
             in_sem, left_sem, corner_sem, out_sems):
    device = lax.axis_index(AXES)
    kind = device % 4
    copy = pltpu.make_async_copy(own, stage, in_sem)
    copy.start()
    left[...] = jnp.zeros_like(left)
    total[:, z.window * z.block:] = jnp.zeros((z.span, z.block), jnp.float32)
    copy.wait()
    scatter(z, left, 0, stage, columns, z.start(device), positions)
    left_copy = pltpu.make_async_copy(left, left_out, left_sem)
    left_copy.start()
    half = z.span // 2

    def corner(start):
        def go(rows, cols):
            copy = pltpu.make_async_copy(left.at[rows, cols], corner_out, corner_sem)
            copy.start() if start else copy.wait()
        pl.when(kind == 1)(lambda: go(pl.ds(0, half), pl.ds(0, z.span)))
        pl.when(kind != 1)(
            lambda: go(pl.ds(half, half), pl.ds((z.chunks - 1) * z.span, z.span))
        )

    corner(True)
    middle = slice(z.hops * z.span, (z.hops + 1) * z.span)

    def multiply(n, carry):
        cols = pl.ds(aligned(n, z.span), z.span)
        total[:, cols] = jnp.dot(left[:, middle], left[:, cols], preferred_element_type=jnp.float32)
        return carry

    lax.fori_loop(0, z.chunks, multiply, 0)
    trace[...] = jnp.zeros_like(trace)
    add_trace(trace, jnp.float32(1), left[:, middle], left[:, middle])
    emit(z, total, positions, out_stage, out, out_sems)
    corner(False)
    left_copy.wait()


def near_body(z, names, left_in, positions, prev, trace_in, corner, *refs):
    refs = list(refs)
    take = lambda count: [refs.pop(0) for _ in range(count)]
    columns = dict(zip(names, take(len(names))))
    sources = {name: take(2 if name == "mixed" else 1) for name in names}
    out, relay_left, trace = take(3)
    left, stage, right, total, out_stage, prev_stage = take(6)
    left_sem, in_sem, prev_sem, relay_sem, out_sems = take(5)
    device = lax.axis_index(AXES)
    kind = device % 4
    start = z.start(device)
    place = {name: pick(table, kind) + z.hops for name, table in OFFSETS.items()}

    def chunk(n):
        return pl.ds(aligned(n, z.span), z.span)

    def fetch(index, begin):
        def go(source):
            copy = pltpu.make_async_copy(source, stage.at[index % 2], in_sem.at[index % 2])
            copy.start() if begin else copy.wait()
        source = sources[names[index]]
        if len(source) == 1:
            go(source[0])
        else:
            use_second = pick(USE_SECOND, kind)
            pl.when(use_second == 0)(lambda: go(source[0]))
            pl.when(use_second != 0)(lambda: go(source[1]))

    left_copy = pltpu.make_async_copy(left_in, left, left_sem)
    left_copy.start()
    fetch(0, True)
    fetch(1, True)
    prev_copy = pltpu.make_async_copy(prev, prev_stage, prev_sem)
    prev_copy.start()
    total[...] = jnp.zeros_like(total)
    trace[...] = trace_in[...]
    left_copy.wait()
    relay_copies = []
    for index, name in enumerate(("relay", "relay_beside")):
        copy = pltpu.make_async_copy(
            left.at[:, chunk(place[name])], relay_left.at[:, pl.ds(index * z.span, z.span)], relay_sem.at[index]
        )
        copy.start()
        relay_copies.append(copy)
    dense_of = {}
    for index, name in enumerate(names):
        dense = right.at[index]
        dense_of[name] = dense
        spot = place[name]
        dense[...] = jnp.zeros_like(dense)
        fetch(index, False)
        scatter(z, dense, 0, stage.at[index % 2], columns[name], start)
        if index + 2 < len(names):
            fetch(index + 2, True)

        def multiply(n, carry):
            total[:, chunk(n)] += jnp.dot(
                left[:, chunk(spot)], dense[:, chunk(n)], preferred_element_type=jnp.float32
            )
            return carry

        lax.fori_loop(jnp.maximum(0, spot - z.hops), jnp.minimum(z.chunks, spot + z.hops + 1), multiply, 0)
        weight = pick(COUNTS[name], kind)
        pl.when(weight != 0)(
            lambda: add_trace(trace, weight, left[:, chunk(spot)], dense[:, chunk(z.hops)])
        )
    for (one, other), table in OUTSIDE.items():
        weight = pick(table, kind)
        pl.when(weight != 0)(lambda: add_trace(
            trace, weight, dense_of[one][:, chunk(place[other])], dense_of[other][:, chunk(place[one])]
        ))
    half = z.span // 2
    last = (z.chunks - 1) * z.span
    pl.when(kind == 1)(lambda: add_trace(trace, jnp.float32(2), left[:, half:z.span], corner[...]))
    pl.when(kind == 2)(
        lambda: add_trace(trace, jnp.float32(2), left[:half, last:last + half], corner[:, :half])
    )
    prev_copy.wait()
    emit(z, total, positions, out_stage, out, out_sems, prev_stage)
    for copy in relay_copies:
        copy.wait()


def last_body(z, left_in, positions, prev, columns_a, columns_b, source_a, source_b, out,
              left, stage, right, total, out_stage, prev_stage, left_sem, in_sem, prev_sem, out_sems):
    device = lax.axis_index(AXES)
    kind = device % 4
    start = z.start(device)
    copies = [
        pltpu.make_async_copy(source_a, stage.at[0], in_sem.at[0]),
        pltpu.make_async_copy(source_b, stage.at[1], in_sem.at[1]),
        pltpu.make_async_copy(left_in, left, left_sem),
        pltpu.make_async_copy(prev, prev_stage, prev_sem),
    ]
    for copy in copies:
        copy.start()
    place_a = pick(OFFSETS["relay"], kind) + z.hops
    place_b = pick(OFFSETS["relay_beside"], kind) + z.hops
    low = jnp.maximum(0, jnp.minimum(place_a, place_b) - z.hops)
    high = jnp.minimum(z.chunks, jnp.maximum(place_a, place_b) + z.hops + 1)

    def chunk(n):
        return pl.ds(aligned(n, z.span), z.span)

    def clear_total(n, carry):
        total[:, chunk(n)] = jnp.zeros((z.span, z.span), jnp.float32)
        return carry

    def clear_right(n, carry):
        right[:, chunk(n)] = jnp.zeros((2 * z.span, z.span), right.dtype)
        return carry

    lax.fori_loop(low, high, clear_right, 0)
    lax.fori_loop(0, low, clear_total, 0)
    lax.fori_loop(high, z.chunks, clear_total, 0)
    total[:, z.window * z.block:] = jnp.zeros((z.span, z.block), jnp.float32)
    copies[0].wait()
    scatter(z, right, 0, stage.at[0], columns_a, start)
    copies[1].wait()
    scatter(z, right, z.span, stage.at[1], columns_b, start)
    copies[2].wait()

    def multiply(n, carry):
        total[:, chunk(n)] = jnp.dot(left[...], right[:, chunk(n)], preferred_element_type=jnp.float32)
        return carry

    lax.fori_loop(low, high, multiply, 0)
    copies[3].wait()
    emit(z, total, positions, out_stage, out, out_sems, prev_stage)


ANY = pl.BlockSpec(memory_space=pl.ANY)
SMEM = pl.BlockSpec(memory_space=pltpu.SMEM)
VMEM = pl.BlockSpec(memory_space=pltpu.VMEM)
DMA = pltpu.SemaphoreType.DMA


def call(z, kernel, operands, in_specs, out_shape, out_specs, scratch, pieces):
    return pl.pallas_call(
        kernel,
        out_shape=out_shape,
        in_specs=in_specs,
        out_specs=out_specs,
        scratch_shapes=scratch,
        compiler_params=pltpu.CompilerParams(vmem_limit_bytes=VMEM_LIMIT),
        cost_estimate=pl.CostEstimate(
            flops=2 * z.span * z.span * z.window * z.block * pieces,
            bytes_accessed=2 * z.span * z.slots * z.block * (pieces + 4),
            transcendentals=0,
        ),
    )(*operands)


def shards(tiles, columns):
    devices = lax.axis_size(AXES)
    z = Sizes(tiles.shape, devices)
    assert z.hops == 3 and z.rows == 4 and devices % 4 == 0 and devices > 8
    dtype = tiles.dtype
    shape = jax.ShapeDtypeStruct
    sums = shape(tiles.shape, jnp.float32)
    line = shape((1, z.span), jnp.float32)
    dense = pltpu.VMEM((z.span, z.wide), dtype)
    total_buffer = pltpu.VMEM((z.span, z.wide), jnp.float32)

    first = receive(tiles, FIRST)
    second = receive(tiles, SECOND)
    column_of = {name: receive(columns, table) for name, table in OFFSETS.items()}
    beside = receive(tiles, PARTNER)

    total, left, corner, positions, trace = call(
        z, functools.partial(own_body, z), [tiles, columns], [ANY, SMEM],
        [
            sums, shape((z.span, z.wide), dtype), shape((z.span // 2, z.span), dtype),
            shape((z.rows, z.slots), jnp.int32), line,
        ],
        [ANY, ANY, ANY, SMEM, VMEM],
        [
            pltpu.VMEM(tiles.shape, dtype), dense, total_buffer, pltpu.VMEM(tiles.shape, jnp.float32),
            DMA, DMA, DMA, DMA((z.rows,)),
        ],
        1,
    )
    corner = receive(corner, (0, CORNER[1], CORNER[2], 0), (1, 2))
    first, second, beside, column_of, corner, total = lax.optimization_barrier(
        (first, second, beside, column_of, corner, total)
    )
    relay = receive(first, RELAY_FROM)
    mixed = [
        receive(first, PARTNER, [m for m in range(4) if not USE_SECOND[m]]),
        receive(second, PARTNER, [m for m in range(4) if USE_SECOND[m]]),
    ]
    names = ("beside", "first", "second", "mixed")
    total, relay_left, trace = call(
        z, functools.partial(near_body, z, names),
        [left, positions, total, trace, corner, *[column_of[name] for name in names], beside, first, second, *mixed],
        [ANY, SMEM, ANY, VMEM, VMEM] + [SMEM] * 4 + [ANY] * 5,
        [sums, shape((z.span, 2 * z.span), dtype), line],
        [ANY, ANY, VMEM],
        [
            dense, pltpu.VMEM((2,) + tiles.shape, dtype), pltpu.VMEM((4, z.span, z.wide), dtype), total_buffer,
            pltpu.VMEM(tiles.shape, jnp.float32), pltpu.VMEM(tiles.shape, jnp.float32),
            DMA, DMA((2,)), DMA, DMA((2,)), DMA((z.rows,)),
        ],
        4,
    )
    relay, total, trace = lax.optimization_barrier((relay, total, trace))
    relay_beside = receive(relay, PARTNER)
    trace = total_over_devices(trace)
    square = call(
        z, functools.partial(last_body, z),
        [
            relay_left, positions, total, column_of["relay"], column_of["relay_beside"], relay, relay_beside,
        ],
        [ANY, SMEM, ANY, SMEM, SMEM, ANY, ANY],
        [shape(tiles.shape, dtype)],
        [ANY],
        [
            pltpu.VMEM((z.span, 2 * z.span), dtype), pltpu.VMEM((2,) + tiles.shape, dtype),
            pltpu.VMEM((2 * z.span, z.wide), dtype), total_buffer,
            pltpu.VMEM(tiles.shape, dtype), pltpu.VMEM(tiles.shape, jnp.float32),
            DMA, DMA((2,)), DMA, DMA((z.rows,)),
        ],
        2,
    )[0]
    return square, jnp.sum(trace) / (z.all_rows * z.block)


def solution(mesh):
    return jax.shard_map(
        shards,
        mesh=mesh,
        in_specs=(P(AXES, None, None, None), P(AXES, None)),
        out_specs=(P(AXES, None, None, None), P()),
        check_vma=False,
    )
```

time: 542 us -> 158 us (0.29)
  local copies, waits for them, and re-layouts: 181 us -> 6.21 us
  matrix products: 105 us -> 0 us
  starting transfers between devices: 128 us -> 28.7 us
  blocking collectives: 92.6 us -> 0 us
  waiting for transfers between devices: 27 us -> 81.9 us
  Pallas kernels: 0 us -> 37.5 us
    dot_general x8 -> x0, matrix products: 105 us -> none  [the longest x4 77.5 us: one_row(): jnp.einsum('tus,tubc->tsbc', routing, far_tiles, preferred_element_type=j...]
    ppermute x12 -> x19, starting transfers between devices: 128 us -> 28.7 us  [the longest x14 28.7 us: receive(): return lax.ppermute(shard, AXES, pairs)]
    psum x1 -> x0, blocking collectives: 92.6 us -> none  [shards(): total_trace = lax.psum(jnp.sum(traces), ('blk', 'grp'))]
    dot_general x4 -> x0, local copies, waits for them, and re-layouts: 78.1 us -> none  [one_row(): jnp.einsum('tus,tubc->tsbc', routing, far_tiles, preferred_element_type=j...]
    ppermute x12 -> x19, waiting for transfers between devices: 27 us -> 81.9 us  [the longest x14 62.3 us: receive(): return lax.ppermute(shard, AXES, pairs)]
    gather x8 -> x0, local copies, waits for them, and re-layouts: 52.9 us -> none  [the longest x4 50.7 us: one_row(): far_tiles = row_tiles[position]]
    pallas_call x0 -> x3, Pallas kernels: none -> 37.5 us  [call(): pl.pallas_call(kernel, out_shape=out_shape, in_specs=in_specs, out_specs=...]
    dynamic_update_slice x24 -> x0, local copies, waits for them, and re-layouts: 23.6 us -> none  [the longest x3 10.7 us: advance(): lax.dynamic_update_index_in_dim(tile_acc, lower_piece[0], below_slot, 0)]
  transfers between devices with their start and end apart: 12 -> 19, of which waited for: 3 -> 14; matrix products, arithmetic and copies ran while one was open for 4% -> 0% of each run, Pallas kernels for 0% -> 18%
where the time goes in v3:
time: 158 us; the launch traced here: 157 us
  waiting for transfers between devices  81.9 us (52%)
  Pallas kernels  37.5 us (24%)
  starting transfers between devices  28.7 us (18%)
  local copies, waits for them, and re-layouts  6.21 us (4%)
  between operations  2.55 us (2%)
    ppermute x14, waiting for transfers between devices, receive(): return lax.ppermute(shard, AXES, pairs)  62.3 us
    pallas_call x3, Pallas kernels, call(): pl.pallas_call(kernel, out_shape=out_shape, in_specs=in_specs, out_specs=...  37.5 us
    ppermute x14, starting transfers between devices, receive(): return lax.ppermute(shard, AXES, pairs)  28.7 us
    ppermute x5, waiting for transfers between devices, total_over_devices(): lax.ppermute(value, AXES, [(d, d ^ step) for d in range(size)])  19.6 us
    unnamed x16, local copies, waits for them, and re-layouts  6.21 us
  transfers between devices with their start and end apart: 19, of which 14 were waited for; matrix products, arithmetic and copies ran while one was open for 0% of the time, Pallas kernels for 18%

profile of v3, /device:TPU:0, one launch (start us, length us, event | category | flops | bytes accessed | tf_op | source)
XLA Modules:
  0.0 157.5 jit_solution(768245736356971514)
XLA Ops:
  0.6 5.5 %collective-permute-start = (bf16[4,20,128,128]{3,2,1,0:T(8,128)(2,1)}, bf16[4,20,128,128]{3,2,1,0:T(8,128)(2,1)S(1)}, u32[]{:S(2)}, u32[]{:S(2)}) collective-permute-start(bf16[4,20,128,128]{3,2,1,0:T(8,128)(2,1)} %own.1), channel_id=1, source_target_pairs={{2,0},{4,1},{31,2},{1,3},{6,4},{8,5},{3,6},{5,7},{10,8},{12,9},{7,... | collective-permute-start | bytes 7864328 | tf_op jit(solution)/shard_map/ppermute | solution.py:46
  6.1 0.0 collective-permute-start.1
  6.1 0.0 collective-permute-start.2
  6.1 0.0 copy-start.2
  6.1 1.8 %copy-done.2 = bf16[4,20,128,128]{3,2,1,0:T(8,128)(2,1)S(1)} copy-done((bf16[4,20,128,128]{3,2,1,0:T(8,128)(2,1)S(1)}, bf16[4,20,128,128]{3,2,1,0:T(8,128)(2,1)}, u32[]{:S(2)}) %copy-start.2) | copy-done | bytes 2621464
  7.9 0.0 copy-start.3
  7.9 0.7 copy-done.3
  8.6 8.4 %shard_map.41 = (f32[4,20,128,128]{3,2,1,0:T(8,128)}, bf16[512,3712]{1,0:T(8,128)(2,1)}, bf16[256,512]{1,0:T(8,128)(2,1)S(1)}, s32[4,20]{1,0:T(4,128)S(1)}, f32[1,512]{1,0:T(1,128)S(1)}) custom-call(bf16[4,20,128,128]{3,2,1,0:T(8,128)(2,1)S(1)} %copy-done.2, s32[4,20]{1,0:T(4,128)S(1)} %copy-done.3), custom_call_target="tpu_custom_call" | custom-call | flops 1879048192 | bytes 13107200 | tf_op jit(solution)/shard_map/pallas_call | solution.py:300
  17.1 0.7 collective-permute-start.9
  17.8 4.6 %collective-permute-start.3 = (s32[4,20]{1,0:T(4,128)S(1)}, s32[4,20]{1,0:T(4,128)S(1)}, u32[]{:S(2)}, u32[]{:S(2)}) collective-permute-start(s32[4,20]{1,0:T(4,128)S(1)} %copy-done.3), channel_id=1, source_target_pairs={{1,0},{0,1},{3,2},{2,3},{5,4},{4,5},{7,6},{6,7},{9,8},{8,9},{11,10... | collective-permute-start | bytes 968 | tf_op jit(solution)/shard_map/ppermute | solution.py:46
  22.4 0.8 collective-permute-done.3.refs_0_
  23.2 1.4 collective-permute-start.4
  24.6 39.8 %collective-permute-done.4.refs_1_ = s32[4,20]{1,0:T(4,128)S(1)} collective-permute-done((s32[4,20]{1,0:T(4,128)S(1)}, s32[4,20]{1,0:T(4,128)S(1)}, u32[]{:S(2)}, u32[]{:S(2)}) %collective-permute-start.4) | collective-permute-done | bytes 352 | tf_op jit(solution)/shard_map/ppermute | solution.py:46
  64.4 0.2 collective-permute-start.5
  64.7 2.8 %collective-permute-done.5.refs_3_ = s32[4,20]{1,0:T(4,128)S(1)} collective-permute-done((s32[4,20]{1,0:T(4,128)S(1)}, s32[4,20]{1,0:T(4,128)S(1)}, u32[]{:S(2)}, u32[]{:S(2)}) %collective-permute-start.5) | collective-permute-done | bytes 352 | tf_op jit(solution)/shard_map/ppermute | solution.py:46
  67.4 4.6 %collective-permute-start.6 = (s32[4,20]{1,0:T(4,128)S(1)}, s32[4,20]{1,0:T(4,128)S(1)}, u32[]{:S(2)}, u32[]{:S(2)}) collective-permute-start(s32[4,20]{1,0:T(4,128)S(1)} %copy-done.3), channel_id=1, source_target_pairs={{31,0},{30,1},{5,2},{4,3},{3,4},{2,5},{9,6},{8,7},{7,8},{6,9},{13,... | collective-permute-start | bytes 968 | tf_op jit(solution)/shard_map/ppermute | solution.py:46
  72.0 2.0 %collective-permute-done.6.columns_a = s32[4,20]{1,0:T(4,128)S(1)} collective-permute-done((s32[4,20]{1,0:T(4,128)S(1)}, s32[4,20]{1,0:T(4,128)S(1)}, u32[]{:S(2)}, u32[]{:S(2)}) %collective-permute-start.6) | collective-permute-done | bytes 352 | tf_op jit(solution)/shard_map/ppermute | solution.py:46
  74.1 5.4 %collective-permute-start.7 = (s32[4,20]{1,0:T(4,128)S(1)}, s32[4,20]{1,0:T(4,128)S(1)}, u32[]{:S(2)}, u32[]{:S(2)}) collective-permute-start(s32[4,20]{1,0:T(4,128)S(1)} %copy-done.3), channel_id=1, source_target_pairs={{30,0},{31,1},{4,2},{5,3},{2,4},{3,5},{8,6},{9,7},{6,8},{7,9},{12,... | collective-permute-start | bytes 968 | tf_op jit(solution)/shard_map/ppermute | solution.py:46
  79.4 1.8 %collective-permute-done.7.columns_b = s32[4,20]{1,0:T(4,128)S(1)} collective-permute-done((s32[4,20]{1,0:T(4,128)S(1)}, s32[4,20]{1,0:T(4,128)S(1)}, u32[]{:S(2)}, u32[]{:S(2)}) %collective-permute-start.7) | collective-permute-done | bytes 352 | tf_op jit(solution)/shard_map/ppermute | solution.py:46
  81.2 0.0 collective-permute-start.8
  81.2 5.7 %collective-permute-done.8.refs_2_ = s32[4,20]{1,0:T(4,128)S(1)} collective-permute-done((s32[4,20]{1,0:T(4,128)S(1)}, s32[4,20]{1,0:T(4,128)S(1)}, u32[]{:S(2)}, u32[]{:S(2)}) %collective-permute-start.8) | collective-permute-done | bytes 352 | tf_op jit(solution)/shard_map/ppermute | solution.py:46
  86.9 0.0 collective-permute-done.9.corner
  86.9 0.0 collective-permute-done.refs_5_
  87.0 0.0 copy-start.4
  87.0 0.0 collective-permute-done.1.refs_6_
  87.0 0.0 copy-start.5
  87.0 0.0 collective-permute-done.2.refs_4_
  87.0 1.5 collective-permute-start.10
  88.5 1.3 collective-permute-start.11
  89.8 0.1 collective-permute-start.12
  89.8 3.0 %collective-permute-done.10.refs_7_ = bf16[4,20,128,128]{3,2,1,0:T(8,128)(2,1)S(1)} collective-permute-done((bf16[4,20,128,128]{3,2,1,0:T(8,128)(2,1)S(1)}, bf16[4,20,128,128]{3,2,1,0:T(8,128)(2,1)S(1)}, u32[]{:S(2)}, u32[]{:S(2)}) %collective-permute-start.10) | collective-permute-done | bytes 2621472 | tf_op jit(solution)/shard_map/ppermute | solution.py:46
  92.8 0.0 copy-start.6
  92.8 2.5 %collective-permute-done.11.refs_8_ = bf16[4,20,128,128]{3,2,1,0:T(8,128)(2,1)S(1)} collective-permute-done((bf16[4,20,128,128]{3,2,1,0:T(8,128)(2,1)S(1)}, bf16[4,20,128,128]{3,2,1,0:T(8,128)(2,1)S(1)}, u32[]{:S(2)}, u32[]{:S(2)}) %collective-permute-start.11) | collective-permute-done | bytes 2621472 | tf_op jit(solution)/shard_map/ppermute | solution.py:46
  95.3 0.0 copy-start.7
  95.3 0.0 copy-done.6
  95.3 1.5 copy-done.7
  96.8 0.0 copy-done.4
  96.8 0.0 copy-done.5
  96.8 19.7 %shard_map.42 = (f32[4,20,128,128]{3,2,1,0:T(8,128)}, bf16[512,1024]{1,0:T(8,128)(2,1)S(1)}, f32[1,512]{1,0:T(1,128)S(1)}) custom-call(bf16[512,3712]{1,0:T(8,128)(2,1)} %get-tuple-element.24.left_in, s32[4,20]{1,0:T(4,128)S(1)} %get-tuple-element.25.positions, f32[4,20,128,128]{3,2,1,0:T(8,128)} %get-tuple-element.28.prev, ...), custom_call_target="tpu_custom_call" | custom-call | flops 7516192768 | bytes 20971520 | tf_op jit(solution)/shard_map/pallas_call | solution.py:300
  116.5 0.0 copy-start
  116.5 1.0 copy-done
  117.5 4.0 %collective-permute-done.12.source_a = bf16[4,20,128,128]{3,2,1,0:T(8,128)(2,1)S(1)} collective-permute-done((bf16[4,20,128,128]{3,2,1,0:T(8,128)(2,1)S(1)}, bf16[4,20,128,128]{3,2,1,0:T(8,128)(2,1)S(1)}, u32[]{:S(2)}, u32[]{:S(2)}) %collective-permute-start.12) | collective-permute-done | bytes 2621472 | tf_op jit(solution)/shard_map/ppermute | solution.py:46
  121.5 3.4 %collective-permute-start.13 = (bf16[4,20,128,128]{3,2,1,0:T(8,128)(2,1)S(1)}, bf16[4,20,128,128]{3,2,1,0:T(8,128)(2,1)}, u32[]{:S(2)}, u32[]{:S(2)}) collective-permute-start(bf16[4,20,128,128]{3,2,1,0:T(8,128)(2,1)S(1)} %collective-permute-done.12.source_a), channel_id=1, source_target_pairs={{1,0},{0,1},{3,2},{2,3},{5,4},{4,5},{7,6},{6,7},{9,8},{8,9},{11,10... | collective-permute-start | bytes 7864328 | tf_op jit(solution)/shard_map/ppermute | solution.py:46
  124.9 0.0 collective-permute-start.14
  124.9 4.4 %collective-permute-done.14 = f32[1,512]{1,0:T(1,128)S(1)} collective-permute-done((f32[1,512]{1,0:T(1,128)S(1)}, f32[1,512]{1,0:T(1,128)S(1)}, u32[]{:S(2)}, u32[]{:S(2)}) %collective-permute-start.14) | collective-permute-done | bytes 2080 | tf_op jit(solution)/shard_map/ppermute | solution.py:54
  129.3 0.0 collective-permute-start.15
  129.3 3.6 %collective-permute-done.15 = f32[1,512]{1,0:T(1,128)S(1)} collective-permute-done((f32[1,512]{1,0:T(1,128)S(1)}, f32[1,512]{1,0:T(1,128)S(1)}, u32[]{:S(2)}, u32[]{:S(2)}) %collective-permute-start.15) | collective-permute-done | bytes 2080 | tf_op jit(solution)/shard_map/ppermute | solution.py:54
  132.9 0.0 collective-permute-start.16
  132.9 3.6 %collective-permute-done.16 = f32[1,512]{1,0:T(1,128)S(1)} collective-permute-done((f32[1,512]{1,0:T(1,128)S(1)}, f32[1,512]{1,0:T(1,128)S(1)}, u32[]{:S(2)}, u32[]{:S(2)}) %collective-permute-start.16) | collective-permute-done | bytes 2080 | tf_op jit(solution)/shard_map/ppermute | solution.py:54
  136.5 0.0 collective-permute-start.17
  136.5 3.6 %collective-permute-done.17 = f32[1,512]{1,0:T(1,128)S(1)} collective-permute-done((f32[1,512]{1,0:T(1,128)S(1)}, f32[1,512]{1,0:T(1,128)S(1)}, u32[]{:S(2)}, u32[]{:S(2)}) %collective-permute-start.17) | collective-permute-done | bytes 2080 | tf_op jit(solution)/shard_map/ppermute | solution.py:54
  140.1 0.0 collective-permute-start.18
  140.1 4.5 %collective-permute-done.18 = f32[1,512]{1,0:T(1,128)S(1)} collective-permute-done((f32[1,512]{1,0:T(1,128)S(1)}, f32[1,512]{1,0:T(1,128)S(1)}, u32[]{:S(2)}, u32[]{:S(2)}) %collective-permute-start.18) | collective-permute-done | bytes 2080 | tf_op jit(solution)/shard_map/ppermute | solution.py:54
  144.5 0.6 add_reduce_fusion
  145.8 0.0 collective-permute-done.13.source_b
  145.8 0.0 copy-start.1
  145.8 1.2 copy-done.1
  147.0 9.3 %shard_map.43 = bf16[4,20,128,128]{3,2,1,0:T(8,128)(2,1)} custom-call(bf16[512,1024]{1,0:T(8,128)(2,1)S(1)} %copy-done.1, s32[4,20]{1,0:T(4,128)S(1)} %get-tuple-element.25.positions, f32[4,20,128,128]{3,2,1,0:T(8,128)} %get-tuple-element.41.prev, s32[4,20]{1,0:T(4,128)S(1)} %collective-permute-done.6.columns_a, ...), custom_call_target="tpu_custom_call" | custom-call | flops 3758096384 | bytes 15728640 | tf_op jit(solution)/shard_map/pallas_call | solution.py:300
  (4 shorter events, 0.0 us)
Async XLA Ops:
  0.6 86.3 %collective-permute-start = (bf16[4,20,128,128]{3,2,1,0:T(8,128)(2,1)}, bf16[4,20,128,128]{3,2,1,0:T(8,128)(2,1)S(1)}, u32[]{:S(2)}, u32[]{:S(2)}) collective-permute-start(bf16[4,20,128,128]{3,2,1,0:T(8,128)(2,1)} %own.1), channel_id=1, source_target_pairs={{2,0},{4,1},{31,2},{1,3},{6,4},{8,5},{3,6},{5,7},{10,8},{12,9},{7,... | collective-permute-start | bytes 7864328 | tf_op jit(solution)/shard_map/ppermute | solution.py:46
  6.1 80.8 %collective-permute-start.1 = (bf16[4,20,128,128]{3,2,1,0:T(8,128)(2,1)}, bf16[4,20,128,128]{3,2,1,0:T(8,128)(2,1)S(1)}, u32[]{:S(2)}, u32[]{:S(2)}) collective-permute-start(bf16[4,20,128,128]{3,2,1,0:T(8,128)(2,1)} %own.1), channel_id=1, source_target_pairs={{29,0},{3,1},{0,2},{6,3},{1,4},{7,5},{4,6},{10,7},{5,8},{11,9},{8,... | collective-permute-start | bytes 7864328 | tf_op jit(solution)/shard_map/ppermute | solution.py:46
  6.1 80.8 %collective-permute-start.2 = (bf16[4,20,128,128]{3,2,1,0:T(8,128)(2,1)}, bf16[4,20,128,128]{3,2,1,0:T(8,128)(2,1)S(1)}, u32[]{:S(2)}, u32[]{:S(2)}) collective-permute-start(bf16[4,20,128,128]{3,2,1,0:T(8,128)(2,1)} %own.1), channel_id=1, source_target_pairs={{1,0},{0,1},{3,2},{2,3},{5,4},{4,5},{7,6},{6,7},{9,8},{8,9},{11,10... | collective-permute-start | bytes 7864328 | tf_op jit(solution)/shard_map/ppermute | solution.py:46
  6.1 1.8 %copy-start.2 = (bf16[4,20,128,128]{3,2,1,0:T(8,128)(2,1)S(1)}, bf16[4,20,128,128]{3,2,1,0:T(8,128)(2,1)}, u32[]{:S(2)}) copy-start(bf16[4,20,128,128]{3,2,1,0:T(8,128)(2,1)} %own.1) | copy-start | bytes 7864324
  7.9 0.7 copy-start.3
  17.1 69.9 %collective-permute-start.9 = (bf16[256,512]{1,0:T(8,128)(2,1)S(1)}, bf16[256,512]{1,0:T(8,128)(2,1)S(1)}, u32[]{:S(2)}, u32[]{:S(2)}) collective-permute-start(bf16[256,512]{1,0:T(8,128)(2,1)S(1)} %get-tuple-element.26), channel_id=1, source_target_pairs={{30,1},{5,2},{2,5},{9,6},{6,9},{13,10},{10,13},{17,14},{14,17},{21... | collective-permute-start | bytes 786440 | tf_op jit(solution)/shard_map/ppermute | solution.py:46
  17.8 5.4 %collective-permute-start.3 = (s32[4,20]{1,0:T(4,128)S(1)}, s32[4,20]{1,0:T(4,128)S(1)}, u32[]{:S(2)}, u32[]{:S(2)}) collective-permute-start(s32[4,20]{1,0:T(4,128)S(1)} %copy-done.3), channel_id=1, source_target_pairs={{1,0},{0,1},{3,2},{2,3},{5,4},{4,5},{7,6},{6,7},{9,8},{8,9},{11,10... | collective-permute-start | bytes 968 | tf_op jit(solution)/shard_map/ppermute | solution.py:46
  23.2 41.2 %collective-permute-start.4 = (s32[4,20]{1,0:T(4,128)S(1)}, s32[4,20]{1,0:T(4,128)S(1)}, u32[]{:S(2)}, u32[]{:S(2)}) collective-permute-start(s32[4,20]{1,0:T(4,128)S(1)} %copy-done.3), channel_id=1, source_target_pairs={{2,0},{4,1},{31,2},{1,3},{6,4},{8,5},{3,6},{5,7},{10,8},{12,9},{7,... | collective-permute-start | bytes 968 | tf_op jit(solution)/shard_map/ppermute | solution.py:46
  64.4 3.0 %collective-permute-start.5 = (s32[4,20]{1,0:T(4,128)S(1)}, s32[4,20]{1,0:T(4,128)S(1)}, u32[]{:S(2)}, u32[]{:S(2)}) collective-permute-start(s32[4,20]{1,0:T(4,128)S(1)} %copy-done.3), channel_id=1, source_target_pairs={{3,0},{2,1},{1,2},{0,3},{7,4},{6,5},{5,6},{4,7},{11,8},{10,9},{9,1... | collective-permute-start | bytes 968 | tf_op jit(solution)/shard_map/ppermute | solution.py:46
  67.4 6.6 %collective-permute-start.6 = (s32[4,20]{1,0:T(4,128)S(1)}, s32[4,20]{1,0:T(4,128)S(1)}, u32[]{:S(2)}, u32[]{:S(2)}) collective-permute-start(s32[4,20]{1,0:T(4,128)S(1)} %copy-done.3), channel_id=1, source_target_pairs={{31,0},{30,1},{5,2},{4,3},{3,4},{2,5},{9,6},{8,7},{7,8},{6,9},{13,... | collective-permute-start | bytes 968 | tf_op jit(solution)/shard_map/ppermute | solution.py:46
  74.1 7.2 %collective-permute-start.7 = (s32[4,20]{1,0:T(4,128)S(1)}, s32[4,20]{1,0:T(4,128)S(1)}, u32[]{:S(2)}, u32[]{:S(2)}) collective-permute-start(s32[4,20]{1,0:T(4,128)S(1)} %copy-done.3), channel_id=1, source_target_pairs={{30,0},{31,1},{4,2},{5,3},{2,4},{3,5},{8,6},{9,7},{6,8},{7,9},{12,... | collective-permute-start | bytes 968 | tf_op jit(solution)/shard_map/ppermute | solution.py:46
  81.2 5.7 %collective-permute-start.8 = (s32[4,20]{1,0:T(4,128)S(1)}, s32[4,20]{1,0:T(4,128)S(1)}, u32[]{:S(2)}, u32[]{:S(2)}) collective-permute-start(s32[4,20]{1,0:T(4,128)S(1)} %copy-done.3), channel_id=1, source_target_pairs={{29,0},{3,1},{0,2},{6,3},{1,4},{7,5},{4,6},{10,7},{5,8},{11,9},{8,... | collective-permute-start | bytes 968 | tf_op jit(solution)/shard_map/ppermute | solution.py:46
  87.0 9.8 %copy-start.4 = (bf16[4,20,128,128]{3,2,1,0:T(8,128)(2,1)}, bf16[4,20,128,128]{3,2,1,0:T(8,128)(2,1)S(1)}, u32[]{:S(2)}) copy-start(bf16[4,20,128,128]{3,2,1,0:T(8,128)(2,1)S(1)} %collective-permute-done.refs_5_) | copy-start | bytes 7864324
  87.0 9.8 %copy-start.5 = (bf16[4,20,128,128]{3,2,1,0:T(8,128)(2,1)}, bf16[4,20,128,128]{3,2,1,0:T(8,128)(2,1)S(1)}, u32[]{:S(2)}) copy-start(bf16[4,20,128,128]{3,2,1,0:T(8,128)(2,1)S(1)} %collective-permute-done.1.refs_6_) | copy-start | bytes 7864324
  87.0 5.8 %collective-permute-start.10 = (bf16[4,20,128,128]{3,2,1,0:T(8,128)(2,1)S(1)}, bf16[4,20,128,128]{3,2,1,0:T(8,128)(2,1)S(1)}, u32[]{:S(2)}, u32[]{:S(2)}) collective-permute-start(bf16[4,20,128,128]{3,2,1,0:T(8,128)(2,1)S(1)} %collective-permute-done.refs_5_), channel_id=1, source_target_pairs={{0,1},{3,2},{4,5},{7,6},{8,9},{11,10},{12,13},{15,14},{16,17},{19,... | collective-permute-start | bytes 7864328 | tf_op jit(solution)/shard_map/ppermute | solution.py:46
  88.5 6.8 %collective-permute-start.11 = (bf16[4,20,128,128]{3,2,1,0:T(8,128)(2,1)S(1)}, bf16[4,20,128,128]{3,2,1,0:T(8,128)(2,1)S(1)}, u32[]{:S(2)}, u32[]{:S(2)}) collective-permute-start(bf16[4,20,128,128]{3,2,1,0:T(8,128)(2,1)S(1)} %collective-permute-done.1.refs_6_), channel_id=1, source_target_pairs={{1,0},{2,3},{5,4},{6,7},{9,8},{10,11},{13,12},{14,15},{17,16},{18,... | collective-permute-start | bytes 7864328 | tf_op jit(solution)/shard_map/ppermute | solution.py:46
  89.8 31.7 %collective-permute-start.12 = (bf16[4,20,128,128]{3,2,1,0:T(8,128)(2,1)S(1)}, bf16[4,20,128,128]{3,2,1,0:T(8,128)(2,1)S(1)}, u32[]{:S(2)}, u32[]{:S(2)}) collective-permute-start(bf16[4,20,128,128]{3,2,1,0:T(8,128)(2,1)S(1)} %collective-permute-done.refs_5_), channel_id=1, source_target_pairs={{2,0},{28,1},{7,2},{1,3},{6,4},{0,5},{11,6},{5,7},{10,8},{4,9},{15... | collective-permute-start | bytes 7864328 | tf_op jit(solution)/shard_map/ppermute | solution.py:46
  92.8 2.5 %copy-start.6 = (bf16[4,20,128,128]{3,2,1,0:T(8,128)(2,1)}, bf16[4,20,128,128]{3,2,1,0:T(8,128)(2,1)S(1)}, u32[]{:S(2)}) copy-start(bf16[4,20,128,128]{3,2,1,0:T(8,128)(2,1)S(1)} %collective-permute-done.10.refs_7_) | copy-start | bytes 7864324
  95.3 1.5 copy-start.7
  116.5 1.0 copy-start
  121.5 24.3 %collective-permute-start.13 = (bf16[4,20,128,128]{3,2,1,0:T(8,128)(2,1)S(1)}, bf16[4,20,128,128]{3,2,1,0:T(8,128)(2,1)}, u32[]{:S(2)}, u32[]{:S(2)}) collective-permute-start(bf16[4,20,128,128]{3,2,1,0:T(8,128)(2,1)S(1)} %collective-permute-done.12.source_a), channel_id=1, source_target_pairs={{1,0},{0,1},{3,2},{2,3},{5,4},{4,5},{7,6},{6,7},{9,8},{8,9},{11,10... | collective-permute-start | bytes 7864328 | tf_op jit(solution)/shard_map/ppermute | solution.py:46
  124.9 4.4 %collective-permute-start.14 = (f32[1,512]{1,0:T(1,128)S(1)}, f32[1,512]{1,0:T(1,128)S(1)}, u32[]{:S(2)}, u32[]{:S(2)}) collective-permute-start(f32[1,512]{1,0:T(1,128)S(1)} %get-tuple-element.45), channel_id=1, source_target_pairs={{0,1},{1,0},{2,3},{3,2},{4,5},{5,4},{6,7},{7,6},{8,9},{9,8},{10,11... | collective-permute-start | bytes 6152 | tf_op jit(solution)/shard_map/ppermute | solution.py:54
  129.3 3.6 %collective-permute-start.15 = (f32[1,512]{1,0:T(1,128)S(1)}, f32[1,512]{1,0:T(1,128)S(1)}, u32[]{:S(2)}, u32[]{:S(2)}) collective-permute-start(f32[1,512]{1,0:T(1,128)S(1)} %add.15), channel_id=1, source_target_pairs={{0,2},{1,3},{2,0},{3,1},{4,6},{5,7},{6,4},{7,5},{8,10},{9,11},{10,... | collective-permute-start | bytes 6152 | tf_op jit(solution)/shard_map/ppermute | solution.py:54
  132.9 3.6 %collective-permute-start.16 = (f32[1,512]{1,0:T(1,128)S(1)}, f32[1,512]{1,0:T(1,128)S(1)}, u32[]{:S(2)}, u32[]{:S(2)}) collective-permute-start(f32[1,512]{1,0:T(1,128)S(1)} %add.16), channel_id=1, source_target_pairs={{0,4},{1,5},{2,6},{3,7},{4,0},{5,1},{6,2},{7,3},{8,12},{9,13},{10,... | collective-permute-start | bytes 6152 | tf_op jit(solution)/shard_map/ppermute | solution.py:54
  136.5 3.6 %collective-permute-start.17 = (f32[1,512]{1,0:T(1,128)S(1)}, f32[1,512]{1,0:T(1,128)S(1)}, u32[]{:S(2)}, u32[]{:S(2)}) collective-permute-start(f32[1,512]{1,0:T(1,128)S(1)} %add.17), channel_id=1, source_target_pairs={{0,8},{1,9},{2,10},{3,11},{4,12},{5,13},{6,14},{7,15},{8,0},{9,1},... | collective-permute-start | bytes 6152 | tf_op jit(solution)/shard_map/ppermute | solution.py:54
  140.1 4.5 %collective-permute-start.18 = (f32[1,512]{1,0:T(1,128)S(1)}, f32[1,512]{1,0:T(1,128)S(1)}, u32[]{:S(2)}, u32[]{:S(2)}) collective-permute-start(f32[1,512]{1,0:T(1,128)S(1)} %add.18), channel_id=1, source_target_pairs={{0,16},{1,17},{2,18},{3,19},{4,20},{5,21},{6,22},{7,23},{8,24},{9,... | collective-permute-start | bytes 6152 | tf_op jit(solution)/shard_map/ppermute | solution.py:54
  145.8 1.2 copy-start.1

commit v4 on v3

--- a/solution.py
+++ b/solution.py
@@ -10,6 +10,8 @@
 REACH = 12
 AXES = ("blk", "grp")
 VMEM_LIMIT = 48 * 1024 * 1024
+WHOLE_VMEM = 60 * 1024 * 1024
+EMPTY = 64
 
 FIRST = (2, 3, -3, -2)
 SECOND = (-3, 2, -2, 3)
@@ -46,14 +48,9 @@
     return lax.ppermute(shard, AXES, pairs)
 
 
-def total_over_devices(value):
+def exchange(value, step):
     size = lax.axis_size(AXES)
-    assert size & (size - 1) == 0
-    step = 1
-    while step < size:
-        value = value + lax.ppermute(value, AXES, [(d, d ^ step) for d in range(size)])
-        step *= 2
-    return value
+    return value + lax.ppermute(value, AXES, [(d, d ^ step) for d in range(size)])
 
 
 def pick(table, kind):
@@ -88,15 +85,52 @@
         return jnp.minimum(place, self.window)
 
 
-def scatter(z, dense, top, source, columns, start, save=None):
+def scatter(z, dense, top, source, place):
     for r in range(z.rows):
         def one(u, carry):
-            place = z.position(columns[r, u], start)
-            if save is not None:
-                save[r, u] = place
-            dense[top + r * z.block:top + (r + 1) * z.block, pl.ds(aligned(place, z.block), z.block)] = source[r, u]
+            column = pl.ds(aligned(place(r, u), z.block), z.block)
+            dense[top + r * z.block:top + (r + 1) * z.block, column] = source[r * z.slots + u]
             return carry
         lax.fori_loop(0, z.slots, one, 0, unroll=4)
+
+
+def decode(z, offsets, spot, vector, scalars, sem):
+    value = offsets[0:16, :].astype(jnp.float32).astype(jnp.int32)
+    value = value + spot * z.rows + lax.broadcasted_iota(jnp.int32, value.shape, 0)
+    vector[...] = jnp.where((value < 0) | (value > z.window), z.window, value)
+    copy = pltpu.make_async_copy(vector, scalars, sem)
+    copy.start()
+    return copy
+
+
+def pack_body(z, tiles, columns, out, stage, padded, offsets, in_sems, out_sems):
+    copies = []
+    for r in range(z.rows):
+        rows = pl.ds(r * z.slots, z.slots)
+        copies.append((
+            pltpu.make_async_copy(tiles.at[r], stage.at[rows], in_sems.at[r]),
+            pltpu.make_async_copy(stage.at[rows], out.at[rows], out_sems.at[r]),
+        ))
+    for copy, _ in copies:
+        copy.start()
+    padded[...] = jnp.full(padded.shape, -1, jnp.int32)
+    padded[:z.rows, :z.slots] = columns[...]
+    column = padded[...]
+    row = lax.axis_index(AXES) * z.rows + lax.broadcasted_iota(jnp.int32, column.shape, 0)
+    offset = column - row
+    offset = jnp.where(offset > z.all_rows // 2, offset - z.all_rows, offset)
+    offset = jnp.where(offset < -(z.all_rows // 2), offset + z.all_rows, offset)
+    offset = jnp.where(column < 0, EMPTY, offset)
+    offsets[...] = jnp.zeros_like(offsets)
+    offsets[0:16, :] = offset.astype(jnp.float32).astype(offsets.dtype)
+    last = pltpu.make_async_copy(offsets, out.at[z.rows * z.slots], out_sems.at[z.rows])
+    last.start()
+    for load, store in copies:
+        load.wait()
+        store.start()
+    for _, store in copies:
+        store.wait()
+    last.wait()
 
 
 def emit(z, total, positions, stage, out, sems, prev=None):
@@ -129,7 +163,14 @@
     left[...] = jnp.zeros_like(left)
     total[:, z.window * z.block:] = jnp.zeros((z.span, z.block), jnp.float32)
     copy.wait()
-    scatter(z, left, 0, stage, columns, z.start(device), positions)
+    start = z.start(device)
+    for r in range(z.rows):
+        def place(u, carry):
+            column = z.position(columns[r, u], start)
+            positions[r, u] = column
+            left[r * z.block:(r + 1) * z.block, pl.ds(aligned(column, z.block), z.block)] = stage[r, u]
+            return carry
+        lax.fori_loop(0, z.slots, place, 0, unroll=4)
     left_copy = pltpu.make_async_copy(left, left_out, left_sem)
     left_copy.start()
     half = z.span // 2
@@ -159,17 +200,18 @@
     left_copy.wait()
 
 
-def near_body(z, names, left_in, positions, prev, trace_in, corner, *refs):
+def near_body(z, names, left_in, positions, prev, trace_in, *refs):
     refs = list(refs)
     take = lambda count: [refs.pop(0) for _ in range(count)]
-    columns = dict(zip(names, take(len(names))))
+    final = "mixed" in names
+    corner = take(1)[0] if final else None
     sources = {name: take(2 if name == "mixed" else 1) for name in names}
-    out, relay_left, trace = take(3)
-    left, stage, right, total, out_stage, prev_stage = take(6)
-    left_sem, in_sem, prev_sem, relay_sem, out_sems = take(5)
+    out, trace = take(2)
+    relay_left = take(1)[0] if final else None
+    left, stage, right, total, out_stage, prev_stage, vector, scalars = take(8)
+    left_sem, in_sem, prev_sem, place_sem, relay_sem, out_sems = take(6)
     device = lax.axis_index(AXES)
     kind = device % 4
-    start = z.start(device)
     place = {name: pick(table, kind) + z.hops for name, table in OFFSETS.items()}
 
     def chunk(n):
@@ -189,28 +231,35 @@
 
     left_copy = pltpu.make_async_copy(left_in, left, left_sem)
     left_copy.start()
-    fetch(0, True)
-    fetch(1, True)
+    for index in range(min(2, len(names))):
+        fetch(index, True)
     prev_copy = pltpu.make_async_copy(prev, prev_stage, prev_sem)
     prev_copy.start()
     total[...] = jnp.zeros_like(total)
     trace[...] = trace_in[...]
     left_copy.wait()
     relay_copies = []
-    for index, name in enumerate(("relay", "relay_beside")):
-        copy = pltpu.make_async_copy(
-            left.at[:, chunk(place[name])], relay_left.at[:, pl.ds(index * z.span, z.span)], relay_sem.at[index]
-        )
-        copy.start()
-        relay_copies.append(copy)
+    if final:
+        for index, name in enumerate(("relay", "relay_beside")):
+            copy = pltpu.make_async_copy(
+                left.at[:, chunk(place[name])], relay_left.at[:, pl.ds(index * z.span, z.span)],
+                relay_sem.at[index],
+            )
+            copy.start()
+            relay_copies.append(copy)
     dense_of = {}
     for index, name in enumerate(names):
         dense = right.at[index]
         dense_of[name] = dense
         spot = place[name]
+        slot = index % 2
+        fetch(index, False)
+        decoding = decode(
+            z, stage.at[slot, z.rows * z.slots], spot, vector.at[slot], scalars.at[slot], place_sem.at[slot]
+        )
         dense[...] = jnp.zeros_like(dense)
-        fetch(index, False)
-        scatter(z, dense, 0, stage.at[index % 2], columns[name], start)
+        decoding.wait()
+        scatter(z, dense, 0, stage.at[slot], lambda r, u: scalars[slot, r, u])
         if index + 2 < len(names):
             fetch(index + 2, True)
 
@@ -225,28 +274,27 @@
         pl.when(weight != 0)(
             lambda: add_trace(trace, weight, left[:, chunk(spot)], dense[:, chunk(z.hops)])
         )
-    for (one, other), table in OUTSIDE.items():
-        weight = pick(table, kind)
-        pl.when(weight != 0)(lambda: add_trace(
-            trace, weight, dense_of[one][:, chunk(place[other])], dense_of[other][:, chunk(place[one])]
-        ))
-    half = z.span // 2
-    last = (z.chunks - 1) * z.span
-    pl.when(kind == 1)(lambda: add_trace(trace, jnp.float32(2), left[:, half:z.span], corner[...]))
-    pl.when(kind == 2)(
-        lambda: add_trace(trace, jnp.float32(2), left[:half, last:last + half], corner[:, :half])
-    )
+    if final:
+        for (one, other), table in OUTSIDE.items():
+            weight = pick(table, kind)
+            pl.when(weight != 0)(lambda: add_trace(
+                trace, weight, dense_of[one][:, chunk(place[other])], dense_of[other][:, chunk(place[one])]
+            ))
+        half = z.span // 2
+        last = (z.chunks - 1) * z.span
+        pl.when(kind == 1)(lambda: add_trace(trace, jnp.float32(2), left[:, half:z.span], corner[...]))
+        pl.when(kind == 2)(
+            lambda: add_trace(trace, jnp.float32(2), left[:half, last:last + half], corner[:, :half])
+        )
     prev_copy.wait()
     emit(z, total, positions, out_stage, out, out_sems, prev_stage)
     for copy in relay_copies:
         copy.wait()
 
 
-def last_body(z, left_in, positions, prev, columns_a, columns_b, source_a, source_b, out,
-              left, stage, right, total, out_stage, prev_stage, left_sem, in_sem, prev_sem, out_sems):
-    device = lax.axis_index(AXES)
-    kind = device % 4
-    start = z.start(device)
+def last_body(z, left_in, positions, prev, source_a, source_b, out, left, stage, right, total, out_stage,
+              prev_stage, vector, scalars, left_sem, in_sem, prev_sem, place_sem, out_sems):
+    kind = lax.axis_index(AXES) % 4
     copies = [
         pltpu.make_async_copy(source_a, stage.at[0], in_sem.at[0]),
         pltpu.make_async_copy(source_b, stage.at[1], in_sem.at[1]),
@@ -255,10 +303,9 @@
     ]
     for copy in copies:
         copy.start()
-    place_a = pick(OFFSETS["relay"], kind) + z.hops
-    place_b = pick(OFFSETS["relay_beside"], kind) + z.hops
-    low = jnp.maximum(0, jnp.minimum(place_a, place_b) - z.hops)
-    high = jnp.minimum(z.chunks, jnp.maximum(place_a, place_b) + z.hops + 1)
+    places = [pick(OFFSETS[name], kind) + z.hops for name in ("relay", "relay_beside")]
+    low = jnp.maximum(0, jnp.minimum(*places) - z.hops)
+    high = jnp.minimum(z.chunks, jnp.maximum(*places) + z.hops + 1)
 
     def chunk(n):
         return pl.ds(aligned(n, z.span), z.span)
@@ -271,14 +318,20 @@
         right[:, chunk(n)] = jnp.zeros((2 * z.span, z.span), right.dtype)
         return carry
 
-    lax.fori_loop(low, high, clear_right, 0)
     lax.fori_loop(0, low, clear_total, 0)
     lax.fori_loop(high, z.chunks, clear_total, 0)
     total[:, z.window * z.block:] = jnp.zeros((z.span, z.block), jnp.float32)
-    copies[0].wait()
-    scatter(z, right, 0, stage.at[0], columns_a, start)
-    copies[1].wait()
-    scatter(z, right, z.span, stage.at[1], columns_b, start)
+    decodings = []
+    for index in range(2):
+        copies[index].wait()
+        decodings.append(decode(
+            z, stage.at[index, z.rows * z.slots], places[index], vector.at[index], scalars.at[index],
+            place_sem.at[index],
+        ))
+    lax.fori_loop(low, high, clear_right, 0)
+    for index in range(2):
+        decodings[index].wait()
+        scatter(z, right, index * z.span, stage.at[index], lambda r, u: scalars[index, r, u])
     copies[2].wait()
 
     def multiply(n, carry):
@@ -296,14 +349,14 @@
 DMA = pltpu.SemaphoreType.DMA
 
 
-def call(z, kernel, operands, in_specs, out_shape, out_specs, scratch, pieces):
+def call(z, kernel, operands, in_specs, out_shape, out_specs, scratch, pieces, limit=VMEM_LIMIT):
     return pl.pallas_call(
         kernel,
         out_shape=out_shape,
         in_specs=in_specs,
         out_specs=out_specs,
         scratch_shapes=scratch,
-        compiler_params=pltpu.CompilerParams(vmem_limit_bytes=VMEM_LIMIT),
+        compiler_params=pltpu.CompilerParams(vmem_limit_bytes=limit),
         cost_estimate=pl.CostEstimate(
             flops=2 * z.span * z.span * z.window * z.block * pieces,
             bytes_accessed=2 * z.span * z.slots * z.block * (pieces + 4),
@@ -323,10 +376,21 @@
     dense = pltpu.VMEM((z.span, z.wide), dtype)
     total_buffer = pltpu.VMEM((z.span, z.wide), jnp.float32)
 
-    first = receive(tiles, FIRST)
-    second = receive(tiles, SECOND)
-    column_of = {name: receive(columns, table) for name, table in OFFSETS.items()}
-    beside = receive(tiles, PARTNER)
+    payload_shape = (z.rows * z.slots + 1, z.block, z.block)
+    places = [pltpu.VMEM((2, 16, z.block), jnp.int32), pltpu.SMEM((2, 16, z.block), jnp.int32)]
+
+    payload = call(
+        z, functools.partial(pack_body, z), [tiles, columns], [ANY, VMEM],
+        shape(payload_shape, dtype), ANY,
+        [
+            pltpu.VMEM((z.rows * z.slots, z.block, z.block), dtype), pltpu.VMEM((16, z.block), jnp.int32),
+            pltpu.VMEM((z.block, z.block), dtype), DMA((z.rows,)), DMA((z.rows + 1,)),
+        ],
+        0, WHOLE_VMEM,
+    )
+    first = receive(payload, FIRST)
+    second = receive(payload, SECOND)
+    beside = receive(payload, PARTNER)
 
     total, left, corner, positions, trace = call(
         z, functools.partial(own_body, z), [tiles, columns], [ANY, SMEM],
@@ -342,46 +406,54 @@
         1,
     )
     corner = receive(corner, (0, CORNER[1], CORNER[2], 0), (1, 2))
-    first, second, beside, column_of, corner, total = lax.optimization_barrier(
-        (first, second, beside, column_of, corner, total)
-    )
+
+    def near(names, arrays, total, trace):
+        final = "mixed" in names
+        extra = [shape((z.span, 2 * z.span), dtype)] if final else []
+        return call(
+            z, functools.partial(near_body, z, names),
+            [left, positions, total, trace] + ([corner] if final else []) + arrays,
+            [ANY, SMEM, ANY, VMEM] + [VMEM] * final + [ANY] * len(arrays),
+            [sums, line] + extra,
+            [ANY, VMEM] + [ANY] * len(extra),
+            [
+                dense, pltpu.VMEM((2,) + payload_shape, dtype),
+                pltpu.VMEM((len(names), z.span, z.wide), dtype), total_buffer,
+                pltpu.VMEM(tiles.shape, jnp.float32), pltpu.VMEM(tiles.shape, jnp.float32), *places,
+                DMA, DMA((2,)), DMA, DMA((2,)), DMA((2,)), DMA((z.rows,)),
+            ],
+            len(names),
+        )
+
+    total, trace = near(("beside",), [beside], total, trace)
+    first, second, total, trace = lax.optimization_barrier((first, second, total, trace))
     relay = receive(first, RELAY_FROM)
     mixed = [
         receive(first, PARTNER, [m for m in range(4) if not USE_SECOND[m]]),
         receive(second, PARTNER, [m for m in range(4) if USE_SECOND[m]]),
     ]
-    names = ("beside", "first", "second", "mixed")
-    total, relay_left, trace = call(
-        z, functools.partial(near_body, z, names),
-        [left, positions, total, trace, corner, *[column_of[name] for name in names], beside, first, second, *mixed],
-        [ANY, SMEM, ANY, VMEM, VMEM] + [SMEM] * 4 + [ANY] * 5,
-        [sums, shape((z.span, 2 * z.span), dtype), line],
-        [ANY, ANY, VMEM],
-        [
-            dense, pltpu.VMEM((2,) + tiles.shape, dtype), pltpu.VMEM((4, z.span, z.wide), dtype), total_buffer,
-            pltpu.VMEM(tiles.shape, jnp.float32), pltpu.VMEM(tiles.shape, jnp.float32),
-            DMA, DMA((2,)), DMA, DMA((2,)), DMA((z.rows,)),
-        ],
-        4,
-    )
+    total, trace, relay_left = near(("first", "second", "mixed"), [first, second, *mixed], total, trace)
+    assert devices & (devices - 1) == 0
+    steps = [1 << bit for bit in range(devices.bit_length() - 1)]
+    for step in steps[:1] + steps[3:]:
+        trace = exchange(trace, step)
     relay, total, trace = lax.optimization_barrier((relay, total, trace))
     relay_beside = receive(relay, PARTNER)
-    trace = total_over_devices(trace)
+    trace = exchange(trace, steps[2])
+    relay_beside, trace = lax.optimization_barrier((relay_beside, trace))
+    trace = exchange(trace, steps[1])
     square = call(
-        z, functools.partial(last_body, z),
-        [
-            relay_left, positions, total, column_of["relay"], column_of["relay_beside"], relay, relay_beside,
-        ],
-        [ANY, SMEM, ANY, SMEM, SMEM, ANY, ANY],
+        z, functools.partial(last_body, z), [relay_left, positions, total, relay, relay_beside],
+        [ANY, SMEM, ANY, ANY, ANY],
         [shape(tiles.shape, dtype)],
         [ANY],
         [
-            pltpu.VMEM((z.span, 2 * z.span), dtype), pltpu.VMEM((2,) + tiles.shape, dtype),
+            pltpu.VMEM((z.span, 2 * z.span), dtype), pltpu.VMEM((2,) + payload_shape, dtype),
             pltpu.VMEM((2 * z.span, z.wide), dtype), total_buffer,
-            pltpu.VMEM(tiles.shape, dtype), pltpu.VMEM(tiles.shape, jnp.float32),
-            DMA, DMA((2,)), DMA, DMA((z.rows,)),
+            pltpu.VMEM(tiles.shape, dtype), pltpu.VMEM(tiles.shape, jnp.float32), *places,
+            DMA, DMA((2,)), DMA, DMA((2,)), DMA((z.rows,)),
         ],
-        2,
+        2, WHOLE_VMEM,
     )[0]
     return square, jnp.sum(trace) / (z.all_rows * z.block)
 

time: 158 us -> 157 us (level)
  waiting for transfers between devices: 81.9 us -> 47.1 us
  starting transfers between devices: 28.7 us -> 53.6 us
  Pallas kernels: 37.5 us -> 50.1 us
  local copies, waits for them, and re-layouts: 6.21 us -> 3.13 us
    ppermute x5, starting transfers between devices: 0.01 us -> 38.2 us  [exchange(): lax.ppermute(value, AXES, [(d, d ^ step) for d in range(size)])]
    ppermute x14 -> x8, waiting for transfers between devices: 62.3 us -> 37.2 us  [receive(): return lax.ppermute(shard, AXES, pairs)]
    ppermute x14 -> x8, starting transfers between devices: 28.7 us -> 15.4 us  [receive(): return lax.ppermute(shard, AXES, pairs)]
    pallas_call x3 -> x5, Pallas kernels: 37.5 us -> 50.1 us  [call(): pl.pallas_call(kernel, out_shape=out_shape, in_specs=in_specs, out_specs=...]
    ppermute x5, waiting for transfers between devices: 19.6 us -> 9.92 us  [exchange(): lax.ppermute(value, AXES, [(d, d ^ step) for d in range(size)])]
    unnamed x16 -> x14, local copies, waits for them, and re-layouts: 6.21 us -> 3.13 us
  transfers between devices with their start and end apart: 19 -> 13, of which waited for: 14 -> 7; matrix products, arithmetic and copies ran while one was open for 0% -> 0% of each run, Pallas kernels for 18% -> 30%
where the time goes in v4:
time: 157 us
  starting transfers between devices  53.6 us (34%)
  Pallas kernels  50.1 us (32%)
  waiting for transfers between devices  47.1 us (30%)
  local copies, waits for them, and re-layouts  3.13 us (2%)
  between operations  2.58 us (2%)
    pallas_call x5, Pallas kernels, call(): pl.pallas_call(kernel, out_shape=out_shape, in_specs=in_specs, out_specs=...  50.1 us
    ppermute x5, starting transfers between devices, exchange(): lax.ppermute(value, AXES, [(d, d ^ step) for d in range(size)])  38.2 us
    ppermute x8, waiting for transfers between devices, receive(): return lax.ppermute(shard, AXES, pairs)  37.2 us
    ppermute x8, starting transfers between devices, receive(): return lax.ppermute(shard, AXES, pairs)  15.4 us
    ppermute x5, waiting for transfers between devices, exchange(): lax.ppermute(value, AXES, [(d, d ^ step) for d in range(size)])  9.92 us
  transfers between devices with their start and end apart: 13, of which 7 were waited for; matrix products, arithmetic and copies ran while one was open for 0% of the time, Pallas kernels for 30%

profile of v4, /device:TPU:0, one launch (start us, length us, event | category | flops | bytes accessed | tf_op | source)
XLA Modules:
  0.0 157.0 jit_solution(8396200215212161139)
XLA Ops:
  0.6 0.0 copy-start
  0.6 0.0 copy-start.3
  0.6 3.5 %shard_map.42 = bf16[81,128,128]{2,1,0:T(8,128)(2,1)} custom-call(bf16[4,20,128,128]{3,2,1,0:T(8,128)(2,1)} %tiles.1, s32[4,20]{1,0:T(4,128)} %columns.3), custom_call_target="tpu_custom_call" | custom-call | bytes 10485760 | tf_op jit(solution)/shard_map/pallas_call | solution.py:353
  4.2 0.5 collective-permute-start.2
  4.7 5.7 %collective-permute-start = (bf16[81,128,128]{2,1,0:T(8,128)(2,1)}, bf16[81,128,128]{2,1,0:T(8,128)(2,1)S(1)}, u32[]{:S(2)}, u32[]{:S(2)}) collective-permute-start(bf16[81,128,128]{2,1,0:T(8,128)(2,1)} %shard_map.42), channel_id=1, source_target_pairs={{2,0},{4,1},{31,2},{1,3},{6,4},{8,5},{3,6},{5,7},{10,8},{12,9},{7,... | collective-permute-start | bytes 7962632 | tf_op jit(solution)/shard_map/ppermute | solution.py:48
  10.4 0.0 collective-permute-start.1
  10.4 0.0 copy-done
  10.4 0.0 copy-done.3
  10.4 8.4 %shard_map.41 = (f32[4,20,128,128]{3,2,1,0:T(8,128)}, bf16[512,3712]{1,0:T(8,128)(2,1)}, bf16[256,512]{1,0:T(8,128)(2,1)S(1)}, s32[4,20]{1,0:T(4,128)S(1)}, f32[1,512]{1,0:T(1,128)S(1)}) custom-call(bf16[4,20,128,128]{3,2,1,0:T(8,128)(2,1)S(1)} %copy-done, s32[4,20]{1,0:T(4,128)S(1)} %copy-done.3), custom_call_target="tpu_custom_call" | custom-call | flops 1879048192 | bytes 13107200 | tf_op jit(solution)/shard_map/pallas_call | solution.py:353
  18.8 0.0 copy-start.2
  18.8 0.0 collective-permute-done.2.refs_0_
  18.8 9.9 %shard_map.43 = (f32[4,20,128,128]{3,2,1,0:T(8,128)}, f32[1,512]{1,0:T(1,128)S(1)}) custom-call(bf16[512,3712]{1,0:T(8,128)(2,1)} %get-tuple-element.21.left_in, s32[4,20]{1,0:T(4,128)S(1)} %get-tuple-element.22.positions, f32[4,20,128,128]{3,2,1,0:T(8,128)} %get-tuple-element.23.prev, f32[1,512]{1,0:T(1,128)S(1)} %get-tuple-element.24.trace_in, ...), custom_call_target="tpu_custom_call" | custom-call | flops 1879048192 | bytes 13107200 | tf_op jit(solution)/shard_map/pallas_call | solution.py:353
  28.7 35.9 %collective-permute-done.refs_1_ = bf16[81,128,128]{2,1,0:T(8,128)(2,1)S(1)} collective-permute-done((bf16[81,128,128]{2,1,0:T(8,128)(2,1)}, bf16[81,128,128]{2,1,0:T(8,128)(2,1)S(1)}, u32[]{:S(2)}, u32[]{:S(2)}) %collective-permute-start) | collective-permute-done | bytes 2654240 | tf_op jit(solution)/shard_map/ppermute | solution.py:48
  64.7 0.3 collective-permute-done.1.refs_2_
  65.0 2.9 %collective-permute-start.4 = (bf16[81,128,128]{2,1,0:T(8,128)(2,1)S(1)}, bf16[81,128,128]{2,1,0:T(8,128)(2,1)S(1)}, u32[]{:S(2)}, u32[]{:S(2)}) collective-permute-start(bf16[81,128,128]{2,1,0:T(8,128)(2,1)S(1)} %collective-permute-done.refs_1_), channel_id=1, source_target_pairs={{0,1},{3,2},{4,5},{7,6},{8,9},{11,10},{12,13},{15,14},{16,17},{19,... | collective-permute-start | bytes 7962632 | tf_op jit(solution)/shard_map/ppermute | solution.py:48
  67.9 1.3 collective-permute-start.5
  69.2 4.3 %collective-permute-start.6 = (bf16[81,128,128]{2,1,0:T(8,128)(2,1)S(1)}, bf16[81,128,128]{2,1,0:T(8,128)(2,1)S(1)}, u32[]{:S(2)}, u32[]{:S(2)}) collective-permute-start(bf16[81,128,128]{2,1,0:T(8,128)(2,1)S(1)} %collective-permute-done.refs_1_), channel_id=1, source_target_pairs={{2,0},{28,1},{7,2},{1,3},{6,4},{0,5},{11,6},{5,7},{10,8},{4,9},{15... | collective-permute-start | bytes 7962632 | tf_op jit(solution)/shard_map/ppermute | solution.py:48
  73.5 0.7 collective-permute-start.3
  74.2 0.0 collective-permute-done.3.refs_0_
  74.2 0.0 collective-permute-done.4.refs_3_
  74.2 0.0 copy-start.6
  74.2 0.9 collective-permute-done.5.refs_4_
  75.1 0.0 copy-done.2
  75.1 0.6 copy-done.6
  75.7 17.2 %shard_map.44 = (f32[4,20,128,128]{3,2,1,0:T(8,128)}, f32[1,512]{1,0:T(1,128)S(1)}, bf16[512,1024]{1,0:T(8,128)(2,1)S(1)}) custom-call(bf16[512,3712]{1,0:T(8,128)(2,1)} %get-tuple-element.21.left_in, s32[4,20]{1,0:T(4,128)S(1)} %get-tuple-element.22.positions, f32[4,20,128,128]{3,2,1,0:T(8,128)} %get-tuple-element.27.prev, ...), custom_call_target="tpu_custom_call" | custom-call | flops 5637144576 | bytes 18350080 | tf_op jit(solution)/shard_map/pallas_call | solution.py:353
  93.0 0.0 copy-start.1
  93.0 1.0 copy-done.1
  93.9 13.8 %collective-permute-start.7 = (f32[1,512]{1,0:T(1,128)S(1)}, f32[1,512]{1,0:T(1,128)S(1)}, u32[]{:S(2)}, u32[]{:S(2)}) collective-permute-start(f32[1,512]{1,0:T(1,128)S(1)} %get-tuple-element.34), channel_id=1, source_target_pairs={{0,1},{1,0},{2,3},{3,2},{4,5},{5,4},{6,7},{7,6},{8,9},{9,8},{10,11... | collective-permute-start | bytes 6152 | tf_op jit(solution)/shard_map/ppermute | solution.py:53
  107.8 0.8 collective-permute-done.7
  108.6 0.0 collective-permute-start.8
  108.6 3.6 %collective-permute-done.8 = f32[1,512]{1,0:T(1,128)S(1)} collective-permute-done((f32[1,512]{1,0:T(1,128)S(1)}, f32[1,512]{1,0:T(1,128)S(1)}, u32[]{:S(2)}, u32[]{:S(2)}) %collective-permute-start.8) | collective-permute-done | bytes 2080 | tf_op jit(solution)/shard_map/ppermute | solution.py:53
  112.2 0.5 collective-permute-start.9
  112.7 4.0 %collective-permute-done.9 = f32[1,512]{1,0:T(1,128)S(1)} collective-permute-done((f32[1,512]{1,0:T(1,128)S(1)}, f32[1,512]{1,0:T(1,128)S(1)}, u32[]{:S(2)}, u32[]{:S(2)}) %collective-permute-start.9) | collective-permute-done | bytes 2080 | tf_op jit(solution)/shard_map/ppermute | solution.py:53
  116.7 0.0 collective-permute-done.6.source_a
  116.7 0.0 copy-start.4
  116.7 1.5 copy-done.4
  118.2 0.0 collective-permute-start.10
  118.2 21.7 %collective-permute-start.11 = (f32[1,512]{1,0:T(1,128)S(1)}, f32[1,512]{1,0:T(1,128)S(1)}, u32[]{:S(2)}, u32[]{:S(2)}) collective-permute-start(f32[1,512]{1,0:T(1,128)S(1)} %add.17), channel_id=1, source_target_pairs={{0,4},{1,5},{2,6},{3,7},{4,0},{5,1},{6,2},{7,3},{8,12},{9,13},{10,... | collective-permute-start | bytes 6152 | tf_op jit(solution)/shard_map/ppermute | solution.py:53
  139.9 1.6 collective-permute-done.11
  141.5 0.0 collective-permute-done.10.source_b
  141.5 0.0 copy-start.5
  141.5 2.1 %collective-permute-start.12 = (f32[1,512]{1,0:T(1,128)S(1)}, f32[1,512]{1,0:T(1,128)S(1)}, u32[]{:S(2)}, u32[]{:S(2)}) collective-permute-start(f32[1,512]{1,0:T(1,128)S(1)} %add.18), channel_id=1, source_target_pairs={{0,2},{1,3},{2,0},{3,1},{4,6},{5,7},{6,4},{7,5},{8,10},{9,11},{10,... | collective-permute-start | bytes 6152 | tf_op jit(solution)/shard_map/ppermute | solution.py:53
  143.6 0.0 copy-done.5
  143.6 11.0 %shard_map.45 = bf16[4,20,128,128]{3,2,1,0:T(8,128)(2,1)} custom-call(bf16[512,1024]{1,0:T(8,128)(2,1)} %copy-done.1, s32[4,20]{1,0:T(4,128)} %copy-done.2, f32[4,20,128,128]{3,2,1,0:T(8,128)} %get-tuple-element.35.prev, bf16[81,128,128]{2,1,0:T(8,128)(2,1)} %copy-done.4, bf16[81,128,128]{2,1,0:T(8,128)(2,1)} %copy-done.5), custom_call_target="tpu_custom_call" | custom-call | flops 3758096384 | bytes 15728640 | tf_op jit(solution)/shard_map/pallas_call | solution.py:353
  154.6 0.0 collective-permute-done.12
  154.7 0.6 add_reduce_fusion
  (4 shorter events, 0.0 us)
Async XLA Ops:
  0.6 9.7 %copy-start = (bf16[4,20,128,128]{3,2,1,0:T(8,128)(2,1)S(1)}, bf16[4,20,128,128]{3,2,1,0:T(8,128)(2,1)}, u32[]{:S(2)}) copy-start(bf16[4,20,128,128]{3,2,1,0:T(8,128)(2,1)} %tiles.1) | copy-start | bytes 7864324
  0.6 9.7 %copy-start.3 = (s32[4,20]{1,0:T(4,128)S(1)}, s32[4,20]{1,0:T(4,128)}, u32[]{:S(2)}) copy-start(s32[4,20]{1,0:T(4,128)} %columns.3) | copy-start | bytes 964
  4.2 14.6 %collective-permute-start.2 = (bf16[81,128,128]{2,1,0:T(8,128)(2,1)}, bf16[81,128,128]{2,1,0:T(8,128)(2,1)S(1)}, u32[]{:S(2)}, u32[]{:S(2)}) collective-permute-start(bf16[81,128,128]{2,1,0:T(8,128)(2,1)} %shard_map.42), channel_id=1, source_target_pairs={{1,0},{0,1},{3,2},{2,3},{5,4},{4,5},{7,6},{6,7},{9,8},{8,9},{11,10... | collective-permute-start | bytes 7962632 | tf_op jit(solution)/shard_map/ppermute | solution.py:48
  4.7 60.0 %collective-permute-start = (bf16[81,128,128]{2,1,0:T(8,128)(2,1)}, bf16[81,128,128]{2,1,0:T(8,128)(2,1)S(1)}, u32[]{:S(2)}, u32[]{:S(2)}) collective-permute-start(bf16[81,128,128]{2,1,0:T(8,128)(2,1)} %shard_map.42), channel_id=1, source_target_pairs={{2,0},{4,1},{31,2},{1,3},{6,4},{8,5},{3,6},{5,7},{10,8},{12,9},{7,... | collective-permute-start | bytes 7962632 | tf_op jit(solution)/shard_map/ppermute | solution.py:48
  10.4 54.6 %collective-permute-start.1 = (bf16[81,128,128]{2,1,0:T(8,128)(2,1)}, bf16[81,128,128]{2,1,0:T(8,128)(2,1)}, u32[]{:S(2)}, u32[]{:S(2)}) collective-permute-start(bf16[81,128,128]{2,1,0:T(8,128)(2,1)} %shard_map.42), channel_id=1, source_target_pairs={{29,0},{3,1},{0,2},{6,3},{1,4},{7,5},{4,6},{10,7},{5,8},{11,9},{8,... | collective-permute-start | bytes 7962632 | tf_op jit(solution)/shard_map/ppermute | solution.py:48
  18.8 56.3 %copy-start.2 = (s32[4,20]{1,0:T(4,128)}, s32[4,20]{1,0:T(4,128)S(1)}, u32[]{:S(2)}) copy-start(s32[4,20]{1,0:T(4,128)S(1)} %get-tuple-element.22.positions) | copy-start | bytes 964
  65.0 9.2 %collective-permute-start.4 = (bf16[81,128,128]{2,1,0:T(8,128)(2,1)S(1)}, bf16[81,128,128]{2,1,0:T(8,128)(2,1)S(1)}, u32[]{:S(2)}, u32[]{:S(2)}) collective-permute-start(bf16[81,128,128]{2,1,0:T(8,128)(2,1)S(1)} %collective-permute-done.refs_1_), channel_id=1, source_target_pairs={{0,1},{3,2},{4,5},{7,6},{8,9},{11,10},{12,13},{15,14},{16,17},{19,... | collective-permute-start | bytes 7962632 | tf_op jit(solution)/shard_map/ppermute | solution.py:48
  67.9 7.2 %collective-permute-start.5 = (bf16[81,128,128]{2,1,0:T(8,128)(2,1)}, bf16[81,128,128]{2,1,0:T(8,128)(2,1)}, u32[]{:S(2)}, u32[]{:S(2)}) collective-permute-start(bf16[81,128,128]{2,1,0:T(8,128)(2,1)} %collective-permute-done.1.refs_2_), channel_id=1, source_target_pairs={{1,0},{2,3},{5,4},{6,7},{9,8},{10,11},{13,12},{14,15},{17,16},{18,... | collective-permute-start | bytes 7962632 | tf_op jit(solution)/shard_map/ppermute | solution.py:48
  69.2 47.5 %collective-permute-start.6 = (bf16[81,128,128]{2,1,0:T(8,128)(2,1)S(1)}, bf16[81,128,128]{2,1,0:T(8,128)(2,1)S(1)}, u32[]{:S(2)}, u32[]{:S(2)}) collective-permute-start(bf16[81,128,128]{2,1,0:T(8,128)(2,1)S(1)} %collective-permute-done.refs_1_), channel_id=1, source_target_pairs={{2,0},{28,1},{7,2},{1,3},{6,4},{0,5},{11,6},{5,7},{10,8},{4,9},{15... | collective-permute-start | bytes 7962632 | tf_op jit(solution)/shard_map/ppermute | solution.py:48
  73.5 0.7 collective-permute-start.3
  74.2 1.5 copy-start.6
  93.0 1.0 copy-start.1
  93.9 14.7 %collective-permute-start.7 = (f32[1,512]{1,0:T(1,128)S(1)}, f32[1,512]{1,0:T(1,128)S(1)}, u32[]{:S(2)}, u32[]{:S(2)}) collective-permute-start(f32[1,512]{1,0:T(1,128)S(1)} %get-tuple-element.34), channel_id=1, source_target_pairs={{0,1},{1,0},{2,3},{3,2},{4,5},{5,4},{6,7},{7,6},{8,9},{9,8},{10,11... | collective-permute-start | bytes 6152 | tf_op jit(solution)/shard_map/ppermute | solution.py:53
  108.6 3.6 %collective-permute-start.8 = (f32[1,512]{1,0:T(1,128)S(1)}, f32[1,512]{1,0:T(1,128)S(1)}, u32[]{:S(2)}, u32[]{:S(2)}) collective-permute-start(f32[1,512]{1,0:T(1,128)S(1)} %add.15), channel_id=1, source_target_pairs={{0,8},{1,9},{2,10},{3,11},{4,12},{5,13},{6,14},{7,15},{8,0},{9,1},... | collective-permute-start | bytes 6152 | tf_op jit(solution)/shard_map/ppermute | solution.py:53
  112.2 4.5 %collective-permute-start.9 = (f32[1,512]{1,0:T(1,128)S(1)}, f32[1,512]{1,0:T(1,128)S(1)}, u32[]{:S(2)}, u32[]{:S(2)}) collective-permute-start(f32[1,512]{1,0:T(1,128)S(1)} %add.16), channel_id=1, source_target_pairs={{0,16},{1,17},{2,18},{3,19},{4,20},{5,21},{6,22},{7,23},{8,24},{9,... | collective-permute-start | bytes 6152 | tf_op jit(solution)/shard_map/ppermute | solution.py:53
  116.7 1.5 copy-start.4
  118.2 23.3 %collective-permute-start.10 = (bf16[81,128,128]{2,1,0:T(8,128)(2,1)S(1)}, bf16[81,128,128]{2,1,0:T(8,128)(2,1)S(1)}, u32[]{:S(2)}, u32[]{:S(2)}) collective-permute-start(bf16[81,128,128]{2,1,0:T(8,128)(2,1)S(1)} %collective-permute-done.6.source_a), channel_id=1, source_target_pairs={{1,0},{0,1},{3,2},{2,3},{5,4},{4,5},{7,6},{6,7},{9,8},{8,9},{11,10... | collective-permute-start | bytes 7962632 | tf_op jit(solution)/shard_map/ppermute | solution.py:48
  118.2 23.3 %collective-permute-start.11 = (f32[1,512]{1,0:T(1,128)S(1)}, f32[1,512]{1,0:T(1,128)S(1)}, u32[]{:S(2)}, u32[]{:S(2)}) collective-permute-start(f32[1,512]{1,0:T(1,128)S(1)} %add.17), channel_id=1, source_target_pairs={{0,4},{1,5},{2,6},{3,7},{4,0},{5,1},{6,2},{7,3},{8,12},{9,13},{10,... | collective-permute-start | bytes 6152 | tf_op jit(solution)/shard_map/ppermute | solution.py:53
  141.5 2.1 %copy-start.5 = (bf16[81,128,128]{2,1,0:T(8,128)(2,1)}, bf16[81,128,128]{2,1,0:T(8,128)(2,1)S(1)}, u32[]{:S(2)}) copy-start(bf16[81,128,128]{2,1,0:T(8,128)(2,1)S(1)} %collective-permute-done.10.source_b) | copy-start | bytes 7962628
  141.5 13.1 %collective-permute-start.12 = (f32[1,512]{1,0:T(1,128)S(1)}, f32[1,512]{1,0:T(1,128)S(1)}, u32[]{:S(2)}, u32[]{:S(2)}) collective-permute-start(f32[1,512]{1,0:T(1,128)S(1)} %add.18), channel_id=1, source_target_pairs={{0,2},{1,3},{2,0},{3,1},{4,6},{5,7},{6,4},{7,5},{8,10},{9,11},{10,... | collective-permute-start | bytes 6152 | tf_op jit(solution)/shard_map/ppermute | solution.py:53

commit v5 on v4

--- a/solution.py
+++ b/solution.py
@@ -9,12 +9,12 @@
 
 REACH = 12
 AXES = ("blk", "grp")
-VMEM_LIMIT = 48 * 1024 * 1024
+VMEM_LIMIT = 36 * 1024 * 1024
 WHOLE_VMEM = 60 * 1024 * 1024
 EMPTY = 64
 
 FIRST = (2, 3, -3, -2)
-SECOND = (-3, 2, -2, 3)
+LAST = (-3, 2, -2, 3)
 RELAY_FROM = (2, -5, 5, -2)
 PARTNER = (1, -1, 1, -1)
 RELAY = tuple(RELAY_FROM[m] + FIRST[(m + RELAY_FROM[m]) % 4] for m in range(4))
@@ -24,22 +24,24 @@
     return tuple(PARTNER[m] + table[m ^ 1] for m in range(4))
 
 
-USE_SECOND = tuple(int(abs(offset) > 3) for offset in across(FIRST))
-MIXED = tuple(
-    second if use else first
-    for first, second, use in zip(across(FIRST), across(SECOND), USE_SECOND)
-)
 OFFSETS = {
     "beside": PARTNER,
     "first": FIRST,
-    "second": SECOND,
-    "mixed": MIXED,
+    "first_beside": across(FIRST),
     "relay": RELAY,
     "relay_beside": across(RELAY),
+    "last": LAST,
+    "last_beside": across(LAST),
 }
-COUNTS = {"beside": (2, 0, 2, 0), "first": (2, 0, 2, 0), "second": (2, 2, 0, 0), "mixed": (2, 2, 0, 0)}
-OUTSIDE = {("first", "mixed"): (0, 2, 2, 0), ("first", "second"): (0, 2, 0, 0)}
-CORNER = {1: -3, 2: 3}
+NEEDED = {name: tuple(int(abs(offset) <= 3) for offset in table) for name, table in OFFSETS.items()}
+COUNTS = {
+    "beside": (2, 0, 0, 2),
+    "first": (2, 2, 2, 2),
+    "first_beside": (0, 2, 0, 0),
+    "relay": (2, 0, 2, 0),
+    "relay_beside": (0, 2, 2, 0),
+}
+LOWER, UPPER = 0, 3
 
 
 def receive(shard, offsets, kinds=range(4)):
@@ -179,8 +181,8 @@
         def go(rows, cols):
             copy = pltpu.make_async_copy(left.at[rows, cols], corner_out, corner_sem)
             copy.start() if start else copy.wait()
-        pl.when(kind == 1)(lambda: go(pl.ds(0, half), pl.ds(0, z.span)))
-        pl.when(kind != 1)(
+        pl.when(kind == UPPER)(lambda: go(pl.ds(0, half), pl.ds(0, z.span)))
+        pl.when(kind != UPPER)(
             lambda: go(pl.ds(half, half), pl.ds((z.chunks - 1) * z.span, z.span))
         )
 
@@ -200,95 +202,83 @@
     left_copy.wait()
 
 
-def near_body(z, names, left_in, positions, prev, trace_in, *refs):
+def near_body(z, names, hand_on, left_in, positions, prev, trace_in, *refs):
     refs = list(refs)
     take = lambda count: [refs.pop(0) for _ in range(count)]
-    final = "mixed" in names
-    corner = take(1)[0] if final else None
-    sources = {name: take(2 if name == "mixed" else 1) for name in names}
+    corner = None if hand_on else take(1)[0]
+    sources = take(len(names))
     out, trace = take(2)
-    relay_left = take(1)[0] if final else None
+    last_left = take(1)[0] if hand_on else None
     left, stage, right, total, out_stage, prev_stage, vector, scalars = take(8)
-    left_sem, in_sem, prev_sem, place_sem, relay_sem, out_sems = take(6)
-    device = lax.axis_index(AXES)
-    kind = device % 4
+    left_sem, in_sem, prev_sem, place_sem, last_sem, out_sems = take(6)
+    kind = lax.axis_index(AXES) % 4
     place = {name: pick(table, kind) + z.hops for name, table in OFFSETS.items()}
 
     def chunk(n):
         return pl.ds(aligned(n, z.span), z.span)
 
-    def fetch(index, begin):
-        def go(source):
-            copy = pltpu.make_async_copy(source, stage.at[index % 2], in_sem.at[index % 2])
-            copy.start() if begin else copy.wait()
-        source = sources[names[index]]
-        if len(source) == 1:
-            go(source[0])
-        else:
-            use_second = pick(USE_SECOND, kind)
-            pl.when(use_second == 0)(lambda: go(source[0]))
-            pl.when(use_second != 0)(lambda: go(source[1]))
+    def fetch(index):
+        return pltpu.make_async_copy(sources[index], stage.at[index % 2], in_sem.at[index % 2])
 
     left_copy = pltpu.make_async_copy(left_in, left, left_sem)
     left_copy.start()
     for index in range(min(2, len(names))):
-        fetch(index, True)
+        fetch(index).start()
     prev_copy = pltpu.make_async_copy(prev, prev_stage, prev_sem)
     prev_copy.start()
     total[...] = jnp.zeros_like(total)
     trace[...] = trace_in[...]
     left_copy.wait()
-    relay_copies = []
-    if final:
-        for index, name in enumerate(("relay", "relay_beside")):
+    last_copies = []
+    if hand_on:
+        for index, name in enumerate(("last", "last_beside")):
+            spot = jnp.clip(place[name], 0, z.chunks - 1)
             copy = pltpu.make_async_copy(
-                left.at[:, chunk(place[name])], relay_left.at[:, pl.ds(index * z.span, z.span)],
-                relay_sem.at[index],
+                left.at[:, chunk(spot)], last_left.at[:, pl.ds(index * z.span, z.span)], last_sem.at[index]
             )
             copy.start()
-            relay_copies.append(copy)
-    dense_of = {}
+            last_copies.append(copy)
     for index, name in enumerate(names):
-        dense = right.at[index]
-        dense_of[name] = dense
         spot = place[name]
         slot = index % 2
-        fetch(index, False)
-        decoding = decode(
-            z, stage.at[slot, z.rows * z.slots], spot, vector.at[slot], scalars.at[slot], place_sem.at[slot]
-        )
-        dense[...] = jnp.zeros_like(dense)
-        decoding.wait()
-        scatter(z, dense, 0, stage.at[slot], lambda r, u: scalars[slot, r, u])
+        fetch(index).wait()
+
+        def add():
+            decoding = decode(
+                z, stage.at[slot, z.rows * z.slots], spot, vector.at[slot], scalars.at[slot], place_sem.at[slot]
+            )
+            right[...] = jnp.zeros_like(right)
+            decoding.wait()
+            scatter(z, right, 0, stage.at[slot], lambda r, u: scalars[slot, r, u])
+
+            def multiply(n, carry):
+                total[:, chunk(n)] += jnp.dot(
+                    left[:, chunk(spot)], right[:, chunk(n)], preferred_element_type=jnp.float32
+                )
+                return carry
+
+            lax.fori_loop(jnp.maximum(0, spot - z.hops), jnp.minimum(z.chunks, spot + z.hops + 1), multiply, 0)
+            weight = pick(COUNTS[name], kind)
+            pl.when(weight != 0)(
+                lambda: add_trace(trace, weight, left[:, chunk(spot)], right[:, chunk(z.hops)])
+            )
+
+        if all(NEEDED[name]):
+            add()
+        else:
+            pl.when(pick(NEEDED[name], kind) != 0)(add)
         if index + 2 < len(names):
-            fetch(index + 2, True)
-
-        def multiply(n, carry):
-            total[:, chunk(n)] += jnp.dot(
-                left[:, chunk(spot)], dense[:, chunk(n)], preferred_element_type=jnp.float32
-            )
-            return carry
-
-        lax.fori_loop(jnp.maximum(0, spot - z.hops), jnp.minimum(z.chunks, spot + z.hops + 1), multiply, 0)
-        weight = pick(COUNTS[name], kind)
-        pl.when(weight != 0)(
-            lambda: add_trace(trace, weight, left[:, chunk(spot)], dense[:, chunk(z.hops)])
-        )
-    if final:
-        for (one, other), table in OUTSIDE.items():
-            weight = pick(table, kind)
-            pl.when(weight != 0)(lambda: add_trace(
-                trace, weight, dense_of[one][:, chunk(place[other])], dense_of[other][:, chunk(place[one])]
-            ))
+            fetch(index + 2).start()
+    if corner is not None:
         half = z.span // 2
-        last = (z.chunks - 1) * z.span
-        pl.when(kind == 1)(lambda: add_trace(trace, jnp.float32(2), left[:, half:z.span], corner[...]))
-        pl.when(kind == 2)(
-            lambda: add_trace(trace, jnp.float32(2), left[:half, last:last + half], corner[:, :half])
+        end = (z.chunks - 1) * z.span
+        pl.when(kind == UPPER)(lambda: add_trace(trace, jnp.float32(2), left[:, half:z.span], corner[...]))
+        pl.when(kind == LOWER)(
+            lambda: add_trace(trace, jnp.float32(2), left[:half, end:end + half], corner[:, :half])
         )
     prev_copy.wait()
     emit(z, total, positions, out_stage, out, out_sems, prev_stage)
-    for copy in relay_copies:
+    for copy in last_copies:
         copy.wait()
 
 
@@ -303,42 +293,65 @@
     ]
     for copy in copies:
         copy.start()
-    places = [pick(OFFSETS[name], kind) + z.hops for name in ("relay", "relay_beside")]
-    low = jnp.maximum(0, jnp.minimum(*places) - z.hops)
-    high = jnp.minimum(z.chunks, jnp.maximum(*places) + z.hops + 1)
+    place_a = pick(OFFSETS["last"], kind) + z.hops
+    place_b = pick(OFFSETS["last_beside"], kind) + z.hops
+    needed_b = pick(NEEDED["last_beside"], kind) != 0
 
     def chunk(n):
         return pl.ds(aligned(n, z.span), z.span)
+
+    def reach(spot):
+        return jnp.maximum(0, spot - z.hops), jnp.minimum(z.chunks, spot + z.hops + 1)
 
     def clear_total(n, carry):
         total[:, chunk(n)] = jnp.zeros((z.span, z.span), jnp.float32)
         return carry
 
-    def clear_right(n, carry):
-        right[:, chunk(n)] = jnp.zeros((2 * z.span, z.span), right.dtype)
-        return carry
-
+    def prepare(index, spot):
+        copies[index].wait()
+        decoding = decode(
+            z, stage.at[index, z.rows * z.slots], spot, vector.at[index], scalars.at[index], place_sem.at[index]
+        )
+
+        def clear(n, carry):
+            right[index, :, chunk(n)] = jnp.zeros((z.span, z.span), right.dtype)
+            return carry
+
+        lax.fori_loop(*reach(spot), clear, 0)
+        decoding.wait()
+        scatter(z, right.at[index], 0, stage.at[index], lambda r, u: scalars[index, r, u])
+
+    low, high = reach(place_a)
     lax.fori_loop(0, low, clear_total, 0)
     lax.fori_loop(high, z.chunks, clear_total, 0)
     total[:, z.window * z.block:] = jnp.zeros((z.span, z.block), jnp.float32)
-    decodings = []
-    for index in range(2):
-        copies[index].wait()
-        decodings.append(decode(
-            z, stage.at[index, z.rows * z.slots], places[index], vector.at[index], scalars.at[index],
-            place_sem.at[index],
-        ))
-    lax.fori_loop(low, high, clear_right, 0)
-    for index in range(2):
-        decodings[index].wait()
-        scatter(z, right, index * z.span, stage.at[index], lambda r, u: scalars[index, r, u])
+    prepare(0, place_a)
     copies[2].wait()
 
     def multiply(n, carry):
-        total[:, chunk(n)] = jnp.dot(left[...], right[:, chunk(n)], preferred_element_type=jnp.float32)
+        total[:, chunk(n)] = jnp.dot(
+            left[:, :z.span], right[0, :, chunk(n)], preferred_element_type=jnp.float32
+        )
         return carry
 
     lax.fori_loop(low, high, multiply, 0)
+
+    @pl.when(needed_b)
+    def _():
+        prepare(1, place_b)
+
+        def multiply_add(n, carry):
+            total[:, chunk(n)] += jnp.dot(
+                left[:, z.span:], right[1, :, chunk(n)], preferred_element_type=jnp.float32
+            )
+            return carry
+
+        lax.fori_loop(*reach(place_b), multiply_add, 0)
+
+    @pl.when(jnp.logical_not(needed_b))
+    def _():
+        copies[1].wait()
+
     copies[3].wait()
     emit(z, total, positions, out_stage, out, out_sems, prev_stage)
 
@@ -389,7 +402,6 @@
         0, WHOLE_VMEM,
     )
     first = receive(payload, FIRST)
-    second = receive(payload, SECOND)
     beside = receive(payload, PARTNER)
 
     total, left, corner, positions, trace = call(
@@ -405,55 +417,57 @@
         ],
         1,
     )
-    corner = receive(corner, (0, CORNER[1], CORNER[2], 0), (1, 2))
-
-    def near(names, arrays, total, trace):
-        final = "mixed" in names
-        extra = [shape((z.span, 2 * z.span), dtype)] if final else []
+    corner = receive(corner, (3, 0, 0, -3), (LOWER, UPPER))
+
+    def near(names, arrays, total, trace, corner=None):
+        hand_on = corner is None
+        extra = [shape((z.span, 2 * z.span), dtype)] * hand_on
         return call(
-            z, functools.partial(near_body, z, names),
-            [left, positions, total, trace] + ([corner] if final else []) + arrays,
-            [ANY, SMEM, ANY, VMEM] + [VMEM] * final + [ANY] * len(arrays),
+            z, functools.partial(near_body, z, names, hand_on),
+            [left, positions, total, trace] + ([] if hand_on else [corner]) + arrays,
+            [ANY, SMEM, ANY, VMEM] + [VMEM] * (not hand_on) + [ANY] * len(arrays),
             [sums, line] + extra,
             [ANY, VMEM] + [ANY] * len(extra),
             [
-                dense, pltpu.VMEM((2,) + payload_shape, dtype),
-                pltpu.VMEM((len(names), z.span, z.wide), dtype), total_buffer,
+                dense, pltpu.VMEM((2,) + payload_shape, dtype), dense, total_buffer,
                 pltpu.VMEM(tiles.shape, jnp.float32), pltpu.VMEM(tiles.shape, jnp.float32), *places,
                 DMA, DMA((2,)), DMA, DMA((2,)), DMA((2,)), DMA((z.rows,)),
             ],
             len(names),
         )
 
-    total, trace = near(("beside",), [beside], total, trace)
-    first, second, total, trace = lax.optimization_barrier((first, second, total, trace))
+    def from_partner(array, name):
+        return receive(array, PARTNER, [m for m in range(4) if NEEDED[name][m]])
+
+    first, corner, total = lax.optimization_barrier((first, corner, total))
     relay = receive(first, RELAY_FROM)
-    mixed = [
-        receive(first, PARTNER, [m for m in range(4) if not USE_SECOND[m]]),
-        receive(second, PARTNER, [m for m in range(4) if USE_SECOND[m]]),
-    ]
-    total, trace, relay_left = near(("first", "second", "mixed"), [first, second, *mixed], total, trace)
+    first_beside = from_partner(first, "first_beside")
+    total, trace = near(("beside", "first", "first_beside"), [beside, first, first_beside], total, trace, corner)
+    relay, payload, total, trace = lax.optimization_barrier((relay, payload, total, trace))
+    last = receive(payload, LAST)
+    relay_beside = receive(relay, PARTNER)
+    total, trace, last_left = near(("relay", "relay_beside"), [relay, relay_beside], total, trace)
     assert devices & (devices - 1) == 0
     steps = [1 << bit for bit in range(devices.bit_length() - 1)]
     for step in steps[:1] + steps[3:]:
         trace = exchange(trace, step)
-    relay, total, trace = lax.optimization_barrier((relay, total, trace))
-    relay_beside = receive(relay, PARTNER)
+    last, total, trace = lax.optimization_barrier((last, total, trace))
+    last_beside = from_partner(last, "last_beside")
     trace = exchange(trace, steps[2])
-    relay_beside, trace = lax.optimization_barrier((relay_beside, trace))
+    last_beside, trace = lax.optimization_barrier((last_beside, trace))
     trace = exchange(trace, steps[1])
     square = call(
-        z, functools.partial(last_body, z), [relay_left, positions, total, relay, relay_beside],
+        z, functools.partial(last_body, z), [last_left, positions, total, last, last_beside],
         [ANY, SMEM, ANY, ANY, ANY],
         [shape(tiles.shape, dtype)],
         [ANY],
         [
             pltpu.VMEM((z.span, 2 * z.span), dtype), pltpu.VMEM((2,) + payload_shape, dtype),
-            pltpu.VMEM((2 * z.span, z.wide), dtype), total_buffer,
+            pltpu.VMEM((2, z.span, z.wide), dtype), total_buffer,
             pltpu.VMEM(tiles.shape, dtype), pltpu.VMEM(tiles.shape, jnp.float32), *places,
             DMA, DMA((2,)), DMA, DMA((2,)), DMA((z.rows,)),
         ],
-        2, WHOLE_VMEM,
+        2,
     )[0]
     return square, jnp.sum(trace) / (z.all_rows * z.block)
 

time: 157 us -> 133 us (0.85)
  starting transfers between devices: 53.6 us -> 16.9 us
  waiting for transfers between devices: 47.1 us -> 63.5 us
  Pallas kernels: 50.1 us -> 44.6 us
    ppermute x5, starting transfers between devices: 38.2 us -> 3.69 us  [exchange(): lax.ppermute(value, AXES, [(d, d ^ step) for d in range(size)])]
    ppermute x8, waiting for transfers between devices: 37.2 us -> 51.3 us  [receive(): return lax.ppermute(shard, AXES, pairs)]
    pallas_call x5, Pallas kernels: 50.1 us -> 44.6 us  [call(): pl.pallas_call(kernel, out_shape=out_shape, in_specs=in_specs, out_specs=...]
    ppermute x5, waiting for transfers between devices: 9.92 us -> 12.2 us  [exchange(): lax.ppermute(value, AXES, [(d, d ^ step) for d in range(size)])]
    ppermute x8, starting transfers between devices: 15.4 us -> 13.2 us  [receive(): return lax.ppermute(shard, AXES, pairs)]
    unnamed x14 -> x8, local copies, waits for them, and re-layouts: 3.13 us -> 4.59 us
  transfers between devices with their start and end apart: 13 -> 13, of which waited for: 7 -> 11; matrix products, arithmetic and copies ran while one was open for 0% -> 0% of each run, Pallas kernels for 30% -> 31%
where the time goes in v5:
time: 133 us
  waiting for transfers between devices  63.5 us (48%)
  Pallas kernels  44.6 us (34%)
  starting transfers between devices  16.9 us (13%)
  local copies, waits for them, and re-layouts  4.59 us (3%)
  between operations  2.56 us (2%)
    ppermute x8, waiting for transfers between devices, receive(): return lax.ppermute(shard, AXES, pairs)  51.3 us
    pallas_call x5, Pallas kernels, call(): pl.pallas_call(kernel, out_shape=out_shape, in_specs=in_specs, out_specs=...  44.6 us
    ppermute x8, starting transfers between devices, receive(): return lax.ppermute(shard, AXES, pairs)  13.2 us
    ppermute x5, waiting for transfers between devices, exchange(): lax.ppermute(value, AXES, [(d, d ^ step) for d in range(size)])  12.2 us
    unnamed x8, local copies, waits for them, and re-layouts  4.59 us
    ppermute x5, starting transfers between devices, exchange(): lax.ppermute(value, AXES, [(d, d ^ step) for d in range(size)])  3.69 us
  transfers between devices with their start and end apart: 13, of which 11 were waited for; matrix products, arithmetic and copies ran while one was open for 0% of the time, Pallas kernels for 31%

profile of v5, /device:TPU:0, one launch (start us, length us, event | category | flops | bytes accessed | tf_op | source)
XLA Modules:
  0.0 132.7 jit_solution(14355873471598071498)
XLA Ops:
  0.6 0.0 copy-start.2
  0.6 0.0 copy-start.1
  0.6 3.5 %shard_map.42 = bf16[81,128,128]{2,1,0:T(8,128)(2,1)} custom-call(bf16[4,20,128,128]{3,2,1,0:T(8,128)(2,1)} %tiles.1, s32[4,20]{1,0:T(4,128)} %columns.3), custom_call_target="tpu_custom_call" | custom-call | bytes 10485760 | tf_op jit(solution)/shard_map/pallas_call | solution.py:366
  4.1 5.5 %collective-permute-start = (bf16[81,128,128]{2,1,0:T(8,128)(2,1)}, bf16[81,128,128]{2,1,0:T(8,128)(2,1)S(1)}, u32[]{:S(2)}, u32[]{:S(2)}) collective-permute-start(bf16[81,128,128]{2,1,0:T(8,128)(2,1)} %shard_map.42), channel_id=1, source_target_pairs={{2,0},{4,1},{31,2},{1,3},{6,4},{8,5},{3,6},{5,7},{10,8},{12,9},{7,... | collective-permute-start | bytes 7962632 | tf_op jit(solution)/shard_map/ppermute | solution.py:50
  9.6 0.0 copy-done.2
  9.6 0.0 copy-done.1
  9.6 7.3 %shard_map.41 = (f32[4,20,128,128]{3,2,1,0:T(8,128)S(1)}, bf16[512,3712]{1,0:T(8,128)(2,1)S(1)}, bf16[256,512]{1,0:T(8,128)(2,1)S(1)}, s32[4,20]{1,0:T(4,128)S(1)}, f32[1,512]{1,0:T(1,128)S(1)}) custom-call(bf16[4,20,128,128]{3,2,1,0:T(8,128)(2,1)S(1)} %copy-done.1, s32[4,20]{1,0:T(4,128)S(1)} %copy-done.2), custom_call_target="tpu_custom_call" | custom-call | flops 1879048192 | bytes 13107200 | tf_op jit(solution)/shard_map/pallas_call | solution.py:366
  17.0 0.0 copy-start.3
  17.0 2.3 %copy-done.3 = f32[4,20,128,128]{3,2,1,0:T(8,128)} copy-done((f32[4,20,128,128]{3,2,1,0:T(8,128)}, f32[4,20,128,128]{3,2,1,0:T(8,128)S(1)}, u32[]{:S(2)}) %copy-start.3) | copy-done | bytes 5242904
  19.3 1.9 %collective-permute-start.1 = (bf16[256,512]{1,0:T(8,128)(2,1)S(1)}, bf16[256,512]{1,0:T(8,128)(2,1)S(1)}, u32[]{:S(2)}, u32[]{:S(2)}) collective-permute-start(bf16[256,512]{1,0:T(8,128)(2,1)S(1)} %get-tuple-element.26), channel_id=1, source_target_pairs={{3,0},{0,3},{7,4},{4,7},{11,8},{8,11},{15,12},{12,15},{19,16},{16,... | collective-permute-start | bytes 786440 | tf_op jit(solution)/shard_map/ppermute | solution.py:50
  21.2 0.1 collective-permute-start.3
  21.3 8.6 %collective-permute-done.1.refs_0_ = bf16[256,512]{1,0:T(8,128)(2,1)S(1)} collective-permute-done((bf16[256,512]{1,0:T(8,128)(2,1)S(1)}, bf16[256,512]{1,0:T(8,128)(2,1)S(1)}, u32[]{:S(2)}, u32[]{:S(2)}) %collective-permute-start.1) | collective-permute-done | bytes 262176 | tf_op jit(solution)/shard_map/ppermute | solution.py:50
  29.8 10.3 %collective-permute-done.refs_2_ = bf16[81,128,128]{2,1,0:T(8,128)(2,1)S(1)} collective-permute-done((bf16[81,128,128]{2,1,0:T(8,128)(2,1)}, bf16[81,128,128]{2,1,0:T(8,128)(2,1)S(1)}, u32[]{:S(2)}, u32[]{:S(2)}) %collective-permute-start) | collective-permute-done | bytes 2654240 | tf_op jit(solution)/shard_map/ppermute | solution.py:50
  40.1 1.4 %collective-permute-start.4 = (bf16[81,128,128]{2,1,0:T(8,128)(2,1)S(1)}, bf16[81,128,128]{2,1,0:T(8,128)(2,1)S(1)}, u32[]{:S(2)}, u32[]{:S(2)}) collective-permute-start(bf16[81,128,128]{2,1,0:T(8,128)(2,1)S(1)} %collective-permute-done.refs_2_), channel_id=1, source_target_pairs={{0,1},{3,2},{4,5},{7,6},{8,9},{11,10},{12,13},{15,14},{16,17},{19,... | collective-permute-start | bytes 7962632 | tf_op jit(solution)/shard_map/ppermute | solution.py:50
  41.6 0.1 collective-permute-start.2
  41.7 0.0 collective-permute-done.3.refs_1_
  41.7 4.3 %collective-permute-done.4.refs_3_ = bf16[81,128,128]{2,1,0:T(8,128)(2,1)S(1)} collective-permute-done((bf16[81,128,128]{2,1,0:T(8,128)(2,1)S(1)}, bf16[81,128,128]{2,1,0:T(8,128)(2,1)S(1)}, u32[]{:S(2)}, u32[]{:S(2)}) %collective-permute-start.4) | collective-permute-done | bytes 2654240 | tf_op jit(solution)/shard_map/ppermute | solution.py:50
  46.0 12.5 %shard_map.43 = (f32[4,20,128,128]{3,2,1,0:T(8,128)S(1)}, f32[1,512]{1,0:T(1,128)S(1)}) custom-call(bf16[512,3712]{1,0:T(8,128)(2,1)S(1)} %get-tuple-element.24.left_in, s32[4,20]{1,0:T(4,128)S(1)} %get-tuple-element.25.positions, f32[4,20,128,128]{3,2,1,0:T(8,128)} %copy-done.3, f32[1,512]{1,0:T(1,128)S(1)} %get-tuple-element.30.trace_in, ...), custom_call_target="tpu_custom_call" | custom-call | flops 5637144576 | bytes 18350080 | tf_op jit(solution)/shard_map/pallas_call | solution.py:366
  58.5 0.0 copy-start
  58.5 2.3 %copy-done = f32[4,20,128,128]{3,2,1,0:T(8,128)} copy-done((f32[4,20,128,128]{3,2,1,0:T(8,128)}, f32[4,20,128,128]{3,2,1,0:T(8,128)S(1)}, u32[]{:S(2)}) %copy-start) | copy-done | bytes 5242904
  60.8 12.9 %collective-permute-done.2.refs_0_ = bf16[81,128,128]{2,1,0:T(8,128)(2,1)S(1)} collective-permute-done((bf16[81,128,128]{2,1,0:T(8,128)(2,1)S(1)}, bf16[81,128,128]{2,1,0:T(8,128)(2,1)S(1)}, u32[]{:S(2)}, u32[]{:S(2)}) %collective-permute-start.2) | collective-permute-done | bytes 2654240 | tf_op jit(solution)/shard_map/ppermute | solution.py:50
  73.7 2.9 %collective-permute-start.5 = (bf16[81,128,128]{2,1,0:T(8,128)(2,1)S(1)}, bf16[81,128,128]{2,1,0:T(8,128)(2,1)S(1)}, u32[]{:S(2)}, u32[]{:S(2)}) collective-permute-start(bf16[81,128,128]{2,1,0:T(8,128)(2,1)S(1)} %collective-permute-done.2.refs_0_), channel_id=1, source_target_pairs={{1,0},{0,1},{3,2},{2,3},{5,4},{4,5},{7,6},{6,7},{9,8},{8,9},{11,10... | collective-permute-start | bytes 7962632 | tf_op jit(solution)/shard_map/ppermute | solution.py:50
  76.5 0.0 collective-permute-start.6
  76.5 4.6 %collective-permute-done.5.refs_1_ = bf16[81,128,128]{2,1,0:T(8,128)(2,1)S(1)} collective-permute-done((bf16[81,128,128]{2,1,0:T(8,128)(2,1)S(1)}, bf16[81,128,128]{2,1,0:T(8,128)(2,1)S(1)}, u32[]{:S(2)}, u32[]{:S(2)}) %collective-permute-start.5) | collective-permute-done | bytes 2654240 | tf_op jit(solution)/shard_map/ppermute | solution.py:50
  81.1 11.8 %shard_map.44 = (f32[4,20,128,128]{3,2,1,0:T(8,128)S(1)}, f32[1,512]{1,0:T(1,128)S(1)}, bf16[512,1024]{1,0:T(8,128)(2,1)S(1)}) custom-call(bf16[512,3712]{1,0:T(8,128)(2,1)S(1)} %get-tuple-element.24.left_in, s32[4,20]{1,0:T(4,128)S(1)} %get-tuple-element.25.positions, f32[4,20,128,128]{3,2,1,0:T(8,128)} %copy-done, ...), custom_call_target="tpu_custom_call" | custom-call | flops 3758096384 | bytes 15728640 | tf_op jit(solution)/shard_map/pallas_call | solution.py:366
  92.9 0.1 collective-permute-start.7
  93.0 1.1 collective-permute-done.7
  94.1 0.0 collective-permute-start.8
  94.1 3.6 %collective-permute-done.8 = f32[1,512]{1,0:T(1,128)S(1)} collective-permute-done((f32[1,512]{1,0:T(1,128)S(1)}, f32[1,512]{1,0:T(1,128)S(1)}, u32[]{:S(2)}, u32[]{:S(2)}) %collective-permute-start.8) | collective-permute-done | bytes 2080 | tf_op jit(solution)/shard_map/ppermute | solution.py:55
  97.7 0.6 collective-permute-start.9
  98.3 3.9 %collective-permute-done.9 = f32[1,512]{1,0:T(1,128)S(1)} collective-permute-done((f32[1,512]{1,0:T(1,128)S(1)}, f32[1,512]{1,0:T(1,128)S(1)}, u32[]{:S(2)}, u32[]{:S(2)}) %collective-permute-start.9) | collective-permute-done | bytes 2080 | tf_op jit(solution)/shard_map/ppermute | solution.py:55
  102.2 8.7 %collective-permute-done.6.source_a = bf16[81,128,128]{2,1,0:T(8,128)(2,1)S(1)} collective-permute-done((bf16[81,128,128]{2,1,0:T(8,128)(2,1)}, bf16[81,128,128]{2,1,0:T(8,128)(2,1)S(1)}, u32[]{:S(2)}, u32[]{:S(2)}) %collective-permute-start.6) | collective-permute-done | bytes 2654240 | tf_op jit(solution)/shard_map/ppermute | solution.py:50
  110.9 1.3 collective-permute-start.10
  112.2 0.1 collective-permute-start.11
  112.3 3.6 %collective-permute-done.11 = f32[1,512]{1,0:T(1,128)S(1)} collective-permute-done((f32[1,512]{1,0:T(1,128)S(1)}, f32[1,512]{1,0:T(1,128)S(1)}, u32[]{:S(2)}, u32[]{:S(2)}) %collective-permute-start.11) | collective-permute-done | bytes 2080 | tf_op jit(solution)/shard_map/ppermute | solution.py:55
  115.9 1.9 %collective-permute-done.10.source_b = bf16[81,128,128]{2,1,0:T(8,128)(2,1)S(1)} collective-permute-done((bf16[81,128,128]{2,1,0:T(8,128)(2,1)S(1)}, bf16[81,128,128]{2,1,0:T(8,128)(2,1)S(1)}, u32[]{:S(2)}, u32[]{:S(2)}) %collective-permute-start.10) | collective-permute-done | bytes 2654240 | tf_op jit(solution)/shard_map/ppermute | solution.py:50
  117.8 2.9 %collective-permute-start.12 = (f32[1,512]{1,0:T(1,128)S(1)}, f32[1,512]{1,0:T(1,128)S(1)}, u32[]{:S(2)}, u32[]{:S(2)}) collective-permute-start(f32[1,512]{1,0:T(1,128)S(1)} %add.18), channel_id=1, source_target_pairs={{0,2},{1,3},{2,0},{3,1},{4,6},{5,7},{6,4},{7,5},{8,10},{9,11},{10,... | collective-permute-start | bytes 6152 | tf_op jit(solution)/shard_map/ppermute | solution.py:55
  120.7 9.6 %shard_map.45 = bf16[4,20,128,128]{3,2,1,0:T(8,128)(2,1)} custom-call(bf16[512,1024]{1,0:T(8,128)(2,1)S(1)} %get-tuple-element.37.left_in, s32[4,20]{1,0:T(4,128)S(1)} %get-tuple-element.25.positions, f32[4,20,128,128]{3,2,1,0:T(8,128)S(1)} %get-tuple-element.41.prev, bf16[81,128,128]{2,1,0:T(8,128)(2,1)S(1)} %collective-permute-done.6.source_a, ...), custom_call_target="tpu_custom_call" | custom-call | flops 3758096384 | bytes 15728640 | tf_op jit(solution)/shard_map/pallas_call | solution.py:366
  130.3 0.0 collective-permute-done.12
  130.4 0.6 add_reduce_fusion
  (4 shorter events, 0.0 us)
Async XLA Ops:
  0.6 9.0 %copy-start.2 = (s32[4,20]{1,0:T(4,128)S(1)}, s32[4,20]{1,0:T(4,128)}, u32[]{:S(2)}) copy-start(s32[4,20]{1,0:T(4,128)} %columns.3) | copy-start | bytes 964
  0.6 9.0 %copy-start.1 = (bf16[4,20,128,128]{3,2,1,0:T(8,128)(2,1)S(1)}, bf16[4,20,128,128]{3,2,1,0:T(8,128)(2,1)}, u32[]{:S(2)}) copy-start(bf16[4,20,128,128]{3,2,1,0:T(8,128)(2,1)} %tiles.1) | copy-start | bytes 7864324
  4.1 36.0 %collective-permute-start = (bf16[81,128,128]{2,1,0:T(8,128)(2,1)}, bf16[81,128,128]{2,1,0:T(8,128)(2,1)S(1)}, u32[]{:S(2)}, u32[]{:S(2)}) collective-permute-start(bf16[81,128,128]{2,1,0:T(8,128)(2,1)} %shard_map.42), channel_id=1, source_target_pairs={{2,0},{4,1},{31,2},{1,3},{6,4},{8,5},{3,6},{5,7},{10,8},{12,9},{7,... | collective-permute-start | bytes 7962632 | tf_op jit(solution)/shard_map/ppermute | solution.py:50
  17.0 2.3 %copy-start.3 = (f32[4,20,128,128]{3,2,1,0:T(8,128)}, f32[4,20,128,128]{3,2,1,0:T(8,128)S(1)}, u32[]{:S(2)}) copy-start(f32[4,20,128,128]{3,2,1,0:T(8,128)S(1)} %get-tuple-element.29.prev) | copy-start | bytes 15728644
  19.3 10.6 %collective-permute-start.1 = (bf16[256,512]{1,0:T(8,128)(2,1)S(1)}, bf16[256,512]{1,0:T(8,128)(2,1)S(1)}, u32[]{:S(2)}, u32[]{:S(2)}) collective-permute-start(bf16[256,512]{1,0:T(8,128)(2,1)S(1)} %get-tuple-element.26), channel_id=1, source_target_pairs={{3,0},{0,3},{7,4},{4,7},{11,8},{8,11},{15,12},{12,15},{19,16},{16,... | collective-permute-start | bytes 786440 | tf_op jit(solution)/shard_map/ppermute | solution.py:50
  21.2 20.5 %collective-permute-start.3 = (bf16[81,128,128]{2,1,0:T(8,128)(2,1)}, bf16[81,128,128]{2,1,0:T(8,128)(2,1)S(1)}, u32[]{:S(2)}, u32[]{:S(2)}) collective-permute-start(bf16[81,128,128]{2,1,0:T(8,128)(2,1)} %shard_map.42), channel_id=1, source_target_pairs={{1,0},{0,1},{3,2},{2,3},{5,4},{4,5},{7,6},{6,7},{9,8},{8,9},{11,10... | collective-permute-start | bytes 7962632 | tf_op jit(solution)/shard_map/ppermute | solution.py:50
  40.1 5.9 %collective-permute-start.4 = (bf16[81,128,128]{2,1,0:T(8,128)(2,1)S(1)}, bf16[81,128,128]{2,1,0:T(8,128)(2,1)S(1)}, u32[]{:S(2)}, u32[]{:S(2)}) collective-permute-start(bf16[81,128,128]{2,1,0:T(8,128)(2,1)S(1)} %collective-permute-done.refs_2_), channel_id=1, source_target_pairs={{0,1},{3,2},{4,5},{7,6},{8,9},{11,10},{12,13},{15,14},{16,17},{19,... | collective-permute-start | bytes 7962632 | tf_op jit(solution)/shard_map/ppermute | solution.py:50
  41.6 32.1 %collective-permute-start.2 = (bf16[81,128,128]{2,1,0:T(8,128)(2,1)S(1)}, bf16[81,128,128]{2,1,0:T(8,128)(2,1)S(1)}, u32[]{:S(2)}, u32[]{:S(2)}) collective-permute-start(bf16[81,128,128]{2,1,0:T(8,128)(2,1)S(1)} %collective-permute-done.refs_2_), channel_id=1, source_target_pairs={{2,0},{28,1},{7,2},{1,3},{6,4},{0,5},{11,6},{5,7},{10,8},{4,9},{15... | collective-permute-start | bytes 7962632 | tf_op jit(solution)/shard_map/ppermute | solution.py:50
  58.5 2.3 %copy-start = (f32[4,20,128,128]{3,2,1,0:T(8,128)}, f32[4,20,128,128]{3,2,1,0:T(8,128)S(1)}, u32[]{:S(2)}) copy-start(f32[4,20,128,128]{3,2,1,0:T(8,128)S(1)} %get-tuple-element.34.prev) | copy-start | bytes 15728644
  73.7 7.5 %collective-permute-start.5 = (bf16[81,128,128]{2,1,0:T(8,128)(2,1)S(1)}, bf16[81,128,128]{2,1,0:T(8,128)(2,1)S(1)}, u32[]{:S(2)}, u32[]{:S(2)}) collective-permute-start(bf16[81,128,128]{2,1,0:T(8,128)(2,1)S(1)} %collective-permute-done.2.refs_0_), channel_id=1, source_target_pairs={{1,0},{0,1},{3,2},{2,3},{5,4},{4,5},{7,6},{6,7},{9,8},{8,9},{11,10... | collective-permute-start | bytes 7962632 | tf_op jit(solution)/shard_map/ppermute | solution.py:50
  76.5 34.4 %collective-permute-start.6 = (bf16[81,128,128]{2,1,0:T(8,128)(2,1)}, bf16[81,128,128]{2,1,0:T(8,128)(2,1)S(1)}, u32[]{:S(2)}, u32[]{:S(2)}) collective-permute-start(bf16[81,128,128]{2,1,0:T(8,128)(2,1)} %shard_map.42), channel_id=1, source_target_pairs={{29,0},{3,1},{0,2},{6,3},{1,4},{7,5},{4,6},{10,7},{5,8},{11,9},{8,... | collective-permute-start | bytes 7962632 | tf_op jit(solution)/shard_map/ppermute | solution.py:50
  92.9 1.2 collective-permute-start.7
  94.1 3.6 %collective-permute-start.8 = (f32[1,512]{1,0:T(1,128)S(1)}, f32[1,512]{1,0:T(1,128)S(1)}, u32[]{:S(2)}, u32[]{:S(2)}) collective-permute-start(f32[1,512]{1,0:T(1,128)S(1)} %add.15), channel_id=1, source_target_pairs={{0,8},{1,9},{2,10},{3,11},{4,12},{5,13},{6,14},{7,15},{8,0},{9,1},... | collective-permute-start | bytes 6152 | tf_op jit(solution)/shard_map/ppermute | solution.py:55
  97.7 4.5 %collective-permute-start.9 = (f32[1,512]{1,0:T(1,128)S(1)}, f32[1,512]{1,0:T(1,128)S(1)}, u32[]{:S(2)}, u32[]{:S(2)}) collective-permute-start(f32[1,512]{1,0:T(1,128)S(1)} %add.16), channel_id=1, source_target_pairs={{0,16},{1,17},{2,18},{3,19},{4,20},{5,21},{6,22},{7,23},{8,24},{9,... | collective-permute-start | bytes 6152 | tf_op jit(solution)/shard_map/ppermute | solution.py:55
  110.9 6.8 %collective-permute-start.10 = (bf16[81,128,128]{2,1,0:T(8,128)(2,1)S(1)}, bf16[81,128,128]{2,1,0:T(8,128)(2,1)S(1)}, u32[]{:S(2)}, u32[]{:S(2)}) collective-permute-start(bf16[81,128,128]{2,1,0:T(8,128)(2,1)S(1)} %collective-permute-done.6.source_a), channel_id=1, source_target_pairs={{1,0},{2,3},{5,4},{6,7},{9,8},{10,11},{13,12},{14,15},{17,16},{18,... | collective-permute-start | bytes 7962632 | tf_op jit(solution)/shard_map/ppermute | solution.py:50
  112.2 3.7 %collective-permute-start.11 = (f32[1,512]{1,0:T(1,128)S(1)}, f32[1,512]{1,0:T(1,128)S(1)}, u32[]{:S(2)}, u32[]{:S(2)}) collective-permute-start(f32[1,512]{1,0:T(1,128)S(1)} %add.17), channel_id=1, source_target_pairs={{0,4},{1,5},{2,6},{3,7},{4,0},{5,1},{6,2},{7,3},{8,12},{9,13},{10,... | collective-permute-start | bytes 6152 | tf_op jit(solution)/shard_map/ppermute | solution.py:55
  117.8 12.6 %collective-permute-start.12 = (f32[1,512]{1,0:T(1,128)S(1)}, f32[1,512]{1,0:T(1,128)S(1)}, u32[]{:S(2)}, u32[]{:S(2)}) collective-permute-start(f32[1,512]{1,0:T(1,128)S(1)} %add.18), channel_id=1, source_target_pairs={{0,2},{1,3},{2,0},{3,1},{4,6},{5,7},{6,4},{7,5},{8,10},{9,11},{10,... | collective-permute-start | bytes 6152 | tf_op jit(solution)/shard_map/ppermute | solution.py:55

commit v6 on v5

--- a/solution.py
+++ b/solution.py
@@ -50,9 +50,12 @@
     return lax.ppermute(shard, AXES, pairs)
 
 
+def fetch(value, step):
+    return lax.ppermute(value, AXES, [(d, d ^ step) for d in range(lax.axis_size(AXES))])
+
+
 def exchange(value, step):
-    size = lax.axis_size(AXES)
-    return value + lax.ppermute(value, AXES, [(d, d ^ step) for d in range(size)])
+    return value + fetch(value, step)
 
 
 def pick(table, kind):
@@ -88,10 +91,11 @@
 
 
 def scatter(z, dense, top, source, place):
+    half = z.rows // 2
     for r in range(z.rows):
         def one(u, carry):
             column = pl.ds(aligned(place(r, u), z.block), z.block)
-            dense[top + r * z.block:top + (r + 1) * z.block, column] = source[r * z.slots + u]
+            dense[top + r * z.block:top + (r + 1) * z.block, column] = source[r // half, r % half * z.slots + u]
             return carry
         lax.fori_loop(0, z.slots, one, 0, unroll=4)
 
@@ -105,13 +109,14 @@
     return copy
 
 
-def pack_body(z, tiles, columns, out, stage, padded, offsets, in_sems, out_sems):
+def pack_body(z, tiles, columns, lower, upper, stage, padded, offsets, in_sems, out_sems):
     copies = []
+    half = z.rows // 2
     for r in range(z.rows):
-        rows = pl.ds(r * z.slots, z.slots)
+        target = (lower, upper)[r // half].at[pl.ds(r % half * z.slots, z.slots)]
         copies.append((
-            pltpu.make_async_copy(tiles.at[r], stage.at[rows], in_sems.at[r]),
-            pltpu.make_async_copy(stage.at[rows], out.at[rows], out_sems.at[r]),
+            pltpu.make_async_copy(tiles.at[r], stage.at[r], in_sems.at[r]),
+            pltpu.make_async_copy(stage.at[r], target, out_sems.at[r]),
         ))
     for copy, _ in copies:
         copy.start()
@@ -125,14 +130,17 @@
     offset = jnp.where(column < 0, EMPTY, offset)
     offsets[...] = jnp.zeros_like(offsets)
     offsets[0:16, :] = offset.astype(jnp.float32).astype(offsets.dtype)
-    last = pltpu.make_async_copy(offsets, out.at[z.rows * z.slots], out_sems.at[z.rows])
-    last.start()
+    ends = []
+    for index, out in enumerate((lower, upper)):
+        ends.append(pltpu.make_async_copy(offsets, out.at[half * z.slots], out_sems.at[z.rows + index]))
+        ends[-1].start()
     for load, store in copies:
         load.wait()
         store.start()
     for _, store in copies:
         store.wait()
-    last.wait()
+    for copy in ends:
+        copy.wait()
 
 
 def emit(z, total, positions, stage, out, sems, prev=None):
@@ -202,11 +210,11 @@
     left_copy.wait()
 
 
-def near_body(z, names, hand_on, left_in, positions, prev, trace_in, *refs):
+def near_body(z, names, with_corner, hand_on, left_in, positions, prev, trace_in, *refs):
     refs = list(refs)
     take = lambda count: [refs.pop(0) for _ in range(count)]
-    corner = None if hand_on else take(1)[0]
-    sources = take(len(names))
+    corner = take(1)[0] if with_corner else None
+    sources = [take(2) for _ in names]
     out, trace = take(2)
     last_left = take(1)[0] if hand_on else None
     left, stage, right, total, out_stage, prev_stage, vector, scalars = take(8)
@@ -217,13 +225,15 @@
     def chunk(n):
         return pl.ds(aligned(n, z.span), z.span)
 
-    def fetch(index):
-        return pltpu.make_async_copy(sources[index], stage.at[index % 2], in_sem.at[index % 2])
+    def fetch(index, begin):
+        for h in range(2):
+            copy = pltpu.make_async_copy(sources[index][h], stage.at[index % 2, h], in_sem.at[index % 2, h])
+            copy.start() if begin else copy.wait()
 
     left_copy = pltpu.make_async_copy(left_in, left, left_sem)
     left_copy.start()
     for index in range(min(2, len(names))):
-        fetch(index).start()
+        fetch(index, True)
     prev_copy = pltpu.make_async_copy(prev, prev_stage, prev_sem)
     prev_copy.start()
     total[...] = jnp.zeros_like(total)
@@ -241,11 +251,11 @@
     for index, name in enumerate(names):
         spot = place[name]
         slot = index % 2
-        fetch(index).wait()
+        fetch(index, False)
 
         def add():
             decoding = decode(
-                z, stage.at[slot, z.rows * z.slots], spot, vector.at[slot], scalars.at[slot], place_sem.at[slot]
+                z, stage.at[slot, 0, z.rows // 2 * z.slots], spot, vector.at[slot], scalars.at[slot], place_sem.at[slot]
             )
             right[...] = jnp.zeros_like(right)
             decoding.wait()
@@ -268,7 +278,7 @@
         else:
             pl.when(pick(NEEDED[name], kind) != 0)(add)
         if index + 2 < len(names):
-            fetch(index + 2).start()
+            fetch(index + 2, True)
     if corner is not None:
         half = z.span // 2
         end = (z.chunks - 1) * z.span
@@ -282,12 +292,14 @@
         copy.wait()
 
 
-def last_body(z, left_in, positions, prev, source_a, source_b, out, left, stage, right, total, out_stage,
+def last_body(z, left_in, positions, prev, a_lower, a_upper, b_lower, b_upper, out, left, stage, right, total, out_stage,
               prev_stage, vector, scalars, left_sem, in_sem, prev_sem, place_sem, out_sems):
     kind = lax.axis_index(AXES) % 4
     copies = [
-        pltpu.make_async_copy(source_a, stage.at[0], in_sem.at[0]),
-        pltpu.make_async_copy(source_b, stage.at[1], in_sem.at[1]),
+        *[
+            pltpu.make_async_copy(source, stage.at[index // 2, index % 2], in_sem.at[index // 2, index % 2])
+            for index, source in enumerate((a_lower, a_upper, b_lower, b_upper))
+        ],
         pltpu.make_async_copy(left_in, left, left_sem),
         pltpu.make_async_copy(prev, prev_stage, prev_sem),
     ]
@@ -308,9 +320,10 @@
         return carry
 
     def prepare(index, spot):
-        copies[index].wait()
+        copies[2 * index].wait()
+        copies[2 * index + 1].wait()
         decoding = decode(
-            z, stage.at[index, z.rows * z.slots], spot, vector.at[index], scalars.at[index], place_sem.at[index]
+            z, stage.at[index, 0, z.rows // 2 * z.slots], spot, vector.at[index], scalars.at[index], place_sem.at[index]
         )
 
         def clear(n, carry):
@@ -326,7 +339,7 @@
     lax.fori_loop(high, z.chunks, clear_total, 0)
     total[:, z.window * z.block:] = jnp.zeros((z.span, z.block), jnp.float32)
     prepare(0, place_a)
-    copies[2].wait()
+    copies[4].wait()
 
     def multiply(n, carry):
         total[:, chunk(n)] = jnp.dot(
@@ -350,9 +363,10 @@
 
     @pl.when(jnp.logical_not(needed_b))
     def _():
-        copies[1].wait()
-
-    copies[3].wait()
+        copies[2].wait()
+        copies[3].wait()
+
+    copies[5].wait()
     emit(z, total, positions, out_stage, out, out_sems, prev_stage)
 
 
@@ -389,15 +403,15 @@
     dense = pltpu.VMEM((z.span, z.wide), dtype)
     total_buffer = pltpu.VMEM((z.span, z.wide), jnp.float32)
 
-    payload_shape = (z.rows * z.slots + 1, z.block, z.block)
+    half_shape = (z.rows // 2 * z.slots + 1, z.block, z.block)
     places = [pltpu.VMEM((2, 16, z.block), jnp.int32), pltpu.SMEM((2, 16, z.block), jnp.int32)]
 
     payload = call(
         z, functools.partial(pack_body, z), [tiles, columns], [ANY, VMEM],
-        shape(payload_shape, dtype), ANY,
+        [shape(half_shape, dtype)] * 2, [ANY] * 2,
         [
-            pltpu.VMEM((z.rows * z.slots, z.block, z.block), dtype), pltpu.VMEM((16, z.block), jnp.int32),
-            pltpu.VMEM((z.block, z.block), dtype), DMA((z.rows,)), DMA((z.rows + 1,)),
+            pltpu.VMEM(tiles.shape, dtype), pltpu.VMEM((16, z.block), jnp.int32),
+            pltpu.VMEM((z.block, z.block), dtype), DMA((z.rows,)), DMA((z.rows + 2,)),
         ],
         0, WHOLE_VMEM,
     )
@@ -419,19 +433,19 @@
     )
     corner = receive(corner, (3, 0, 0, -3), (LOWER, UPPER))
 
-    def near(names, arrays, total, trace, corner=None):
-        hand_on = corner is None
+    def near(names, arrays, total, trace, corner=None, hand_on=False):
+        corners = [] if corner is None else [corner]
         extra = [shape((z.span, 2 * z.span), dtype)] * hand_on
         return call(
-            z, functools.partial(near_body, z, names, hand_on),
-            [left, positions, total, trace] + ([] if hand_on else [corner]) + arrays,
-            [ANY, SMEM, ANY, VMEM] + [VMEM] * (not hand_on) + [ANY] * len(arrays),
+            z, functools.partial(near_body, z, names, corner is not None, hand_on),
+            [left, positions, total, trace] + corners + [half for pair in arrays for half in pair],
+            [ANY, SMEM, ANY, VMEM] + [VMEM] * len(corners) + [ANY] * (2 * len(arrays)),
             [sums, line] + extra,
             [ANY, VMEM] + [ANY] * len(extra),
             [
-                dense, pltpu.VMEM((2,) + payload_shape, dtype), dense, total_buffer,
+                dense, pltpu.VMEM((2, 2) + half_shape, dtype), dense, total_buffer,
                 pltpu.VMEM(tiles.shape, jnp.float32), pltpu.VMEM(tiles.shape, jnp.float32), *places,
-                DMA, DMA((2,)), DMA, DMA((2,)), DMA((2,)), DMA((z.rows,)),
+                DMA, DMA((2, 2)), DMA, DMA((2,)), DMA((2,)), DMA((z.rows,)),
             ],
             len(names),
         )
@@ -439,37 +453,49 @@
     def from_partner(array, name):
         return receive(array, PARTNER, [m for m in range(4) if NEEDED[name][m]])
 
-    first, corner, total = lax.optimization_barrier((first, corner, total))
-    relay = receive(first, RELAY_FROM)
+    first_lower, total, trace = lax.optimization_barrier((first[0], total, trace))
+    relay_lower = receive(first_lower, RELAY_FROM)
+    total, trace = near(("beside",), [beside], total, trace)
+    first_lower, first_upper, corner, total, trace = lax.optimization_barrier(
+        (first_lower, first[1], corner, total, trace)
+    )
+    relay_upper = receive(first_upper, RELAY_FROM)
+    first = (first_lower, first_upper)
     first_beside = from_partner(first, "first_beside")
-    total, trace = near(("beside", "first", "first_beside"), [beside, first, first_beside], total, trace, corner)
-    relay, payload, total, trace = lax.optimization_barrier((relay, payload, total, trace))
+    relay_lower, total, trace = lax.optimization_barrier((relay_lower, total, trace))
+    relay_beside_lower = receive(relay_lower, PARTNER)
+    total, trace = near(("first", "first_beside"), [first, first_beside], total, trace, corner)
+    relay_upper, payload, total, trace = lax.optimization_barrier((relay_upper, payload, total, trace))
     last = receive(payload, LAST)
-    relay_beside = receive(relay, PARTNER)
-    total, trace, last_left = near(("relay", "relay_beside"), [relay, relay_beside], total, trace)
+    relay_beside_upper = receive(relay_upper, PARTNER)
+    relay = (relay_lower, relay_upper)
+    relay_beside = (relay_beside_lower, relay_beside_upper)
+    total, trace, last_left = near(
+        ("relay", "relay_beside"), [relay, relay_beside], total, trace, hand_on=True
+    )
     assert devices & (devices - 1) == 0
     steps = [1 << bit for bit in range(devices.bit_length() - 1)]
     for step in steps[:1] + steps[3:]:
         trace = exchange(trace, step)
-    last, total, trace = lax.optimization_barrier((last, total, trace))
+    others = [fetch(trace, step) for step in (steps[1], steps[2], steps[1] + steps[2])]
+    last_lower, total = lax.optimization_barrier((last[0], total))
+    last = (last_lower, last[1])
     last_beside = from_partner(last, "last_beside")
-    trace = exchange(trace, steps[2])
-    last_beside, trace = lax.optimization_barrier((last_beside, trace))
-    trace = exchange(trace, steps[1])
     square = call(
-        z, functools.partial(last_body, z), [last_left, positions, total, last, last_beside],
-        [ANY, SMEM, ANY, ANY, ANY],
+        z, functools.partial(last_body, z), [last_left, positions, total, *last, *last_beside],
+        [ANY, SMEM] + [ANY] * 5,
         [shape(tiles.shape, dtype)],
         [ANY],
         [
-            pltpu.VMEM((z.span, 2 * z.span), dtype), pltpu.VMEM((2,) + payload_shape, dtype),
+            pltpu.VMEM((z.span, 2 * z.span), dtype), pltpu.VMEM((2, 2) + half_shape, dtype),
             pltpu.VMEM((2, z.span, z.wide), dtype), total_buffer,
             pltpu.VMEM(tiles.shape, dtype), pltpu.VMEM(tiles.shape, jnp.float32), *places,
-            DMA, DMA((2,)), DMA, DMA((2,)), DMA((z.rows,)),
+            DMA, DMA((2, 2)), DMA, DMA((2,)), DMA((z.rows,)),
         ],
         2,
     )[0]
-    return square, jnp.sum(trace) / (z.all_rows * z.block)
+    square, trace, others = lax.optimization_barrier((square, trace, others))
+    return square, jnp.sum((trace + others[0]) + (others[1] + others[2])) / (z.all_rows * z.block)
 
 
 def solution(mesh):

time: 133 us -> 139 us (1.045)
  starting transfers between devices: 16.9 us -> 39.2 us
  waiting for transfers between devices: 63.5 us -> 43.3 us
  Pallas kernels: 44.6 us -> 48.1 us
    ppermute x8 -> x15, starting transfers between devices: 13.2 us -> 34.4 us  [receive(): return lax.ppermute(shard, AXES, pairs)]
    ppermute x8 -> x15, waiting for transfers between devices: 51.3 us -> 32.8 us  [receive(): return lax.ppermute(shard, AXES, pairs)]
    pallas_call x5 -> x6, Pallas kernels: 44.6 us -> 48.1 us  [call(): pl.pallas_call(kernel, out_shape=out_shape, in_specs=in_specs, out_specs=...]
    ppermute x5 -> x6, waiting for transfers between devices: 12.2 us -> 10.5 us  [fetch(): lax.ppermute(value, AXES, [(d, d ^ step) for d in range(lax.axis_size(AXE...]
    ppermute x5 -> x6, starting transfers between devices: 3.69 us -> 4.77 us  [fetch(): lax.ppermute(value, AXES, [(d, d ^ step) for d in range(lax.axis_size(AXE...]
    unnamed x8 -> x12, local copies, waits for them, and re-layouts: 4.59 us -> 4.66 us
  transfers between devices with their start and end apart: 13 -> 21, of which waited for: 11 -> 10; matrix products, arithmetic and copies ran while one was open for 0% -> 0% of each run, Pallas kernels for 31% -> 32%
where the time goes in v6:
time: 139 us; the launch traced here: 138 us
  Pallas kernels  48.1 us (35%)
  waiting for transfers between devices  43.3 us (31%)
  starting transfers between devices  39.2 us (28%)
  local copies, waits for them, and re-layouts  4.66 us (3%)
  between operations  2.59 us (2%)
    pallas_call x6, Pallas kernels, call(): pl.pallas_call(kernel, out_shape=out_shape, in_specs=in_specs, out_specs=...  48.1 us
    ppermute x15, starting transfers between devices, receive(): return lax.ppermute(shard, AXES, pairs)  34.4 us
    ppermute x15, waiting for transfers between devices, receive(): return lax.ppermute(shard, AXES, pairs)  32.8 us
    ppermute x6, waiting for transfers between devices, fetch(): lax.ppermute(value, AXES, [(d, d ^ step) for d in range(lax.axis_size(AXE...  10.5 us
    ppermute x6, starting transfers between devices, fetch(): lax.ppermute(value, AXES, [(d, d ^ step) for d in range(lax.axis_size(AXE...  4.77 us
    unnamed x12, local copies, waits for them, and re-layouts  4.66 us
  transfers between devices with their start and end apart: 21, of which 10 were waited for; matrix products, arithmetic and copies ran while one was open for 0% of the time, Pallas kernels for 32%

profile of v6, /device:TPU:0, one launch (start us, length us, event | category | flops | bytes accessed | tf_op | source)
XLA Modules:
  0.0 138.4 jit_solution(6494457242930922979)
XLA Ops:
  0.6 0.0 copy-start.2
  0.6 0.0 copy-start.3
  0.6 3.5 %shard_map.42 = (bf16[41,128,128]{2,1,0:T(8,128)(2,1)}, bf16[41,128,128]{2,1,0:T(8,128)(2,1)}) custom-call(bf16[4,20,128,128]{3,2,1,0:T(8,128)(2,1)} %tiles.1, s32[4,20]{1,0:T(4,128)} %columns.3), custom_call_target="tpu_custom_call" | custom-call | bytes 10485760 | tf_op jit(solution)/shard_map/pallas_call | solution.py:380
  4.2 5.5 %collective-permute-start = (bf16[41,128,128]{2,1,0:T(8,128)(2,1)}, bf16[41,128,128]{2,1,0:T(8,128)(2,1)S(1)}, u32[]{:S(2)}, u32[]{:S(2)}) collective-permute-start(bf16[41,128,128]{2,1,0:T(8,128)(2,1)} %get-tuple-element.65), channel_id=1, source_target_pairs={{2,0},{4,1},{31,2},{1,3},{6,4},{8,5},{3,6},{5,7},{10,8},{12,9},{7,... | collective-permute-start | bytes 4030472 | tf_op jit(solution)/shard_map/ppermute | solution.py:50
  9.7 0.0 collective-permute-start.3
  9.7 0.5 collective-permute-start.4
  10.2 1.2 collective-permute-start.1
  11.4 0.0 copy-done.2
  11.4 0.0 copy-done.3
  11.4 7.3 %shard_map.41 = (f32[4,20,128,128]{3,2,1,0:T(8,128)S(1)}, bf16[512,3712]{1,0:T(8,128)(2,1)S(1)}, bf16[256,512]{1,0:T(8,128)(2,1)S(1)}, s32[4,20]{1,0:T(4,128)S(1)}, f32[1,512]{1,0:T(1,128)S(1)}) custom-call(bf16[4,20,128,128]{3,2,1,0:T(8,128)(2,1)S(1)} %copy-done.2, s32[4,20]{1,0:T(4,128)S(1)} %copy-done.3), custom_call_target="tpu_custom_call" | custom-call | flops 1879048192 | bytes 13107200 | tf_op jit(solution)/shard_map/pallas_call | solution.py:380
  18.7 1.9 %collective-permute-start.2 = (bf16[256,512]{1,0:T(8,128)(2,1)S(1)}, bf16[256,512]{1,0:T(8,128)(2,1)S(1)}, u32[]{:S(2)}, u32[]{:S(2)}) collective-permute-start(bf16[256,512]{1,0:T(8,128)(2,1)S(1)} %get-tuple-element.46), channel_id=1, source_target_pairs={{3,0},{0,3},{7,4},{4,7},{11,8},{8,11},{15,12},{12,15},{19,16},{16,... | collective-permute-start | bytes 786440 | tf_op jit(solution)/shard_map/ppermute | solution.py:50
  20.7 4.8 %collective-permute-done.refs_1_ = bf16[41,128,128]{2,1,0:T(8,128)(2,1)S(1)} collective-permute-done((bf16[41,128,128]{2,1,0:T(8,128)(2,1)}, bf16[41,128,128]{2,1,0:T(8,128)(2,1)S(1)}, u32[]{:S(2)}, u32[]{:S(2)}) %collective-permute-start) | collective-permute-done | bytes 1343520 | tf_op jit(solution)/shard_map/ppermute | solution.py:50
  25.5 0.0 collective-permute-start.6
  25.5 0.0 collective-permute-done.3.refs_0_
  25.5 0.0 collective-permute-done.4.refs_1_
  25.5 8.0 %shard_map.43 = (f32[4,20,128,128]{3,2,1,0:T(8,128)S(1)}, f32[1,512]{1,0:T(1,128)S(1)}) custom-call(bf16[512,3712]{1,0:T(8,128)(2,1)S(1)} %get-tuple-element.39.left_in, s32[4,20]{1,0:T(4,128)S(1)} %get-tuple-element.40.positions, f32[4,20,128,128]{3,2,1,0:T(8,128)S(1)} %get-tuple-element.47.prev, f32[1,512]{1,0:T(1,128)S(1)} %get-tuple-element.48.trace_in, ...), custom_call_target="tpu_custom_call" | custom-call | flops 1879048192 | bytes 13107200 | tf_op jit(solution)/shard_map/pallas_call | solution.py:380
  33.5 0.0 copy-start.1
  33.5 2.3 %copy-done.1 = f32[4,20,128,128]{3,2,1,0:T(8,128)} copy-done((f32[4,20,128,128]{3,2,1,0:T(8,128)}, f32[4,20,128,128]{3,2,1,0:T(8,128)S(1)}, u32[]{:S(2)}) %copy-start.1) | copy-done | bytes 5242904
  35.8 0.0 collective-permute-done.2.refs_0_
  35.8 4.7 %collective-permute-done.1.refs_2_ = bf16[41,128,128]{2,1,0:T(8,128)(2,1)S(1)} collective-permute-done((bf16[41,128,128]{2,1,0:T(8,128)(2,1)}, bf16[41,128,128]{2,1,0:T(8,128)(2,1)S(1)}, u32[]{:S(2)}, u32[]{:S(2)}) %collective-permute-start.1) | collective-permute-done | bytes 1343520 | tf_op jit(solution)/shard_map/ppermute | solution.py:50
  40.5 0.0 copy-start.5
  40.5 0.0 copy-start.4
  40.5 14.0 %collective-permute-start.7 = (bf16[41,128,128]{2,1,0:T(8,128)(2,1)S(1)}, bf16[41,128,128]{2,1,0:T(8,128)(2,1)S(1)}, u32[]{:S(2)}, u32[]{:S(2)}) collective-permute-start(bf16[41,128,128]{2,1,0:T(8,128)(2,1)S(1)} %collective-permute-done.refs_1_), channel_id=1, source_target_pairs={{0,1},{3,2},{4,5},{7,6},{8,9},{11,10},{12,13},{15,14},{16,17},{19,... | collective-permute-start | bytes 4030472 | tf_op jit(solution)/shard_map/ppermute | solution.py:50
  54.5 1.4 collective-permute-start.8
  55.9 0.1 collective-permute-start.5
  56.0 0.0 collective-permute-done.6.refs_0_
  56.0 1.1 collective-permute-done.7.refs_3_
  57.1 1.9 %collective-permute-done.8.refs_4_ = bf16[41,128,128]{2,1,0:T(8,128)(2,1)S(1)} collective-permute-done((bf16[41,128,128]{2,1,0:T(8,128)(2,1)S(1)}, bf16[41,128,128]{2,1,0:T(8,128)(2,1)S(1)}, u32[]{:S(2)}, u32[]{:S(2)}) %collective-permute-start.8) | collective-permute-done | bytes 1343520 | tf_op jit(solution)/shard_map/ppermute | solution.py:50
  59.0 7.7 %shard_map.44 = (f32[4,20,128,128]{3,2,1,0:T(8,128)S(1)}, f32[1,512]{1,0:T(1,128)S(1)}) custom-call(bf16[512,3712]{1,0:T(8,128)(2,1)S(1)} %get-tuple-element.39.left_in, s32[4,20]{1,0:T(4,128)S(1)} %get-tuple-element.40.positions, f32[4,20,128,128]{3,2,1,0:T(8,128)} %copy-done.1, f32[1,512]{1,0:T(1,128)S(1)} %get-tuple-element.55.trace_in, ...), custom_call_target="tpu_custom_call" | custom-call | flops 3758096384 | bytes 15728640 | tf_op jit(solution)/shard_map/pallas_call | solution.py:380
  66.7 0.0 copy-start
  66.7 2.3 %copy-done = f32[4,20,128,128]{3,2,1,0:T(8,128)} copy-done((f32[4,20,128,128]{3,2,1,0:T(8,128)}, f32[4,20,128,128]{3,2,1,0:T(8,128)S(1)}, u32[]{:S(2)}) %copy-start) | copy-done | bytes 5242904
  69.0 4.9 %collective-permute-done.5.refs_1_ = bf16[41,128,128]{2,1,0:T(8,128)(2,1)S(1)} collective-permute-done((bf16[41,128,128]{2,1,0:T(8,128)(2,1)S(1)}, bf16[41,128,128]{2,1,0:T(8,128)(2,1)S(1)}, u32[]{:S(2)}, u32[]{:S(2)}) %collective-permute-start.5) | collective-permute-done | bytes 1343520 | tf_op jit(solution)/shard_map/ppermute | solution.py:50
  73.9 1.3 collective-permute-start.10
  75.3 0.0 collective-permute-start.9
  75.3 0.0 copy-done.5
  75.3 0.8 collective-permute-start.11
  76.1 0.0 copy-done.4
  76.1 5.2 %collective-permute-start.12 = (bf16[41,128,128]{2,1,0:T(8,128)(2,1)S(1)}, bf16[41,128,128]{2,1,0:T(8,128)(2,1)S(1)}, u32[]{:S(2)}, u32[]{:S(2)}) collective-permute-start(bf16[41,128,128]{2,1,0:T(8,128)(2,1)S(1)} %copy-done.4), channel_id=1, source_target_pairs={{29,0},{3,1},{0,2},{6,3},{1,4},{7,5},{4,6},{10,7},{5,8},{11,9},{8,... | collective-permute-start | bytes 4030472 | tf_op jit(solution)/shard_map/ppermute | solution.py:50
  81.2 0.0 collective-permute-done.10.refs_3_
  81.2 0.0 collective-permute-done.9.refs_2_
  81.3 11.9 %shard_map.45 = (f32[4,20,128,128]{3,2,1,0:T(8,128)S(1)}, f32[1,512]{1,0:T(1,128)S(1)}, bf16[512,1024]{1,0:T(8,128)(2,1)S(1)}) custom-call(bf16[512,3712]{1,0:T(8,128)(2,1)S(1)} %get-tuple-element.39.left_in, s32[4,20]{1,0:T(4,128)S(1)} %get-tuple-element.40.positions, f32[4,20,128,128]{3,2,1,0:T(8,128)} %copy-done, ...), custom_call_target="tpu_custom_call" | custom-call | flops 3758096384 | bytes 15728640 | tf_op jit(solution)/shard_map/pallas_call | solution.py:380
  93.1 2.2 %collective-permute-done.11.a_lower = bf16[41,128,128]{2,1,0:T(8,128)(2,1)S(1)} collective-permute-done((bf16[41,128,128]{2,1,0:T(8,128)(2,1)S(1)}, bf16[41,128,128]{2,1,0:T(8,128)(2,1)S(1)}, u32[]{:S(2)}, u32[]{:S(2)}) %collective-permute-start.11) | collective-permute-done | bytes 1343520 | tf_op jit(solution)/shard_map/ppermute | solution.py:50
  95.3 1.3 collective-permute-start.13
  96.6 13.1 %collective-permute-done.12.a_upper = bf16[41,128,128]{2,1,0:T(8,128)(2,1)S(1)} collective-permute-done((bf16[41,128,128]{2,1,0:T(8,128)(2,1)S(1)}, bf16[41,128,128]{2,1,0:T(8,128)(2,1)S(1)}, u32[]{:S(2)}, u32[]{:S(2)}) %collective-permute-start.12) | collective-permute-done | bytes 1343520 | tf_op jit(solution)/shard_map/ppermute | solution.py:50
  109.7 1.3 collective-permute-start.14
  111.0 1.3 collective-permute-start.15
  112.3 2.4 %collective-permute-done.15 = f32[1,512]{1,0:T(1,128)S(1)} collective-permute-done((f32[1,512]{1,0:T(1,128)S(1)}, f32[1,512]{1,0:T(1,128)S(1)}, u32[]{:S(2)}, u32[]{:S(2)}) %collective-permute-start.15) | collective-permute-done | bytes 2080 | tf_op jit(solution)/shard_map/ppermute | solution.py:54
  114.7 0.0 collective-permute-start.16
  114.7 3.6 %collective-permute-done.16 = f32[1,512]{1,0:T(1,128)S(1)} collective-permute-done((f32[1,512]{1,0:T(1,128)S(1)}, f32[1,512]{1,0:T(1,128)S(1)}, u32[]{:S(2)}, u32[]{:S(2)}) %collective-permute-start.16) | collective-permute-done | bytes 2080 | tf_op jit(solution)/shard_map/ppermute | solution.py:54
  118.3 0.0 collective-permute-start.17
  118.3 4.5 %collective-permute-done.17 = f32[1,512]{1,0:T(1,128)S(1)} collective-permute-done((f32[1,512]{1,0:T(1,128)S(1)}, f32[1,512]{1,0:T(1,128)S(1)}, u32[]{:S(2)}, u32[]{:S(2)}) %collective-permute-start.17) | collective-permute-done | bytes 2080 | tf_op jit(solution)/shard_map/ppermute | solution.py:54
  122.8 0.4 collective-permute-start.18
  123.2 1.8 %collective-permute-start.19 = (f32[1,512]{1,0:T(1,128)S(1)}, f32[1,512]{1,0:T(1,128)S(1)}, u32[]{:S(2)}, u32[]{:S(2)}) collective-permute-start(f32[1,512]{1,0:T(1,128)S(1)} %add.20), channel_id=1, source_target_pairs={{0,4},{1,5},{2,6},{3,7},{4,0},{5,1},{6,2},{7,3},{8,12},{9,13},{10,... | collective-permute-start | bytes 6152 | tf_op jit(solution)/shard_map/ppermute | solution.py:54
  125.0 1.3 collective-permute-start.20
  126.3 0.0 collective-permute-done.13.b_lower
  126.3 0.0 collective-permute-done.14.b_upper
  126.3 9.7 %shard_map.46 = bf16[4,20,128,128]{3,2,1,0:T(8,128)(2,1)} custom-call(bf16[512,1024]{1,0:T(8,128)(2,1)S(1)} %get-tuple-element.64.left_in, s32[4,20]{1,0:T(4,128)S(1)} %get-tuple-element.40.positions, f32[4,20,128,128]{3,2,1,0:T(8,128)S(1)} %get-tuple-element.67.prev, bf16[41,128,128]{2,1,0:T(8,128)(2,1)S(1)} %collective-permute-done.11.a_lower, ...), custom_call_target="tpu_custom_call" | custom-call | flops 3758096384 | bytes 15728640 | tf_op jit(solution)/shard_map/pallas_call | solution.py:380
  136.0 0.0 collective-permute-done.18
  136.0 0.0 collective-permute-done.19
  136.0 0.0 collective-permute-done.20
  136.1 0.6 add_reduce_fusion
  (3 shorter events, 0.0 us)
Async XLA Ops:
  0.6 10.8 %copy-start.2 = (bf16[4,20,128,128]{3,2,1,0:T(8,128)(2,1)S(1)}, bf16[4,20,128,128]{3,2,1,0:T(8,128)(2,1)}, u32[]{:S(2)}) copy-start(bf16[4,20,128,128]{3,2,1,0:T(8,128)(2,1)} %tiles.1) | copy-start | bytes 7864324
  0.6 10.8 %copy-start.3 = (s32[4,20]{1,0:T(4,128)S(1)}, s32[4,20]{1,0:T(4,128)}, u32[]{:S(2)}) copy-start(s32[4,20]{1,0:T(4,128)} %columns.3) | copy-start | bytes 964
  4.2 21.3 %collective-permute-start = (bf16[41,128,128]{2,1,0:T(8,128)(2,1)}, bf16[41,128,128]{2,1,0:T(8,128)(2,1)S(1)}, u32[]{:S(2)}, u32[]{:S(2)}) collective-permute-start(bf16[41,128,128]{2,1,0:T(8,128)(2,1)} %get-tuple-element.65), channel_id=1, source_target_pairs={{2,0},{4,1},{31,2},{1,3},{6,4},{8,5},{3,6},{5,7},{10,8},{12,9},{7,... | collective-permute-start | bytes 4030472 | tf_op jit(solution)/shard_map/ppermute | solution.py:50
  9.7 15.8 %collective-permute-start.3 = (bf16[41,128,128]{2,1,0:T(8,128)(2,1)}, bf16[41,128,128]{2,1,0:T(8,128)(2,1)S(1)}, u32[]{:S(2)}, u32[]{:S(2)}) collective-permute-start(bf16[41,128,128]{2,1,0:T(8,128)(2,1)} %get-tuple-element.65), channel_id=1, source_target_pairs={{1,0},{0,1},{3,2},{2,3},{5,4},{4,5},{7,6},{6,7},{9,8},{8,9},{11,10... | collective-permute-start | bytes 4030472 | tf_op jit(solution)/shard_map/ppermute | solution.py:50
  9.7 15.8 %collective-permute-start.4 = (bf16[41,128,128]{2,1,0:T(8,128)(2,1)}, bf16[41,128,128]{2,1,0:T(8,128)(2,1)S(1)}, u32[]{:S(2)}, u32[]{:S(2)}) collective-permute-start(bf16[41,128,128]{2,1,0:T(8,128)(2,1)} %get-tuple-element.69), channel_id=1, source_target_pairs={{1,0},{0,1},{3,2},{2,3},{5,4},{4,5},{7,6},{6,7},{9,8},{8,9},{11,10... | collective-permute-start | bytes 4030472 | tf_op jit(solution)/shard_map/ppermute | solution.py:50
  10.2 30.3 %collective-permute-start.1 = (bf16[41,128,128]{2,1,0:T(8,128)(2,1)}, bf16[41,128,128]{2,1,0:T(8,128)(2,1)S(1)}, u32[]{:S(2)}, u32[]{:S(2)}) collective-permute-start(bf16[41,128,128]{2,1,0:T(8,128)(2,1)} %get-tuple-element.69), channel_id=1, source_target_pairs={{2,0},{4,1},{31,2},{1,3},{6,4},{8,5},{3,6},{5,7},{10,8},{12,9},{7,... | collective-permute-start | bytes 4030472 | tf_op jit(solution)/shard_map/ppermute | solution.py:50
  18.7 17.1 %collective-permute-start.2 = (bf16[256,512]{1,0:T(8,128)(2,1)S(1)}, bf16[256,512]{1,0:T(8,128)(2,1)S(1)}, u32[]{:S(2)}, u32[]{:S(2)}) collective-permute-start(bf16[256,512]{1,0:T(8,128)(2,1)S(1)} %get-tuple-element.46), channel_id=1, source_target_pairs={{3,0},{0,3},{7,4},{4,7},{11,8},{8,11},{15,12},{12,15},{19,16},{16,... | collective-permute-start | bytes 786440 | tf_op jit(solution)/shard_map/ppermute | solution.py:50
  25.5 30.5 %collective-permute-start.6 = (bf16[41,128,128]{2,1,0:T(8,128)(2,1)S(1)}, bf16[41,128,128]{2,1,0:T(8,128)(2,1)S(1)}, u32[]{:S(2)}, u32[]{:S(2)}) collective-permute-start(bf16[41,128,128]{2,1,0:T(8,128)(2,1)S(1)} %collective-permute-done.refs_1_), channel_id=1, source_target_pairs={{2,0},{28,1},{7,2},{1,3},{6,4},{0,5},{11,6},{5,7},{10,8},{4,9},{15... | collective-permute-start | bytes 4030472 | tf_op jit(solution)/shard_map/ppermute | solution.py:50
  33.5 2.3 %copy-start.1 = (f32[4,20,128,128]{3,2,1,0:T(8,128)}, f32[4,20,128,128]{3,2,1,0:T(8,128)S(1)}, u32[]{:S(2)}) copy-start(f32[4,20,128,128]{3,2,1,0:T(8,128)S(1)} %get-tuple-element.54.prev) | copy-start | bytes 15728644
  40.5 34.7 %copy-start.5 = (bf16[41,128,128]{2,1,0:T(8,128)(2,1)S(1)}, bf16[41,128,128]{2,1,0:T(8,128)(2,1)}, u32[]{:S(2)}) copy-start(bf16[41,128,128]{2,1,0:T(8,128)(2,1)} %get-tuple-element.65) | copy-start | bytes 4030468
  40.5 35.5 %copy-start.4 = (bf16[41,128,128]{2,1,0:T(8,128)(2,1)S(1)}, bf16[41,128,128]{2,1,0:T(8,128)(2,1)}, u32[]{:S(2)}) copy-start(bf16[41,128,128]{2,1,0:T(8,128)(2,1)} %get-tuple-element.69) | copy-start | bytes 4030468
  40.5 16.6 %collective-permute-start.7 = (bf16[41,128,128]{2,1,0:T(8,128)(2,1)S(1)}, bf16[41,128,128]{2,1,0:T(8,128)(2,1)S(1)}, u32[]{:S(2)}, u32[]{:S(2)}) collective-permute-start(bf16[41,128,128]{2,1,0:T(8,128)(2,1)S(1)} %collective-permute-done.refs_1_), channel_id=1, source_target_pairs={{0,1},{3,2},{4,5},{7,6},{8,9},{11,10},{12,13},{15,14},{16,17},{19,... | collective-permute-start | bytes 4030472 | tf_op jit(solution)/shard_map/ppermute | solution.py:50
  54.5 4.5 %collective-permute-start.8 = (bf16[41,128,128]{2,1,0:T(8,128)(2,1)S(1)}, bf16[41,128,128]{2,1,0:T(8,128)(2,1)S(1)}, u32[]{:S(2)}, u32[]{:S(2)}) collective-permute-start(bf16[41,128,128]{2,1,0:T(8,128)(2,1)S(1)} %collective-permute-done.1.refs_2_), channel_id=1, source_target_pairs={{0,1},{3,2},{4,5},{7,6},{8,9},{11,10},{12,13},{15,14},{16,17},{19,... | collective-permute-start | bytes 4030472 | tf_op jit(solution)/shard_map/ppermute | solution.py:50
  55.9 18.0 %collective-permute-start.5 = (bf16[41,128,128]{2,1,0:T(8,128)(2,1)S(1)}, bf16[41,128,128]{2,1,0:T(8,128)(2,1)S(1)}, u32[]{:S(2)}, u32[]{:S(2)}) collective-permute-start(bf16[41,128,128]{2,1,0:T(8,128)(2,1)S(1)} %collective-permute-done.1.refs_2_), channel_id=1, source_target_pairs={{2,0},{28,1},{7,2},{1,3},{6,4},{0,5},{11,6},{5,7},{10,8},{4,9},{15... | collective-permute-start | bytes 4030472 | tf_op jit(solution)/shard_map/ppermute | solution.py:50
  66.7 2.3 %copy-start = (f32[4,20,128,128]{3,2,1,0:T(8,128)}, f32[4,20,128,128]{3,2,1,0:T(8,128)S(1)}, u32[]{:S(2)}) copy-start(f32[4,20,128,128]{3,2,1,0:T(8,128)S(1)} %get-tuple-element.60.prev) | copy-start | bytes 15728644
  73.9 7.3 %collective-permute-start.10 = (bf16[41,128,128]{2,1,0:T(8,128)(2,1)S(1)}, bf16[41,128,128]{2,1,0:T(8,128)(2,1)S(1)}, u32[]{:S(2)}, u32[]{:S(2)}) collective-permute-start(bf16[41,128,128]{2,1,0:T(8,128)(2,1)S(1)} %collective-permute-done.5.refs_1_), channel_id=1, source_target_pairs={{1,0},{0,1},{3,2},{2,3},{5,4},{4,5},{7,6},{6,7},{9,8},{8,9},{11,10... | collective-permute-start | bytes 4030472 | tf_op jit(solution)/shard_map/ppermute | solution.py:50
  75.3 6.0 %collective-permute-start.9 = (bf16[41,128,128]{2,1,0:T(8,128)(2,1)S(1)}, bf16[41,128,128]{2,1,0:T(8,128)(2,1)S(1)}, u32[]{:S(2)}, u32[]{:S(2)}) collective-permute-start(bf16[41,128,128]{2,1,0:T(8,128)(2,1)S(1)} %collective-permute-done.6.refs_0_), channel_id=1, source_target_pairs={{1,0},{0,1},{3,2},{2,3},{5,4},{4,5},{7,6},{6,7},{9,8},{8,9},{11,10... | collective-permute-start | bytes 4030472 | tf_op jit(solution)/shard_map/ppermute | solution.py:50
  75.3 20.1 %collective-permute-start.11 = (bf16[41,128,128]{2,1,0:T(8,128)(2,1)S(1)}, bf16[41,128,128]{2,1,0:T(8,128)(2,1)S(1)}, u32[]{:S(2)}, u32[]{:S(2)}) collective-permute-start(bf16[41,128,128]{2,1,0:T(8,128)(2,1)S(1)} %copy-done.5), channel_id=1, source_target_pairs={{29,0},{3,1},{0,2},{6,3},{1,4},{7,5},{4,6},{10,7},{5,8},{11,9},{8,... | collective-permute-start | bytes 4030472 | tf_op jit(solution)/shard_map/ppermute | solution.py:50
  76.1 33.7 %collective-permute-start.12 = (bf16[41,128,128]{2,1,0:T(8,128)(2,1)S(1)}, bf16[41,128,128]{2,1,0:T(8,128)(2,1)S(1)}, u32[]{:S(2)}, u32[]{:S(2)}) collective-permute-start(bf16[41,128,128]{2,1,0:T(8,128)(2,1)S(1)} %copy-done.4), channel_id=1, source_target_pairs={{29,0},{3,1},{0,2},{6,3},{1,4},{7,5},{4,6},{10,7},{5,8},{11,9},{8,... | collective-permute-start | bytes 4030472 | tf_op jit(solution)/shard_map/ppermute | solution.py:50
  95.3 30.9 %collective-permute-start.13 = (bf16[41,128,128]{2,1,0:T(8,128)(2,1)S(1)}, bf16[41,128,128]{2,1,0:T(8,128)(2,1)S(1)}, u32[]{:S(2)}, u32[]{:S(2)}) collective-permute-start(bf16[41,128,128]{2,1,0:T(8,128)(2,1)S(1)} %collective-permute-done.11.a_lower), channel_id=1, source_target_pairs={{1,0},{2,3},{5,4},{6,7},{9,8},{10,11},{13,12},{14,15},{17,16},{18,... | collective-permute-start | bytes 4030472 | tf_op jit(solution)/shard_map/ppermute | solution.py:50
  109.7 16.5 %collective-permute-start.14 = (bf16[41,128,128]{2,1,0:T(8,128)(2,1)S(1)}, bf16[41,128,128]{2,1,0:T(8,128)(2,1)S(1)}, u32[]{:S(2)}, u32[]{:S(2)}) collective-permute-start(bf16[41,128,128]{2,1,0:T(8,128)(2,1)S(1)} %collective-permute-done.12.a_upper), channel_id=1, source_target_pairs={{1,0},{2,3},{5,4},{6,7},{9,8},{10,11},{13,12},{14,15},{17,16},{18,... | collective-permute-start | bytes 4030472 | tf_op jit(solution)/shard_map/ppermute | solution.py:50
  111.0 3.7 %collective-permute-start.15 = (f32[1,512]{1,0:T(1,128)S(1)}, f32[1,512]{1,0:T(1,128)S(1)}, u32[]{:S(2)}, u32[]{:S(2)}) collective-permute-start(f32[1,512]{1,0:T(1,128)S(1)} %get-tuple-element.70), channel_id=1, source_target_pairs={{0,1},{1,0},{2,3},{3,2},{4,5},{5,4},{6,7},{7,6},{8,9},{9,8},{10,11... | collective-permute-start | bytes 6152 | tf_op jit(solution)/shard_map/ppermute | solution.py:54
  114.7 3.6 %collective-permute-start.16 = (f32[1,512]{1,0:T(1,128)S(1)}, f32[1,512]{1,0:T(1,128)S(1)}, u32[]{:S(2)}, u32[]{:S(2)}) collective-permute-start(f32[1,512]{1,0:T(1,128)S(1)} %add.18), channel_id=1, source_target_pairs={{0,8},{1,9},{2,10},{3,11},{4,12},{5,13},{6,14},{7,15},{8,0},{9,1},... | collective-permute-start | bytes 6152 | tf_op jit(solution)/shard_map/ppermute | solution.py:54
  118.3 4.5 %collective-permute-start.17 = (f32[1,512]{1,0:T(1,128)S(1)}, f32[1,512]{1,0:T(1,128)S(1)}, u32[]{:S(2)}, u32[]{:S(2)}) collective-permute-start(f32[1,512]{1,0:T(1,128)S(1)} %add.19), channel_id=1, source_target_pairs={{0,16},{1,17},{2,18},{3,19},{4,20},{5,21},{6,22},{7,23},{8,24},{9,... | collective-permute-start | bytes 6152 | tf_op jit(solution)/shard_map/ppermute | solution.py:54
  122.8 13.2 %collective-permute-start.18 = (f32[1,512]{1,0:T(1,128)S(1)}, f32[1,512]{1,0:T(1,128)S(1)}, u32[]{:S(2)}, u32[]{:S(2)}) collective-permute-start(f32[1,512]{1,0:T(1,128)S(1)} %add.20), channel_id=1, source_target_pairs={{0,2},{1,3},{2,0},{3,1},{4,6},{5,7},{6,4},{7,5},{8,10},{9,11},{10,... | collective-permute-start | bytes 6152 | tf_op jit(solution)/shard_map/ppermute | solution.py:54
  123.2 12.8 %collective-permute-start.19 = (f32[1,512]{1,0:T(1,128)S(1)}, f32[1,512]{1,0:T(1,128)S(1)}, u32[]{:S(2)}, u32[]{:S(2)}) collective-permute-start(f32[1,512]{1,0:T(1,128)S(1)} %add.20), channel_id=1, source_target_pairs={{0,4},{1,5},{2,6},{3,7},{4,0},{5,1},{6,2},{7,3},{8,12},{9,13},{10,... | collective-permute-start | bytes 6152 | tf_op jit(solution)/shard_map/ppermute | solution.py:54
  125.0 11.1 %collective-permute-start.20 = (f32[1,512]{1,0:T(1,128)S(1)}, f32[1,512]{1,0:T(1,128)S(1)}, u32[]{:S(2)}, u32[]{:S(2)}) collective-permute-start(f32[1,512]{1,0:T(1,128)S(1)} %add.20), channel_id=1, source_target_pairs={{0,6},{1,7},{2,4},{3,5},{4,2},{5,3},{6,0},{7,1},{8,14},{9,15},{10,... | collective-permute-start | bytes 6152 | tf_op jit(solution)/shard_map/ppermute | solution.py:54

commit v7 on v4

--- a/solution.py
+++ b/solution.py
@@ -9,7 +9,7 @@
 
 REACH = 12
 AXES = ("blk", "grp")
-VMEM_LIMIT = 48 * 1024 * 1024
+VMEM_LIMIT = 36 * 1024 * 1024
 WHOLE_VMEM = 60 * 1024 * 1024
 EMPTY = 64
 
@@ -37,9 +37,10 @@
     "relay": RELAY,
     "relay_beside": across(RELAY),
 }
-COUNTS = {"beside": (2, 0, 2, 0), "first": (2, 0, 2, 0), "second": (2, 2, 0, 0), "mixed": (2, 2, 0, 0)}
+COUNTS = {"beside": (2, 0, 2, 0), "first": (2, 0, 0, 2), "second": (2, 0, 0, 2), "mixed": (0, 0, 2, 2)}
 OUTSIDE = {("first", "mixed"): (0, 2, 2, 0), ("first", "second"): (0, 2, 0, 0)}
-CORNER = {1: -3, 2: 3}
+LOWER, UPPER = 2, 1
+KEPT = {"beside": 0, "first": 0, "second": 1, "mixed": 2}
 
 
 def receive(shard, offsets, kinds=range(4)):
@@ -48,9 +49,12 @@
     return lax.ppermute(shard, AXES, pairs)
 
 
+def fetch(value, step):
+    return lax.ppermute(value, AXES, [(d, d ^ step) for d in range(lax.axis_size(AXES))])
+
+
 def exchange(value, step):
-    size = lax.axis_size(AXES)
-    return value + lax.ppermute(value, AXES, [(d, d ^ step) for d in range(size)])
+    return value + fetch(value, step)
 
 
 def pick(table, kind):
@@ -179,8 +183,8 @@
         def go(rows, cols):
             copy = pltpu.make_async_copy(left.at[rows, cols], corner_out, corner_sem)
             copy.start() if start else copy.wait()
-        pl.when(kind == 1)(lambda: go(pl.ds(0, half), pl.ds(0, z.span)))
-        pl.when(kind != 1)(
+        pl.when(kind == UPPER)(lambda: go(pl.ds(0, half), pl.ds(0, z.span)))
+        pl.when(kind != UPPER)(
             lambda: go(pl.ds(half, half), pl.ds((z.chunks - 1) * z.span, z.span))
         )
 
@@ -203,12 +207,10 @@
 def near_body(z, names, left_in, positions, prev, trace_in, *refs):
     refs = list(refs)
     take = lambda count: [refs.pop(0) for _ in range(count)]
-    final = "mixed" in names
-    corner = take(1)[0] if final else None
+    corner = take(1)[0]
     sources = {name: take(2 if name == "mixed" else 1) for name in names}
-    out, trace = take(2)
-    relay_left = take(1)[0] if final else None
-    left, stage, right, total, out_stage, prev_stage, vector, scalars = take(8)
+    out, trace, relay_left = take(3)
+    left, stage, right, total, sums, vector, scalars = take(7)
     left_sem, in_sem, prev_sem, place_sem, relay_sem, out_sems = take(6)
     device = lax.axis_index(AXES)
     kind = device % 4
@@ -233,35 +235,43 @@
     left_copy.start()
     for index in range(min(2, len(names))):
         fetch(index, True)
-    prev_copy = pltpu.make_async_copy(prev, prev_stage, prev_sem)
+    prev_copy = pltpu.make_async_copy(prev, sums, prev_sem)
     prev_copy.start()
     total[...] = jnp.zeros_like(total)
     trace[...] = trace_in[...]
     left_copy.wait()
     relay_copies = []
-    if final:
-        for index, name in enumerate(("relay", "relay_beside")):
-            copy = pltpu.make_async_copy(
-                left.at[:, chunk(place[name])], relay_left.at[:, pl.ds(index * z.span, z.span)],
-                relay_sem.at[index],
-            )
-            copy.start()
-            relay_copies.append(copy)
+    for index, name in enumerate(("relay", "relay_beside")):
+        copy = pltpu.make_async_copy(
+            left.at[:, chunk(place[name])], relay_left.at[:, pl.ds(index * z.span, z.span)],
+            relay_sem.at[index],
+        )
+        copy.start()
+        relay_copies.append(copy)
+    decodings = []
+
+    def begin_decode(index):
+        slot = index % 2
+        fetch(index, False)
+        decodings.append(decode(
+            z, stage.at[slot, z.rows * z.slots], place[names[index]], vector.at[slot], scalars.at[slot],
+            place_sem.at[slot],
+        ))
+
+    begin_decode(0)
     dense_of = {}
     for index, name in enumerate(names):
-        dense = right.at[index]
+        dense = right.at[KEPT[name]]
         dense_of[name] = dense
         spot = place[name]
         slot = index % 2
-        fetch(index, False)
-        decoding = decode(
-            z, stage.at[slot, z.rows * z.slots], spot, vector.at[slot], scalars.at[slot], place_sem.at[slot]
-        )
         dense[...] = jnp.zeros_like(dense)
-        decoding.wait()
+        decodings[index].wait()
         scatter(z, dense, 0, stage.at[slot], lambda r, u: scalars[slot, r, u])
         if index + 2 < len(names):
             fetch(index + 2, True)
+        if index + 1 < len(names):
+            begin_decode(index + 1)
 
         def multiply(n, carry):
             total[:, chunk(n)] += jnp.dot(
@@ -274,20 +284,19 @@
         pl.when(weight != 0)(
             lambda: add_trace(trace, weight, left[:, chunk(spot)], dense[:, chunk(z.hops)])
         )
-    if final:
-        for (one, other), table in OUTSIDE.items():
-            weight = pick(table, kind)
-            pl.when(weight != 0)(lambda: add_trace(
-                trace, weight, dense_of[one][:, chunk(place[other])], dense_of[other][:, chunk(place[one])]
-            ))
-        half = z.span // 2
-        last = (z.chunks - 1) * z.span
-        pl.when(kind == 1)(lambda: add_trace(trace, jnp.float32(2), left[:, half:z.span], corner[...]))
-        pl.when(kind == 2)(
-            lambda: add_trace(trace, jnp.float32(2), left[:half, last:last + half], corner[:, :half])
-        )
+    for (one, other), table in OUTSIDE.items():
+        weight = pick(table, kind)
+        pl.when(weight != 0)(lambda: add_trace(
+            trace, weight, dense_of[one][:, chunk(place[other])], dense_of[other][:, chunk(place[one])]
+        ))
+    half = z.span // 2
+    last = (z.chunks - 1) * z.span
+    pl.when(kind == UPPER)(lambda: add_trace(trace, jnp.float32(2), left[:, half:z.span], corner[...]))
+    pl.when(kind == LOWER)(
+        lambda: add_trace(trace, jnp.float32(2), left[:half, last:last + half], corner[:, :half])
+    )
     prev_copy.wait()
-    emit(z, total, positions, out_stage, out, out_sems, prev_stage)
+    emit(z, total, positions, sums, out, out_sems, sums)
     for copy in relay_copies:
         copy.wait()
 
@@ -390,7 +399,6 @@
     )
     first = receive(payload, FIRST)
     second = receive(payload, SECOND)
-    beside = receive(payload, PARTNER)
 
     total, left, corner, positions, trace = call(
         z, functools.partial(own_body, z), [tiles, columns], [ANY, SMEM],
@@ -405,43 +413,39 @@
         ],
         1,
     )
-    corner = receive(corner, (0, CORNER[1], CORNER[2], 0), (1, 2))
-
-    def near(names, arrays, total, trace):
-        final = "mixed" in names
-        extra = [shape((z.span, 2 * z.span), dtype)] if final else []
-        return call(
-            z, functools.partial(near_body, z, names),
-            [left, positions, total, trace] + ([corner] if final else []) + arrays,
-            [ANY, SMEM, ANY, VMEM] + [VMEM] * final + [ANY] * len(arrays),
-            [sums, line] + extra,
-            [ANY, VMEM] + [ANY] * len(extra),
-            [
-                dense, pltpu.VMEM((2,) + payload_shape, dtype),
-                pltpu.VMEM((len(names), z.span, z.wide), dtype), total_buffer,
-                pltpu.VMEM(tiles.shape, jnp.float32), pltpu.VMEM(tiles.shape, jnp.float32), *places,
-                DMA, DMA((2,)), DMA, DMA((2,)), DMA((2,)), DMA((z.rows,)),
-            ],
-            len(names),
-        )
-
-    total, trace = near(("beside",), [beside], total, trace)
-    first, second, total, trace = lax.optimization_barrier((first, second, total, trace))
+    corner = receive(corner, (0, -3, 3, 0), (LOWER, UPPER))
+
+    first, total, trace = lax.optimization_barrier((first, total, trace))
     relay = receive(first, RELAY_FROM)
+    first, second, corner, payload, total, trace = lax.optimization_barrier(
+        (first, second, corner, payload, total, trace)
+    )
+    beside = receive(payload, PARTNER)
     mixed = [
         receive(first, PARTNER, [m for m in range(4) if not USE_SECOND[m]]),
         receive(second, PARTNER, [m for m in range(4) if USE_SECOND[m]]),
     ]
-    total, trace, relay_left = near(("first", "second", "mixed"), [first, second, *mixed], total, trace)
+    names = ("beside", "first", "second", "mixed")
+    total, trace, relay_left = call(
+        z, functools.partial(near_body, z, names),
+        [left, positions, total, trace, corner, beside, first, second, *mixed],
+        [ANY, SMEM, ANY, VMEM, VMEM] + [ANY] * 5,
+        [sums, line, shape((z.span, 2 * z.span), dtype)],
+        [ANY, VMEM, ANY],
+        [
+            dense, pltpu.VMEM((2,) + payload_shape, dtype), pltpu.VMEM((3, z.span, z.wide), dtype), total_buffer,
+            pltpu.VMEM(tiles.shape, jnp.float32), *places,
+            DMA, DMA((2,)), DMA, DMA((2,)), DMA((2,)), DMA((z.rows,)),
+        ],
+        4, 36 * 1024 * 1024,
+    )
     assert devices & (devices - 1) == 0
     steps = [1 << bit for bit in range(devices.bit_length() - 1)]
     for step in steps[:1] + steps[3:]:
         trace = exchange(trace, step)
     relay, total, trace = lax.optimization_barrier((relay, total, trace))
     relay_beside = receive(relay, PARTNER)
-    trace = exchange(trace, steps[2])
-    relay_beside, trace = lax.optimization_barrier((relay_beside, trace))
-    trace = exchange(trace, steps[1])
+    others = [fetch(trace, step) for step in (steps[1], steps[2], steps[1] + steps[2])]
     square = call(
         z, functools.partial(last_body, z), [relay_left, positions, total, relay, relay_beside],
         [ANY, SMEM, ANY, ANY, ANY],
@@ -453,9 +457,10 @@
             pltpu.VMEM(tiles.shape, dtype), pltpu.VMEM(tiles.shape, jnp.float32), *places,
             DMA, DMA((2,)), DMA, DMA((2,)), DMA((z.rows,)),
         ],
-        2, WHOLE_VMEM,
+        2, 44 * 1024 * 1024,
     )[0]
-    return square, jnp.sum(trace) / (z.all_rows * z.block)
+    square, trace, others = lax.optimization_barrier((square, trace, others))
+    return square, jnp.sum((trace + others[0]) + (others[1] + others[2])) / (z.all_rows * z.block)
 
 
 def solution(mesh):

time: 157 us -> 128 us (0.82)
  starting transfers between devices: 53.6 us -> 25.7 us
  Pallas kernels: 50.1 us -> 39.4 us
  waiting for transfers between devices: 47.1 us -> 52.7 us
  local copies, waits for them, and re-layouts: 3.13 us -> 5.54 us
    ppermute x5 -> x6, starting transfers between devices: 38.2 us -> 11 us  [fetch(): lax.ppermute(value, AXES, [(d, d ^ step) for d in range(lax.axis_size(AXE...]
    ppermute x8, waiting for transfers between devices: 37.2 us -> 48 us  [receive(): return lax.ppermute(shard, AXES, pairs)]
    pallas_call x5 -> x4, Pallas kernels: 50.1 us -> 39.4 us  [call(): pl.pallas_call(kernel, out_shape=out_shape, in_specs=in_specs, out_specs=...]
    ppermute x5 -> x6, waiting for transfers between devices: 9.92 us -> 4.74 us  [fetch(): lax.ppermute(value, AXES, [(d, d ^ step) for d in range(lax.axis_size(AXE...]
    unnamed x14 -> x12, local copies, waits for them, and re-layouts: 3.13 us -> 5.54 us
  transfers between devices with their start and end apart: 13 -> 14, of which waited for: 7 -> 7; matrix products, arithmetic and copies ran while one was open for 0% -> 0% of each run, Pallas kernels for 30% -> 28%
where the time goes in v7:
time: 128 us; the launch traced here: 126 us
  waiting for transfers between devices  52.7 us (41%)
  Pallas kernels  39.4 us (31%)
  starting transfers between devices  25.7 us (20%)
  local copies, waits for them, and re-layouts  5.54 us (4%)
  between operations  2.55 us (2%)
    ppermute x8, waiting for transfers between devices, receive(): return lax.ppermute(shard, AXES, pairs)  48 us
    pallas_call x4, Pallas kernels, call(): pl.pallas_call(kernel, out_shape=out_shape, in_specs=in_specs, out_specs=...  39.4 us
    ppermute x8, starting transfers between devices, receive(): return lax.ppermute(shard, AXES, pairs)  14.7 us
    ppermute x6, starting transfers between devices, fetch(): lax.ppermute(value, AXES, [(d, d ^ step) for d in range(lax.axis_size(AXE...  11 us
    unnamed x12, local copies, waits for them, and re-layouts  5.54 us
    ppermute x6, waiting for transfers between devices, fetch(): lax.ppermute(value, AXES, [(d, d ^ step) for d in range(lax.axis_size(AXE...  4.74 us
  transfers between devices with their start and end apart: 14, of which 7 were waited for; matrix products, arithmetic and copies ran while one was open for 0% of the time, Pallas kernels for 28%

profile of v7, /device:TPU:0, one launch (start us, length us, event | category | flops | bytes accessed | tf_op | source)
XLA Modules:
  0.0 126.5 jit_solution(6268068188873496074)
XLA Ops:
  0.6 0.0 copy-start.1
  0.6 0.0 copy-start
  0.6 3.5 %shard_map.42 = bf16[81,128,128]{2,1,0:T(8,128)(2,1)} custom-call(bf16[4,20,128,128]{3,2,1,0:T(8,128)(2,1)} %tiles.1, s32[4,20]{1,0:T(4,128)} %columns.3), custom_call_target="tpu_custom_call" | custom-call | bytes 10485760 | tf_op jit(solution)/shard_map/pallas_call | solution.py:362
  4.1 0.0 copy-start.5
  4.1 5.5 %collective-permute-start = (bf16[81,128,128]{2,1,0:T(8,128)(2,1)}, bf16[81,128,128]{2,1,0:T(8,128)(2,1)S(1)}, u32[]{:S(2)}, u32[]{:S(2)}) collective-permute-start(bf16[81,128,128]{2,1,0:T(8,128)(2,1)} %shard_map.42), channel_id=1, source_target_pairs={{2,0},{4,1},{31,2},{1,3},{6,4},{8,5},{3,6},{5,7},{10,8},{12,9},{7,... | collective-permute-start | bytes 7962632 | tf_op jit(solution)/shard_map/ppermute | solution.py:49
  9.7 0.0 collective-permute-start.1
  9.7 0.0 copy-done.1
  9.7 0.0 copy-done
  9.7 7.3 %shard_map.41 = (f32[4,20,128,128]{3,2,1,0:T(8,128)S(1)}, bf16[512,3712]{1,0:T(8,128)(2,1)S(1)}, bf16[256,512]{1,0:T(8,128)(2,1)S(1)}, s32[4,20]{1,0:T(4,128)S(1)}, f32[1,512]{1,0:T(1,128)S(1)}) custom-call(bf16[4,20,128,128]{3,2,1,0:T(8,128)(2,1)S(1)} %copy-done, s32[4,20]{1,0:T(4,128)S(1)} %copy-done.1), custom_call_target="tpu_custom_call" | custom-call | flops 1879048192 | bytes 13107200 | tf_op jit(solution)/shard_map/pallas_call | solution.py:362
  17.0 0.0 copy-start.4
  17.0 2.3 %copy-done.4 = f32[4,20,128,128]{3,2,1,0:T(8,128)} copy-done((f32[4,20,128,128]{3,2,1,0:T(8,128)}, f32[4,20,128,128]{3,2,1,0:T(8,128)S(1)}, u32[]{:S(2)}) %copy-start.4) | copy-done | bytes 5242904
  19.3 0.7 collective-permute-start.2
  20.0 44.8 %collective-permute-done.refs_2_ = bf16[81,128,128]{2,1,0:T(8,128)(2,1)S(1)} collective-permute-done((bf16[81,128,128]{2,1,0:T(8,128)(2,1)}, bf16[81,128,128]{2,1,0:T(8,128)(2,1)S(1)}, u32[]{:S(2)}, u32[]{:S(2)}) %collective-permute-start) | collective-permute-done | bytes 2654240 | tf_op jit(solution)/shard_map/ppermute | solution.py:49
  64.8 0.0 collective-permute-done.2.refs_0_
  64.8 2.3 %collective-permute-done.1.refs_3_ = bf16[81,128,128]{2,1,0:T(8,128)(2,1)S(1)} collective-permute-done((bf16[81,128,128]{2,1,0:T(8,128)(2,1)}, bf16[81,128,128]{2,1,0:T(8,128)(2,1)S(1)}, u32[]{:S(2)}, u32[]{:S(2)}) %collective-permute-start.1) | collective-permute-done | bytes 2654240 | tf_op jit(solution)/shard_map/ppermute | solution.py:49
  67.1 0.0 copy-done.5
  67.1 1.4 %collective-permute-start.3 = (bf16[81,128,128]{2,1,0:T(8,128)(2,1)S(1)}, bf16[81,128,128]{2,1,0:T(8,128)(2,1)S(1)}, u32[]{:S(2)}, u32[]{:S(2)}) collective-permute-start(bf16[81,128,128]{2,1,0:T(8,128)(2,1)S(1)} %copy-done.5), channel_id=1, source_target_pairs={{1,0},{0,1},{3,2},{2,3},{5,4},{4,5},{7,6},{6,7},{9,8},{8,9},{11,10... | collective-permute-start | bytes 7962632 | tf_op jit(solution)/shard_map/ppermute | solution.py:49
  68.5 2.1 %collective-permute-start.4 = (bf16[81,128,128]{2,1,0:T(8,128)(2,1)S(1)}, bf16[81,128,128]{2,1,0:T(8,128)(2,1)S(1)}, u32[]{:S(2)}, u32[]{:S(2)}) collective-permute-start(bf16[81,128,128]{2,1,0:T(8,128)(2,1)S(1)} %collective-permute-done.refs_2_), channel_id=1, source_target_pairs={{0,1},{3,2},{4,5},{7,6},{8,9},{11,10},{12,13},{15,14},{16,17},{19,... | collective-permute-start | bytes 7962632 | tf_op jit(solution)/shard_map/ppermute | solution.py:49
  70.6 1.3 %collective-permute-start.5 = (bf16[81,128,128]{2,1,0:T(8,128)(2,1)S(1)}, bf16[81,128,128]{2,1,0:T(8,128)(2,1)S(1)}, u32[]{:S(2)}, u32[]{:S(2)}) collective-permute-start(bf16[81,128,128]{2,1,0:T(8,128)(2,1)S(1)} %collective-permute-done.1.refs_3_), channel_id=1, source_target_pairs={{1,0},{2,3},{5,4},{6,7},{9,8},{10,11},{13,12},{14,15},{17,16},{18,... | collective-permute-start | bytes 7962632 | tf_op jit(solution)/shard_map/ppermute | solution.py:49
  71.9 0.0 copy-start.2
  71.9 1.5 %copy-done.2 = bf16[81,128,128]{2,1,0:T(8,128)(2,1)} copy-done((bf16[81,128,128]{2,1,0:T(8,128)(2,1)}, bf16[81,128,128]{2,1,0:T(8,128)(2,1)S(1)}, u32[]{:S(2)}) %copy-start.2) | copy-done | bytes 2654232
  73.4 3.2 %collective-permute-start.6 = (bf16[81,128,128]{2,1,0:T(8,128)(2,1)S(1)}, bf16[81,128,128]{2,1,0:T(8,128)(2,1)S(1)}, u32[]{:S(2)}, u32[]{:S(2)}) collective-permute-start(bf16[81,128,128]{2,1,0:T(8,128)(2,1)S(1)} %collective-permute-done.refs_2_), channel_id=1, source_target_pairs={{2,0},{28,1},{7,2},{1,3},{6,4},{0,5},{11,6},{5,7},{10,8},{4,9},{15... | collective-permute-start | bytes 7962632 | tf_op jit(solution)/shard_map/ppermute | solution.py:49
  76.6 0.0 collective-permute-done.3.refs_1_
  76.6 0.3 collective-permute-done.4.refs_4_
  76.9 0.6 collective-permute-done.5.refs_5_
  77.5 0.0 copy-start.3
  77.5 1.7 %copy-done.3 = bf16[81,128,128]{2,1,0:T(8,128)(2,1)S(1)} copy-done((bf16[81,128,128]{2,1,0:T(8,128)(2,1)S(1)}, bf16[81,128,128]{2,1,0:T(8,128)(2,1)}, u32[]{:S(2)}) %copy-start.3) | copy-done | bytes 2654232
  79.2 19.3 %shard_map.43 = (f32[4,20,128,128]{3,2,1,0:T(8,128)}, f32[1,512]{1,0:T(1,128)S(1)}, bf16[512,1024]{1,0:T(8,128)(2,1)S(1)}) custom-call(bf16[512,3712]{1,0:T(8,128)(2,1)S(1)} %get-tuple-element.27.left_in, s32[4,20]{1,0:T(4,128)S(1)} %get-tuple-element.28.positions, f32[4,20,128,128]{3,2,1,0:T(8,128)} %copy-done.4, f32[1,512]{1,0:T(1,128)S(1)} %get-tuple-element.36.trace_in, ...), custom_call_target="tpu_custom_call" | custom-call | flops 7516192768 | bytes 20971520 | tf_op jit(solution)/shard_map/pallas_call | solution.py:362
  98.5 0.9 collective-permute-start.7
  99.5 0.8 collective-permute-done.7
  100.3 1.6 %collective-permute-start.8 = (f32[1,512]{1,0:T(1,128)S(1)}, f32[1,512]{1,0:T(1,128)S(1)}, u32[]{:S(2)}, u32[]{:S(2)}) collective-permute-start(f32[1,512]{1,0:T(1,128)S(1)} %add.18), channel_id=1, source_target_pairs={{0,8},{1,9},{2,10},{3,11},{4,12},{5,13},{6,14},{7,15},{8,0},{9,1},... | collective-permute-start | bytes 6152 | tf_op jit(solution)/shard_map/ppermute | solution.py:53
  101.9 2.0 %collective-permute-done.8 = f32[1,512]{1,0:T(1,128)S(1)} collective-permute-done((f32[1,512]{1,0:T(1,128)S(1)}, f32[1,512]{1,0:T(1,128)S(1)}, u32[]{:S(2)}, u32[]{:S(2)}) %collective-permute-start.8) | collective-permute-done | bytes 2080 | tf_op jit(solution)/shard_map/ppermute | solution.py:53
  103.9 2.6 %collective-permute-start.9 = (f32[1,512]{1,0:T(1,128)S(1)}, f32[1,512]{1,0:T(1,128)S(1)}, u32[]{:S(2)}, u32[]{:S(2)}) collective-permute-start(f32[1,512]{1,0:T(1,128)S(1)} %add.19), channel_id=1, source_target_pairs={{0,16},{1,17},{2,18},{3,19},{4,20},{5,21},{6,22},{7,23},{8,24},{9,... | collective-permute-start | bytes 6152 | tf_op jit(solution)/shard_map/ppermute | solution.py:53
  106.5 1.9 %collective-permute-done.9 = f32[1,512]{1,0:T(1,128)S(1)} collective-permute-done((f32[1,512]{1,0:T(1,128)S(1)}, f32[1,512]{1,0:T(1,128)S(1)}, u32[]{:S(2)}, u32[]{:S(2)}) %collective-permute-start.9) | collective-permute-done | bytes 2080 | tf_op jit(solution)/shard_map/ppermute | solution.py:53
  108.4 0.0 collective-permute-done.6.source_a
  108.4 0.5 collective-permute-start.10
  108.9 2.8 %collective-permute-start.13 = (f32[1,512]{1,0:T(1,128)S(1)}, f32[1,512]{1,0:T(1,128)S(1)}, u32[]{:S(2)}, u32[]{:S(2)}) collective-permute-start(f32[1,512]{1,0:T(1,128)S(1)} %add.20), channel_id=1, source_target_pairs={{0,6},{1,7},{2,4},{3,5},{4,2},{5,3},{6,0},{7,1},{8,14},{9,15},{10,... | collective-permute-start | bytes 6152 | tf_op jit(solution)/shard_map/ppermute | solution.py:53
  111.7 3.1 %collective-permute-start.12 = (f32[1,512]{1,0:T(1,128)S(1)}, f32[1,512]{1,0:T(1,128)S(1)}, u32[]{:S(2)}, u32[]{:S(2)}) collective-permute-start(f32[1,512]{1,0:T(1,128)S(1)} %add.20), channel_id=1, source_target_pairs={{0,4},{1,5},{2,6},{3,7},{4,0},{5,1},{6,2},{7,3},{8,12},{9,13},{10,... | collective-permute-start | bytes 6152 | tf_op jit(solution)/shard_map/ppermute | solution.py:53
  114.8 0.0 collective-permute-start.11
  114.8 0.0 collective-permute-done.10.source_b
  114.8 9.2 %shard_map.44 = bf16[4,20,128,128]{3,2,1,0:T(8,128)(2,1)} custom-call(bf16[512,1024]{1,0:T(8,128)(2,1)S(1)} %get-tuple-element.41.left_in, s32[4,20]{1,0:T(4,128)S(1)} %get-tuple-element.28.positions, f32[4,20,128,128]{3,2,1,0:T(8,128)} %get-tuple-element.44.prev, bf16[81,128,128]{2,1,0:T(8,128)(2,1)S(1)} %collective-permute-done.6.source_a, ...), custom_call_target="tpu_custom_call" | custom-call | flops 3758096384 | bytes 15728640 | tf_op jit(solution)/shard_map/pallas_call | solution.py:362
  124.1 0.0 collective-permute-done.13
  124.1 0.0 collective-permute-done.12
  124.1 0.0 collective-permute-done.11
  124.1 0.6 add_reduce_fusion
  (3 shorter events, 0.0 us)
Async XLA Ops:
  0.6 9.0 %copy-start.1 = (s32[4,20]{1,0:T(4,128)S(1)}, s32[4,20]{1,0:T(4,128)}, u32[]{:S(2)}) copy-start(s32[4,20]{1,0:T(4,128)} %columns.3) | copy-start | bytes 964
  0.6 9.0 %copy-start = (bf16[4,20,128,128]{3,2,1,0:T(8,128)(2,1)S(1)}, bf16[4,20,128,128]{3,2,1,0:T(8,128)(2,1)}, u32[]{:S(2)}) copy-start(bf16[4,20,128,128]{3,2,1,0:T(8,128)(2,1)} %tiles.1) | copy-start | bytes 7864324
  4.1 63.0 %copy-start.5 = (bf16[81,128,128]{2,1,0:T(8,128)(2,1)S(1)}, bf16[81,128,128]{2,1,0:T(8,128)(2,1)}, u32[]{:S(2)}) copy-start(bf16[81,128,128]{2,1,0:T(8,128)(2,1)} %shard_map.42) | copy-start | bytes 7962628
  4.1 60.7 %collective-permute-start = (bf16[81,128,128]{2,1,0:T(8,128)(2,1)}, bf16[81,128,128]{2,1,0:T(8,128)(2,1)S(1)}, u32[]{:S(2)}, u32[]{:S(2)}) collective-permute-start(bf16[81,128,128]{2,1,0:T(8,128)(2,1)} %shard_map.42), channel_id=1, source_target_pairs={{2,0},{4,1},{31,2},{1,3},{6,4},{8,5},{3,6},{5,7},{10,8},{12,9},{7,... | collective-permute-start | bytes 7962632 | tf_op jit(solution)/shard_map/ppermute | solution.py:49
  9.7 57.4 %collective-permute-start.1 = (bf16[81,128,128]{2,1,0:T(8,128)(2,1)}, bf16[81,128,128]{2,1,0:T(8,128)(2,1)S(1)}, u32[]{:S(2)}, u32[]{:S(2)}) collective-permute-start(bf16[81,128,128]{2,1,0:T(8,128)(2,1)} %shard_map.42), channel_id=1, source_target_pairs={{29,0},{3,1},{0,2},{6,3},{1,4},{7,5},{4,6},{10,7},{5,8},{11,9},{8,... | collective-permute-start | bytes 7962632 | tf_op jit(solution)/shard_map/ppermute | solution.py:49
  17.0 2.3 %copy-start.4 = (f32[4,20,128,128]{3,2,1,0:T(8,128)}, f32[4,20,128,128]{3,2,1,0:T(8,128)S(1)}, u32[]{:S(2)}) copy-start(f32[4,20,128,128]{3,2,1,0:T(8,128)S(1)} %get-tuple-element.35.prev) | copy-start | bytes 15728644
  19.3 45.5 %collective-permute-start.2 = (bf16[256,512]{1,0:T(8,128)(2,1)S(1)}, bf16[256,512]{1,0:T(8,128)(2,1)S(1)}, u32[]{:S(2)}, u32[]{:S(2)}) collective-permute-start(bf16[256,512]{1,0:T(8,128)(2,1)S(1)} %get-tuple-element.32), channel_id=1, source_target_pairs={{30,1},{5,2},{2,5},{9,6},{6,9},{13,10},{10,13},{17,14},{14,17},{21... | collective-permute-start | bytes 786440 | tf_op jit(solution)/shard_map/ppermute | solution.py:49
  67.1 9.5 %collective-permute-start.3 = (bf16[81,128,128]{2,1,0:T(8,128)(2,1)S(1)}, bf16[81,128,128]{2,1,0:T(8,128)(2,1)S(1)}, u32[]{:S(2)}, u32[]{:S(2)}) collective-permute-start(bf16[81,128,128]{2,1,0:T(8,128)(2,1)S(1)} %copy-done.5), channel_id=1, source_target_pairs={{1,0},{0,1},{3,2},{2,3},{5,4},{4,5},{7,6},{6,7},{9,8},{8,9},{11,10... | collective-permute-start | bytes 7962632 | tf_op jit(solution)/shard_map/ppermute | solution.py:49
  68.5 8.4 %collective-permute-start.4 = (bf16[81,128,128]{2,1,0:T(8,128)(2,1)S(1)}, bf16[81,128,128]{2,1,0:T(8,128)(2,1)S(1)}, u32[]{:S(2)}, u32[]{:S(2)}) collective-permute-start(bf16[81,128,128]{2,1,0:T(8,128)(2,1)S(1)} %collective-permute-done.refs_2_), channel_id=1, source_target_pairs={{0,1},{3,2},{4,5},{7,6},{8,9},{11,10},{12,13},{15,14},{16,17},{19,... | collective-permute-start | bytes 7962632 | tf_op jit(solution)/shard_map/ppermute | solution.py:49
  70.6 6.9 %collective-permute-start.5 = (bf16[81,128,128]{2,1,0:T(8,128)(2,1)S(1)}, bf16[81,128,128]{2,1,0:T(8,128)(2,1)S(1)}, u32[]{:S(2)}, u32[]{:S(2)}) collective-permute-start(bf16[81,128,128]{2,1,0:T(8,128)(2,1)S(1)} %collective-permute-done.1.refs_3_), channel_id=1, source_target_pairs={{1,0},{2,3},{5,4},{6,7},{9,8},{10,11},{13,12},{14,15},{17,16},{18,... | collective-permute-start | bytes 7962632 | tf_op jit(solution)/shard_map/ppermute | solution.py:49
  71.9 1.5 %copy-start.2 = (bf16[81,128,128]{2,1,0:T(8,128)(2,1)}, bf16[81,128,128]{2,1,0:T(8,128)(2,1)S(1)}, u32[]{:S(2)}) copy-start(bf16[81,128,128]{2,1,0:T(8,128)(2,1)S(1)} %collective-permute-done.1.refs_3_) | copy-start | bytes 7962628
  73.4 35.0 %collective-permute-start.6 = (bf16[81,128,128]{2,1,0:T(8,128)(2,1)S(1)}, bf16[81,128,128]{2,1,0:T(8,128)(2,1)S(1)}, u32[]{:S(2)}, u32[]{:S(2)}) collective-permute-start(bf16[81,128,128]{2,1,0:T(8,128)(2,1)S(1)} %collective-permute-done.refs_2_), channel_id=1, source_target_pairs={{2,0},{28,1},{7,2},{1,3},{6,4},{0,5},{11,6},{5,7},{10,8},{4,9},{15... | collective-permute-start | bytes 7962632 | tf_op jit(solution)/shard_map/ppermute | solution.py:49
  77.5 1.8 %copy-start.3 = (bf16[81,128,128]{2,1,0:T(8,128)(2,1)S(1)}, bf16[81,128,128]{2,1,0:T(8,128)(2,1)}, u32[]{:S(2)}) copy-start(bf16[81,128,128]{2,1,0:T(8,128)(2,1)} %copy-done.2) | copy-start | bytes 7962628
  98.5 1.8 %collective-permute-start.7 = (f32[1,512]{1,0:T(1,128)S(1)}, f32[1,512]{1,0:T(1,128)S(1)}, u32[]{:S(2)}, u32[]{:S(2)}) collective-permute-start(f32[1,512]{1,0:T(1,128)S(1)} %get-tuple-element.43), channel_id=1, source_target_pairs={{0,1},{1,0},{2,3},{3,2},{4,5},{5,4},{6,7},{7,6},{8,9},{9,8},{10,11... | collective-permute-start | bytes 6152 | tf_op jit(solution)/shard_map/ppermute | solution.py:53
  100.3 3.6 %collective-permute-start.8 = (f32[1,512]{1,0:T(1,128)S(1)}, f32[1,512]{1,0:T(1,128)S(1)}, u32[]{:S(2)}, u32[]{:S(2)}) collective-permute-start(f32[1,512]{1,0:T(1,128)S(1)} %add.18), channel_id=1, source_target_pairs={{0,8},{1,9},{2,10},{3,11},{4,12},{5,13},{6,14},{7,15},{8,0},{9,1},... | collective-permute-start | bytes 6152 | tf_op jit(solution)/shard_map/ppermute | solution.py:53
  103.9 4.5 %collective-permute-start.9 = (f32[1,512]{1,0:T(1,128)S(1)}, f32[1,512]{1,0:T(1,128)S(1)}, u32[]{:S(2)}, u32[]{:S(2)}) collective-permute-start(f32[1,512]{1,0:T(1,128)S(1)} %add.19), channel_id=1, source_target_pairs={{0,16},{1,17},{2,18},{3,19},{4,20},{5,21},{6,22},{7,23},{8,24},{9,... | collective-permute-start | bytes 6152 | tf_op jit(solution)/shard_map/ppermute | solution.py:53
  108.4 6.5 %collective-permute-start.10 = (bf16[81,128,128]{2,1,0:T(8,128)(2,1)S(1)}, bf16[81,128,128]{2,1,0:T(8,128)(2,1)S(1)}, u32[]{:S(2)}, u32[]{:S(2)}) collective-permute-start(bf16[81,128,128]{2,1,0:T(8,128)(2,1)S(1)} %collective-permute-done.6.source_a), channel_id=1, source_target_pairs={{1,0},{0,1},{3,2},{2,3},{5,4},{4,5},{7,6},{6,7},{9,8},{8,9},{11,10... | collective-permute-start | bytes 7962632 | tf_op jit(solution)/shard_map/ppermute | solution.py:49
  108.9 15.2 %collective-permute-start.13 = (f32[1,512]{1,0:T(1,128)S(1)}, f32[1,512]{1,0:T(1,128)S(1)}, u32[]{:S(2)}, u32[]{:S(2)}) collective-permute-start(f32[1,512]{1,0:T(1,128)S(1)} %add.20), channel_id=1, source_target_pairs={{0,6},{1,7},{2,4},{3,5},{4,2},{5,3},{6,0},{7,1},{8,14},{9,15},{10,... | collective-permute-start | bytes 6152 | tf_op jit(solution)/shard_map/ppermute | solution.py:53
  111.7 12.3 %collective-permute-start.12 = (f32[1,512]{1,0:T(1,128)S(1)}, f32[1,512]{1,0:T(1,128)S(1)}, u32[]{:S(2)}, u32[]{:S(2)}) collective-permute-start(f32[1,512]{1,0:T(1,128)S(1)} %add.20), channel_id=1, source_target_pairs={{0,4},{1,5},{2,6},{3,7},{4,0},{5,1},{6,2},{7,3},{8,12},{9,13},{10,... | collective-permute-start | bytes 6152 | tf_op jit(solution)/shard_map/ppermute | solution.py:53
  114.8 9.3 %collective-permute-start.11 = (f32[1,512]{1,0:T(1,128)S(1)}, f32[1,512]{1,0:T(1,128)S(1)}, u32[]{:S(2)}, u32[]{:S(2)}) collective-permute-start(f32[1,512]{1,0:T(1,128)S(1)} %add.20), channel_id=1, source_target_pairs={{0,2},{1,3},{2,0},{3,1},{4,6},{5,7},{6,4},{7,5},{8,10},{9,11},{10,... | collective-permute-start | bytes 6152 | tf_op jit(solution)/shard_map/ppermute | solution.py:53

commit v8 on v7

--- a/solution.py
+++ b/solution.py
@@ -9,38 +9,35 @@
 
 REACH = 12
 AXES = ("blk", "grp")
-VMEM_LIMIT = 36 * 1024 * 1024
+VMEM_LIMIT = 42 * 1024 * 1024
 WHOLE_VMEM = 60 * 1024 * 1024
 EMPTY = 64
 
-FIRST = (2, 3, -3, -2)
-SECOND = (-3, 2, -2, 3)
+OVER_X = (2, 2, -2, -2)
+OVER_Y = (-3, 3, -3, 3)
 RELAY_FROM = (2, -5, 5, -2)
+RELAY_X, RELAY_Y = (1, 2), (0, 3)
 PARTNER = (1, -1, 1, -1)
-RELAY = tuple(RELAY_FROM[m] + FIRST[(m + RELAY_FROM[m]) % 4] for m in range(4))
+RELAY = tuple(
+    RELAY_FROM[m] + (OVER_X if m in RELAY_X else OVER_Y)[(m + RELAY_FROM[m]) % 4] for m in range(4)
+)
 
 
 def across(table):
     return tuple(PARTNER[m] + table[m ^ 1] for m in range(4))
 
 
-USE_SECOND = tuple(int(abs(offset) > 3) for offset in across(FIRST))
-MIXED = tuple(
-    second if use else first
-    for first, second, use in zip(across(FIRST), across(SECOND), USE_SECOND)
-)
 OFFSETS = {
     "beside": PARTNER,
-    "first": FIRST,
-    "second": SECOND,
-    "mixed": MIXED,
+    "x": OVER_X,
+    "y": OVER_Y,
+    "x_beside": across(OVER_X),
     "relay": RELAY,
     "relay_beside": across(RELAY),
 }
-COUNTS = {"beside": (2, 0, 2, 0), "first": (2, 0, 0, 2), "second": (2, 0, 0, 2), "mixed": (0, 0, 2, 2)}
-OUTSIDE = {("first", "mixed"): (0, 2, 2, 0), ("first", "second"): (0, 2, 0, 0)}
+COUNTS = {"beside": (2, 0, 2, 0), "x": (2, 0, 0, 2), "y": (2, 0, 0, 2), "x_beside": (0, 0, 2, 2)}
+OUTSIDE = {("y", "x_beside"): (0, 2, 2, 0), ("y", "x"): (0, 2, 0, 0)}
 LOWER, UPPER = 2, 1
-KEPT = {"beside": 0, "first": 0, "second": 1, "mixed": 2}
 
 
 def receive(shard, offsets, kinds=range(4)):
@@ -204,12 +201,13 @@
     left_copy.wait()
 
 
-def near_body(z, names, left_in, positions, prev, trace_in, *refs):
+def near_body(z, names, final, left_in, positions, prev, trace_in, *refs):
     refs = list(refs)
     take = lambda count: [refs.pop(0) for _ in range(count)]
-    corner = take(1)[0]
-    sources = {name: take(2 if name == "mixed" else 1) for name in names}
-    out, trace, relay_left = take(3)
+    corner = take(1)[0] if final else None
+    sources = take(len(names))
+    out, trace = take(2)
+    relay_left = take(1)[0] if final else None
     left, stage, right, total, sums, vector, scalars = take(7)
     left_sem, in_sem, prev_sem, place_sem, relay_sem, out_sems = take(6)
     device = lax.axis_index(AXES)
@@ -219,29 +217,20 @@
     def chunk(n):
         return pl.ds(aligned(n, z.span), z.span)
 
-    def fetch(index, begin):
-        def go(source):
-            copy = pltpu.make_async_copy(source, stage.at[index % 2], in_sem.at[index % 2])
-            copy.start() if begin else copy.wait()
-        source = sources[names[index]]
-        if len(source) == 1:
-            go(source[0])
-        else:
-            use_second = pick(USE_SECOND, kind)
-            pl.when(use_second == 0)(lambda: go(source[0]))
-            pl.when(use_second != 0)(lambda: go(source[1]))
+    def fetch(index):
+        return pltpu.make_async_copy(sources[index], stage.at[index % 2], in_sem.at[index % 2])
 
     left_copy = pltpu.make_async_copy(left_in, left, left_sem)
     left_copy.start()
     for index in range(min(2, len(names))):
-        fetch(index, True)
+        fetch(index).start()
     prev_copy = pltpu.make_async_copy(prev, sums, prev_sem)
     prev_copy.start()
     total[...] = jnp.zeros_like(total)
     trace[...] = trace_in[...]
     left_copy.wait()
     relay_copies = []
-    for index, name in enumerate(("relay", "relay_beside")):
+    for index, name in enumerate(("relay", "relay_beside") if final else ()):
         copy = pltpu.make_async_copy(
             left.at[:, chunk(place[name])], relay_left.at[:, pl.ds(index * z.span, z.span)],
             relay_sem.at[index],
@@ -252,7 +241,7 @@
 
     def begin_decode(index):
         slot = index % 2
-        fetch(index, False)
+        fetch(index).wait()
         decodings.append(decode(
             z, stage.at[slot, z.rows * z.slots], place[names[index]], vector.at[slot], scalars.at[slot],
             place_sem.at[slot],
@@ -261,7 +250,7 @@
     begin_decode(0)
     dense_of = {}
     for index, name in enumerate(names):
-        dense = right.at[KEPT[name]]
+        dense = right.at[index]
         dense_of[name] = dense
         spot = place[name]
         slot = index % 2
@@ -269,7 +258,7 @@
         decodings[index].wait()
         scatter(z, dense, 0, stage.at[slot], lambda r, u: scalars[slot, r, u])
         if index + 2 < len(names):
-            fetch(index + 2, True)
+            fetch(index + 2).start()
         if index + 1 < len(names):
             begin_decode(index + 1)
 
@@ -284,33 +273,39 @@
         pl.when(weight != 0)(
             lambda: add_trace(trace, weight, left[:, chunk(spot)], dense[:, chunk(z.hops)])
         )
-    for (one, other), table in OUTSIDE.items():
+    for (one, other), table in OUTSIDE.items() if final else ():
         weight = pick(table, kind)
         pl.when(weight != 0)(lambda: add_trace(
             trace, weight, dense_of[one][:, chunk(place[other])], dense_of[other][:, chunk(place[one])]
         ))
-    half = z.span // 2
-    last = (z.chunks - 1) * z.span
-    pl.when(kind == UPPER)(lambda: add_trace(trace, jnp.float32(2), left[:, half:z.span], corner[...]))
-    pl.when(kind == LOWER)(
-        lambda: add_trace(trace, jnp.float32(2), left[:half, last:last + half], corner[:, :half])
-    )
+    if final:
+        half = z.span // 2
+        end = (z.chunks - 1) * z.span
+        pl.when(kind == UPPER)(lambda: add_trace(trace, jnp.float32(2), left[:, half:z.span], corner[...]))
+        pl.when(kind == LOWER)(
+            lambda: add_trace(trace, jnp.float32(2), left[:half, end:end + half], corner[:, :half])
+        )
     prev_copy.wait()
     emit(z, total, positions, sums, out, out_sems, sums)
     for copy in relay_copies:
         copy.wait()
 
 
-def last_body(z, left_in, positions, prev, source_a, source_b, out, left, stage, right, total, out_stage,
+def last_body(z, left_in, positions, prev, relay_x, relay_y, beside_x, beside_y, out, left, stage, right, total, out_stage,
               prev_stage, vector, scalars, left_sem, in_sem, prev_sem, place_sem, out_sems):
     kind = lax.axis_index(AXES) % 4
+    gets_x = (kind == RELAY_X[0]) | (kind == RELAY_X[1])
+    for over_x, index, source in ((True, 0, relay_x), (False, 0, relay_y), (False, 1, beside_x), (True, 1, beside_y)):
+        @pl.when(gets_x == over_x)
+        def _():
+            pltpu.make_async_copy(source, stage.at[index], in_sem.at[index]).start()
     copies = [
-        pltpu.make_async_copy(source_a, stage.at[0], in_sem.at[0]),
-        pltpu.make_async_copy(source_b, stage.at[1], in_sem.at[1]),
+        pltpu.make_async_copy(relay_x, stage.at[0], in_sem.at[0]),
+        pltpu.make_async_copy(beside_x, stage.at[1], in_sem.at[1]),
         pltpu.make_async_copy(left_in, left, left_sem),
         pltpu.make_async_copy(prev, prev_stage, prev_sem),
     ]
-    for copy in copies:
+    for copy in copies[2:]:
         copy.start()
     places = [pick(OFFSETS[name], kind) + z.hops for name in ("relay", "relay_beside")]
     low = jnp.maximum(0, jnp.minimum(*places) - z.hops)
@@ -397,8 +392,9 @@
         ],
         0, WHOLE_VMEM,
     )
-    first = receive(payload, FIRST)
-    second = receive(payload, SECOND)
+    over_x = receive(payload, OVER_X)
+    over_y = receive(payload, OVER_Y)
+    beside = receive(payload, PARTNER)
 
     total, left, corner, positions, trace = call(
         z, functools.partial(own_body, z), [tiles, columns], [ANY, SMEM],
@@ -411,44 +407,48 @@
             pltpu.VMEM(tiles.shape, dtype), dense, total_buffer, pltpu.VMEM(tiles.shape, jnp.float32),
             DMA, DMA, DMA, DMA((z.rows,)),
         ],
-        1,
+        1, WHOLE_VMEM,
     )
-    corner = receive(corner, (0, -3, 3, 0), (LOWER, UPPER))
-
-    first, total, trace = lax.optimization_barrier((first, total, trace))
-    relay = receive(first, RELAY_FROM)
-    first, second, corner, payload, total, trace = lax.optimization_barrier(
-        (first, second, corner, payload, total, trace)
-    )
-    beside = receive(payload, PARTNER)
-    mixed = [
-        receive(first, PARTNER, [m for m in range(4) if not USE_SECOND[m]]),
-        receive(second, PARTNER, [m for m in range(4) if USE_SECOND[m]]),
-    ]
-    names = ("beside", "first", "second", "mixed")
-    total, trace, relay_left = call(
-        z, functools.partial(near_body, z, names),
-        [left, positions, total, trace, corner, beside, first, second, *mixed],
-        [ANY, SMEM, ANY, VMEM, VMEM] + [ANY] * 5,
-        [sums, line, shape((z.span, 2 * z.span), dtype)],
-        [ANY, VMEM, ANY],
-        [
-            dense, pltpu.VMEM((2,) + payload_shape, dtype), pltpu.VMEM((3, z.span, z.wide), dtype), total_buffer,
-            pltpu.VMEM(tiles.shape, jnp.float32), *places,
-            DMA, DMA((2,)), DMA, DMA((2,)), DMA((2,)), DMA((z.rows,)),
-        ],
-        4, 36 * 1024 * 1024,
+    corner = receive(corner, PARTNER, (0, 3))
+
+    def near(names, arrays, total, trace, corner=None):
+        final = corner is not None
+        extra = [shape((z.span, 2 * z.span), dtype)] * final
+        return call(
+            z, functools.partial(near_body, z, names, final),
+            [left, positions, total, trace] + [corner] * final + arrays,
+            [ANY, SMEM, ANY, VMEM] + [VMEM] * final + [ANY] * len(arrays),
+            [sums, line] + extra,
+            [ANY, VMEM] + [ANY] * final,
+            [
+                dense, pltpu.VMEM((2,) + payload_shape, dtype),
+                pltpu.VMEM((len(names), z.span, z.wide), dtype), total_buffer,
+                pltpu.VMEM(tiles.shape, jnp.float32), *places,
+                DMA, DMA((2,)), DMA, DMA((2,)), DMA((2,)), DMA((z.rows,)),
+            ],
+            len(names), VMEM_LIMIT if final else WHOLE_VMEM,
+        )
+
+    total, trace = near(("beside",), [beside], total, trace)
+    over_x, over_y, corner, total, trace = lax.optimization_barrier((over_x, over_y, corner, total, trace))
+    relay_x = receive(over_x, RELAY_FROM, RELAY_X)
+    relay_y = receive(over_y, RELAY_FROM, RELAY_Y)
+    x_beside = receive(over_x, PARTNER)
+    corner = receive(corner, (0, -2, 2, 0), (LOWER, UPPER))
+    total, trace, relay_left = near(
+        ("x", "y", "x_beside"), [over_x, over_y, x_beside], total, trace, corner
     )
     assert devices & (devices - 1) == 0
     steps = [1 << bit for bit in range(devices.bit_length() - 1)]
     for step in steps[:1] + steps[3:]:
         trace = exchange(trace, step)
-    relay, total, trace = lax.optimization_barrier((relay, total, trace))
-    relay_beside = receive(relay, PARTNER)
+    relay_x, relay_y, total, trace = lax.optimization_barrier((relay_x, relay_y, total, trace))
+    beside_x = receive(relay_x, PARTNER, RELAY_Y)
+    beside_y = receive(relay_y, PARTNER, RELAY_X)
     others = [fetch(trace, step) for step in (steps[1], steps[2], steps[1] + steps[2])]
     square = call(
-        z, functools.partial(last_body, z), [relay_left, positions, total, relay, relay_beside],
-        [ANY, SMEM, ANY, ANY, ANY],
+        z, functools.partial(last_body, z), [relay_left, positions, total, relay_x, relay_y, beside_x, beside_y],
+        [ANY, SMEM] + [ANY] * 5,
         [shape(tiles.shape, dtype)],
         [ANY],
         [
@@ -457,7 +457,7 @@
             pltpu.VMEM(tiles.shape, dtype), pltpu.VMEM(tiles.shape, jnp.float32), *places,
             DMA, DMA((2,)), DMA, DMA((2,)), DMA((z.rows,)),
         ],
-        2, 44 * 1024 * 1024,
+        2, 40 * 1024 * 1024,
     )[0]
     square, trace, others = lax.optimization_barrier((square, trace, others))
     return square, jnp.sum((trace + others[0]) + (others[1] + others[2])) / (z.all_rows * z.block)

time: 128 us -> 138 us (1.078)
  starting transfers between devices: 25.7 us -> 38.7 us
  Pallas kernels: 39.4 us -> 49.6 us
  waiting for transfers between devices: 52.7 us -> 45 us
  local copies, waits for them, and re-layouts: 5.54 us -> 0.69 us
    ppermute x8 -> x10, starting transfers between devices: 14.7 us -> 27.2 us  [receive(): return lax.ppermute(shard, AXES, pairs)]
    ppermute x8 -> x10, waiting for transfers between devices: 48 us -> 36.1 us  [receive(): return lax.ppermute(shard, AXES, pairs)]
    pallas_call x4 -> x5, Pallas kernels: 39.4 us -> 49.6 us  [call(): pl.pallas_call(kernel, out_shape=out_shape, in_specs=in_specs, out_specs=...]
    unnamed x12 -> x4, local copies, waits for them, and re-layouts: 5.54 us -> 0.69 us
    ppermute x6, waiting for transfers between devices: 4.74 us -> 8.89 us  [fetch(): lax.ppermute(value, AXES, [(d, d ^ step) for d in range(lax.axis_size(AXE...]
  transfers between devices with their start and end apart: 14 -> 16, of which waited for: 7 -> 6; matrix products, arithmetic and copies ran while one was open for 0% -> 0% of each run, Pallas kernels for 28% -> 34%
where the time goes in v8:
time: 138 us; the launch traced here: 137 us
  Pallas kernels  49.6 us (36%)
  waiting for transfers between devices  45 us (33%)
  starting transfers between devices  38.7 us (28%)
  between operations  2.58 us (2%)
    pallas_call x5, Pallas kernels, call(): pl.pallas_call(kernel, out_shape=out_shape, in_specs=in_specs, out_specs=...  49.6 us
    ppermute x10, waiting for transfers between devices, receive(): return lax.ppermute(shard, AXES, pairs)  36.1 us
    ppermute x10, starting transfers between devices, receive(): return lax.ppermute(shard, AXES, pairs)  27.2 us
    ppermute x6, starting transfers between devices, fetch(): lax.ppermute(value, AXES, [(d, d ^ step) for d in range(lax.axis_size(AXE...  11.5 us
    ppermute x6, waiting for transfers between devices, fetch(): lax.ppermute(value, AXES, [(d, d ^ step) for d in range(lax.axis_size(AXE...  8.89 us
  transfers between devices with their start and end apart: 16, of which 6 were waited for; matrix products, arithmetic and copies ran while one was open for 0% of the time, Pallas kernels for 34%

profile of v8, /device:TPU:0, one launch (start us, length us, event | category | flops | bytes accessed | tf_op | source)
XLA Modules:
  0.0 137.2 jit_solution(16542229194472368163)
XLA Ops:
  0.6 3.4 %shard_map.42 = bf16[81,128,128]{2,1,0:T(8,128)(2,1)} custom-call(bf16[4,20,128,128]{3,2,1,0:T(8,128)(2,1)} %tiles.1, s32[4,20]{1,0:T(4,128)} %columns.3), custom_call_target="tpu_custom_call" | custom-call | bytes 10485760 | tf_op jit(solution)/shard_map/pallas_call | solution.py:357
  4.0 0.5 collective-permute-start.3
  4.5 2.6 %collective-permute-start = (bf16[81,128,128]{2,1,0:T(8,128)(2,1)}, bf16[81,128,128]{2,1,0:T(8,128)(2,1)S(1)}, u32[]{:S(2)}, u32[]{:S(2)}) collective-permute-start(bf16[81,128,128]{2,1,0:T(8,128)(2,1)} %shard_map.42), channel_id=1, source_target_pairs={{2,0},{3,1},{0,2},{1,3},{6,4},{7,5},{4,6},{5,7},{10,8},{11,9},{8,1... | collective-permute-start | bytes 7962632 | tf_op jit(solution)/shard_map/ppermute | solution.py:46
  7.1 4.3 %collective-permute-start.1 = (bf16[81,128,128]{2,1,0:T(8,128)(2,1)}, bf16[81,128,128]{2,1,0:T(8,128)(2,1)}, u32[]{:S(2)}, u32[]{:S(2)}) collective-permute-start(bf16[81,128,128]{2,1,0:T(8,128)(2,1)} %shard_map.42), channel_id=1, source_target_pairs={{29,0},{4,1},{31,2},{6,3},{1,4},{8,5},{3,6},{10,7},{5,8},{12,9},{7... | collective-permute-start | bytes 7962632 | tf_op jit(solution)/shard_map/ppermute | solution.py:46
  11.4 9.8 %shard_map.41 = (f32[4,20,128,128]{3,2,1,0:T(8,128)}, bf16[512,3712]{1,0:T(8,128)(2,1)}, bf16[256,512]{1,0:T(8,128)(2,1)}, s32[4,20]{1,0:T(4,128)}, f32[1,512]{1,0:T(1,128)}) custom-call(bf16[4,20,128,128]{3,2,1,0:T(8,128)(2,1)} %tiles.1, s32[4,20]{1,0:T(4,128)} %columns.3), custom_call_target="tpu_custom_call" | custom-call | flops 1879048192 | bytes 13107200 | tf_op jit(solution)/shard_map/pallas_call | solution.py:357
  21.2 1.3 collective-permute-start.2
  22.5 0.0 collective-permute-done.3.refs_0_
  22.5 0.0 copy-start
  22.5 11.5 %shard_map.43 = (f32[4,20,128,128]{3,2,1,0:T(8,128)}, f32[1,512]{1,0:T(1,128)}) custom-call(bf16[512,3712]{1,0:T(8,128)(2,1)} %get-tuple-element.26.left_in, s32[4,20]{1,0:T(4,128)} %get-tuple-element.27.positions, f32[4,20,128,128]{3,2,1,0:T(8,128)} %get-tuple-element.29.prev, f32[1,512]{1,0:T(1,128)} %get-tuple-element.30.trace_in, ...), custom_call_target="tpu_custom_call" | custom-call | flops 1879048192 | bytes 13107200 | tf_op jit(solution)/shard_map/pallas_call | solution.py:357
  34.0 0.0 collective-permute-done.2
  34.0 31.4 %collective-permute-done.refs_1_ = bf16[81,128,128]{2,1,0:T(8,128)(2,1)S(1)} collective-permute-done((bf16[81,128,128]{2,1,0:T(8,128)(2,1)}, bf16[81,128,128]{2,1,0:T(8,128)(2,1)S(1)}, u32[]{:S(2)}, u32[]{:S(2)}) %collective-permute-start) | collective-permute-done | bytes 2654240 | tf_op jit(solution)/shard_map/ppermute | solution.py:46
  65.5 0.0 collective-permute-done.1.refs_2_
  65.5 2.0 %collective-permute-start.5 = (bf16[81,128,128]{2,1,0:T(8,128)(2,1)S(1)}, bf16[81,128,128]{2,1,0:T(8,128)(2,1)S(1)}, u32[]{:S(2)}, u32[]{:S(2)}) collective-permute-start(bf16[81,128,128]{2,1,0:T(8,128)(2,1)S(1)} %collective-permute-done.refs_1_), channel_id=1, source_target_pairs={{1,0},{0,1},{3,2},{2,3},{5,4},{4,5},{7,6},{6,7},{9,8},{8,9},{11,10... | collective-permute-start | bytes 7962632 | tf_op jit(solution)/shard_map/ppermute | solution.py:46
  67.4 3.5 %collective-permute-start.6 = (bf16[81,128,128]{2,1,0:T(8,128)(2,1)S(1)}, bf16[81,128,128]{2,1,0:T(8,128)(2,1)S(1)}, u32[]{:S(2)}, u32[]{:S(2)}) collective-permute-start(bf16[81,128,128]{2,1,0:T(8,128)(2,1)S(1)} %collective-permute-done.refs_1_), channel_id=1, source_target_pairs={{28,1},{7,2},{0,5},{11,6},{4,9},{15,10},{8,13},{19,14},{12,17},{23... | collective-permute-start | bytes 7962632 | tf_op jit(solution)/shard_map/ppermute | solution.py:46
  71.0 1.3 collective-permute-start.7
  72.3 7.0 %collective-permute-start.4 = (bf16[256,512]{1,0:T(8,128)(2,1)S(1)}, bf16[256,512]{1,0:T(8,128)(2,1)S(1)}, u32[]{:S(2)}, u32[]{:S(2)}) collective-permute-start(bf16[256,512]{1,0:T(8,128)(2,1)S(1)} %collective-permute-done.2), channel_id=1, source_target_pairs={{31,1},{4,2},{3,5},{8,6},{7,9},{12,10},{11,13},{16,14},{15,17},{20... | collective-permute-start | bytes 786440 | tf_op jit(solution)/shard_map/ppermute | solution.py:46
  79.3 3.9 %collective-permute-done.4.refs_0_ = bf16[256,512]{1,0:T(8,128)(2,1)S(1)} collective-permute-done((bf16[256,512]{1,0:T(8,128)(2,1)S(1)}, bf16[256,512]{1,0:T(8,128)(2,1)S(1)}, u32[]{:S(2)}, u32[]{:S(2)}) %collective-permute-start.4) | collective-permute-done | bytes 262176 | tf_op jit(solution)/shard_map/ppermute | solution.py:46
  83.2 0.0 collective-permute-done.5.refs_3_
  83.2 0.0 copy-done
  83.2 0.0 copy-start.1
  83.2 0.7 copy-done.1
  83.9 15.7 %shard_map.44 = (f32[4,20,128,128]{3,2,1,0:T(8,128)}, f32[1,512]{1,0:T(1,128)S(1)}, bf16[512,1024]{1,0:T(8,128)(2,1)S(1)}) custom-call(bf16[512,3712]{1,0:T(8,128)(2,1)} %get-tuple-element.26.left_in, s32[4,20]{1,0:T(4,128)S(1)} %copy-done, f32[4,20,128,128]{3,2,1,0:T(8,128)} %get-tuple-element.33.prev, f32[1,512]{1,0:T(1,128)S(1)} %copy-done.1, ...), custom_call_target="tpu_custom_call" | custom-call | flops 5637144576 | bytes 18350080 | tf_op jit(solution)/shard_map/pallas_call | solution.py:357
  99.6 8.0 %collective-permute-start.8 = (f32[1,512]{1,0:T(1,128)S(1)}, f32[1,512]{1,0:T(1,128)S(1)}, u32[]{:S(2)}, u32[]{:S(2)}) collective-permute-start(f32[1,512]{1,0:T(1,128)S(1)} %get-tuple-element.40), channel_id=1, source_target_pairs={{0,1},{1,0},{2,3},{3,2},{4,5},{5,4},{6,7},{7,6},{8,9},{9,8},{10,11... | collective-permute-start | bytes 6152 | tf_op jit(solution)/shard_map/ppermute | solution.py:50
  107.6 0.8 collective-permute-done.8
  108.4 0.0 collective-permute-start.9
  108.4 3.6 %collective-permute-done.9 = f32[1,512]{1,0:T(1,128)S(1)} collective-permute-done((f32[1,512]{1,0:T(1,128)S(1)}, f32[1,512]{1,0:T(1,128)S(1)}, u32[]{:S(2)}, u32[]{:S(2)}) %collective-permute-start.9) | collective-permute-done | bytes 2080 | tf_op jit(solution)/shard_map/ppermute | solution.py:50
  112.0 0.0 collective-permute-start.10
  112.0 4.5 %collective-permute-done.10 = f32[1,512]{1,0:T(1,128)S(1)} collective-permute-done((f32[1,512]{1,0:T(1,128)S(1)}, f32[1,512]{1,0:T(1,128)S(1)}, u32[]{:S(2)}, u32[]{:S(2)}) %collective-permute-start.10) | collective-permute-done | bytes 2080 | tf_op jit(solution)/shard_map/ppermute | solution.py:50
  116.5 0.0 collective-permute-done.6.relay_x
  116.5 0.0 collective-permute-done.7.relay_y
  116.5 1.3 collective-permute-start.11
  117.8 3.4 %collective-permute-start.12 = (bf16[81,128,128]{2,1,0:T(8,128)(2,1)S(1)}, bf16[81,128,128]{2,1,0:T(8,128)(2,1)S(1)}, u32[]{:S(2)}, u32[]{:S(2)}) collective-permute-start(bf16[81,128,128]{2,1,0:T(8,128)(2,1)S(1)} %collective-permute-done.7.relay_y), channel_id=1, source_target_pairs={{0,1},{3,2},{4,5},{7,6},{8,9},{11,10},{12,13},{15,14},{16,17},{19,... | collective-permute-start | bytes 7962632 | tf_op jit(solution)/shard_map/ppermute | solution.py:46
  121.2 0.1 collective-permute-start.13
  121.3 0.1 collective-permute-start.14
  121.3 3.4 %collective-permute-start.15 = (f32[1,512]{1,0:T(1,128)S(1)}, f32[1,512]{1,0:T(1,128)S(1)}, u32[]{:S(2)}, u32[]{:S(2)}) collective-permute-start(f32[1,512]{1,0:T(1,128)S(1)} %add.20), channel_id=1, source_target_pairs={{0,6},{1,7},{2,4},{3,5},{4,2},{5,3},{6,0},{7,1},{8,14},{9,15},{10,... | collective-permute-start | bytes 6152 | tf_op jit(solution)/shard_map/ppermute | solution.py:50
  124.7 0.0 collective-permute-done.11.beside_x
  124.7 0.8 collective-permute-done.12.beside_y
  125.6 9.2 %shard_map.45 = bf16[4,20,128,128]{3,2,1,0:T(8,128)(2,1)} custom-call(bf16[512,1024]{1,0:T(8,128)(2,1)S(1)} %get-tuple-element.38.left_in, s32[4,20]{1,0:T(4,128)S(1)} %copy-done, f32[4,20,128,128]{3,2,1,0:T(8,128)} %get-tuple-element.41.prev, bf16[81,128,128]{2,1,0:T(8,128)(2,1)S(1)} %collective-permute-done.6.relay_x, ...), custom_call_target="tpu_custom_call" | custom-call | flops 3758096384 | bytes 15728640 | tf_op jit(solution)/shard_map/pallas_call | solution.py:357
  134.8 0.0 collective-permute-done.13
  134.8 0.0 collective-permute-done.14
  134.8 0.0 collective-permute-done.15
  134.8 0.6 add_reduce_fusion
  (3 shorter events, 0.0 us)
Async XLA Ops:
  4.0 18.5 %collective-permute-start.3 = (bf16[81,128,128]{2,1,0:T(8,128)(2,1)}, bf16[81,128,128]{2,1,0:T(8,128)(2,1)}, u32[]{:S(2)}, u32[]{:S(2)}) collective-permute-start(bf16[81,128,128]{2,1,0:T(8,128)(2,1)} %shard_map.42), channel_id=1, source_target_pairs={{1,0},{0,1},{3,2},{2,3},{5,4},{4,5},{7,6},{6,7},{9,8},{8,9},{11,10... | collective-permute-start | bytes 7962632 | tf_op jit(solution)/shard_map/ppermute | solution.py:46
  4.5 60.9 %collective-permute-start = (bf16[81,128,128]{2,1,0:T(8,128)(2,1)}, bf16[81,128,128]{2,1,0:T(8,128)(2,1)S(1)}, u32[]{:S(2)}, u32[]{:S(2)}) collective-permute-start(bf16[81,128,128]{2,1,0:T(8,128)(2,1)} %shard_map.42), channel_id=1, source_target_pairs={{2,0},{3,1},{0,2},{1,3},{6,4},{7,5},{4,6},{5,7},{10,8},{11,9},{8,1... | collective-permute-start | bytes 7962632 | tf_op jit(solution)/shard_map/ppermute | solution.py:46
  7.1 58.4 %collective-permute-start.1 = (bf16[81,128,128]{2,1,0:T(8,128)(2,1)}, bf16[81,128,128]{2,1,0:T(8,128)(2,1)}, u32[]{:S(2)}, u32[]{:S(2)}) collective-permute-start(bf16[81,128,128]{2,1,0:T(8,128)(2,1)} %shard_map.42), channel_id=1, source_target_pairs={{29,0},{4,1},{31,2},{6,3},{1,4},{8,5},{3,6},{10,7},{5,8},{12,9},{7... | collective-permute-start | bytes 7962632 | tf_op jit(solution)/shard_map/ppermute | solution.py:46
  21.2 12.8 %collective-permute-start.2 = (bf16[256,512]{1,0:T(8,128)(2,1)}, bf16[256,512]{1,0:T(8,128)(2,1)S(1)}, u32[]{:S(2)}, u32[]{:S(2)}) collective-permute-start(bf16[256,512]{1,0:T(8,128)(2,1)} %get-tuple-element.28), channel_id=1, source_target_pairs={{1,0},{2,3},{5,4},{6,7},{9,8},{10,11},{13,12},{14,15},{17,16},{18,... | collective-permute-start | bytes 786440 | tf_op jit(solution)/shard_map/ppermute | solution.py:46
  22.5 60.7 %copy-start = (s32[4,20]{1,0:T(4,128)S(1)}, s32[4,20]{1,0:T(4,128)}, u32[]{:S(2)}) copy-start(s32[4,20]{1,0:T(4,128)} %get-tuple-element.27.positions) | copy-start | bytes 964
  65.5 17.7 %collective-permute-start.5 = (bf16[81,128,128]{2,1,0:T(8,128)(2,1)S(1)}, bf16[81,128,128]{2,1,0:T(8,128)(2,1)S(1)}, u32[]{:S(2)}, u32[]{:S(2)}) collective-permute-start(bf16[81,128,128]{2,1,0:T(8,128)(2,1)S(1)} %collective-permute-done.refs_1_), channel_id=1, source_target_pairs={{1,0},{0,1},{3,2},{2,3},{5,4},{4,5},{7,6},{6,7},{9,8},{8,9},{11,10... | collective-permute-start | bytes 7962632 | tf_op jit(solution)/shard_map/ppermute | solution.py:46
  67.4 49.0 %collective-permute-start.6 = (bf16[81,128,128]{2,1,0:T(8,128)(2,1)S(1)}, bf16[81,128,128]{2,1,0:T(8,128)(2,1)S(1)}, u32[]{:S(2)}, u32[]{:S(2)}) collective-permute-start(bf16[81,128,128]{2,1,0:T(8,128)(2,1)S(1)} %collective-permute-done.refs_1_), channel_id=1, source_target_pairs={{28,1},{7,2},{0,5},{11,6},{4,9},{15,10},{8,13},{19,14},{12,17},{23... | collective-permute-start | bytes 7962632 | tf_op jit(solution)/shard_map/ppermute | solution.py:46
  71.0 45.5 %collective-permute-start.7 = (bf16[81,128,128]{2,1,0:T(8,128)(2,1)}, bf16[81,128,128]{2,1,0:T(8,128)(2,1)S(1)}, u32[]{:S(2)}, u32[]{:S(2)}) collective-permute-start(bf16[81,128,128]{2,1,0:T(8,128)(2,1)} %collective-permute-done.1.refs_2_), channel_id=1, source_target_pairs={{2,0},{1,3},{6,4},{5,7},{10,8},{9,11},{14,12},{13,15},{18,16},{17,... | collective-permute-start | bytes 7962632 | tf_op jit(solution)/shard_map/ppermute | solution.py:46
  72.3 10.9 %collective-permute-start.4 = (bf16[256,512]{1,0:T(8,128)(2,1)S(1)}, bf16[256,512]{1,0:T(8,128)(2,1)S(1)}, u32[]{:S(2)}, u32[]{:S(2)}) collective-permute-start(bf16[256,512]{1,0:T(8,128)(2,1)S(1)} %collective-permute-done.2), channel_id=1, source_target_pairs={{31,1},{4,2},{3,5},{8,6},{7,9},{12,10},{11,13},{16,14},{15,17},{20... | collective-permute-start | bytes 786440 | tf_op jit(solution)/shard_map/ppermute | solution.py:46
  83.2 0.7 copy-start.1
  99.6 8.8 %collective-permute-start.8 = (f32[1,512]{1,0:T(1,128)S(1)}, f32[1,512]{1,0:T(1,128)S(1)}, u32[]{:S(2)}, u32[]{:S(2)}) collective-permute-start(f32[1,512]{1,0:T(1,128)S(1)} %get-tuple-element.40), channel_id=1, source_target_pairs={{0,1},{1,0},{2,3},{3,2},{4,5},{5,4},{6,7},{7,6},{8,9},{9,8},{10,11... | collective-permute-start | bytes 6152 | tf_op jit(solution)/shard_map/ppermute | solution.py:50
  108.4 3.6 %collective-permute-start.9 = (f32[1,512]{1,0:T(1,128)S(1)}, f32[1,512]{1,0:T(1,128)S(1)}, u32[]{:S(2)}, u32[]{:S(2)}) collective-permute-start(f32[1,512]{1,0:T(1,128)S(1)} %add.18), channel_id=1, source_target_pairs={{0,8},{1,9},{2,10},{3,11},{4,12},{5,13},{6,14},{7,15},{8,0},{9,1},... | collective-permute-start | bytes 6152 | tf_op jit(solution)/shard_map/ppermute | solution.py:50
  112.0 4.5 %collective-permute-start.10 = (f32[1,512]{1,0:T(1,128)S(1)}, f32[1,512]{1,0:T(1,128)S(1)}, u32[]{:S(2)}, u32[]{:S(2)}) collective-permute-start(f32[1,512]{1,0:T(1,128)S(1)} %add.19), channel_id=1, source_target_pairs={{0,16},{1,17},{2,18},{3,19},{4,20},{5,21},{6,22},{7,23},{8,24},{9,... | collective-permute-start | bytes 6152 | tf_op jit(solution)/shard_map/ppermute | solution.py:50
  116.5 8.2 %collective-permute-start.11 = (bf16[81,128,128]{2,1,0:T(8,128)(2,1)S(1)}, bf16[81,128,128]{2,1,0:T(8,128)(2,1)S(1)}, u32[]{:S(2)}, u32[]{:S(2)}) collective-permute-start(bf16[81,128,128]{2,1,0:T(8,128)(2,1)S(1)} %collective-permute-done.6.relay_x), channel_id=1, source_target_pairs={{1,0},{2,3},{5,4},{6,7},{9,8},{10,11},{13,12},{14,15},{17,16},{18,... | collective-permute-start | bytes 7962632 | tf_op jit(solution)/shard_map/ppermute | solution.py:46
  117.8 7.8 %collective-permute-start.12 = (bf16[81,128,128]{2,1,0:T(8,128)(2,1)S(1)}, bf16[81,128,128]{2,1,0:T(8,128)(2,1)S(1)}, u32[]{:S(2)}, u32[]{:S(2)}) collective-permute-start(bf16[81,128,128]{2,1,0:T(8,128)(2,1)S(1)} %collective-permute-done.7.relay_y), channel_id=1, source_target_pairs={{0,1},{3,2},{4,5},{7,6},{8,9},{11,10},{12,13},{15,14},{16,17},{19,... | collective-permute-start | bytes 7962632 | tf_op jit(solution)/shard_map/ppermute | solution.py:46
  121.2 13.6 %collective-permute-start.13 = (f32[1,512]{1,0:T(1,128)S(1)}, f32[1,512]{1,0:T(1,128)S(1)}, u32[]{:S(2)}, u32[]{:S(2)}) collective-permute-start(f32[1,512]{1,0:T(1,128)S(1)} %add.20), channel_id=1, source_target_pairs={{0,2},{1,3},{2,0},{3,1},{4,6},{5,7},{6,4},{7,5},{8,10},{9,11},{10,... | collective-permute-start | bytes 6152 | tf_op jit(solution)/shard_map/ppermute | solution.py:50
  121.3 13.6 %collective-permute-start.14 = (f32[1,512]{1,0:T(1,128)S(1)}, f32[1,512]{1,0:T(1,128)S(1)}, u32[]{:S(2)}, u32[]{:S(2)}) collective-permute-start(f32[1,512]{1,0:T(1,128)S(1)} %add.20), channel_id=1, source_target_pairs={{0,4},{1,5},{2,6},{3,7},{4,0},{5,1},{6,2},{7,3},{8,12},{9,13},{10,... | collective-permute-start | bytes 6152 | tf_op jit(solution)/shard_map/ppermute | solution.py:50
  121.3 13.5 %collective-permute-start.15 = (f32[1,512]{1,0:T(1,128)S(1)}, f32[1,512]{1,0:T(1,128)S(1)}, u32[]{:S(2)}, u32[]{:S(2)}) collective-permute-start(f32[1,512]{1,0:T(1,128)S(1)} %add.20), channel_id=1, source_target_pairs={{0,6},{1,7},{2,4},{3,5},{4,2},{5,3},{6,0},{7,1},{8,14},{9,15},{10,... | collective-permute-start | bytes 6152 | tf_op jit(solution)/shard_map/ppermute | solution.py:50

commit v9 on v8

--- a/solution.py
+++ b/solution.py
@@ -50,8 +50,11 @@
     return lax.ppermute(value, AXES, [(d, d ^ step) for d in range(lax.axis_size(AXES))])
 
 
-def exchange(value, step):
-    return value + fetch(value, step)
+def round_of(value, steps):
+    if len(steps) == 1:
+        return value + fetch(value, steps[0])
+    one, other = steps
+    return (value + fetch(value, one)) + (fetch(value, other) + fetch(value, one + other))
 
 
 def pick(table, kind):
@@ -92,7 +95,7 @@
             column = pl.ds(aligned(place(r, u), z.block), z.block)
             dense[top + r * z.block:top + (r + 1) * z.block, column] = source[r * z.slots + u]
             return carry
-        lax.fori_loop(0, z.slots, one, 0, unroll=4)
+        lax.fori_loop(0, z.slots, one, 0, unroll=10)
 
 
 def decode(z, offsets, spot, vector, scalars, sem):
@@ -142,7 +145,7 @@
                 value = value + prev[r, s]
             stage[r, s] = value.astype(stage.dtype)
             return carry
-        lax.fori_loop(0, z.slots, one, 0, unroll=4)
+        lax.fori_loop(0, z.slots, one, 0, unroll=10)
         pltpu.make_async_copy(stage.at[r], out.at[r], sems.at[r]).start()
     for r in range(z.rows):
         pltpu.make_async_copy(stage.at[r], out.at[r], sems.at[r]).wait()
@@ -171,7 +174,7 @@
             positions[r, u] = column
             left[r * z.block:(r + 1) * z.block, pl.ds(aligned(column, z.block), z.block)] = stage[r, u]
             return carry
-        lax.fori_loop(0, z.slots, place, 0, unroll=4)
+        lax.fori_loop(0, z.slots, place, 0, unroll=10)
     left_copy = pltpu.make_async_copy(left, left_out, left_sem)
     left_copy.start()
     half = z.span // 2
@@ -204,7 +207,6 @@
 def near_body(z, names, final, left_in, positions, prev, trace_in, *refs):
     refs = list(refs)
     take = lambda count: [refs.pop(0) for _ in range(count)]
-    corner = take(1)[0] if final else None
     sources = take(len(names))
     out, trace = take(2)
     relay_left = take(1)[0] if final else None
@@ -278,17 +280,31 @@
         pl.when(weight != 0)(lambda: add_trace(
             trace, weight, dense_of[one][:, chunk(place[other])], dense_of[other][:, chunk(place[one])]
         ))
-    if final:
-        half = z.span // 2
-        end = (z.chunks - 1) * z.span
-        pl.when(kind == UPPER)(lambda: add_trace(trace, jnp.float32(2), left[:, half:z.span], corner[...]))
-        pl.when(kind == LOWER)(
-            lambda: add_trace(trace, jnp.float32(2), left[:half, end:end + half], corner[:, :half])
-        )
     prev_copy.wait()
     emit(z, total, positions, sums, out, out_sems, sums)
     for copy in relay_copies:
         copy.wait()
+
+
+def corner_body(z, left, corner, trace_in, trace, rows, sem):
+    kind = lax.axis_index(AXES) % 4
+    half = z.span // 2
+    end = (z.chunks - 1) * z.span
+    trace[...] = trace_in[...]
+
+    @pl.when(kind == UPPER)
+    def _():
+        copy = pltpu.make_async_copy(left.at[:, pl.ds(half, half)], rows, sem)
+        copy.start()
+        copy.wait()
+        add_trace(trace, jnp.float32(2), rows[...], corner[...])
+
+    @pl.when(kind == LOWER)
+    def _():
+        copy = pltpu.make_async_copy(left.at[pl.ds(0, half), pl.ds(end, half)], rows.at[pl.ds(0, half)], sem)
+        copy.start()
+        copy.wait()
+        add_trace(trace, jnp.float32(2), rows[:half], corner[:, :half])
 
 
 def last_body(z, left_in, positions, prev, relay_x, relay_y, beside_x, beside_y, out, left, stage, right, total, out_stage,
@@ -411,13 +427,12 @@
     )
     corner = receive(corner, PARTNER, (0, 3))
 
-    def near(names, arrays, total, trace, corner=None):
-        final = corner is not None
+    def near(names, arrays, total, trace, final=False):
         extra = [shape((z.span, 2 * z.span), dtype)] * final
         return call(
             z, functools.partial(near_body, z, names, final),
-            [left, positions, total, trace] + [corner] * final + arrays,
-            [ANY, SMEM, ANY, VMEM] + [VMEM] * final + [ANY] * len(arrays),
+            [left, positions, total, trace] + arrays,
+            [ANY, SMEM, ANY, VMEM] + [ANY] * len(arrays),
             [sums, line] + extra,
             [ANY, VMEM] + [ANY] * final,
             [
@@ -436,12 +451,17 @@
     x_beside = receive(over_x, PARTNER)
     corner = receive(corner, (0, -2, 2, 0), (LOWER, UPPER))
     total, trace, relay_left = near(
-        ("x", "y", "x_beside"), [over_x, over_y, x_beside], total, trace, corner
+        ("x", "y", "x_beside"), [over_x, over_y, x_beside], total, trace, True
+    )
+    trace = call(
+        z, functools.partial(corner_body, z), [left, corner, trace], [ANY, VMEM, VMEM], line, VMEM,
+        [pltpu.VMEM((z.span, z.span // 2), dtype), DMA], 0,
     )
     assert devices & (devices - 1) == 0
     steps = [1 << bit for bit in range(devices.bit_length() - 1)]
-    for step in steps[:1] + steps[3:]:
-        trace = exchange(trace, step)
+    trace = trace + fetch(trace, steps[0])
+    for index in range(3, len(steps), 2):
+        trace = round_of(trace, steps[index:index + 2])
     relay_x, relay_y, total, trace = lax.optimization_barrier((relay_x, relay_y, total, trace))
     beside_x = receive(relay_x, PARTNER, RELAY_Y)
     beside_y = receive(relay_y, PARTNER, RELAY_X)

time: 138 us -> 129 us (0.935)
  starting transfers between devices: 38.7 us -> 34.5 us
  waiting for transfers between devices: 45 us -> 40.9 us
    ppermute x6 -> x7, waiting for transfers between devices: 8.89 us -> 3.83 us  [fetch(): lax.ppermute(value, AXES, [(d, d ^ step) for d in range(lax.axis_size(AXE...]
    ppermute x6 -> x7, starting transfers between devices: 11.5 us -> 7.11 us  [fetch(): lax.ppermute(value, AXES, [(d, d ^ step) for d in range(lax.axis_size(AXE...]
    pallas_call x5 -> x6, Pallas kernels: 49.6 us -> 49.1 us  [call(): pl.pallas_call(kernel, out_shape=out_shape, in_specs=in_specs, out_specs=...]
  transfers between devices with their start and end apart: 16 -> 17, of which waited for: 6 -> 6; matrix products, arithmetic and copies ran while one was open for 0% -> 0% of each run, Pallas kernels for 34% -> 36%
where the time goes in v9:
time: 129 us; the launch traced here: 128 us
  Pallas kernels  49.1 us (38%)
  waiting for transfers between devices  40.9 us (32%)
  starting transfers between devices  34.5 us (27%)
  between operations  2.61 us (2%)
    pallas_call x6, Pallas kernels, call(): pl.pallas_call(kernel, out_shape=out_shape, in_specs=in_specs, out_specs=...  49.1 us
    ppermute x10, waiting for transfers between devices, receive(): return lax.ppermute(shard, AXES, pairs)  37.1 us
    ppermute x10, starting transfers between devices, receive(): return lax.ppermute(shard, AXES, pairs)  27.4 us
    ppermute x7, starting transfers between devices, fetch(): lax.ppermute(value, AXES, [(d, d ^ step) for d in range(lax.axis_size(AXE...  7.11 us
    ppermute x7, waiting for transfers between devices, fetch(): lax.ppermute(value, AXES, [(d, d ^ step) for d in range(lax.axis_size(AXE...  3.83 us
  transfers between devices with their start and end apart: 17, of which 6 were waited for; matrix products, arithmetic and copies ran while one was open for 0% of the time, Pallas kernels for 36%

profile of v9, /device:TPU:0, one launch (start us, length us, event | category | flops | bytes accessed | tf_op | source)
XLA Modules:
  0.0 128.5 jit_solution(9892545381134060239)
XLA Ops:
  0.6 3.4 %shard_map.42 = bf16[81,128,128]{2,1,0:T(8,128)(2,1)} custom-call(bf16[4,20,128,128]{3,2,1,0:T(8,128)(2,1)} %tiles.1, s32[4,20]{1,0:T(4,128)} %columns.3), custom_call_target="tpu_custom_call" | custom-call | bytes 10485760 | tf_op jit(solution)/shard_map/pallas_call | solution.py:373
  4.0 0.5 collective-permute-start.3
  4.5 2.6 %collective-permute-start = (bf16[81,128,128]{2,1,0:T(8,128)(2,1)}, bf16[81,128,128]{2,1,0:T(8,128)(2,1)S(1)}, u32[]{:S(2)}, u32[]{:S(2)}) collective-permute-start(bf16[81,128,128]{2,1,0:T(8,128)(2,1)} %shard_map.42), channel_id=1, source_target_pairs={{2,0},{3,1},{0,2},{1,3},{6,4},{7,5},{4,6},{5,7},{10,8},{11,9},{8,1... | collective-permute-start | bytes 7962632 | tf_op jit(solution)/shard_map/ppermute | solution.py:46
  7.1 4.3 %collective-permute-start.1 = (bf16[81,128,128]{2,1,0:T(8,128)(2,1)}, bf16[81,128,128]{2,1,0:T(8,128)(2,1)}, u32[]{:S(2)}, u32[]{:S(2)}) collective-permute-start(bf16[81,128,128]{2,1,0:T(8,128)(2,1)} %shard_map.42), channel_id=1, source_target_pairs={{29,0},{4,1},{31,2},{6,3},{1,4},{8,5},{3,6},{10,7},{5,8},{12,9},{7... | collective-permute-start | bytes 7962632 | tf_op jit(solution)/shard_map/ppermute | solution.py:46
  11.4 9.7 %shard_map.41 = (f32[4,20,128,128]{3,2,1,0:T(8,128)}, bf16[512,3712]{1,0:T(8,128)(2,1)}, bf16[256,512]{1,0:T(8,128)(2,1)}, s32[4,20]{1,0:T(4,128)}, f32[1,512]{1,0:T(1,128)}) custom-call(bf16[4,20,128,128]{3,2,1,0:T(8,128)(2,1)} %tiles.1, s32[4,20]{1,0:T(4,128)} %columns.3), custom_call_target="tpu_custom_call" | custom-call | flops 1879048192 | bytes 13107200 | tf_op jit(solution)/shard_map/pallas_call | solution.py:373
  21.1 1.3 %collective-permute-start.2 = (bf16[256,512]{1,0:T(8,128)(2,1)}, bf16[256,512]{1,0:T(8,128)(2,1)S(1)}, u32[]{:S(2)}, u32[]{:S(2)}) collective-permute-start(bf16[256,512]{1,0:T(8,128)(2,1)} %get-tuple-element.28), channel_id=1, source_target_pairs={{1,0},{2,3},{5,4},{6,7},{9,8},{10,11},{13,12},{14,15},{17,16},{18,... | collective-permute-start | bytes 786440 | tf_op jit(solution)/shard_map/ppermute | solution.py:46
  22.4 0.0 collective-permute-done.3.refs_0_
  22.4 0.0 copy-start.1
  22.4 11.4 %shard_map.43 = (f32[4,20,128,128]{3,2,1,0:T(8,128)}, f32[1,512]{1,0:T(1,128)}) custom-call(bf16[512,3712]{1,0:T(8,128)(2,1)} %get-tuple-element.26.left_in.left, s32[4,20]{1,0:T(4,128)} %get-tuple-element.27.positions, f32[4,20,128,128]{3,2,1,0:T(8,128)} %get-tuple-element.29.prev, f32[1,512]{1,0:T(1,128)} %get-tuple-element.30.trace_in, ...), custom_call_target="tpu_custom_call" | custom-call | flops 1879048192 | bytes 13107200 | tf_op jit(solution)/shard_map/pallas_call | solution.py:373
  33.8 0.0 collective-permute-done.2
  33.9 31.6 %collective-permute-done.refs_0_ = bf16[81,128,128]{2,1,0:T(8,128)(2,1)S(1)} collective-permute-done((bf16[81,128,128]{2,1,0:T(8,128)(2,1)}, bf16[81,128,128]{2,1,0:T(8,128)(2,1)S(1)}, u32[]{:S(2)}, u32[]{:S(2)}) %collective-permute-start) | collective-permute-done | bytes 2654240 | tf_op jit(solution)/shard_map/ppermute | solution.py:46
  65.5 0.0 collective-permute-done.1.refs_1_
  65.5 0.0 copy-start
  65.5 2.0 %collective-permute-start.4 = (bf16[81,128,128]{2,1,0:T(8,128)(2,1)S(1)}, bf16[81,128,128]{2,1,0:T(8,128)(2,1)S(1)}, u32[]{:S(2)}, u32[]{:S(2)}) collective-permute-start(bf16[81,128,128]{2,1,0:T(8,128)(2,1)S(1)} %collective-permute-done.refs_0_), channel_id=1, source_target_pairs={{1,0},{0,1},{3,2},{2,3},{5,4},{4,5},{7,6},{6,7},{9,8},{8,9},{11,10... | collective-permute-start | bytes 7962632 | tf_op jit(solution)/shard_map/ppermute | solution.py:46
  67.5 3.5 %collective-permute-start.5 = (bf16[81,128,128]{2,1,0:T(8,128)(2,1)S(1)}, bf16[81,128,128]{2,1,0:T(8,128)(2,1)S(1)}, u32[]{:S(2)}, u32[]{:S(2)}) collective-permute-start(bf16[81,128,128]{2,1,0:T(8,128)(2,1)S(1)} %collective-permute-done.refs_0_), channel_id=1, source_target_pairs={{28,1},{7,2},{0,5},{11,6},{4,9},{15,10},{8,13},{19,14},{12,17},{23... | collective-permute-start | bytes 7962632 | tf_op jit(solution)/shard_map/ppermute | solution.py:46
  71.0 1.3 %collective-permute-start.6 = (bf16[81,128,128]{2,1,0:T(8,128)(2,1)}, bf16[81,128,128]{2,1,0:T(8,128)(2,1)S(1)}, u32[]{:S(2)}, u32[]{:S(2)}) collective-permute-start(bf16[81,128,128]{2,1,0:T(8,128)(2,1)} %collective-permute-done.1.refs_1_), channel_id=1, source_target_pairs={{2,0},{1,3},{6,4},{5,7},{10,8},{9,11},{14,12},{13,15},{18,16},{17,... | collective-permute-start | bytes 7962632 | tf_op jit(solution)/shard_map/ppermute | solution.py:46
  72.3 7.3 %collective-permute-start.7 = (bf16[256,512]{1,0:T(8,128)(2,1)S(1)}, bf16[256,512]{1,0:T(8,128)(2,1)S(1)}, u32[]{:S(2)}, u32[]{:S(2)}) collective-permute-start(bf16[256,512]{1,0:T(8,128)(2,1)S(1)} %collective-permute-done.2), channel_id=1, source_target_pairs={{31,1},{4,2},{3,5},{8,6},{7,9},{12,10},{11,13},{16,14},{15,17},{20... | collective-permute-start | bytes 786440 | tf_op jit(solution)/shard_map/ppermute | solution.py:46
  79.6 0.0 collective-permute-done.4.refs_2_
  79.6 0.0 copy-done.1
  79.6 0.0 copy-start.2
  79.6 0.7 copy-done.2
  80.3 15.5 %shard_map.44 = (f32[4,20,128,128]{3,2,1,0:T(8,128)}, f32[1,512]{1,0:T(1,128)S(1)}, bf16[512,1024]{1,0:T(8,128)(2,1)S(1)}) custom-call(bf16[512,3712]{1,0:T(8,128)(2,1)} %get-tuple-element.26.left_in.left, s32[4,20]{1,0:T(4,128)S(1)} %copy-done.1, f32[4,20,128,128]{3,2,1,0:T(8,128)} %get-tuple-element.33.prev, f32[1,512]{1,0:T(1,128)S(1)} %copy-done.2, ...), custom_call_target="tpu_custom_call" | custom-call | flops 5637144576 | bytes 18350080 | tf_op jit(solution)/shard_map/pallas_call | solution.py:373
  95.8 0.0 collective-permute-done.7.corner
  95.8 0.0 copy-done
  95.9 0.1 collective-permute-start.8
  95.9 1.1 collective-permute-done.8
  97.1 0.8 collective-permute-start.10
  97.9 1.3 %collective-permute-start.11 = (f32[1,512]{1,0:T(1,128)S(1)}, f32[1,512]{1,0:T(1,128)S(1)}, u32[]{:S(2)}, u32[]{:S(2)}) collective-permute-start(f32[1,512]{1,0:T(1,128)S(1)} %add.21), channel_id=1, source_target_pairs={{0,24},{1,25},{2,26},{3,27},{4,28},{5,29},{6,30},{7,31},{8,16},{9,... | collective-permute-start | bytes 6152 | tf_op jit(solution)/shard_map/ppermute | solution.py:50
  99.2 1.4 %collective-permute-start.9 = (f32[1,512]{1,0:T(1,128)S(1)}, f32[1,512]{1,0:T(1,128)S(1)}, u32[]{:S(2)}, u32[]{:S(2)}) collective-permute-start(f32[1,512]{1,0:T(1,128)S(1)} %add.21), channel_id=1, source_target_pairs={{0,8},{1,9},{2,10},{3,11},{4,12},{5,13},{6,14},{7,15},{8,0},{9,1},... | collective-permute-start | bytes 6152 | tf_op jit(solution)/shard_map/ppermute | solution.py:50
  100.6 1.0 collective-permute-done.10
  101.6 1.7 %collective-permute-done.11 = f32[1,512]{1,0:T(1,128)S(1)} collective-permute-done((f32[1,512]{1,0:T(1,128)S(1)}, f32[1,512]{1,0:T(1,128)S(1)}, u32[]{:S(2)}, u32[]{:S(2)}) %collective-permute-start.11) | collective-permute-done | bytes 2080 | tf_op jit(solution)/shard_map/ppermute | solution.py:50
  103.3 0.0 collective-permute-done.9
  103.3 0.0 collective-permute-done.5.relay_x
  103.3 4.6 %collective-permute-done.6.relay_y = bf16[81,128,128]{2,1,0:T(8,128)(2,1)S(1)} collective-permute-done((bf16[81,128,128]{2,1,0:T(8,128)(2,1)}, bf16[81,128,128]{2,1,0:T(8,128)(2,1)S(1)}, u32[]{:S(2)}, u32[]{:S(2)}) %collective-permute-start.6) | collective-permute-done | bytes 2654240 | tf_op jit(solution)/shard_map/ppermute | solution.py:46
  107.9 1.3 collective-permute-start.12
  109.2 3.4 %collective-permute-start.13 = (bf16[81,128,128]{2,1,0:T(8,128)(2,1)S(1)}, bf16[81,128,128]{2,1,0:T(8,128)(2,1)S(1)}, u32[]{:S(2)}, u32[]{:S(2)}) collective-permute-start(bf16[81,128,128]{2,1,0:T(8,128)(2,1)S(1)} %collective-permute-done.6.relay_y), channel_id=1, source_target_pairs={{0,1},{3,2},{4,5},{7,6},{8,9},{11,10},{12,13},{15,14},{16,17},{19,... | collective-permute-start | bytes 7962632 | tf_op jit(solution)/shard_map/ppermute | solution.py:46
  112.6 1.5 %collective-permute-start.14 = (f32[1,512]{1,0:T(1,128)S(1)}, f32[1,512]{1,0:T(1,128)S(1)}, u32[]{:S(2)}, u32[]{:S(2)}) collective-permute-start(f32[1,512]{1,0:T(1,128)S(1)} %add_add_fusion), channel_id=1, source_target_pairs={{0,2},{1,3},{2,0},{3,1},{4,6},{5,7},{6,4},{7,5},{8,10},{9,11},{10,... | collective-permute-start | bytes 6152 | tf_op jit(solution)/shard_map/ppermute | solution.py:50
  114.0 0.1 collective-permute-start.15
  114.2 2.0 %collective-permute-start.16 = (f32[1,512]{1,0:T(1,128)S(1)}, f32[1,512]{1,0:T(1,128)S(1)}, u32[]{:S(2)}, u32[]{:S(2)}) collective-permute-start(f32[1,512]{1,0:T(1,128)S(1)} %add_add_fusion), channel_id=1, source_target_pairs={{0,6},{1,7},{2,4},{3,5},{4,2},{5,3},{6,0},{7,1},{8,14},{9,15},{10,... | collective-permute-start | bytes 6152 | tf_op jit(solution)/shard_map/ppermute | solution.py:50
  116.1 0.0 collective-permute-done.12.beside_x
  116.1 0.8 collective-permute-done.13.beside_y
  117.0 9.1 %shard_map.46 = bf16[4,20,128,128]{3,2,1,0:T(8,128)(2,1)} custom-call(bf16[512,1024]{1,0:T(8,128)(2,1)S(1)} %get-tuple-element.37.left_in, s32[4,20]{1,0:T(4,128)S(1)} %copy-done.1, f32[4,20,128,128]{3,2,1,0:T(8,128)} %get-tuple-element.41.prev, bf16[81,128,128]{2,1,0:T(8,128)(2,1)S(1)} %collective-permute-done.5.relay_x, ...), custom_call_target="tpu_custom_call" | custom-call | flops 3758096384 | bytes 15728640 | tf_op jit(solution)/shard_map/pallas_call | solution.py:373
  126.0 0.0 collective-permute-done.14
  126.1 0.0 collective-permute-done.15
  126.1 0.0 collective-permute-done.16
  126.1 0.6 add_reduce_fusion
  (3 shorter events, 0.0 us)
Async XLA Ops:
  4.0 18.4 %collective-permute-start.3 = (bf16[81,128,128]{2,1,0:T(8,128)(2,1)}, bf16[81,128,128]{2,1,0:T(8,128)(2,1)}, u32[]{:S(2)}, u32[]{:S(2)}) collective-permute-start(bf16[81,128,128]{2,1,0:T(8,128)(2,1)} %shard_map.42), channel_id=1, source_target_pairs={{1,0},{0,1},{3,2},{2,3},{5,4},{4,5},{7,6},{6,7},{9,8},{8,9},{11,10... | collective-permute-start | bytes 7962632 | tf_op jit(solution)/shard_map/ppermute | solution.py:46
  4.5 60.9 %collective-permute-start = (bf16[81,128,128]{2,1,0:T(8,128)(2,1)}, bf16[81,128,128]{2,1,0:T(8,128)(2,1)S(1)}, u32[]{:S(2)}, u32[]{:S(2)}) collective-permute-start(bf16[81,128,128]{2,1,0:T(8,128)(2,1)} %shard_map.42), channel_id=1, source_target_pairs={{2,0},{3,1},{0,2},{1,3},{6,4},{7,5},{4,6},{5,7},{10,8},{11,9},{8,1... | collective-permute-start | bytes 7962632 | tf_op jit(solution)/shard_map/ppermute | solution.py:46
  7.1 58.4 %collective-permute-start.1 = (bf16[81,128,128]{2,1,0:T(8,128)(2,1)}, bf16[81,128,128]{2,1,0:T(8,128)(2,1)}, u32[]{:S(2)}, u32[]{:S(2)}) collective-permute-start(bf16[81,128,128]{2,1,0:T(8,128)(2,1)} %shard_map.42), channel_id=1, source_target_pairs={{29,0},{4,1},{31,2},{6,3},{1,4},{8,5},{3,6},{10,7},{5,8},{12,9},{7... | collective-permute-start | bytes 7962632 | tf_op jit(solution)/shard_map/ppermute | solution.py:46
  21.1 12.7 %collective-permute-start.2 = (bf16[256,512]{1,0:T(8,128)(2,1)}, bf16[256,512]{1,0:T(8,128)(2,1)S(1)}, u32[]{:S(2)}, u32[]{:S(2)}) collective-permute-start(bf16[256,512]{1,0:T(8,128)(2,1)} %get-tuple-element.28), channel_id=1, source_target_pairs={{1,0},{2,3},{5,4},{6,7},{9,8},{10,11},{13,12},{14,15},{17,16},{18,... | collective-permute-start | bytes 786440 | tf_op jit(solution)/shard_map/ppermute | solution.py:46
  22.4 57.2 %copy-start.1 = (s32[4,20]{1,0:T(4,128)S(1)}, s32[4,20]{1,0:T(4,128)}, u32[]{:S(2)}) copy-start(s32[4,20]{1,0:T(4,128)} %get-tuple-element.27.positions) | copy-start | bytes 964
  65.5 30.3 %copy-start = (bf16[512,3712]{1,0:T(8,128)(2,1)S(1)}, bf16[512,3712]{1,0:T(8,128)(2,1)}, u32[]{:S(2)}) copy-start(bf16[512,3712]{1,0:T(8,128)(2,1)} %get-tuple-element.26.left_in.left) | copy-start | bytes 11403268
  65.5 14.1 %collective-permute-start.4 = (bf16[81,128,128]{2,1,0:T(8,128)(2,1)S(1)}, bf16[81,128,128]{2,1,0:T(8,128)(2,1)S(1)}, u32[]{:S(2)}, u32[]{:S(2)}) collective-permute-start(bf16[81,128,128]{2,1,0:T(8,128)(2,1)S(1)} %collective-permute-done.refs_0_), channel_id=1, source_target_pairs={{1,0},{0,1},{3,2},{2,3},{5,4},{4,5},{7,6},{6,7},{9,8},{8,9},{11,10... | collective-permute-start | bytes 7962632 | tf_op jit(solution)/shard_map/ppermute | solution.py:46
  67.5 35.8 %collective-permute-start.5 = (bf16[81,128,128]{2,1,0:T(8,128)(2,1)S(1)}, bf16[81,128,128]{2,1,0:T(8,128)(2,1)S(1)}, u32[]{:S(2)}, u32[]{:S(2)}) collective-permute-start(bf16[81,128,128]{2,1,0:T(8,128)(2,1)S(1)} %collective-permute-done.refs_0_), channel_id=1, source_target_pairs={{28,1},{7,2},{0,5},{11,6},{4,9},{15,10},{8,13},{19,14},{12,17},{23... | collective-permute-start | bytes 7962632 | tf_op jit(solution)/shard_map/ppermute | solution.py:46
  71.0 36.9 %collective-permute-start.6 = (bf16[81,128,128]{2,1,0:T(8,128)(2,1)}, bf16[81,128,128]{2,1,0:T(8,128)(2,1)S(1)}, u32[]{:S(2)}, u32[]{:S(2)}) collective-permute-start(bf16[81,128,128]{2,1,0:T(8,128)(2,1)} %collective-permute-done.1.refs_1_), channel_id=1, source_target_pairs={{2,0},{1,3},{6,4},{5,7},{10,8},{9,11},{14,12},{13,15},{18,16},{17,... | collective-permute-start | bytes 7962632 | tf_op jit(solution)/shard_map/ppermute | solution.py:46
  72.3 23.5 %collective-permute-start.7 = (bf16[256,512]{1,0:T(8,128)(2,1)S(1)}, bf16[256,512]{1,0:T(8,128)(2,1)S(1)}, u32[]{:S(2)}, u32[]{:S(2)}) collective-permute-start(bf16[256,512]{1,0:T(8,128)(2,1)S(1)} %collective-permute-done.2), channel_id=1, source_target_pairs={{31,1},{4,2},{3,5},{8,6},{7,9},{12,10},{11,13},{16,14},{15,17},{20... | collective-permute-start | bytes 786440 | tf_op jit(solution)/shard_map/ppermute | solution.py:46
  79.6 0.7 copy-start.2
  95.9 1.2 collective-permute-start.8
  97.1 4.5 %collective-permute-start.10 = (f32[1,512]{1,0:T(1,128)S(1)}, f32[1,512]{1,0:T(1,128)S(1)}, u32[]{:S(2)}, u32[]{:S(2)}) collective-permute-start(f32[1,512]{1,0:T(1,128)S(1)} %add.21), channel_id=1, source_target_pairs={{0,16},{1,17},{2,18},{3,19},{4,20},{5,21},{6,22},{7,23},{8,24},{9,... | collective-permute-start | bytes 6152 | tf_op jit(solution)/shard_map/ppermute | solution.py:50
  97.9 5.4 %collective-permute-start.11 = (f32[1,512]{1,0:T(1,128)S(1)}, f32[1,512]{1,0:T(1,128)S(1)}, u32[]{:S(2)}, u32[]{:S(2)}) collective-permute-start(f32[1,512]{1,0:T(1,128)S(1)} %add.21), channel_id=1, source_target_pairs={{0,24},{1,25},{2,26},{3,27},{4,28},{5,29},{6,30},{7,31},{8,16},{9,... | collective-permute-start | bytes 6152 | tf_op jit(solution)/shard_map/ppermute | solution.py:50
  99.2 4.0 %collective-permute-start.9 = (f32[1,512]{1,0:T(1,128)S(1)}, f32[1,512]{1,0:T(1,128)S(1)}, u32[]{:S(2)}, u32[]{:S(2)}) collective-permute-start(f32[1,512]{1,0:T(1,128)S(1)} %add.21), channel_id=1, source_target_pairs={{0,8},{1,9},{2,10},{3,11},{4,12},{5,13},{6,14},{7,15},{8,0},{9,1},... | collective-permute-start | bytes 6152 | tf_op jit(solution)/shard_map/ppermute | solution.py:50
  107.9 8.2 %collective-permute-start.12 = (bf16[81,128,128]{2,1,0:T(8,128)(2,1)S(1)}, bf16[81,128,128]{2,1,0:T(8,128)(2,1)S(1)}, u32[]{:S(2)}, u32[]{:S(2)}) collective-permute-start(bf16[81,128,128]{2,1,0:T(8,128)(2,1)S(1)} %collective-permute-done.5.relay_x), channel_id=1, source_target_pairs={{1,0},{2,3},{5,4},{6,7},{9,8},{10,11},{13,12},{14,15},{17,16},{18,... | collective-permute-start | bytes 7962632 | tf_op jit(solution)/shard_map/ppermute | solution.py:46
  109.2 7.8 %collective-permute-start.13 = (bf16[81,128,128]{2,1,0:T(8,128)(2,1)S(1)}, bf16[81,128,128]{2,1,0:T(8,128)(2,1)S(1)}, u32[]{:S(2)}, u32[]{:S(2)}) collective-permute-start(bf16[81,128,128]{2,1,0:T(8,128)(2,1)S(1)} %collective-permute-done.6.relay_y), channel_id=1, source_target_pairs={{0,1},{3,2},{4,5},{7,6},{8,9},{11,10},{12,13},{15,14},{16,17},{19,... | collective-permute-start | bytes 7962632 | tf_op jit(solution)/shard_map/ppermute | solution.py:46
  112.6 13.5 %collective-permute-start.14 = (f32[1,512]{1,0:T(1,128)S(1)}, f32[1,512]{1,0:T(1,128)S(1)}, u32[]{:S(2)}, u32[]{:S(2)}) collective-permute-start(f32[1,512]{1,0:T(1,128)S(1)} %add_add_fusion), channel_id=1, source_target_pairs={{0,2},{1,3},{2,0},{3,1},{4,6},{5,7},{6,4},{7,5},{8,10},{9,11},{10,... | collective-permute-start | bytes 6152 | tf_op jit(solution)/shard_map/ppermute | solution.py:50
  114.0 12.0 %collective-permute-start.15 = (f32[1,512]{1,0:T(1,128)S(1)}, f32[1,512]{1,0:T(1,128)S(1)}, u32[]{:S(2)}, u32[]{:S(2)}) collective-permute-start(f32[1,512]{1,0:T(1,128)S(1)} %add_add_fusion), channel_id=1, source_target_pairs={{0,4},{1,5},{2,6},{3,7},{4,0},{5,1},{6,2},{7,3},{8,12},{9,13},{10,... | collective-permute-start | bytes 6152 | tf_op jit(solution)/shard_map/ppermute | solution.py:50
  114.2 11.9 %collective-permute-start.16 = (f32[1,512]{1,0:T(1,128)S(1)}, f32[1,512]{1,0:T(1,128)S(1)}, u32[]{:S(2)}, u32[]{:S(2)}) collective-permute-start(f32[1,512]{1,0:T(1,128)S(1)} %add_add_fusion), channel_id=1, source_target_pairs={{0,6},{1,7},{2,4},{3,5},{4,2},{5,3},{6,0},{7,1},{8,14},{9,15},{10,... | collective-permute-start | bytes 6152 | tf_op jit(solution)/shard_map/ppermute | solution.py:50

commit v10 on v9

--- a/solution.py
+++ b/solution.py
@@ -462,10 +462,10 @@
     trace = trace + fetch(trace, steps[0])
     for index in range(3, len(steps), 2):
         trace = round_of(trace, steps[index:index + 2])
-    relay_x, relay_y, total, trace = lax.optimization_barrier((relay_x, relay_y, total, trace))
+    others = [fetch(trace, step) for step in (steps[1], steps[2], steps[1] + steps[2])]
+    relay_x, relay_y, total, others = lax.optimization_barrier((relay_x, relay_y, total, others))
     beside_x = receive(relay_x, PARTNER, RELAY_Y)
     beside_y = receive(relay_y, PARTNER, RELAY_X)
-    others = [fetch(trace, step) for step in (steps[1], steps[2], steps[1] + steps[2])]
     square = call(
         z, functools.partial(last_body, z), [relay_left, positions, total, relay_x, relay_y, beside_x, beside_y],
         [ANY, SMEM] + [ANY] * 5,
@@ -479,7 +479,6 @@
         ],
         2, 40 * 1024 * 1024,
     )[0]
-    square, trace, others = lax.optimization_barrier((square, trace, others))
     return square, jnp.sum((trace + others[0]) + (others[1] + others[2])) / (z.all_rows * z.block)
 
 

time: 129 us -> 140 us (1.085)
  local copies, waits for them, and re-layouts: 0.67 us -> 5.21 us
  starting transfers between devices: 34.5 us -> 38.4 us
  Pallas kernels: 49.1 us -> 51.5 us
    unnamed x6 -> x14, local copies, waits for them, and re-layouts: 0.67 us -> 5.21 us
    ppermute x7, waiting for transfers between devices: 3.83 us -> 7.81 us  [fetch(): lax.ppermute(value, AXES, [(d, d ^ step) for d in range(lax.axis_size(AXE...]
    ppermute x10, starting transfers between devices: 27.4 us -> 31.3 us  [receive(): return lax.ppermute(shard, AXES, pairs)]
    ppermute x10, waiting for transfers between devices: 37.1 us -> 33.7 us  [receive(): return lax.ppermute(shard, AXES, pairs)]
    pallas_call x6, Pallas kernels: 49.1 us -> 51.5 us  [call(): pl.pallas_call(kernel, out_shape=out_shape, in_specs=in_specs, out_specs=...]
  transfers between devices with their start and end apart: 17 -> 17, of which waited for: 6 -> 8; matrix products, arithmetic and copies ran while one was open for 0% -> 0% of each run, Pallas kernels for 36% -> 27%
where the time goes in v10:
time: 140 us
  Pallas kernels  51.5 us (37%)
  waiting for transfers between devices  41.5 us (30%)
  starting transfers between devices  38.4 us (27%)
  local copies, waits for them, and re-layouts  5.21 us (4%)
  between operations  2.61 us (2%)
    pallas_call x6, Pallas kernels, call(): pl.pallas_call(kernel, out_shape=out_shape, in_specs=in_specs, out_specs=...  51.5 us
    ppermute x10, waiting for transfers between devices, receive(): return lax.ppermute(shard, AXES, pairs)  33.7 us
    ppermute x10, starting transfers between devices, receive(): return lax.ppermute(shard, AXES, pairs)  31.3 us
    ppermute x7, waiting for transfers between devices, fetch(): lax.ppermute(value, AXES, [(d, d ^ step) for d in range(lax.axis_size(AXE...  7.81 us
    ppermute x7, starting transfers between devices, fetch(): lax.ppermute(value, AXES, [(d, d ^ step) for d in range(lax.axis_size(AXE...  7.11 us
    unnamed x14, local copies, waits for them, and re-layouts  5.21 us
  transfers between devices with their start and end apart: 17, of which 8 were waited for; matrix products, arithmetic and copies ran while one was open for 0% of the time, Pallas kernels for 27%

profile of v10, /device:TPU:0, one launch (start us, length us, event | category | flops | bytes accessed | tf_op | source)
XLA Modules:
  0.0 139.9 jit_solution(11378507683036637850)
XLA Ops:
  0.6 3.4 %shard_map.42 = bf16[81,128,128]{2,1,0:T(8,128)(2,1)} custom-call(bf16[4,20,128,128]{3,2,1,0:T(8,128)(2,1)} %tiles.1, s32[4,20]{1,0:T(4,128)} %columns.3), custom_call_target="tpu_custom_call" | custom-call | bytes 10485760 | tf_op jit(solution)/shard_map/pallas_call | solution.py:373
  4.0 0.5 collective-permute-start.3
  4.5 2.6 %collective-permute-start = (bf16[81,128,128]{2,1,0:T(8,128)(2,1)}, bf16[81,128,128]{2,1,0:T(8,128)(2,1)}, u32[]{:S(2)}, u32[]{:S(2)}) collective-permute-start(bf16[81,128,128]{2,1,0:T(8,128)(2,1)} %shard_map.42), channel_id=1, source_target_pairs={{2,0},{3,1},{0,2},{1,3},{6,4},{7,5},{4,6},{5,7},{10,8},{11,9},{8,1... | collective-permute-start | bytes 7962632 | tf_op jit(solution)/shard_map/ppermute | solution.py:46
  7.1 4.3 %collective-permute-start.1 = (bf16[81,128,128]{2,1,0:T(8,128)(2,1)}, bf16[81,128,128]{2,1,0:T(8,128)(2,1)S(1)}, u32[]{:S(2)}, u32[]{:S(2)}) collective-permute-start(bf16[81,128,128]{2,1,0:T(8,128)(2,1)} %shard_map.42), channel_id=1, source_target_pairs={{29,0},{4,1},{31,2},{6,3},{1,4},{8,5},{3,6},{10,7},{5,8},{12,9},{7... | collective-permute-start | bytes 7962632 | tf_op jit(solution)/shard_map/ppermute | solution.py:46
  11.4 9.7 %shard_map.41 = (f32[4,20,128,128]{3,2,1,0:T(8,128)}, bf16[512,3712]{1,0:T(8,128)(2,1)}, bf16[256,512]{1,0:T(8,128)(2,1)}, s32[4,20]{1,0:T(4,128)}, f32[1,512]{1,0:T(1,128)}) custom-call(bf16[4,20,128,128]{3,2,1,0:T(8,128)(2,1)} %tiles.1, s32[4,20]{1,0:T(4,128)} %columns.3), custom_call_target="tpu_custom_call" | custom-call | flops 1879048192 | bytes 13107200 | tf_op jit(solution)/shard_map/pallas_call | solution.py:373
  21.1 1.3 collective-permute-start.2
  22.4 0.0 collective-permute-done.3.refs_0_
  22.4 0.0 copy-start.3
  22.4 11.5 %shard_map.43 = (f32[4,20,128,128]{3,2,1,0:T(8,128)}, f32[1,512]{1,0:T(1,128)}) custom-call(bf16[512,3712]{1,0:T(8,128)(2,1)} %get-tuple-element.23.left_in.left, s32[4,20]{1,0:T(4,128)} %get-tuple-element.24.positions, f32[4,20,128,128]{3,2,1,0:T(8,128)} %get-tuple-element.26.prev, f32[1,512]{1,0:T(1,128)} %get-tuple-element.27.trace_in, ...), custom_call_target="tpu_custom_call" | custom-call | flops 1879048192 | bytes 13107200 | tf_op jit(solution)/shard_map/pallas_call | solution.py:373
  33.9 0.0 collective-permute-done.2
  33.9 31.6 %collective-permute-done.refs_0_ = bf16[81,128,128]{2,1,0:T(8,128)(2,1)} collective-permute-done((bf16[81,128,128]{2,1,0:T(8,128)(2,1)}, bf16[81,128,128]{2,1,0:T(8,128)(2,1)}, u32[]{:S(2)}, u32[]{:S(2)}) %collective-permute-start) | collective-permute-done | bytes 2654240 | tf_op jit(solution)/shard_map/ppermute | solution.py:46
  65.6 0.0 collective-permute-done.1.refs_1_
  65.6 0.0 copy-start.4
  65.6 1.5 %copy-done.4 = bf16[81,128,128]{2,1,0:T(8,128)(2,1)} copy-done((bf16[81,128,128]{2,1,0:T(8,128)(2,1)}, bf16[81,128,128]{2,1,0:T(8,128)(2,1)S(1)}, u32[]{:S(2)}) %copy-start.4) | copy-done | bytes 2654232
  67.1 0.0 copy-start
  67.1 1.8 %collective-permute-start.4 = (bf16[81,128,128]{2,1,0:T(8,128)(2,1)}, bf16[81,128,128]{2,1,0:T(8,128)(2,1)S(1)}, u32[]{:S(2)}, u32[]{:S(2)}) collective-permute-start(bf16[81,128,128]{2,1,0:T(8,128)(2,1)} %collective-permute-done.refs_0_), channel_id=1, source_target_pairs={{1,0},{0,1},{3,2},{2,3},{5,4},{4,5},{7,6},{6,7},{9,8},{8,9},{11,10... | collective-permute-start | bytes 7962632 | tf_op jit(solution)/shard_map/ppermute | solution.py:46
  68.9 3.5 %collective-permute-start.5 = (bf16[81,128,128]{2,1,0:T(8,128)(2,1)}, bf16[81,128,128]{2,1,0:T(8,128)(2,1)S(1)}, u32[]{:S(2)}, u32[]{:S(2)}) collective-permute-start(bf16[81,128,128]{2,1,0:T(8,128)(2,1)} %collective-permute-done.refs_0_), channel_id=1, source_target_pairs={{28,1},{7,2},{0,5},{11,6},{4,9},{15,10},{8,13},{19,14},{12,17},{23... | collective-permute-start | bytes 7962632 | tf_op jit(solution)/shard_map/ppermute | solution.py:46
  72.4 1.3 collective-permute-start.6
  73.7 8.6 %collective-permute-start.7 = (bf16[256,512]{1,0:T(8,128)(2,1)S(1)}, bf16[256,512]{1,0:T(8,128)(2,1)S(1)}, u32[]{:S(2)}, u32[]{:S(2)}) collective-permute-start(bf16[256,512]{1,0:T(8,128)(2,1)S(1)} %collective-permute-done.2), channel_id=1, source_target_pairs={{31,1},{4,2},{3,5},{8,6},{7,9},{12,10},{11,13},{16,14},{15,17},{20... | collective-permute-start | bytes 786440 | tf_op jit(solution)/shard_map/ppermute | solution.py:46
  82.3 0.0 collective-permute-done.4.refs_2_
  82.3 0.0 copy-done.3
  82.3 0.0 copy-start.5
  82.4 1.7 %copy-done.5 = bf16[81,128,128]{2,1,0:T(8,128)(2,1)S(1)} copy-done((bf16[81,128,128]{2,1,0:T(8,128)(2,1)S(1)}, bf16[81,128,128]{2,1,0:T(8,128)(2,1)}, u32[]{:S(2)}) %copy-start.5) | copy-done | bytes 2654232
  84.1 0.0 copy-start.6
  84.1 0.7 copy-done.6
  84.8 16.2 %shard_map.44 = (f32[4,20,128,128]{3,2,1,0:T(8,128)}, f32[1,512]{1,0:T(1,128)S(1)}, bf16[512,1024]{1,0:T(8,128)(2,1)S(1)}) custom-call(bf16[512,3712]{1,0:T(8,128)(2,1)} %get-tuple-element.23.left_in.left, s32[4,20]{1,0:T(4,128)S(1)} %copy-done.3, f32[4,20,128,128]{3,2,1,0:T(8,128)} %get-tuple-element.30.prev, f32[1,512]{1,0:T(1,128)S(1)} %copy-done.6, ...), custom_call_target="tpu_custom_call" | custom-call | flops 5637144576 | bytes 18350080 | tf_op jit(solution)/shard_map/pallas_call | solution.py:373
  101.0 0.0 copy-start.1
  101.0 0.0 collective-permute-done.7.corner
  101.0 0.0 copy-done
  101.1 0.1 collective-permute-start.8
  101.2 1.1 collective-permute-done.8
  102.3 0.8 collective-permute-start.10
  103.1 1.4 collective-permute-start.11
  104.4 1.3 collective-permute-start.9
  105.8 1.0 collective-permute-done.10
  106.8 1.7 %collective-permute-done.11 = f32[1,512]{1,0:T(1,128)S(1)} collective-permute-done((f32[1,512]{1,0:T(1,128)S(1)}, f32[1,512]{1,0:T(1,128)S(1)}, u32[]{:S(2)}, u32[]{:S(2)}) %collective-permute-start.11) | collective-permute-done | bytes 2080 | tf_op jit(solution)/shard_map/ppermute | solution.py:50
  108.5 0.0 collective-permute-done.9
  108.5 0.1 collective-permute-start.12
  108.6 3.0 %collective-permute-start.13 = (f32[1,512]{1,0:T(1,128)S(1)}, f32[1,512]{1,0:T(1,128)S(1)}, u32[]{:S(2)}, u32[]{:S(2)}) collective-permute-start(f32[1,512]{1,0:T(1,128)S(1)} %add_add_fusion), channel_id=1, source_target_pairs={{0,4},{1,5},{2,6},{3,7},{4,0},{5,1},{6,2},{7,3},{8,12},{9,13},{10,... | collective-permute-start | bytes 6152 | tf_op jit(solution)/shard_map/ppermute | solution.py:50
  111.5 0.5 collective-permute-start.14
  112.0 0.0 collective-permute-done.5.relay_x
  112.0 0.0 collective-permute-done.6.relay_y
  112.0 0.1 collective-permute-done.12
  112.1 1.0 collective-permute-done.13
  113.1 2.9 %collective-permute-done.14 = f32[1,512]{1,0:T(1,128)S(1)} collective-permute-done((f32[1,512]{1,0:T(1,128)S(1)}, f32[1,512]{1,0:T(1,128)S(1)}, u32[]{:S(2)}, u32[]{:S(2)}) %collective-permute-start.14) | collective-permute-done | bytes 2080 | tf_op jit(solution)/shard_map/ppermute | solution.py:50
  116.0 0.0 copy-done.1
  116.0 1.3 collective-permute-start.15
  117.3 6.1 %collective-permute-start.16 = (bf16[81,128,128]{2,1,0:T(8,128)(2,1)}, bf16[81,128,128]{2,1,0:T(8,128)(2,1)}, u32[]{:S(2)}, u32[]{:S(2)}) collective-permute-start(bf16[81,128,128]{2,1,0:T(8,128)(2,1)} %collective-permute-done.6.relay_y), channel_id=1, source_target_pairs={{0,1},{3,2},{4,5},{7,6},{8,9},{11,10},{12,13},{15,14},{16,17},{19,... | collective-permute-start | bytes 7962632 | tf_op jit(solution)/shard_map/ppermute | solution.py:46
  123.4 0.6 add_reduce_fusion
  124.7 0.0 collective-permute-done.15.beside_x
  124.7 2.0 %collective-permute-done.16.beside_y = bf16[81,128,128]{2,1,0:T(8,128)(2,1)} collective-permute-done((bf16[81,128,128]{2,1,0:T(8,128)(2,1)}, bf16[81,128,128]{2,1,0:T(8,128)(2,1)}, u32[]{:S(2)}, u32[]{:S(2)}) %collective-permute-start.16) | collective-permute-done | bytes 2654240 | tf_op jit(solution)/shard_map/ppermute | solution.py:46
  126.8 0.0 copy-start.2
  126.8 1.2 copy-done.2
  128.0 10.8 %shard_map.46 = bf16[4,20,128,128]{3,2,1,0:T(8,128)(2,1)} custom-call(bf16[512,1024]{1,0:T(8,128)(2,1)S(1)} %copy-done.2, s32[4,20]{1,0:T(4,128)S(1)} %copy-done.3, f32[4,20,128,128]{3,2,1,0:T(8,128)} %get-tuple-element.38.prev, bf16[81,128,128]{2,1,0:T(8,128)(2,1)S(1)} %collective-permute-done.5.relay_x, ...), custom_call_target="tpu_custom_call" | custom-call | flops 3758096384 | bytes 15728640 | tf_op jit(solution)/shard_map/pallas_call | solution.py:373
  (3 shorter events, 0.0 us)
Async XLA Ops:
  4.0 18.4 %collective-permute-start.3 = (bf16[81,128,128]{2,1,0:T(8,128)(2,1)}, bf16[81,128,128]{2,1,0:T(8,128)(2,1)}, u32[]{:S(2)}, u32[]{:S(2)}) collective-permute-start(bf16[81,128,128]{2,1,0:T(8,128)(2,1)} %shard_map.42), channel_id=1, source_target_pairs={{1,0},{0,1},{3,2},{2,3},{5,4},{4,5},{7,6},{6,7},{9,8},{8,9},{11,10... | collective-permute-start | bytes 7962632 | tf_op jit(solution)/shard_map/ppermute | solution.py:46
  4.5 61.0 %collective-permute-start = (bf16[81,128,128]{2,1,0:T(8,128)(2,1)}, bf16[81,128,128]{2,1,0:T(8,128)(2,1)}, u32[]{:S(2)}, u32[]{:S(2)}) collective-permute-start(bf16[81,128,128]{2,1,0:T(8,128)(2,1)} %shard_map.42), channel_id=1, source_target_pairs={{2,0},{3,1},{0,2},{1,3},{6,4},{7,5},{4,6},{5,7},{10,8},{11,9},{8,1... | collective-permute-start | bytes 7962632 | tf_op jit(solution)/shard_map/ppermute | solution.py:46
  7.1 58.5 %collective-permute-start.1 = (bf16[81,128,128]{2,1,0:T(8,128)(2,1)}, bf16[81,128,128]{2,1,0:T(8,128)(2,1)S(1)}, u32[]{:S(2)}, u32[]{:S(2)}) collective-permute-start(bf16[81,128,128]{2,1,0:T(8,128)(2,1)} %shard_map.42), channel_id=1, source_target_pairs={{29,0},{4,1},{31,2},{6,3},{1,4},{8,5},{3,6},{10,7},{5,8},{12,9},{7... | collective-permute-start | bytes 7962632 | tf_op jit(solution)/shard_map/ppermute | solution.py:46
  21.1 12.8 %collective-permute-start.2 = (bf16[256,512]{1,0:T(8,128)(2,1)}, bf16[256,512]{1,0:T(8,128)(2,1)S(1)}, u32[]{:S(2)}, u32[]{:S(2)}) collective-permute-start(bf16[256,512]{1,0:T(8,128)(2,1)} %get-tuple-element.25), channel_id=1, source_target_pairs={{1,0},{2,3},{5,4},{6,7},{9,8},{10,11},{13,12},{14,15},{17,16},{18,... | collective-permute-start | bytes 786440 | tf_op jit(solution)/shard_map/ppermute | solution.py:46
  22.4 59.9 %copy-start.3 = (s32[4,20]{1,0:T(4,128)S(1)}, s32[4,20]{1,0:T(4,128)}, u32[]{:S(2)}) copy-start(s32[4,20]{1,0:T(4,128)} %get-tuple-element.24.positions) | copy-start | bytes 964
  65.6 1.5 %copy-start.4 = (bf16[81,128,128]{2,1,0:T(8,128)(2,1)}, bf16[81,128,128]{2,1,0:T(8,128)(2,1)S(1)}, u32[]{:S(2)}) copy-start(bf16[81,128,128]{2,1,0:T(8,128)(2,1)S(1)} %collective-permute-done.1.refs_1_) | copy-start | bytes 7962628
  67.1 33.9 %copy-start = (bf16[512,3712]{1,0:T(8,128)(2,1)S(1)}, bf16[512,3712]{1,0:T(8,128)(2,1)}, u32[]{:S(2)}) copy-start(bf16[512,3712]{1,0:T(8,128)(2,1)} %get-tuple-element.23.left_in.left) | copy-start | bytes 11403268
  67.1 15.2 %collective-permute-start.4 = (bf16[81,128,128]{2,1,0:T(8,128)(2,1)}, bf16[81,128,128]{2,1,0:T(8,128)(2,1)S(1)}, u32[]{:S(2)}, u32[]{:S(2)}) collective-permute-start(bf16[81,128,128]{2,1,0:T(8,128)(2,1)} %collective-permute-done.refs_0_), channel_id=1, source_target_pairs={{1,0},{0,1},{3,2},{2,3},{5,4},{4,5},{7,6},{6,7},{9,8},{8,9},{11,10... | collective-permute-start | bytes 7962632 | tf_op jit(solution)/shard_map/ppermute | solution.py:46
  68.9 43.2 %collective-permute-start.5 = (bf16[81,128,128]{2,1,0:T(8,128)(2,1)}, bf16[81,128,128]{2,1,0:T(8,128)(2,1)S(1)}, u32[]{:S(2)}, u32[]{:S(2)}) collective-permute-start(bf16[81,128,128]{2,1,0:T(8,128)(2,1)} %collective-permute-done.refs_0_), channel_id=1, source_target_pairs={{28,1},{7,2},{0,5},{11,6},{4,9},{15,10},{8,13},{19,14},{12,17},{23... | collective-permute-start | bytes 7962632 | tf_op jit(solution)/shard_map/ppermute | solution.py:46
  72.4 39.6 %collective-permute-start.6 = (bf16[81,128,128]{2,1,0:T(8,128)(2,1)}, bf16[81,128,128]{2,1,0:T(8,128)(2,1)}, u32[]{:S(2)}, u32[]{:S(2)}) collective-permute-start(bf16[81,128,128]{2,1,0:T(8,128)(2,1)} %copy-done.4), channel_id=1, source_target_pairs={{2,0},{1,3},{6,4},{5,7},{10,8},{9,11},{14,12},{13,15},{18,16},{17,... | collective-permute-start | bytes 7962632 | tf_op jit(solution)/shard_map/ppermute | solution.py:46
  73.7 27.3 %collective-permute-start.7 = (bf16[256,512]{1,0:T(8,128)(2,1)S(1)}, bf16[256,512]{1,0:T(8,128)(2,1)S(1)}, u32[]{:S(2)}, u32[]{:S(2)}) collective-permute-start(bf16[256,512]{1,0:T(8,128)(2,1)S(1)} %collective-permute-done.2), channel_id=1, source_target_pairs={{31,1},{4,2},{3,5},{8,6},{7,9},{12,10},{11,13},{16,14},{15,17},{20... | collective-permute-start | bytes 786440 | tf_op jit(solution)/shard_map/ppermute | solution.py:46
  82.3 1.8 %copy-start.5 = (bf16[81,128,128]{2,1,0:T(8,128)(2,1)S(1)}, bf16[81,128,128]{2,1,0:T(8,128)(2,1)}, u32[]{:S(2)}) copy-start(bf16[81,128,128]{2,1,0:T(8,128)(2,1)} %copy-done.4) | copy-start | bytes 7962628
  84.1 0.7 copy-start.6
  101.0 15.0 %copy-start.1 = (bf16[512,1024]{1,0:T(8,128)(2,1)}, bf16[512,1024]{1,0:T(8,128)(2,1)S(1)}, u32[]{:S(2)}) copy-start(bf16[512,1024]{1,0:T(8,128)(2,1)S(1)} %get-tuple-element.34.left_in) | copy-start | bytes 3145732
  101.1 1.2 collective-permute-start.8
  102.3 4.5 %collective-permute-start.10 = (f32[1,512]{1,0:T(1,128)S(1)}, f32[1,512]{1,0:T(1,128)S(1)}, u32[]{:S(2)}, u32[]{:S(2)}) collective-permute-start(f32[1,512]{1,0:T(1,128)S(1)} %add.21), channel_id=1, source_target_pairs={{0,16},{1,17},{2,18},{3,19},{4,20},{5,21},{6,22},{7,23},{8,24},{9,... | collective-permute-start | bytes 6152 | tf_op jit(solution)/shard_map/ppermute | solution.py:50
  103.1 5.4 %collective-permute-start.11 = (f32[1,512]{1,0:T(1,128)S(1)}, f32[1,512]{1,0:T(1,128)S(1)}, u32[]{:S(2)}, u32[]{:S(2)}) collective-permute-start(f32[1,512]{1,0:T(1,128)S(1)} %add.21), channel_id=1, source_target_pairs={{0,24},{1,25},{2,26},{3,27},{4,28},{5,29},{6,30},{7,31},{8,16},{9,... | collective-permute-start | bytes 6152 | tf_op jit(solution)/shard_map/ppermute | solution.py:50
  104.4 4.0 %collective-permute-start.9 = (f32[1,512]{1,0:T(1,128)S(1)}, f32[1,512]{1,0:T(1,128)S(1)}, u32[]{:S(2)}, u32[]{:S(2)}) collective-permute-start(f32[1,512]{1,0:T(1,128)S(1)} %add.21), channel_id=1, source_target_pairs={{0,8},{1,9},{2,10},{3,11},{4,12},{5,13},{6,14},{7,15},{8,0},{9,1},... | collective-permute-start | bytes 6152 | tf_op jit(solution)/shard_map/ppermute | solution.py:50
  108.5 3.7 %collective-permute-start.12 = (f32[1,512]{1,0:T(1,128)S(1)}, f32[1,512]{1,0:T(1,128)S(1)}, u32[]{:S(2)}, u32[]{:S(2)}) collective-permute-start(f32[1,512]{1,0:T(1,128)S(1)} %add_add_fusion), channel_id=1, source_target_pairs={{0,2},{1,3},{2,0},{3,1},{4,6},{5,7},{6,4},{7,5},{8,10},{9,11},{10,... | collective-permute-start | bytes 6152 | tf_op jit(solution)/shard_map/ppermute | solution.py:50
  108.6 4.5 %collective-permute-start.13 = (f32[1,512]{1,0:T(1,128)S(1)}, f32[1,512]{1,0:T(1,128)S(1)}, u32[]{:S(2)}, u32[]{:S(2)}) collective-permute-start(f32[1,512]{1,0:T(1,128)S(1)} %add_add_fusion), channel_id=1, source_target_pairs={{0,4},{1,5},{2,6},{3,7},{4,0},{5,1},{6,2},{7,3},{8,12},{9,13},{10,... | collective-permute-start | bytes 6152 | tf_op jit(solution)/shard_map/ppermute | solution.py:50
  111.5 4.5 %collective-permute-start.14 = (f32[1,512]{1,0:T(1,128)S(1)}, f32[1,512]{1,0:T(1,128)S(1)}, u32[]{:S(2)}, u32[]{:S(2)}) collective-permute-start(f32[1,512]{1,0:T(1,128)S(1)} %add_add_fusion), channel_id=1, source_target_pairs={{0,6},{1,7},{2,4},{3,5},{4,2},{5,3},{6,0},{7,1},{8,14},{9,15},{10,... | collective-permute-start | bytes 6152 | tf_op jit(solution)/shard_map/ppermute | solution.py:50
  116.0 8.7 %collective-permute-start.15 = (bf16[81,128,128]{2,1,0:T(8,128)(2,1)S(1)}, bf16[81,128,128]{2,1,0:T(8,128)(2,1)}, u32[]{:S(2)}, u32[]{:S(2)}) collective-permute-start(bf16[81,128,128]{2,1,0:T(8,128)(2,1)S(1)} %collective-permute-done.5.relay_x), channel_id=1, source_target_pairs={{1,0},{2,3},{5,4},{6,7},{9,8},{10,11},{13,12},{14,15},{17,16},{18,... | collective-permute-start | bytes 7962632 | tf_op jit(solution)/shard_map/ppermute | solution.py:46
  117.3 9.4 %collective-permute-start.16 = (bf16[81,128,128]{2,1,0:T(8,128)(2,1)}, bf16[81,128,128]{2,1,0:T(8,128)(2,1)}, u32[]{:S(2)}, u32[]{:S(2)}) collective-permute-start(bf16[81,128,128]{2,1,0:T(8,128)(2,1)} %collective-permute-done.6.relay_y), channel_id=1, source_target_pairs={{0,1},{3,2},{4,5},{7,6},{8,9},{11,10},{12,13},{15,14},{16,17},{19,... | collective-permute-start | bytes 7962632 | tf_op jit(solution)/shard_map/ppermute | solution.py:46
  126.8 1.2 copy-start.2

commit v11 on v9

--- a/solution.py
+++ b/solution.py
@@ -13,30 +13,32 @@
 WHOLE_VMEM = 60 * 1024 * 1024
 EMPTY = 64
 
-OVER_X = (2, 2, -2, -2)
-OVER_Y = (-3, 3, -3, 3)
+FIRST = (2, 3, -3, -2)
+SECOND = (-3, 2, -2, 3)
 RELAY_FROM = (2, -5, 5, -2)
-RELAY_X, RELAY_Y = (1, 2), (0, 3)
 PARTNER = (1, -1, 1, -1)
-RELAY = tuple(
-    RELAY_FROM[m] + (OVER_X if m in RELAY_X else OVER_Y)[(m + RELAY_FROM[m]) % 4] for m in range(4)
-)
+RELAY = tuple(RELAY_FROM[m] + FIRST[(m + RELAY_FROM[m]) % 4] for m in range(4))
 
 
 def across(table):
     return tuple(PARTNER[m] + table[m ^ 1] for m in range(4))
 
 
+USE_SECOND = tuple(int(abs(offset) > 3) for offset in across(FIRST))
+MIXED = tuple(
+    second if use else first
+    for first, second, use in zip(across(FIRST), across(SECOND), USE_SECOND)
+)
 OFFSETS = {
     "beside": PARTNER,
-    "x": OVER_X,
-    "y": OVER_Y,
-    "x_beside": across(OVER_X),
+    "first": FIRST,
+    "second": SECOND,
+    "mixed": MIXED,
     "relay": RELAY,
     "relay_beside": across(RELAY),
 }
-COUNTS = {"beside": (2, 0, 2, 0), "x": (2, 0, 0, 2), "y": (2, 0, 0, 2), "x_beside": (0, 0, 2, 2)}
-OUTSIDE = {("y", "x_beside"): (0, 2, 2, 0), ("y", "x"): (0, 2, 0, 0)}
+COUNTS = {"beside": (2, 0, 2, 0), "first": (2, 0, 0, 2), "second": (2, 0, 0, 2), "mixed": (0, 0, 2, 2)}
+OUTSIDE = {("first", "mixed"): (0, 2, 2, 0), ("first", "second"): (0, 2, 0, 0)}
 LOWER, UPPER = 2, 1
 
 
@@ -207,7 +209,7 @@
 def near_body(z, names, final, left_in, positions, prev, trace_in, *refs):
     refs = list(refs)
     take = lambda count: [refs.pop(0) for _ in range(count)]
-    sources = take(len(names))
+    sources = [take(2 if name == "mixed" else 1) for name in names]
     out, trace = take(2)
     relay_left = take(1)[0] if final else None
     left, stage, right, total, sums, vector, scalars = take(7)
@@ -220,12 +222,21 @@
         return pl.ds(aligned(n, z.span), z.span)
 
     def fetch(index):
-        return pltpu.make_async_copy(sources[index], stage.at[index % 2], in_sem.at[index % 2])
+        return pltpu.make_async_copy(sources[index][0], stage.at[index % 2], in_sem.at[index % 2])
+
+    def begin_fetch(index):
+        if len(sources[index]) == 1:
+            fetch(index).start()
+            return
+        for use, source in enumerate(sources[index]):
+            @pl.when(pick(USE_SECOND, kind) == use)
+            def _():
+                pltpu.make_async_copy(source, stage.at[index % 2], in_sem.at[index % 2]).start()
 
     left_copy = pltpu.make_async_copy(left_in, left, left_sem)
     left_copy.start()
     for index in range(min(2, len(names))):
-        fetch(index).start()
+        begin_fetch(index)
     prev_copy = pltpu.make_async_copy(prev, sums, prev_sem)
     prev_copy.start()
     total[...] = jnp.zeros_like(total)
@@ -260,7 +271,7 @@
         decodings[index].wait()
         scatter(z, dense, 0, stage.at[slot], lambda r, u: scalars[slot, r, u])
         if index + 2 < len(names):
-            fetch(index + 2).start()
+            begin_fetch(index + 2)
         if index + 1 < len(names):
             begin_decode(index + 1)
 
@@ -307,21 +318,16 @@
         add_trace(trace, jnp.float32(2), rows[:half], corner[:, :half])
 
 
-def last_body(z, left_in, positions, prev, relay_x, relay_y, beside_x, beside_y, out, left, stage, right, total, out_stage,
+def last_body(z, left_in, positions, prev, source_a, source_b, out, left, stage, right, total, out_stage,
               prev_stage, vector, scalars, left_sem, in_sem, prev_sem, place_sem, out_sems):
     kind = lax.axis_index(AXES) % 4
-    gets_x = (kind == RELAY_X[0]) | (kind == RELAY_X[1])
-    for over_x, index, source in ((True, 0, relay_x), (False, 0, relay_y), (False, 1, beside_x), (True, 1, beside_y)):
-        @pl.when(gets_x == over_x)
-        def _():
-            pltpu.make_async_copy(source, stage.at[index], in_sem.at[index]).start()
     copies = [
-        pltpu.make_async_copy(relay_x, stage.at[0], in_sem.at[0]),
-        pltpu.make_async_copy(beside_x, stage.at[1], in_sem.at[1]),
+        pltpu.make_async_copy(source_a, stage.at[0], in_sem.at[0]),
+        pltpu.make_async_copy(source_b, stage.at[1], in_sem.at[1]),
         pltpu.make_async_copy(left_in, left, left_sem),
         pltpu.make_async_copy(prev, prev_stage, prev_sem),
     ]
-    for copy in copies[2:]:
+    for copy in copies:
         copy.start()
     places = [pick(OFFSETS[name], kind) + z.hops for name in ("relay", "relay_beside")]
     low = jnp.maximum(0, jnp.minimum(*places) - z.hops)
@@ -408,8 +414,8 @@
         ],
         0, WHOLE_VMEM,
     )
-    over_x = receive(payload, OVER_X)
-    over_y = receive(payload, OVER_Y)
+    first = receive(payload, FIRST)
+    second = receive(payload, SECOND)
     beside = receive(payload, PARTNER)
 
     total, left, corner, positions, trace = call(
@@ -445,13 +451,15 @@
         )
 
     total, trace = near(("beside",), [beside], total, trace)
-    over_x, over_y, corner, total, trace = lax.optimization_barrier((over_x, over_y, corner, total, trace))
-    relay_x = receive(over_x, RELAY_FROM, RELAY_X)
-    relay_y = receive(over_y, RELAY_FROM, RELAY_Y)
-    x_beside = receive(over_x, PARTNER)
+    first, second, corner, total, trace = lax.optimization_barrier((first, second, corner, total, trace))
+    relay = receive(first, RELAY_FROM)
+    mixed = [
+        receive(first, PARTNER, [m for m in range(4) if not USE_SECOND[m]]),
+        receive(second, PARTNER, [m for m in range(4) if USE_SECOND[m]]),
+    ]
     corner = receive(corner, (0, -2, 2, 0), (LOWER, UPPER))
     total, trace, relay_left = near(
-        ("x", "y", "x_beside"), [over_x, over_y, x_beside], total, trace, True
+        ("first", "second", "mixed"), [first, second, *mixed], total, trace, True
     )
     trace = call(
         z, functools.partial(corner_body, z), [left, corner, trace], [ANY, VMEM, VMEM], line, VMEM,
@@ -462,13 +470,12 @@
     trace = trace + fetch(trace, steps[0])
     for index in range(3, len(steps), 2):
         trace = round_of(trace, steps[index:index + 2])
-    relay_x, relay_y, total, trace = lax.optimization_barrier((relay_x, relay_y, total, trace))
-    beside_x = receive(relay_x, PARTNER, RELAY_Y)
-    beside_y = receive(relay_y, PARTNER, RELAY_X)
+    relay, total, trace = lax.optimization_barrier((relay, total, trace))
+    relay_beside = receive(relay, PARTNER)
     others = [fetch(trace, step) for step in (steps[1], steps[2], steps[1] + steps[2])]
     square = call(
-        z, functools.partial(last_body, z), [relay_left, positions, total, relay_x, relay_y, beside_x, beside_y],
-        [ANY, SMEM] + [ANY] * 5,
+        z, functools.partial(last_body, z), [relay_left, positions, total, relay, relay_beside],
+        [ANY, SMEM, ANY, ANY, ANY],
         [shape(tiles.shape, dtype)],
         [ANY],
         [
@@ -477,7 +484,7 @@
             pltpu.VMEM(tiles.shape, dtype), pltpu.VMEM(tiles.shape, jnp.float32), *places,
             DMA, DMA((2,)), DMA, DMA((2,)), DMA((z.rows,)),
         ],
-        2, 40 * 1024 * 1024,
+        2, 44 * 1024 * 1024,
     )[0]
     square, trace, others = lax.optimization_barrier((square, trace, others))
     return square, jnp.sum((trace + others[0]) + (others[1] + others[2])) / (z.all_rows * z.block)

time: 129 us -> 124 us (0.961)
  starting transfers between devices: 34.5 us -> 30 us
    ppermute x10 -> x9, starting transfers between devices: 27.4 us -> 22.9 us  [receive(): return lax.ppermute(shard, AXES, pairs)]
    ppermute x10 -> x9, waiting for transfers between devices: 37.1 us -> 36.8 us  [receive(): return lax.ppermute(shard, AXES, pairs)]
  transfers between devices with their start and end apart: 17 -> 16, of which waited for: 6 -> 7; matrix products, arithmetic and copies ran while one was open for 0% -> 0% of each run, Pallas kernels for 36% -> 37%
where the time goes in v11:
time: 124 us
  Pallas kernels  49.1 us (40%)
  waiting for transfers between devices  40.7 us (33%)
  starting transfers between devices  30 us (24%)
  between operations  2.6 us (2%)
    pallas_call x6, Pallas kernels, call(): pl.pallas_call(kernel, out_shape=out_shape, in_specs=in_specs, out_specs=...  49.1 us
    ppermute x9, waiting for transfers between devices, receive(): return lax.ppermute(shard, AXES, pairs)  36.8 us
    ppermute x9, starting transfers between devices, receive(): return lax.ppermute(shard, AXES, pairs)  22.9 us
    ppermute x7, starting transfers between devices, fetch(): lax.ppermute(value, AXES, [(d, d ^ step) for d in range(lax.axis_size(AXE...  7.05 us
    ppermute x7, waiting for transfers between devices, fetch(): lax.ppermute(value, AXES, [(d, d ^ step) for d in range(lax.axis_size(AXE...  3.95 us
  transfers between devices with their start and end apart: 16, of which 7 were waited for; matrix products, arithmetic and copies ran while one was open for 0% of the time, Pallas kernels for 37%

profile of v11, /device:TPU:0, one launch (start us, length us, event | category | flops | bytes accessed | tf_op | source)
XLA Modules:
  0.0 123.7 jit_solution(10863324465103920926)
XLA Ops:
  0.6 3.4 %shard_map.42 = bf16[81,128,128]{2,1,0:T(8,128)(2,1)} custom-call(bf16[4,20,128,128]{3,2,1,0:T(8,128)(2,1)} %tiles.1, s32[4,20]{1,0:T(4,128)} %columns.3), custom_call_target="tpu_custom_call" | custom-call | bytes 10485760 | tf_op jit(solution)/shard_map/pallas_call | solution.py:379
  4.0 0.5 collective-permute-start.3
  4.5 5.7 %collective-permute-start = (bf16[81,128,128]{2,1,0:T(8,128)(2,1)}, bf16[81,128,128]{2,1,0:T(8,128)(2,1)S(1)}, u32[]{:S(2)}, u32[]{:S(2)}) collective-permute-start(bf16[81,128,128]{2,1,0:T(8,128)(2,1)} %shard_map.42), channel_id=1, source_target_pairs={{2,0},{4,1},{31,2},{1,3},{6,4},{8,5},{3,6},{5,7},{10,8},{12,9},{7,... | collective-permute-start | bytes 7962632 | tf_op jit(solution)/shard_map/ppermute | solution.py:48
  10.2 0.0 collective-permute-start.1
  10.2 9.7 %shard_map.41 = (f32[4,20,128,128]{3,2,1,0:T(8,128)}, bf16[512,3712]{1,0:T(8,128)(2,1)}, bf16[256,512]{1,0:T(8,128)(2,1)}, s32[4,20]{1,0:T(4,128)}, f32[1,512]{1,0:T(1,128)}) custom-call(bf16[4,20,128,128]{3,2,1,0:T(8,128)(2,1)} %tiles.1, s32[4,20]{1,0:T(4,128)} %columns.3), custom_call_target="tpu_custom_call" | custom-call | flops 1879048192 | bytes 13107200 | tf_op jit(solution)/shard_map/pallas_call | solution.py:379
  19.9 1.3 %collective-permute-start.2 = (bf16[256,512]{1,0:T(8,128)(2,1)}, bf16[256,512]{1,0:T(8,128)(2,1)S(1)}, u32[]{:S(2)}, u32[]{:S(2)}) collective-permute-start(bf16[256,512]{1,0:T(8,128)(2,1)} %get-tuple-element.27), channel_id=1, source_target_pairs={{1,0},{2,3},{5,4},{6,7},{9,8},{10,11},{13,12},{14,15},{17,16},{18,... | collective-permute-start | bytes 786440 | tf_op jit(solution)/shard_map/ppermute | solution.py:48
  21.2 0.0 collective-permute-done.3.refs_0_
  21.2 0.0 copy-start.1
  21.2 11.4 %shard_map.43 = (f32[4,20,128,128]{3,2,1,0:T(8,128)}, f32[1,512]{1,0:T(1,128)}) custom-call(bf16[512,3712]{1,0:T(8,128)(2,1)} %get-tuple-element.25.left_in.left, s32[4,20]{1,0:T(4,128)} %get-tuple-element.26.positions, f32[4,20,128,128]{3,2,1,0:T(8,128)} %get-tuple-element.28.prev, f32[1,512]{1,0:T(1,128)} %get-tuple-element.29.trace_in, ...), custom_call_target="tpu_custom_call" | custom-call | flops 1879048192 | bytes 13107200 | tf_op jit(solution)/shard_map/pallas_call | solution.py:379
  32.6 0.0 collective-permute-done.2
  32.6 31.9 %collective-permute-done.refs_0_ = bf16[81,128,128]{2,1,0:T(8,128)(2,1)S(1)} collective-permute-done((bf16[81,128,128]{2,1,0:T(8,128)(2,1)}, bf16[81,128,128]{2,1,0:T(8,128)(2,1)S(1)}, u32[]{:S(2)}, u32[]{:S(2)}) %collective-permute-start) | collective-permute-done | bytes 2654240 | tf_op jit(solution)/shard_map/ppermute | solution.py:48
  64.5 0.3 collective-permute-done.1.refs_1_
  64.8 0.0 copy-start
  64.8 3.1 %collective-permute-start.4 = (bf16[81,128,128]{2,1,0:T(8,128)(2,1)S(1)}, bf16[81,128,128]{2,1,0:T(8,128)(2,1)S(1)}, u32[]{:S(2)}, u32[]{:S(2)}) collective-permute-start(bf16[81,128,128]{2,1,0:T(8,128)(2,1)S(1)} %collective-permute-done.refs_0_), channel_id=1, source_target_pairs={{0,1},{3,2},{4,5},{7,6},{8,9},{11,10},{12,13},{15,14},{16,17},{19,... | collective-permute-start | bytes 7962632 | tf_op jit(solution)/shard_map/ppermute | solution.py:48
  68.0 1.3 %collective-permute-start.5 = (bf16[81,128,128]{2,1,0:T(8,128)(2,1)}, bf16[81,128,128]{2,1,0:T(8,128)(2,1)S(1)}, u32[]{:S(2)}, u32[]{:S(2)}) collective-permute-start(bf16[81,128,128]{2,1,0:T(8,128)(2,1)} %collective-permute-done.1.refs_1_), channel_id=1, source_target_pairs={{1,0},{2,3},{5,4},{6,7},{9,8},{10,11},{13,12},{14,15},{17,16},{18,... | collective-permute-start | bytes 7962632 | tf_op jit(solution)/shard_map/ppermute | solution.py:48
  69.3 3.0 %collective-permute-start.6 = (bf16[81,128,128]{2,1,0:T(8,128)(2,1)S(1)}, bf16[81,128,128]{2,1,0:T(8,128)(2,1)S(1)}, u32[]{:S(2)}, u32[]{:S(2)}) collective-permute-start(bf16[81,128,128]{2,1,0:T(8,128)(2,1)S(1)} %collective-permute-done.refs_0_), channel_id=1, source_target_pairs={{2,0},{28,1},{7,2},{1,3},{6,4},{0,5},{11,6},{5,7},{10,8},{4,9},{15... | collective-permute-start | bytes 7962632 | tf_op jit(solution)/shard_map/ppermute | solution.py:48
  72.3 5.9 %collective-permute-start.7 = (bf16[256,512]{1,0:T(8,128)(2,1)S(1)}, bf16[256,512]{1,0:T(8,128)(2,1)S(1)}, u32[]{:S(2)}, u32[]{:S(2)}) collective-permute-start(bf16[256,512]{1,0:T(8,128)(2,1)S(1)} %collective-permute-done.2), channel_id=1, source_target_pairs={{31,1},{4,2},{3,5},{8,6},{7,9},{12,10},{11,13},{16,14},{15,17},{20... | collective-permute-start | bytes 786440 | tf_op jit(solution)/shard_map/ppermute | solution.py:48
  78.2 0.0 collective-permute-done.4.refs_2_
  78.3 0.0 collective-permute-done.5.refs_3_
  78.3 0.0 copy-done.1
  78.3 0.0 copy-start.2
  78.3 0.7 copy-done.2
  79.0 15.5 %shard_map.44 = (f32[4,20,128,128]{3,2,1,0:T(8,128)}, f32[1,512]{1,0:T(1,128)S(1)}, bf16[512,1024]{1,0:T(8,128)(2,1)S(1)}) custom-call(bf16[512,3712]{1,0:T(8,128)(2,1)} %get-tuple-element.25.left_in.left, s32[4,20]{1,0:T(4,128)S(1)} %copy-done.1, f32[4,20,128,128]{3,2,1,0:T(8,128)} %get-tuple-element.32.prev, f32[1,512]{1,0:T(1,128)S(1)} %copy-done.2, ...), custom_call_target="tpu_custom_call" | custom-call | flops 5637144576 | bytes 18350080 | tf_op jit(solution)/shard_map/pallas_call | solution.py:379
  94.5 0.0 collective-permute-done.7.corner
  94.5 0.0 copy-done
  94.6 0.1 collective-permute-start.8
  94.6 1.1 collective-permute-done.8
  95.8 0.9 collective-permute-start.10
  96.7 1.3 %collective-permute-start.11 = (f32[1,512]{1,0:T(1,128)S(1)}, f32[1,512]{1,0:T(1,128)S(1)}, u32[]{:S(2)}, u32[]{:S(2)}) collective-permute-start(f32[1,512]{1,0:T(1,128)S(1)} %add.21), channel_id=1, source_target_pairs={{0,24},{1,25},{2,26},{3,27},{4,28},{5,29},{6,30},{7,31},{8,16},{9,... | collective-permute-start | bytes 6152 | tf_op jit(solution)/shard_map/ppermute | solution.py:52
  98.0 1.2 %collective-permute-start.9 = (f32[1,512]{1,0:T(1,128)S(1)}, f32[1,512]{1,0:T(1,128)S(1)}, u32[]{:S(2)}, u32[]{:S(2)}) collective-permute-start(f32[1,512]{1,0:T(1,128)S(1)} %add.21), channel_id=1, source_target_pairs={{0,8},{1,9},{2,10},{3,11},{4,12},{5,13},{6,14},{7,15},{8,0},{9,1},... | collective-permute-start | bytes 6152 | tf_op jit(solution)/shard_map/ppermute | solution.py:52
  99.3 1.0 collective-permute-done.10
  100.3 1.8 %collective-permute-done.11 = f32[1,512]{1,0:T(1,128)S(1)} collective-permute-done((f32[1,512]{1,0:T(1,128)S(1)}, f32[1,512]{1,0:T(1,128)S(1)}, u32[]{:S(2)}, u32[]{:S(2)}) %collective-permute-start.11) | collective-permute-done | bytes 2080 | tf_op jit(solution)/shard_map/ppermute | solution.py:52
  102.1 0.0 collective-permute-done.9
  102.1 3.5 %collective-permute-done.6.source_a = bf16[81,128,128]{2,1,0:T(8,128)(2,1)S(1)} collective-permute-done((bf16[81,128,128]{2,1,0:T(8,128)(2,1)S(1)}, bf16[81,128,128]{2,1,0:T(8,128)(2,1)S(1)}, u32[]{:S(2)}, u32[]{:S(2)}) %collective-permute-start.6) | collective-permute-done | bytes 2654240 | tf_op jit(solution)/shard_map/ppermute | solution.py:48
  105.6 2.1 %collective-permute-start.12 = (bf16[81,128,128]{2,1,0:T(8,128)(2,1)S(1)}, bf16[81,128,128]{2,1,0:T(8,128)(2,1)S(1)}, u32[]{:S(2)}, u32[]{:S(2)}) collective-permute-start(bf16[81,128,128]{2,1,0:T(8,128)(2,1)S(1)} %collective-permute-done.6.source_a), channel_id=1, source_target_pairs={{1,0},{0,1},{3,2},{2,3},{5,4},{4,5},{7,6},{6,7},{9,8},{8,9},{11,10... | collective-permute-start | bytes 7962632 | tf_op jit(solution)/shard_map/ppermute | solution.py:48
  107.6 1.9 %collective-permute-start.13 = (f32[1,512]{1,0:T(1,128)S(1)}, f32[1,512]{1,0:T(1,128)S(1)}, u32[]{:S(2)}, u32[]{:S(2)}) collective-permute-start(f32[1,512]{1,0:T(1,128)S(1)} %add_add_fusion), channel_id=1, source_target_pairs={{0,2},{1,3},{2,0},{3,1},{4,6},{5,7},{6,4},{7,5},{8,10},{9,11},{10,... | collective-permute-start | bytes 6152 | tf_op jit(solution)/shard_map/ppermute | solution.py:52
  109.5 0.0 collective-permute-start.14
  109.5 1.6 %collective-permute-start.15 = (f32[1,512]{1,0:T(1,128)S(1)}, f32[1,512]{1,0:T(1,128)S(1)}, u32[]{:S(2)}, u32[]{:S(2)}) collective-permute-start(f32[1,512]{1,0:T(1,128)S(1)} %add_add_fusion), channel_id=1, source_target_pairs={{0,6},{1,7},{2,4},{3,5},{4,2},{5,3},{6,0},{7,1},{8,14},{9,15},{10,... | collective-permute-start | bytes 6152 | tf_op jit(solution)/shard_map/ppermute | solution.py:52
  111.1 1.1 collective-permute-done.12.source_b
  112.2 9.1 %shard_map.46 = bf16[4,20,128,128]{3,2,1,0:T(8,128)(2,1)} custom-call(bf16[512,1024]{1,0:T(8,128)(2,1)S(1)} %get-tuple-element.36.left_in, s32[4,20]{1,0:T(4,128)S(1)} %copy-done.1, f32[4,20,128,128]{3,2,1,0:T(8,128)} %get-tuple-element.40.prev, bf16[81,128,128]{2,1,0:T(8,128)(2,1)S(1)} %collective-permute-done.6.source_a, ...), custom_call_target="tpu_custom_call" | custom-call | flops 3758096384 | bytes 15728640 | tf_op jit(solution)/shard_map/pallas_call | solution.py:379
  121.3 0.0 collective-permute-done.13
  121.3 0.0 collective-permute-done.14
  121.3 0.0 collective-permute-done.15
  121.3 0.6 add_reduce_fusion
  (3 shorter events, 0.0 us)
Async XLA Ops:
  4.0 17.2 %collective-permute-start.3 = (bf16[81,128,128]{2,1,0:T(8,128)(2,1)}, bf16[81,128,128]{2,1,0:T(8,128)(2,1)}, u32[]{:S(2)}, u32[]{:S(2)}) collective-permute-start(bf16[81,128,128]{2,1,0:T(8,128)(2,1)} %shard_map.42), channel_id=1, source_target_pairs={{1,0},{0,1},{3,2},{2,3},{5,4},{4,5},{7,6},{6,7},{9,8},{8,9},{11,10... | collective-permute-start | bytes 7962632 | tf_op jit(solution)/shard_map/ppermute | solution.py:48
  4.5 60.0 %collective-permute-start = (bf16[81,128,128]{2,1,0:T(8,128)(2,1)}, bf16[81,128,128]{2,1,0:T(8,128)(2,1)S(1)}, u32[]{:S(2)}, u32[]{:S(2)}) collective-permute-start(bf16[81,128,128]{2,1,0:T(8,128)(2,1)} %shard_map.42), channel_id=1, source_target_pairs={{2,0},{4,1},{31,2},{1,3},{6,4},{8,5},{3,6},{5,7},{10,8},{12,9},{7,... | collective-permute-start | bytes 7962632 | tf_op jit(solution)/shard_map/ppermute | solution.py:48
  10.2 54.6 %collective-permute-start.1 = (bf16[81,128,128]{2,1,0:T(8,128)(2,1)}, bf16[81,128,128]{2,1,0:T(8,128)(2,1)}, u32[]{:S(2)}, u32[]{:S(2)}) collective-permute-start(bf16[81,128,128]{2,1,0:T(8,128)(2,1)} %shard_map.42), channel_id=1, source_target_pairs={{29,0},{3,1},{0,2},{6,3},{1,4},{7,5},{4,6},{10,7},{5,8},{11,9},{8,... | collective-permute-start | bytes 7962632 | tf_op jit(solution)/shard_map/ppermute | solution.py:48
  19.9 12.7 %collective-permute-start.2 = (bf16[256,512]{1,0:T(8,128)(2,1)}, bf16[256,512]{1,0:T(8,128)(2,1)S(1)}, u32[]{:S(2)}, u32[]{:S(2)}) collective-permute-start(bf16[256,512]{1,0:T(8,128)(2,1)} %get-tuple-element.27), channel_id=1, source_target_pairs={{1,0},{2,3},{5,4},{6,7},{9,8},{10,11},{13,12},{14,15},{17,16},{18,... | collective-permute-start | bytes 786440 | tf_op jit(solution)/shard_map/ppermute | solution.py:48
  21.2 57.1 %copy-start.1 = (s32[4,20]{1,0:T(4,128)S(1)}, s32[4,20]{1,0:T(4,128)}, u32[]{:S(2)}) copy-start(s32[4,20]{1,0:T(4,128)} %get-tuple-element.26.positions) | copy-start | bytes 964
  64.8 29.7 %copy-start = (bf16[512,3712]{1,0:T(8,128)(2,1)S(1)}, bf16[512,3712]{1,0:T(8,128)(2,1)}, u32[]{:S(2)}) copy-start(bf16[512,3712]{1,0:T(8,128)(2,1)} %get-tuple-element.25.left_in.left) | copy-start | bytes 11403268
  64.8 13.4 %collective-permute-start.4 = (bf16[81,128,128]{2,1,0:T(8,128)(2,1)S(1)}, bf16[81,128,128]{2,1,0:T(8,128)(2,1)S(1)}, u32[]{:S(2)}, u32[]{:S(2)}) collective-permute-start(bf16[81,128,128]{2,1,0:T(8,128)(2,1)S(1)} %collective-permute-done.refs_0_), channel_id=1, source_target_pairs={{0,1},{3,2},{4,5},{7,6},{8,9},{11,10},{12,13},{15,14},{16,17},{19,... | collective-permute-start | bytes 7962632 | tf_op jit(solution)/shard_map/ppermute | solution.py:48
  68.0 10.3 %collective-permute-start.5 = (bf16[81,128,128]{2,1,0:T(8,128)(2,1)}, bf16[81,128,128]{2,1,0:T(8,128)(2,1)S(1)}, u32[]{:S(2)}, u32[]{:S(2)}) collective-permute-start(bf16[81,128,128]{2,1,0:T(8,128)(2,1)} %collective-permute-done.1.refs_1_), channel_id=1, source_target_pairs={{1,0},{2,3},{5,4},{6,7},{9,8},{10,11},{13,12},{14,15},{17,16},{18,... | collective-permute-start | bytes 7962632 | tf_op jit(solution)/shard_map/ppermute | solution.py:48
  69.3 36.3 %collective-permute-start.6 = (bf16[81,128,128]{2,1,0:T(8,128)(2,1)S(1)}, bf16[81,128,128]{2,1,0:T(8,128)(2,1)S(1)}, u32[]{:S(2)}, u32[]{:S(2)}) collective-permute-start(bf16[81,128,128]{2,1,0:T(8,128)(2,1)S(1)} %collective-permute-done.refs_0_), channel_id=1, source_target_pairs={{2,0},{28,1},{7,2},{1,3},{6,4},{0,5},{11,6},{5,7},{10,8},{4,9},{15... | collective-permute-start | bytes 7962632 | tf_op jit(solution)/shard_map/ppermute | solution.py:48
  72.3 22.2 %collective-permute-start.7 = (bf16[256,512]{1,0:T(8,128)(2,1)S(1)}, bf16[256,512]{1,0:T(8,128)(2,1)S(1)}, u32[]{:S(2)}, u32[]{:S(2)}) collective-permute-start(bf16[256,512]{1,0:T(8,128)(2,1)S(1)} %collective-permute-done.2), channel_id=1, source_target_pairs={{31,1},{4,2},{3,5},{8,6},{7,9},{12,10},{11,13},{16,14},{15,17},{20... | collective-permute-start | bytes 786440 | tf_op jit(solution)/shard_map/ppermute | solution.py:48
  78.3 0.7 copy-start.2
  94.6 1.2 collective-permute-start.8
  95.8 4.5 %collective-permute-start.10 = (f32[1,512]{1,0:T(1,128)S(1)}, f32[1,512]{1,0:T(1,128)S(1)}, u32[]{:S(2)}, u32[]{:S(2)}) collective-permute-start(f32[1,512]{1,0:T(1,128)S(1)} %add.21), channel_id=1, source_target_pairs={{0,16},{1,17},{2,18},{3,19},{4,20},{5,21},{6,22},{7,23},{8,24},{9,... | collective-permute-start | bytes 6152 | tf_op jit(solution)/shard_map/ppermute | solution.py:52
  96.7 5.4 %collective-permute-start.11 = (f32[1,512]{1,0:T(1,128)S(1)}, f32[1,512]{1,0:T(1,128)S(1)}, u32[]{:S(2)}, u32[]{:S(2)}) collective-permute-start(f32[1,512]{1,0:T(1,128)S(1)} %add.21), channel_id=1, source_target_pairs={{0,24},{1,25},{2,26},{3,27},{4,28},{5,29},{6,30},{7,31},{8,16},{9,... | collective-permute-start | bytes 6152 | tf_op jit(solution)/shard_map/ppermute | solution.py:52
  98.0 4.0 %collective-permute-start.9 = (f32[1,512]{1,0:T(1,128)S(1)}, f32[1,512]{1,0:T(1,128)S(1)}, u32[]{:S(2)}, u32[]{:S(2)}) collective-permute-start(f32[1,512]{1,0:T(1,128)S(1)} %add.21), channel_id=1, source_target_pairs={{0,8},{1,9},{2,10},{3,11},{4,12},{5,13},{6,14},{7,15},{8,0},{9,1},... | collective-permute-start | bytes 6152 | tf_op jit(solution)/shard_map/ppermute | solution.py:52
  105.6 6.6 %collective-permute-start.12 = (bf16[81,128,128]{2,1,0:T(8,128)(2,1)S(1)}, bf16[81,128,128]{2,1,0:T(8,128)(2,1)S(1)}, u32[]{:S(2)}, u32[]{:S(2)}) collective-permute-start(bf16[81,128,128]{2,1,0:T(8,128)(2,1)S(1)} %collective-permute-done.6.source_a), channel_id=1, source_target_pairs={{1,0},{0,1},{3,2},{2,3},{5,4},{4,5},{7,6},{6,7},{9,8},{8,9},{11,10... | collective-permute-start | bytes 7962632 | tf_op jit(solution)/shard_map/ppermute | solution.py:48
  107.6 13.7 %collective-permute-start.13 = (f32[1,512]{1,0:T(1,128)S(1)}, f32[1,512]{1,0:T(1,128)S(1)}, u32[]{:S(2)}, u32[]{:S(2)}) collective-permute-start(f32[1,512]{1,0:T(1,128)S(1)} %add_add_fusion), channel_id=1, source_target_pairs={{0,2},{1,3},{2,0},{3,1},{4,6},{5,7},{6,4},{7,5},{8,10},{9,11},{10,... | collective-permute-start | bytes 6152 | tf_op jit(solution)/shard_map/ppermute | solution.py:52
  109.5 11.8 %collective-permute-start.14 = (f32[1,512]{1,0:T(1,128)S(1)}, f32[1,512]{1,0:T(1,128)S(1)}, u32[]{:S(2)}, u32[]{:S(2)}) collective-permute-start(f32[1,512]{1,0:T(1,128)S(1)} %add_add_fusion), channel_id=1, source_target_pairs={{0,4},{1,5},{2,6},{3,7},{4,0},{5,1},{6,2},{7,3},{8,12},{9,13},{10,... | collective-permute-start | bytes 6152 | tf_op jit(solution)/shard_map/ppermute | solution.py:52
  109.5 11.8 %collective-permute-start.15 = (f32[1,512]{1,0:T(1,128)S(1)}, f32[1,512]{1,0:T(1,128)S(1)}, u32[]{:S(2)}, u32[]{:S(2)}) collective-permute-start(f32[1,512]{1,0:T(1,128)S(1)} %add_add_fusion), channel_id=1, source_target_pairs={{0,6},{1,7},{2,4},{3,5},{4,2},{5,3},{6,0},{7,1},{8,14},{9,15},{10,... | collective-permute-start | bytes 6152 | tf_op jit(solution)/shard_map/ppermute | solution.py:52

commit v12 on v11

--- a/solution.py
+++ b/solution.py
@@ -318,12 +318,10 @@
         add_trace(trace, jnp.float32(2), rows[:half], corner[:, :half])
 
 
-def last_body(z, left_in, positions, prev, source_a, source_b, out, left, stage, right, total, out_stage,
-              prev_stage, vector, scalars, left_sem, in_sem, prev_sem, place_sem, out_sems):
+def last_body(z, left_in, positions, prev, source_a, source_b, out, left, right, total, out_stage,
+              prev_stage, vector, scalars, left_sem, prev_sem, place_sem, out_sems):
     kind = lax.axis_index(AXES) % 4
     copies = [
-        pltpu.make_async_copy(source_a, stage.at[0], in_sem.at[0]),
-        pltpu.make_async_copy(source_b, stage.at[1], in_sem.at[1]),
         pltpu.make_async_copy(left_in, left, left_sem),
         pltpu.make_async_copy(prev, prev_stage, prev_sem),
     ]
@@ -349,23 +347,22 @@
     total[:, z.window * z.block:] = jnp.zeros((z.span, z.block), jnp.float32)
     decodings = []
     for index in range(2):
-        copies[index].wait()
         decodings.append(decode(
-            z, stage.at[index, z.rows * z.slots], places[index], vector.at[index], scalars.at[index],
+            z, (source_a, source_b)[index].at[z.rows * z.slots], places[index], vector.at[index], scalars.at[index],
             place_sem.at[index],
         ))
     lax.fori_loop(low, high, clear_right, 0)
     for index in range(2):
         decodings[index].wait()
-        scatter(z, right, index * z.span, stage.at[index], lambda r, u: scalars[index, r, u])
-    copies[2].wait()
+        scatter(z, right, index * z.span, (source_a, source_b)[index], lambda r, u: scalars[index, r, u])
+    copies[0].wait()
 
     def multiply(n, carry):
         total[:, chunk(n)] = jnp.dot(left[...], right[:, chunk(n)], preferred_element_type=jnp.float32)
         return carry
 
     lax.fori_loop(low, high, multiply, 0)
-    copies[3].wait()
+    copies[1].wait()
     emit(z, total, positions, out_stage, out, out_sems, prev_stage)
 
 
@@ -475,14 +472,14 @@
     others = [fetch(trace, step) for step in (steps[1], steps[2], steps[1] + steps[2])]
     square = call(
         z, functools.partial(last_body, z), [relay_left, positions, total, relay, relay_beside],
-        [ANY, SMEM, ANY, ANY, ANY],
+        [ANY, SMEM, ANY, VMEM, VMEM],
         [shape(tiles.shape, dtype)],
         [ANY],
         [
-            pltpu.VMEM((z.span, 2 * z.span), dtype), pltpu.VMEM((2,) + payload_shape, dtype),
+            pltpu.VMEM((z.span, 2 * z.span), dtype),
             pltpu.VMEM((2 * z.span, z.wide), dtype), total_buffer,
             pltpu.VMEM(tiles.shape, dtype), pltpu.VMEM(tiles.shape, jnp.float32), *places,
-            DMA, DMA((2,)), DMA, DMA((2,)), DMA((z.rows,)),
+            DMA, DMA, DMA((2,)), DMA((z.rows,)),
         ],
         2, 44 * 1024 * 1024,
     )[0]

time: 124 us -> 124 us (level)
  no operation moved by 1% of the time
where the time goes in v12:
time: 124 us; the launch traced here: 123 us
  Pallas kernels  48.6 us (39%)
  waiting for transfers between devices  40.7 us (33%)
  starting transfers between devices  30 us (24%)
  between operations  2.6 us (2%)
    pallas_call x6, Pallas kernels, call(): pl.pallas_call(kernel, out_shape=out_shape, in_specs=in_specs, out_specs=...  48.6 us
    ppermute x9, waiting for transfers between devices, receive(): return lax.ppermute(shard, AXES, pairs)  36.8 us
    ppermute x9, starting transfers between devices, receive(): return lax.ppermute(shard, AXES, pairs)  22.9 us
    ppermute x7, starting transfers between devices, fetch(): lax.ppermute(value, AXES, [(d, d ^ step) for d in range(lax.axis_size(AXE...  7.05 us
    ppermute x7, waiting for transfers between devices, fetch(): lax.ppermute(value, AXES, [(d, d ^ step) for d in range(lax.axis_size(AXE...  3.93 us
  transfers between devices with their start and end apart: 16, of which 7 were waited for; matrix products, arithmetic and copies ran while one was open for 0% of the time, Pallas kernels for 37%

profile of v12, /device:TPU:0, one launch (start us, length us, event | category | flops | bytes accessed | tf_op | source)
XLA Modules:
  0.0 123.2 jit_solution(8960902447979609595)
XLA Ops:
  0.6 3.4 %shard_map.42 = bf16[81,128,128]{2,1,0:T(8,128)(2,1)} custom-call(bf16[4,20,128,128]{3,2,1,0:T(8,128)(2,1)} %tiles.1, s32[4,20]{1,0:T(4,128)} %columns.3), custom_call_target="tpu_custom_call" | custom-call | bytes 10485760 | tf_op jit(solution)/shard_map/pallas_call | solution.py:376
  4.0 0.5 collective-permute-start.3
  4.5 5.7 %collective-permute-start = (bf16[81,128,128]{2,1,0:T(8,128)(2,1)}, bf16[81,128,128]{2,1,0:T(8,128)(2,1)S(1)}, u32[]{:S(2)}, u32[]{:S(2)}) collective-permute-start(bf16[81,128,128]{2,1,0:T(8,128)(2,1)} %shard_map.42), channel_id=1, source_target_pairs={{2,0},{4,1},{31,2},{1,3},{6,4},{8,5},{3,6},{5,7},{10,8},{12,9},{7,... | collective-permute-start | bytes 7962632 | tf_op jit(solution)/shard_map/ppermute | solution.py:48
  10.2 0.0 collective-permute-start.1
  10.2 9.7 %shard_map.41 = (f32[4,20,128,128]{3,2,1,0:T(8,128)}, bf16[512,3712]{1,0:T(8,128)(2,1)}, bf16[256,512]{1,0:T(8,128)(2,1)}, s32[4,20]{1,0:T(4,128)}, f32[1,512]{1,0:T(1,128)}) custom-call(bf16[4,20,128,128]{3,2,1,0:T(8,128)(2,1)} %tiles.1, s32[4,20]{1,0:T(4,128)} %columns.3), custom_call_target="tpu_custom_call" | custom-call | flops 1879048192 | bytes 13107200 | tf_op jit(solution)/shard_map/pallas_call | solution.py:376
  19.9 1.3 %collective-permute-start.2 = (bf16[256,512]{1,0:T(8,128)(2,1)}, bf16[256,512]{1,0:T(8,128)(2,1)S(1)}, u32[]{:S(2)}, u32[]{:S(2)}) collective-permute-start(bf16[256,512]{1,0:T(8,128)(2,1)} %get-tuple-element.27), channel_id=1, source_target_pairs={{1,0},{2,3},{5,4},{6,7},{9,8},{10,11},{13,12},{14,15},{17,16},{18,... | collective-permute-start | bytes 786440 | tf_op jit(solution)/shard_map/ppermute | solution.py:48
  21.2 0.0 collective-permute-done.3.refs_0_
  21.2 0.0 copy-start.1
  21.2 11.4 %shard_map.43 = (f32[4,20,128,128]{3,2,1,0:T(8,128)}, f32[1,512]{1,0:T(1,128)}) custom-call(bf16[512,3712]{1,0:T(8,128)(2,1)} %get-tuple-element.25.left_in.left, s32[4,20]{1,0:T(4,128)} %get-tuple-element.26.positions, f32[4,20,128,128]{3,2,1,0:T(8,128)} %get-tuple-element.28.prev, f32[1,512]{1,0:T(1,128)} %get-tuple-element.29.trace_in, ...), custom_call_target="tpu_custom_call" | custom-call | flops 1879048192 | bytes 13107200 | tf_op jit(solution)/shard_map/pallas_call | solution.py:376
  32.6 0.0 collective-permute-done.2
  32.6 31.9 %collective-permute-done.refs_0_ = bf16[81,128,128]{2,1,0:T(8,128)(2,1)S(1)} collective-permute-done((bf16[81,128,128]{2,1,0:T(8,128)(2,1)}, bf16[81,128,128]{2,1,0:T(8,128)(2,1)S(1)}, u32[]{:S(2)}, u32[]{:S(2)}) %collective-permute-start) | collective-permute-done | bytes 2654240 | tf_op jit(solution)/shard_map/ppermute | solution.py:48
  64.5 0.3 collective-permute-done.1.refs_1_
  64.8 0.0 copy-start
  64.8 3.1 %collective-permute-start.4 = (bf16[81,128,128]{2,1,0:T(8,128)(2,1)S(1)}, bf16[81,128,128]{2,1,0:T(8,128)(2,1)S(1)}, u32[]{:S(2)}, u32[]{:S(2)}) collective-permute-start(bf16[81,128,128]{2,1,0:T(8,128)(2,1)S(1)} %collective-permute-done.refs_0_), channel_id=1, source_target_pairs={{0,1},{3,2},{4,5},{7,6},{8,9},{11,10},{12,13},{15,14},{16,17},{19,... | collective-permute-start | bytes 7962632 | tf_op jit(solution)/shard_map/ppermute | solution.py:48
  68.0 1.3 %collective-permute-start.5 = (bf16[81,128,128]{2,1,0:T(8,128)(2,1)}, bf16[81,128,128]{2,1,0:T(8,128)(2,1)S(1)}, u32[]{:S(2)}, u32[]{:S(2)}) collective-permute-start(bf16[81,128,128]{2,1,0:T(8,128)(2,1)} %collective-permute-done.1.refs_1_), channel_id=1, source_target_pairs={{1,0},{2,3},{5,4},{6,7},{9,8},{10,11},{13,12},{14,15},{17,16},{18,... | collective-permute-start | bytes 7962632 | tf_op jit(solution)/shard_map/ppermute | solution.py:48
  69.3 3.0 %collective-permute-start.6 = (bf16[81,128,128]{2,1,0:T(8,128)(2,1)S(1)}, bf16[81,128,128]{2,1,0:T(8,128)(2,1)S(1)}, u32[]{:S(2)}, u32[]{:S(2)}) collective-permute-start(bf16[81,128,128]{2,1,0:T(8,128)(2,1)S(1)} %collective-permute-done.refs_0_), channel_id=1, source_target_pairs={{2,0},{28,1},{7,2},{1,3},{6,4},{0,5},{11,6},{5,7},{10,8},{4,9},{15... | collective-permute-start | bytes 7962632 | tf_op jit(solution)/shard_map/ppermute | solution.py:48
  72.3 5.9 %collective-permute-start.7 = (bf16[256,512]{1,0:T(8,128)(2,1)S(1)}, bf16[256,512]{1,0:T(8,128)(2,1)S(1)}, u32[]{:S(2)}, u32[]{:S(2)}) collective-permute-start(bf16[256,512]{1,0:T(8,128)(2,1)S(1)} %collective-permute-done.2), channel_id=1, source_target_pairs={{31,1},{4,2},{3,5},{8,6},{7,9},{12,10},{11,13},{16,14},{15,17},{20... | collective-permute-start | bytes 786440 | tf_op jit(solution)/shard_map/ppermute | solution.py:48
  78.2 0.0 collective-permute-done.4.refs_2_
  78.3 0.0 collective-permute-done.5.refs_3_
  78.3 0.0 copy-done.1
  78.3 0.0 copy-start.2
  78.3 0.7 copy-done.2
  79.0 15.5 %shard_map.44 = (f32[4,20,128,128]{3,2,1,0:T(8,128)}, f32[1,512]{1,0:T(1,128)S(1)}, bf16[512,1024]{1,0:T(8,128)(2,1)S(1)}) custom-call(bf16[512,3712]{1,0:T(8,128)(2,1)} %get-tuple-element.25.left_in.left, s32[4,20]{1,0:T(4,128)S(1)} %copy-done.1, f32[4,20,128,128]{3,2,1,0:T(8,128)} %get-tuple-element.32.prev, f32[1,512]{1,0:T(1,128)S(1)} %copy-done.2, ...), custom_call_target="tpu_custom_call" | custom-call | flops 5637144576 | bytes 18350080 | tf_op jit(solution)/shard_map/pallas_call | solution.py:376
  94.5 0.0 collective-permute-done.7.corner
  94.5 0.0 copy-done
  94.6 0.1 collective-permute-start.8
  94.6 1.1 collective-permute-done.8
  95.8 0.9 collective-permute-start.10
  96.7 1.4 %collective-permute-start.11 = (f32[1,512]{1,0:T(1,128)S(1)}, f32[1,512]{1,0:T(1,128)S(1)}, u32[]{:S(2)}, u32[]{:S(2)}) collective-permute-start(f32[1,512]{1,0:T(1,128)S(1)} %add.21), channel_id=1, source_target_pairs={{0,24},{1,25},{2,26},{3,27},{4,28},{5,29},{6,30},{7,31},{8,16},{9,... | collective-permute-start | bytes 6152 | tf_op jit(solution)/shard_map/ppermute | solution.py:52
  98.0 1.2 %collective-permute-start.9 = (f32[1,512]{1,0:T(1,128)S(1)}, f32[1,512]{1,0:T(1,128)S(1)}, u32[]{:S(2)}, u32[]{:S(2)}) collective-permute-start(f32[1,512]{1,0:T(1,128)S(1)} %add.21), channel_id=1, source_target_pairs={{0,8},{1,9},{2,10},{3,11},{4,12},{5,13},{6,14},{7,15},{8,0},{9,1},... | collective-permute-start | bytes 6152 | tf_op jit(solution)/shard_map/ppermute | solution.py:52
  99.3 1.0 collective-permute-done.10
  100.3 1.8 %collective-permute-done.11 = f32[1,512]{1,0:T(1,128)S(1)} collective-permute-done((f32[1,512]{1,0:T(1,128)S(1)}, f32[1,512]{1,0:T(1,128)S(1)}, u32[]{:S(2)}, u32[]{:S(2)}) %collective-permute-start.11) | collective-permute-done | bytes 2080 | tf_op jit(solution)/shard_map/ppermute | solution.py:52
  102.1 0.0 collective-permute-done.9
  102.1 3.5 %collective-permute-done.6.source_a = bf16[81,128,128]{2,1,0:T(8,128)(2,1)S(1)} collective-permute-done((bf16[81,128,128]{2,1,0:T(8,128)(2,1)S(1)}, bf16[81,128,128]{2,1,0:T(8,128)(2,1)S(1)}, u32[]{:S(2)}, u32[]{:S(2)}) %collective-permute-start.6) | collective-permute-done | bytes 2654240 | tf_op jit(solution)/shard_map/ppermute | solution.py:48
  105.6 2.1 %collective-permute-start.12 = (bf16[81,128,128]{2,1,0:T(8,128)(2,1)S(1)}, bf16[81,128,128]{2,1,0:T(8,128)(2,1)S(1)}, u32[]{:S(2)}, u32[]{:S(2)}) collective-permute-start(bf16[81,128,128]{2,1,0:T(8,128)(2,1)S(1)} %collective-permute-done.6.source_a), channel_id=1, source_target_pairs={{1,0},{0,1},{3,2},{2,3},{5,4},{4,5},{7,6},{6,7},{9,8},{8,9},{11,10... | collective-permute-start | bytes 7962632 | tf_op jit(solution)/shard_map/ppermute | solution.py:48
  107.6 1.9 %collective-permute-start.13 = (f32[1,512]{1,0:T(1,128)S(1)}, f32[1,512]{1,0:T(1,128)S(1)}, u32[]{:S(2)}, u32[]{:S(2)}) collective-permute-start(f32[1,512]{1,0:T(1,128)S(1)} %add_add_fusion), channel_id=1, source_target_pairs={{0,2},{1,3},{2,0},{3,1},{4,6},{5,7},{6,4},{7,5},{8,10},{9,11},{10,... | collective-permute-start | bytes 6152 | tf_op jit(solution)/shard_map/ppermute | solution.py:52
  109.5 0.0 collective-permute-start.14
  109.5 1.6 %collective-permute-start.15 = (f32[1,512]{1,0:T(1,128)S(1)}, f32[1,512]{1,0:T(1,128)S(1)}, u32[]{:S(2)}, u32[]{:S(2)}) collective-permute-start(f32[1,512]{1,0:T(1,128)S(1)} %add_add_fusion), channel_id=1, source_target_pairs={{0,6},{1,7},{2,4},{3,5},{4,2},{5,3},{6,0},{7,1},{8,14},{9,15},{10,... | collective-permute-start | bytes 6152 | tf_op jit(solution)/shard_map/ppermute | solution.py:52
  111.1 1.1 collective-permute-done.12.source_b
  112.2 8.6 %shard_map.46 = bf16[4,20,128,128]{3,2,1,0:T(8,128)(2,1)} custom-call(bf16[512,1024]{1,0:T(8,128)(2,1)S(1)} %get-tuple-element.36.left_in, s32[4,20]{1,0:T(4,128)S(1)} %copy-done.1, f32[4,20,128,128]{3,2,1,0:T(8,128)} %get-tuple-element.40.prev, bf16[81,128,128]{2,1,0:T(8,128)(2,1)S(1)} %collective-permute-done.6.source_a, ...), custom_call_target="tpu_custom_call" | custom-call | flops 3758096384 | bytes 15728640 | tf_op jit(solution)/shard_map/pallas_call | solution.py:376
  120.8 0.0 collective-permute-done.13
  120.8 0.0 collective-permute-done.14
  120.8 0.0 collective-permute-done.15
  120.9 0.6 add_reduce_fusion
  (3 shorter events, 0.0 us)
Async XLA Ops:
  4.0 17.2 %collective-permute-start.3 = (bf16[81,128,128]{2,1,0:T(8,128)(2,1)}, bf16[81,128,128]{2,1,0:T(8,128)(2,1)}, u32[]{:S(2)}, u32[]{:S(2)}) collective-permute-start(bf16[81,128,128]{2,1,0:T(8,128)(2,1)} %shard_map.42), channel_id=1, source_target_pairs={{1,0},{0,1},{3,2},{2,3},{5,4},{4,5},{7,6},{6,7},{9,8},{8,9},{11,10... | collective-permute-start | bytes 7962632 | tf_op jit(solution)/shard_map/ppermute | solution.py:48
  4.5 60.0 %collective-permute-start = (bf16[81,128,128]{2,1,0:T(8,128)(2,1)}, bf16[81,128,128]{2,1,0:T(8,128)(2,1)S(1)}, u32[]{:S(2)}, u32[]{:S(2)}) collective-permute-start(bf16[81,128,128]{2,1,0:T(8,128)(2,1)} %shard_map.42), channel_id=1, source_target_pairs={{2,0},{4,1},{31,2},{1,3},{6,4},{8,5},{3,6},{5,7},{10,8},{12,9},{7,... | collective-permute-start | bytes 7962632 | tf_op jit(solution)/shard_map/ppermute | solution.py:48
  10.2 54.6 %collective-permute-start.1 = (bf16[81,128,128]{2,1,0:T(8,128)(2,1)}, bf16[81,128,128]{2,1,0:T(8,128)(2,1)}, u32[]{:S(2)}, u32[]{:S(2)}) collective-permute-start(bf16[81,128,128]{2,1,0:T(8,128)(2,1)} %shard_map.42), channel_id=1, source_target_pairs={{29,0},{3,1},{0,2},{6,3},{1,4},{7,5},{4,6},{10,7},{5,8},{11,9},{8,... | collective-permute-start | bytes 7962632 | tf_op jit(solution)/shard_map/ppermute | solution.py:48
  19.9 12.7 %collective-permute-start.2 = (bf16[256,512]{1,0:T(8,128)(2,1)}, bf16[256,512]{1,0:T(8,128)(2,1)S(1)}, u32[]{:S(2)}, u32[]{:S(2)}) collective-permute-start(bf16[256,512]{1,0:T(8,128)(2,1)} %get-tuple-element.27), channel_id=1, source_target_pairs={{1,0},{2,3},{5,4},{6,7},{9,8},{10,11},{13,12},{14,15},{17,16},{18,... | collective-permute-start | bytes 786440 | tf_op jit(solution)/shard_map/ppermute | solution.py:48
  21.2 57.1 %copy-start.1 = (s32[4,20]{1,0:T(4,128)S(1)}, s32[4,20]{1,0:T(4,128)}, u32[]{:S(2)}) copy-start(s32[4,20]{1,0:T(4,128)} %get-tuple-element.26.positions) | copy-start | bytes 964
  64.8 29.7 %copy-start = (bf16[512,3712]{1,0:T(8,128)(2,1)S(1)}, bf16[512,3712]{1,0:T(8,128)(2,1)}, u32[]{:S(2)}) copy-start(bf16[512,3712]{1,0:T(8,128)(2,1)} %get-tuple-element.25.left_in.left) | copy-start | bytes 11403268
  64.8 13.4 %collective-permute-start.4 = (bf16[81,128,128]{2,1,0:T(8,128)(2,1)S(1)}, bf16[81,128,128]{2,1,0:T(8,128)(2,1)S(1)}, u32[]{:S(2)}, u32[]{:S(2)}) collective-permute-start(bf16[81,128,128]{2,1,0:T(8,128)(2,1)S(1)} %collective-permute-done.refs_0_), channel_id=1, source_target_pairs={{0,1},{3,2},{4,5},{7,6},{8,9},{11,10},{12,13},{15,14},{16,17},{19,... | collective-permute-start | bytes 7962632 | tf_op jit(solution)/shard_map/ppermute | solution.py:48
  68.0 10.3 %collective-permute-start.5 = (bf16[81,128,128]{2,1,0:T(8,128)(2,1)}, bf16[81,128,128]{2,1,0:T(8,128)(2,1)S(1)}, u32[]{:S(2)}, u32[]{:S(2)}) collective-permute-start(bf16[81,128,128]{2,1,0:T(8,128)(2,1)} %collective-permute-done.1.refs_1_), channel_id=1, source_target_pairs={{1,0},{2,3},{5,4},{6,7},{9,8},{10,11},{13,12},{14,15},{17,16},{18,... | collective-permute-start | bytes 7962632 | tf_op jit(solution)/shard_map/ppermute | solution.py:48
  69.3 36.3 %collective-permute-start.6 = (bf16[81,128,128]{2,1,0:T(8,128)(2,1)S(1)}, bf16[81,128,128]{2,1,0:T(8,128)(2,1)S(1)}, u32[]{:S(2)}, u32[]{:S(2)}) collective-permute-start(bf16[81,128,128]{2,1,0:T(8,128)(2,1)S(1)} %collective-permute-done.refs_0_), channel_id=1, source_target_pairs={{2,0},{28,1},{7,2},{1,3},{6,4},{0,5},{11,6},{5,7},{10,8},{4,9},{15... | collective-permute-start | bytes 7962632 | tf_op jit(solution)/shard_map/ppermute | solution.py:48
  72.3 22.2 %collective-permute-start.7 = (bf16[256,512]{1,0:T(8,128)(2,1)S(1)}, bf16[256,512]{1,0:T(8,128)(2,1)S(1)}, u32[]{:S(2)}, u32[]{:S(2)}) collective-permute-start(bf16[256,512]{1,0:T(8,128)(2,1)S(1)} %collective-permute-done.2), channel_id=1, source_target_pairs={{31,1},{4,2},{3,5},{8,6},{7,9},{12,10},{11,13},{16,14},{15,17},{20... | collective-permute-start | bytes 786440 | tf_op jit(solution)/shard_map/ppermute | solution.py:48
  78.3 0.7 copy-start.2
  94.6 1.2 collective-permute-start.8
  95.8 4.5 %collective-permute-start.10 = (f32[1,512]{1,0:T(1,128)S(1)}, f32[1,512]{1,0:T(1,128)S(1)}, u32[]{:S(2)}, u32[]{:S(2)}) collective-permute-start(f32[1,512]{1,0:T(1,128)S(1)} %add.21), channel_id=1, source_target_pairs={{0,16},{1,17},{2,18},{3,19},{4,20},{5,21},{6,22},{7,23},{8,24},{9,... | collective-permute-start | bytes 6152 | tf_op jit(solution)/shard_map/ppermute | solution.py:52
  96.7 5.4 %collective-permute-start.11 = (f32[1,512]{1,0:T(1,128)S(1)}, f32[1,512]{1,0:T(1,128)S(1)}, u32[]{:S(2)}, u32[]{:S(2)}) collective-permute-start(f32[1,512]{1,0:T(1,128)S(1)} %add.21), channel_id=1, source_target_pairs={{0,24},{1,25},{2,26},{3,27},{4,28},{5,29},{6,30},{7,31},{8,16},{9,... | collective-permute-start | bytes 6152 | tf_op jit(solution)/shard_map/ppermute | solution.py:52
  98.0 4.0 %collective-permute-start.9 = (f32[1,512]{1,0:T(1,128)S(1)}, f32[1,512]{1,0:T(1,128)S(1)}, u32[]{:S(2)}, u32[]{:S(2)}) collective-permute-start(f32[1,512]{1,0:T(1,128)S(1)} %add.21), channel_id=1, source_target_pairs={{0,8},{1,9},{2,10},{3,11},{4,12},{5,13},{6,14},{7,15},{8,0},{9,1},... | collective-permute-start | bytes 6152 | tf_op jit(solution)/shard_map/ppermute | solution.py:52
  105.6 6.6 %collective-permute-start.12 = (bf16[81,128,128]{2,1,0:T(8,128)(2,1)S(1)}, bf16[81,128,128]{2,1,0:T(8,128)(2,1)S(1)}, u32[]{:S(2)}, u32[]{:S(2)}) collective-permute-start(bf16[81,128,128]{2,1,0:T(8,128)(2,1)S(1)} %collective-permute-done.6.source_a), channel_id=1, source_target_pairs={{1,0},{0,1},{3,2},{2,3},{5,4},{4,5},{7,6},{6,7},{9,8},{8,9},{11,10... | collective-permute-start | bytes 7962632 | tf_op jit(solution)/shard_map/ppermute | solution.py:48
  107.6 13.2 %collective-permute-start.13 = (f32[1,512]{1,0:T(1,128)S(1)}, f32[1,512]{1,0:T(1,128)S(1)}, u32[]{:S(2)}, u32[]{:S(2)}) collective-permute-start(f32[1,512]{1,0:T(1,128)S(1)} %add_add_fusion), channel_id=1, source_target_pairs={{0,2},{1,3},{2,0},{3,1},{4,6},{5,7},{6,4},{7,5},{8,10},{9,11},{10,... | collective-permute-start | bytes 6152 | tf_op jit(solution)/shard_map/ppermute | solution.py:52
  109.5 11.3 %collective-permute-start.14 = (f32[1,512]{1,0:T(1,128)S(1)}, f32[1,512]{1,0:T(1,128)S(1)}, u32[]{:S(2)}, u32[]{:S(2)}) collective-permute-start(f32[1,512]{1,0:T(1,128)S(1)} %add_add_fusion), channel_id=1, source_target_pairs={{0,4},{1,5},{2,6},{3,7},{4,0},{5,1},{6,2},{7,3},{8,12},{9,13},{10,... | collective-permute-start | bytes 6152 | tf_op jit(solution)/shard_map/ppermute | solution.py:52
  109.5 11.3 %collective-permute-start.15 = (f32[1,512]{1,0:T(1,128)S(1)}, f32[1,512]{1,0:T(1,128)S(1)}, u32[]{:S(2)}, u32[]{:S(2)}) collective-permute-start(f32[1,512]{1,0:T(1,128)S(1)} %add_add_fusion), channel_id=1, source_target_pairs={{0,6},{1,7},{2,4},{3,5},{4,2},{5,3},{6,0},{7,1},{8,14},{9,15},{10,... | collective-permute-start | bytes 6152 | tf_op jit(solution)/shard_map/ppermute | solution.py:52

commit v13 on v12

--- a/solution.py
+++ b/solution.py
@@ -450,14 +450,19 @@
     total, trace = near(("beside",), [beside], total, trace)
     first, second, corner, total, trace = lax.optimization_barrier((first, second, corner, total, trace))
     relay = receive(first, RELAY_FROM)
-    mixed = [
-        receive(first, PARTNER, [m for m in range(4) if not USE_SECOND[m]]),
-        receive(second, PARTNER, [m for m in range(4) if USE_SECOND[m]]),
-    ]
     corner = receive(corner, (0, -2, 2, 0), (LOWER, UPPER))
-    total, trace, relay_left = near(
-        ("first", "second", "mixed"), [first, second, *mixed], total, trace, True
-    )
+
+    def nearby(first, second, total, trace):
+        mixed = [
+            receive(first, PARTNER, [m for m in range(4) if not USE_SECOND[m]]),
+            receive(second, PARTNER, [m for m in range(4) if USE_SECOND[m]]),
+        ]
+        return tuple(near(("first", "second", "mixed"), [first, second, *mixed], total, trace, True))
+
+    def nothing(first, second, total, trace):
+        return jnp.zeros_like(total), jnp.zeros_like(trace), jnp.zeros((z.span, 2 * z.span), dtype)
+
+    total, trace, relay_left = lax.cond(positions[0, 0] >= 0, nearby, nothing, first, second, total, trace)
     trace = call(
         z, functools.partial(corner_body, z), [left, corner, trace], [ANY, VMEM, VMEM], line, VMEM,
         [pltpu.VMEM((z.span, z.span // 2), dtype), DMA], 0,

time: 124 us -> 125 us (level)
  local copies, waits for them, and re-layouts: 0.67 us -> 2.01 us
    ppermute x9, starting transfers between devices: 22.9 us -> 18.5 us  [receive(): return lax.ppermute(shard, AXES, pairs)]
    ppermute x7, starting transfers between devices: 7.05 us -> 10.3 us  [fetch(): lax.ppermute(value, AXES, [(d, d ^ step) for d in range(lax.axis_size(AXE...]
    ppermute x9, waiting for transfers between devices: 36.8 us -> 39.2 us  [receive(): return lax.ppermute(shard, AXES, pairs)]
    ppermute x7, waiting for transfers between devices: 3.93 us -> 2.39 us  [fetch(): lax.ppermute(value, AXES, [(d, d ^ step) for d in range(lax.axis_size(AXE...]
  transfers between devices with their start and end apart: 16 -> 16, of which waited for: 7 -> 8; matrix products, arithmetic and copies ran while one was open for 0% -> 0% of each run, Pallas kernels for 37% -> 36%
where the time goes in v13:
time: 125 us
  Pallas kernels  48.7 us (39%)
  waiting for transfers between devices  41.6 us (33%)
  starting transfers between devices  28.8 us (23%)
  between operations  3.22 us (3%)
  local copies, waits for them, and re-layouts  2.01 us (2%)
    pallas_call x6, Pallas kernels, call(): pl.pallas_call(kernel, out_shape=out_shape, in_specs=in_specs, out_specs=...  48.7 us
    ppermute x9, waiting for transfers between devices, receive(): return lax.ppermute(shard, AXES, pairs)  39.2 us
    ppermute x9, starting transfers between devices, receive(): return lax.ppermute(shard, AXES, pairs)  18.5 us
    ppermute x7, starting transfers between devices, fetch(): lax.ppermute(value, AXES, [(d, d ^ step) for d in range(lax.axis_size(AXE...  10.3 us
  transfers between devices with their start and end apart: 16, of which 8 were waited for; matrix products, arithmetic and copies ran while one was open for 0% of the time, Pallas kernels for 36%

profile of v13, /device:TPU:0, one launch (start us, length us, event | category | flops | bytes accessed | tf_op | source)
XLA Modules:
  0.0 125.0 jit_solution(18244448853055977639)
XLA Ops:
  0.6 3.4 %shard_map.42 = bf16[81,128,128]{2,1,0:T(8,128)(2,1)} custom-call(bf16[4,20,128,128]{3,2,1,0:T(8,128)(2,1)} %tiles.1, s32[4,20]{1,0:T(4,128)} %columns.3), custom_call_target="tpu_custom_call" | custom-call | bytes 10485760 | tf_op jit(solution)/shard_map/pallas_call | solution.py:376
  4.0 0.5 collective-permute-start.5
  4.6 2.6 %collective-permute-start.3 = (bf16[81,128,128]{2,1,0:T(8,128)(2,1)}, bf16[81,128,128]{2,1,0:T(8,128)(2,1)}, u32[]{:S(2)}, u32[]{:S(2)}) collective-permute-start(bf16[81,128,128]{2,1,0:T(8,128)(2,1)} %shard_map.42), channel_id=1, source_target_pairs={{29,0},{3,1},{0,2},{6,3},{1,4},{7,5},{4,6},{10,7},{5,8},{11,9},{8,... | collective-permute-start | bytes 7962632 | tf_op jit(solution)/shard_map/ppermute | solution.py:48
  7.1 3.1 %collective-permute-start.2 = (bf16[81,128,128]{2,1,0:T(8,128)(2,1)}, bf16[81,128,128]{2,1,0:T(8,128)(2,1)}, u32[]{:S(2)}, u32[]{:S(2)}) collective-permute-start(bf16[81,128,128]{2,1,0:T(8,128)(2,1)} %shard_map.42), channel_id=1, source_target_pairs={{2,0},{4,1},{31,2},{1,3},{6,4},{8,5},{3,6},{5,7},{10,8},{12,9},{7,... | collective-permute-start | bytes 7962632 | tf_op jit(solution)/shard_map/ppermute | solution.py:48
  10.2 9.7 %shard_map.41 = (f32[4,20,128,128]{3,2,1,0:T(8,128)}, bf16[512,3712]{1,0:T(8,128)(2,1)}, bf16[256,512]{1,0:T(8,128)(2,1)}, s32[4,20]{1,0:T(4,128)S(1)}, f32[1,512]{1,0:T(1,128)}) custom-call(bf16[4,20,128,128]{3,2,1,0:T(8,128)(2,1)} %tiles.1, s32[4,20]{1,0:T(4,128)} %columns.3), custom_call_target="tpu_custom_call" | custom-call | flops 1879048192 | bytes 13107200 | tf_op jit(solution)/shard_map/pallas_call | solution.py:376
  19.9 1.3 %collective-permute-start.4 = (bf16[256,512]{1,0:T(8,128)(2,1)}, bf16[256,512]{1,0:T(8,128)(2,1)S(1)}, u32[]{:S(2)}, u32[]{:S(2)}) collective-permute-start(bf16[256,512]{1,0:T(8,128)(2,1)} %get-tuple-element.44), channel_id=1, source_target_pairs={{1,0},{2,3},{5,4},{6,7},{9,8},{10,11},{13,12},{14,15},{17,16},{18,... | collective-permute-start | bytes 786440 | tf_op jit(solution)/shard_map/ppermute | solution.py:48
  21.2 0.0 collective-permute-done.5.refs_0_
  21.2 0.0 copy-start.1
  21.3 1.5 %copy-done.1 = bf16[81,128,128]{2,1,0:T(8,128)(2,1)} copy-done((bf16[81,128,128]{2,1,0:T(8,128)(2,1)}, bf16[81,128,128]{2,1,0:T(8,128)(2,1)S(1)}, u32[]{:S(2)}) %copy-start.1) | copy-done | bytes 2654232
  22.8 10.8 %shard_map.43 = (f32[4,20,128,128]{3,2,1,0:T(8,128)}, f32[1,512]{1,0:T(1,128)S(1)}) custom-call(bf16[512,3712]{1,0:T(8,128)(2,1)} %get-tuple-element.45.left_in.left, s32[4,20]{1,0:T(4,128)S(1)} %get-tuple-element.43.positions, f32[4,20,128,128]{3,2,1,0:T(8,128)} %get-tuple-element.46.prev, f32[1,512]{1,0:T(1,128)} %get-tuple-element.47.trace_in, ...), custom_call_target="tpu_custom_call" | custom-call | flops 1879048192 | bytes 13107200 | tf_op jit(solution)/shard_map/pallas_call | solution.py:376
  33.5 0.0 collective-permute-done.4
  33.5 31.4 %collective-permute-done.3 = bf16[81,128,128]{2,1,0:T(8,128)(2,1)} collective-permute-done((bf16[81,128,128]{2,1,0:T(8,128)(2,1)}, bf16[81,128,128]{2,1,0:T(8,128)(2,1)}, u32[]{:S(2)}, u32[]{:S(2)}) %collective-permute-start.3) | collective-permute-done | bytes 2654240 | tf_op jit(solution)/shard_map/ppermute | solution.py:48
  64.9 0.7 collective-permute-done.2
  65.6 0.5 collective-permute-start.6
  66.1 7.7 %collective-permute-start.7 = (bf16[256,512]{1,0:T(8,128)(2,1)S(1)}, bf16[256,512]{1,0:T(8,128)(2,1)S(1)}, u32[]{:S(2)}, u32[]{:S(2)}) collective-permute-start(bf16[256,512]{1,0:T(8,128)(2,1)S(1)} %collective-permute-done.4), channel_id=1, source_target_pairs={{31,1},{4,2},{3,5},{8,6},{7,9},{12,10},{11,13},{16,14},{15,17},{20... | collective-permute-start | bytes 786440 | tf_op jit(solution)/shard_map/ppermute | solution.py:48
  73.8 0.5 slice.3
  75.0 24.7 %conditional.1 = ((f32[4,20,128,128]{3,2,1,0:T(8,128)}, f32[1,512]{1,0:T(1,128)S(1)}, bf16[512,1024]{1,0:T(8,128)(2,1)})) conditional(s32[]{:T(128)} %bitcast, () %tuple.18, (bf16[81,128,128]{2,1,0:T(8,128)(2,1)}, bf16[81,128,128]{2,1,0:T(8,128)(2,1)}, bf16[512,3712]{1,0:T(8,128)(2,1)}, s32[4,20]{1,0:T(4,128)S(1)}, f32[4,20,128,128]{3,2,1,0:T(8,128)}, ...), branch_computations={%region_0.0_spmd, %region_1.0_spmd} | conditional | flops 5637144576 | bytes 39583832 | solution.py:465
  75.0 1.5 %collective-permute-start = (bf16[81,128,128]{2,1,0:T(8,128)(2,1)}, bf16[81,128,128]{2,1,0:T(8,128)(2,1)S(1)}, u32[]{:S(2)}, u32[]{:S(2)}) collective-permute-start(bf16[81,128,128]{2,1,0:T(8,128)(2,1)} %get-tuple-element.16.refs_0_), channel_id=1, source_target_pairs={{0,1},{3,2},{4,5},{7,6},{8,9},{11,10},{12,13},{15,14},{16,17},{19,... | collective-permute-start | bytes 7962632 | tf_op jit(solution)/shard_map/cond/branch_1_fun/ppermute | solution.py:48
  76.4 1.3 %collective-permute-start.1 = (bf16[81,128,128]{2,1,0:T(8,128)(2,1)}, bf16[81,128,128]{2,1,0:T(8,128)(2,1)S(1)}, u32[]{:S(2)}, u32[]{:S(2)}) collective-permute-start(bf16[81,128,128]{2,1,0:T(8,128)(2,1)} %get-tuple-element.17.refs_1_), channel_id=1, source_target_pairs={{1,0},{2,3},{5,4},{6,7},{9,8},{10,11},{13,12},{14,15},{17,16},{18,... | collective-permute-start | bytes 7962632 | tf_op jit(solution)/shard_map/cond/branch_1_fun/ppermute | solution.py:48
  77.7 3.3 %collective-permute-done.refs_2_ = bf16[81,128,128]{2,1,0:T(8,128)(2,1)S(1)} collective-permute-done((bf16[81,128,128]{2,1,0:T(8,128)(2,1)}, bf16[81,128,128]{2,1,0:T(8,128)(2,1)S(1)}, u32[]{:S(2)}, u32[]{:S(2)}) %collective-permute-start) | collective-permute-done | bytes 2654240 | tf_op jit(solution)/shard_map/cond/branch_1_fun/ppermute | solution.py:48
  81.1 2.5 %collective-permute-done.1.refs_3_ = bf16[81,128,128]{2,1,0:T(8,128)(2,1)S(1)} collective-permute-done((bf16[81,128,128]{2,1,0:T(8,128)(2,1)}, bf16[81,128,128]{2,1,0:T(8,128)(2,1)S(1)}, u32[]{:S(2)}, u32[]{:S(2)}) %collective-permute-start.1) | collective-permute-done | bytes 2654240 | tf_op jit(solution)/shard_map/cond/branch_1_fun/ppermute | solution.py:48
  83.5 16.2 %branch_1_fun.1 = (f32[4,20,128,128]{3,2,1,0:T(8,128)}, f32[1,512]{1,0:T(1,128)S(1)}, bf16[512,1024]{1,0:T(8,128)(2,1)}) custom-call(bf16[512,3712]{1,0:T(8,128)(2,1)} %get-tuple-element.12.left_in, s32[4,20]{1,0:T(4,128)S(1)} %get-tuple-element.13.positions, f32[4,20,128,128]{3,2,1,0:T(8,128)} %get-tuple-element.14.prev, ...), custom_call_target="tpu_custom_call" | custom-call | flops 5637144576 | bytes 18350080 | tf_op jit(solution)/shard_map/cond/branch_1_fun/pallas_call | solution.py:376
  99.7 0.0 copy-start
  99.7 0.0 collective-permute-done.7.corner
  99.8 2.4 %collective-permute-start.8 = (f32[1,512]{1,0:T(1,128)S(1)}, f32[1,512]{1,0:T(1,128)S(1)}, u32[]{:S(2)}, u32[]{:S(2)}) collective-permute-start(f32[1,512]{1,0:T(1,128)S(1)} %shard_map.44), channel_id=1, source_target_pairs={{0,1},{1,0},{2,3},{3,2},{4,5},{5,4},{6,7},{7,6},{8,9},{9,8},{10,11... | collective-permute-start | bytes 6152 | tf_op jit(solution)/shard_map/ppermute | solution.py:52
  102.2 0.8 collective-permute-done.8
  103.0 0.5 collective-permute-start.11
  103.5 0.0 collective-permute-start.10
  103.5 3.9 %collective-permute-start.9 = (f32[1,512]{1,0:T(1,128)S(1)}, f32[1,512]{1,0:T(1,128)S(1)}, u32[]{:S(2)}, u32[]{:S(2)}) collective-permute-start(f32[1,512]{1,0:T(1,128)S(1)} %add.21), channel_id=1, source_target_pairs={{0,8},{1,9},{2,10},{3,11},{4,12},{5,13},{6,14},{7,15},{8,0},{9,1},... | collective-permute-start | bytes 6152 | tf_op jit(solution)/shard_map/ppermute | solution.py:52
  107.4 1.0 collective-permute-done.11
  108.4 0.0 collective-permute-done.10
  108.4 0.6 collective-permute-done.9
  109.0 0.0 collective-permute-done.6.source_a
  109.0 0.1 collective-permute-start.12
  109.1 0.1 collective-permute-start.15
  109.1 1.2 collective-permute-start.14
  110.4 2.2 %collective-permute-start.13 = (f32[1,512]{1,0:T(1,128)S(1)}, f32[1,512]{1,0:T(1,128)S(1)}, u32[]{:S(2)}, u32[]{:S(2)}) collective-permute-start(f32[1,512]{1,0:T(1,128)S(1)} %add_add_fusion), channel_id=1, source_target_pairs={{0,2},{1,3},{2,0},{3,1},{4,6},{5,7},{6,4},{7,5},{8,10},{9,11},{10,... | collective-permute-start | bytes 6152 | tf_op jit(solution)/shard_map/ppermute | solution.py:52
  112.6 1.4 %collective-permute-done.12.source_b = bf16[81,128,128]{2,1,0:T(8,128)(2,1)S(1)} collective-permute-done((bf16[81,128,128]{2,1,0:T(8,128)(2,1)S(1)}, bf16[81,128,128]{2,1,0:T(8,128)(2,1)S(1)}, u32[]{:S(2)}, u32[]{:S(2)}) %collective-permute-start.12) | collective-permute-done | bytes 2654240 | tf_op jit(solution)/shard_map/ppermute | solution.py:48
  114.0 0.0 copy-done
  114.0 8.6 %shard_map.45 = bf16[4,20,128,128]{3,2,1,0:T(8,128)(2,1)} custom-call(bf16[512,1024]{1,0:T(8,128)(2,1)S(1)} %copy-done, s32[4,20]{1,0:T(4,128)S(1)} %get-tuple-element.43.positions, f32[4,20,128,128]{3,2,1,0:T(8,128)} %get-tuple-element.58.prev, bf16[81,128,128]{2,1,0:T(8,128)(2,1)S(1)} %collective-permute-done.6.source_a, ...), custom_call_target="tpu_custom_call" | custom-call | flops 3758096384 | bytes 15728640 | tf_op jit(solution)/shard_map/pallas_call | solution.py:376
  122.6 0.0 collective-permute-done.15
  122.6 0.0 collective-permute-done.14
  122.6 0.0 collective-permute-done.13
  122.6 0.6 add_reduce_fusion
  (3 shorter events, 0.0 us)
Async XLA Ops:
  4.0 17.2 %collective-permute-start.5 = (bf16[81,128,128]{2,1,0:T(8,128)(2,1)}, bf16[81,128,128]{2,1,0:T(8,128)(2,1)S(1)}, u32[]{:S(2)}, u32[]{:S(2)}) collective-permute-start(bf16[81,128,128]{2,1,0:T(8,128)(2,1)} %shard_map.42), channel_id=1, source_target_pairs={{1,0},{0,1},{3,2},{2,3},{5,4},{4,5},{7,6},{6,7},{9,8},{8,9},{11,10... | collective-permute-start | bytes 7962632 | tf_op jit(solution)/shard_map/ppermute | solution.py:48
  4.6 60.3 %collective-permute-start.3 = (bf16[81,128,128]{2,1,0:T(8,128)(2,1)}, bf16[81,128,128]{2,1,0:T(8,128)(2,1)}, u32[]{:S(2)}, u32[]{:S(2)}) collective-permute-start(bf16[81,128,128]{2,1,0:T(8,128)(2,1)} %shard_map.42), channel_id=1, source_target_pairs={{29,0},{3,1},{0,2},{6,3},{1,4},{7,5},{4,6},{10,7},{5,8},{11,9},{8,... | collective-permute-start | bytes 7962632 | tf_op jit(solution)/shard_map/ppermute | solution.py:48
  7.1 58.5 %collective-permute-start.2 = (bf16[81,128,128]{2,1,0:T(8,128)(2,1)}, bf16[81,128,128]{2,1,0:T(8,128)(2,1)}, u32[]{:S(2)}, u32[]{:S(2)}) collective-permute-start(bf16[81,128,128]{2,1,0:T(8,128)(2,1)} %shard_map.42), channel_id=1, source_target_pairs={{2,0},{4,1},{31,2},{1,3},{6,4},{8,5},{3,6},{5,7},{10,8},{12,9},{7,... | collective-permute-start | bytes 7962632 | tf_op jit(solution)/shard_map/ppermute | solution.py:48
  19.9 13.6 %collective-permute-start.4 = (bf16[256,512]{1,0:T(8,128)(2,1)}, bf16[256,512]{1,0:T(8,128)(2,1)S(1)}, u32[]{:S(2)}, u32[]{:S(2)}) collective-permute-start(bf16[256,512]{1,0:T(8,128)(2,1)} %get-tuple-element.44), channel_id=1, source_target_pairs={{1,0},{2,3},{5,4},{6,7},{9,8},{10,11},{13,12},{14,15},{17,16},{18,... | collective-permute-start | bytes 786440 | tf_op jit(solution)/shard_map/ppermute | solution.py:48
  21.2 1.5 %copy-start.1 = (bf16[81,128,128]{2,1,0:T(8,128)(2,1)}, bf16[81,128,128]{2,1,0:T(8,128)(2,1)S(1)}, u32[]{:S(2)}) copy-start(bf16[81,128,128]{2,1,0:T(8,128)(2,1)S(1)} %collective-permute-done.5.refs_0_) | copy-start | bytes 7962628
  65.6 43.4 %collective-permute-start.6 = (bf16[81,128,128]{2,1,0:T(8,128)(2,1)}, bf16[81,128,128]{2,1,0:T(8,128)(2,1)S(1)}, u32[]{:S(2)}, u32[]{:S(2)}) collective-permute-start(bf16[81,128,128]{2,1,0:T(8,128)(2,1)} %collective-permute-done.2), channel_id=1, source_target_pairs={{2,0},{28,1},{7,2},{1,3},{6,4},{0,5},{11,6},{5,7},{10,8},{4,9},{15... | collective-permute-start | bytes 7962632 | tf_op jit(solution)/shard_map/ppermute | solution.py:48
  66.1 33.6 %collective-permute-start.7 = (bf16[256,512]{1,0:T(8,128)(2,1)S(1)}, bf16[256,512]{1,0:T(8,128)(2,1)S(1)}, u32[]{:S(2)}, u32[]{:S(2)}) collective-permute-start(bf16[256,512]{1,0:T(8,128)(2,1)S(1)} %collective-permute-done.4), channel_id=1, source_target_pairs={{31,1},{4,2},{3,5},{8,6},{7,9},{12,10},{11,13},{16,14},{15,17},{20... | collective-permute-start | bytes 786440 | tf_op jit(solution)/shard_map/ppermute | solution.py:48
  75.0 6.1 %collective-permute-start = (bf16[81,128,128]{2,1,0:T(8,128)(2,1)}, bf16[81,128,128]{2,1,0:T(8,128)(2,1)S(1)}, u32[]{:S(2)}, u32[]{:S(2)}) collective-permute-start(bf16[81,128,128]{2,1,0:T(8,128)(2,1)} %get-tuple-element.16.refs_0_), channel_id=1, source_target_pairs={{0,1},{3,2},{4,5},{7,6},{8,9},{11,10},{12,13},{15,14},{16,17},{19,... | collective-permute-start | bytes 7962632 | tf_op jit(solution)/shard_map/cond/branch_1_fun/ppermute | solution.py:48
  76.4 7.1 %collective-permute-start.1 = (bf16[81,128,128]{2,1,0:T(8,128)(2,1)}, bf16[81,128,128]{2,1,0:T(8,128)(2,1)S(1)}, u32[]{:S(2)}, u32[]{:S(2)}) collective-permute-start(bf16[81,128,128]{2,1,0:T(8,128)(2,1)} %get-tuple-element.17.refs_1_), channel_id=1, source_target_pairs={{1,0},{2,3},{5,4},{6,7},{9,8},{10,11},{13,12},{14,15},{17,16},{18,... | collective-permute-start | bytes 7962632 | tf_op jit(solution)/shard_map/cond/branch_1_fun/ppermute | solution.py:48
  99.7 14.3 %copy-start = (bf16[512,1024]{1,0:T(8,128)(2,1)S(1)}, bf16[512,1024]{1,0:T(8,128)(2,1)}, u32[]{:S(2)}) copy-start(bf16[512,1024]{1,0:T(8,128)(2,1)} %get-tuple-element.54.left_in) | copy-start | bytes 3145732
  99.8 3.2 %collective-permute-start.8 = (f32[1,512]{1,0:T(1,128)S(1)}, f32[1,512]{1,0:T(1,128)S(1)}, u32[]{:S(2)}, u32[]{:S(2)}) collective-permute-start(f32[1,512]{1,0:T(1,128)S(1)} %shard_map.44), channel_id=1, source_target_pairs={{0,1},{1,0},{2,3},{3,2},{4,5},{5,4},{6,7},{7,6},{8,9},{9,8},{10,11... | collective-permute-start | bytes 6152 | tf_op jit(solution)/shard_map/ppermute | solution.py:52
  103.0 5.4 %collective-permute-start.11 = (f32[1,512]{1,0:T(1,128)S(1)}, f32[1,512]{1,0:T(1,128)S(1)}, u32[]{:S(2)}, u32[]{:S(2)}) collective-permute-start(f32[1,512]{1,0:T(1,128)S(1)} %add.21), channel_id=1, source_target_pairs={{0,24},{1,25},{2,26},{3,27},{4,28},{5,29},{6,30},{7,31},{8,16},{9,... | collective-permute-start | bytes 6152 | tf_op jit(solution)/shard_map/ppermute | solution.py:52
  103.5 4.9 %collective-permute-start.10 = (f32[1,512]{1,0:T(1,128)S(1)}, f32[1,512]{1,0:T(1,128)S(1)}, u32[]{:S(2)}, u32[]{:S(2)}) collective-permute-start(f32[1,512]{1,0:T(1,128)S(1)} %add.21), channel_id=1, source_target_pairs={{0,16},{1,17},{2,18},{3,19},{4,20},{5,21},{6,22},{7,23},{8,24},{9,... | collective-permute-start | bytes 6152 | tf_op jit(solution)/shard_map/ppermute | solution.py:52
  103.5 5.5 %collective-permute-start.9 = (f32[1,512]{1,0:T(1,128)S(1)}, f32[1,512]{1,0:T(1,128)S(1)}, u32[]{:S(2)}, u32[]{:S(2)}) collective-permute-start(f32[1,512]{1,0:T(1,128)S(1)} %add.21), channel_id=1, source_target_pairs={{0,8},{1,9},{2,10},{3,11},{4,12},{5,13},{6,14},{7,15},{8,0},{9,1},... | collective-permute-start | bytes 6152 | tf_op jit(solution)/shard_map/ppermute | solution.py:52
  109.0 5.0 %collective-permute-start.12 = (bf16[81,128,128]{2,1,0:T(8,128)(2,1)S(1)}, bf16[81,128,128]{2,1,0:T(8,128)(2,1)S(1)}, u32[]{:S(2)}, u32[]{:S(2)}) collective-permute-start(bf16[81,128,128]{2,1,0:T(8,128)(2,1)S(1)} %collective-permute-done.6.source_a), channel_id=1, source_target_pairs={{1,0},{0,1},{3,2},{2,3},{5,4},{4,5},{7,6},{6,7},{9,8},{8,9},{11,10... | collective-permute-start | bytes 7962632 | tf_op jit(solution)/shard_map/ppermute | solution.py:48
  109.1 13.6 %collective-permute-start.15 = (f32[1,512]{1,0:T(1,128)S(1)}, f32[1,512]{1,0:T(1,128)S(1)}, u32[]{:S(2)}, u32[]{:S(2)}) collective-permute-start(f32[1,512]{1,0:T(1,128)S(1)} %add_add_fusion), channel_id=1, source_target_pairs={{0,6},{1,7},{2,4},{3,5},{4,2},{5,3},{6,0},{7,1},{8,14},{9,15},{10,... | collective-permute-start | bytes 6152 | tf_op jit(solution)/shard_map/ppermute | solution.py:52
  109.1 13.5 %collective-permute-start.14 = (f32[1,512]{1,0:T(1,128)S(1)}, f32[1,512]{1,0:T(1,128)S(1)}, u32[]{:S(2)}, u32[]{:S(2)}) collective-permute-start(f32[1,512]{1,0:T(1,128)S(1)} %add_add_fusion), channel_id=1, source_target_pairs={{0,4},{1,5},{2,6},{3,7},{4,0},{5,1},{6,2},{7,3},{8,12},{9,13},{10,... | collective-permute-start | bytes 6152 | tf_op jit(solution)/shard_map/ppermute | solution.py:52
  110.4 12.3 %collective-permute-start.13 = (f32[1,512]{1,0:T(1,128)S(1)}, f32[1,512]{1,0:T(1,128)S(1)}, u32[]{:S(2)}, u32[]{:S(2)}) collective-permute-start(f32[1,512]{1,0:T(1,128)S(1)} %add_add_fusion), channel_id=1, source_target_pairs={{0,2},{1,3},{2,0},{3,1},{4,6},{5,7},{6,4},{7,5},{8,10},{9,11},{10,... | collective-permute-start | bytes 6152 | tf_op jit(solution)/shard_map/ppermute | solution.py:52

commit v14 on v13

--- a/solution.py
+++ b/solution.py
@@ -209,7 +209,7 @@
 def near_body(z, names, final, left_in, positions, prev, trace_in, *refs):
     refs = list(refs)
     take = lambda count: [refs.pop(0) for _ in range(count)]
-    sources = [take(2 if name == "mixed" else 1) for name in names]
+    sources = take(len(names))
     out, trace = take(2)
     relay_left = take(1)[0] if final else None
     left, stage, right, total, sums, vector, scalars = take(7)
@@ -222,34 +222,25 @@
         return pl.ds(aligned(n, z.span), z.span)
 
     def fetch(index):
-        return pltpu.make_async_copy(sources[index][0], stage.at[index % 2], in_sem.at[index % 2])
-
-    def begin_fetch(index):
-        if len(sources[index]) == 1:
-            fetch(index).start()
-            return
-        for use, source in enumerate(sources[index]):
-            @pl.when(pick(USE_SECOND, kind) == use)
-            def _():
-                pltpu.make_async_copy(source, stage.at[index % 2], in_sem.at[index % 2]).start()
-
+        return pltpu.make_async_copy(sources[index], stage.at[index % 2], in_sem.at[index % 2])
+
+    fetch(0).start()
     left_copy = pltpu.make_async_copy(left_in, left, left_sem)
     left_copy.start()
-    for index in range(min(2, len(names))):
-        begin_fetch(index)
     prev_copy = pltpu.make_async_copy(prev, sums, prev_sem)
-    prev_copy.start()
     total[...] = jnp.zeros_like(total)
     trace[...] = trace_in[...]
-    left_copy.wait()
     relay_copies = []
-    for index, name in enumerate(("relay", "relay_beside") if final else ()):
-        copy = pltpu.make_async_copy(
-            left.at[:, chunk(place[name])], relay_left.at[:, pl.ds(index * z.span, z.span)],
-            relay_sem.at[index],
-        )
-        copy.start()
-        relay_copies.append(copy)
+
+    def hand_on():
+        for index, name in enumerate(("relay", "relay_beside") if final else ()):
+            copy = pltpu.make_async_copy(
+                left.at[:, chunk(place[name])], relay_left.at[:, pl.ds(index * z.span, z.span)],
+                relay_sem.at[index],
+            )
+            copy.start()
+            relay_copies.append(copy)
+
     decodings = []
 
     def begin_decode(index):
@@ -261,6 +252,8 @@
         ))
 
     begin_decode(0)
+    if len(names) > 1:
+        fetch(1).start()
     dense_of = {}
     for index, name in enumerate(names):
         dense = right.at[index]
@@ -270,8 +263,12 @@
         dense[...] = jnp.zeros_like(dense)
         decodings[index].wait()
         scatter(z, dense, 0, stage.at[slot], lambda r, u: scalars[slot, r, u])
+        if index == 0:
+            left_copy.wait()
+            prev_copy.start()
+            hand_on()
         if index + 2 < len(names):
-            begin_fetch(index + 2)
+            fetch(index + 2).start()
         if index + 1 < len(names):
             begin_decode(index + 1)
 
@@ -450,22 +447,24 @@
     total, trace = near(("beside",), [beside], total, trace)
     first, second, corner, total, trace = lax.optimization_barrier((first, second, corner, total, trace))
     relay = receive(first, RELAY_FROM)
-    corner = receive(corner, (0, -2, 2, 0), (LOWER, UPPER))
-
-    def nearby(first, second, total, trace):
-        mixed = [
-            receive(first, PARTNER, [m for m in range(4) if not USE_SECOND[m]]),
-            receive(second, PARTNER, [m for m in range(4) if USE_SECOND[m]]),
-        ]
-        return tuple(near(("first", "second", "mixed"), [first, second, *mixed], total, trace, True))
-
-    def nothing(first, second, total, trace):
+    kind = lax.axis_index(AXES) % 4
+
+    def nearby(first, second, corner, total, trace):
+        use_first = (kind == 0) | (kind == 3)
+        mixed = receive(jnp.where(use_first, first, second), PARTNER)
+        corner = receive(corner, (0, -2, 2, 0), (LOWER, UPPER))
+        total, trace, relay_left = near(("first", "second", "mixed"), [first, second, mixed], total, trace, True)
+        trace = call(
+            z, functools.partial(corner_body, z), [left, corner, trace], [ANY, VMEM, VMEM], line, VMEM,
+            [pltpu.VMEM((z.span, z.span // 2), dtype), DMA], 0,
+        )
+        return total, trace, relay_left
+
+    def nothing(first, second, corner, total, trace):
         return jnp.zeros_like(total), jnp.zeros_like(trace), jnp.zeros((z.span, 2 * z.span), dtype)
 
-    total, trace, relay_left = lax.cond(positions[0, 0] >= 0, nearby, nothing, first, second, total, trace)
-    trace = call(
-        z, functools.partial(corner_body, z), [left, corner, trace], [ANY, VMEM, VMEM], line, VMEM,
-        [pltpu.VMEM((z.span, z.span // 2), dtype), DMA], 0,
+    total, trace, relay_left = lax.cond(
+        positions[0, 0] >= 0, nearby, nothing, first, second, corner, total, trace
     )
     assert devices & (devices - 1) == 0
     steps = [1 << bit for bit in range(devices.bit_length() - 1)]

time: 125 us -> 122 us (0.976)
  Pallas kernels: 48.7 us -> 45.8 us
  other arithmetic: 0.62 us -> 2.8 us
  waiting for transfers between devices: 41.6 us -> 39.5 us
    ppermute x9 -> x8, waiting for transfers between devices: 39.2 us -> 35.7 us  [receive(): return lax.ppermute(shard, AXES, pairs)]
    pallas_call x6, Pallas kernels: 48.7 us -> 45.8 us  [call(): pl.pallas_call(kernel, out_shape=out_shape, in_specs=in_specs, out_specs=...]
    ppermute x7, starting transfers between devices: 10.3 us -> 7.95 us  [fetch(): lax.ppermute(value, AXES, [(d, d ^ step) for d in range(lax.axis_size(AXE...]
    select_n x0 -> x1, other arithmetic: none -> 2.18 us  [nearby(): mixed = receive(jnp.where(use_first, first, second), PARTNER)]
    ppermute x9 -> x8, starting transfers between devices: 18.5 us -> 20.2 us  [receive(): return lax.ppermute(shard, AXES, pairs)]
    ppermute x7, waiting for transfers between devices: 2.39 us -> 3.84 us  [fetch(): lax.ppermute(value, AXES, [(d, d ^ step) for d in range(lax.axis_size(AXE...]
  transfers between devices with their start and end apart: 16 -> 15, of which waited for: 8 -> 6; matrix products, arithmetic and copies ran while one was open for 0% -> 2% of each run, Pallas kernels for 36% -> 35%
where the time goes in v14:
time: 122 us
  Pallas kernels  45.8 us (38%)
  waiting for transfers between devices  39.5 us (32%)
  starting transfers between devices  28.2 us (23%)
  between operations  3.18 us (3%)
  other arithmetic  2.8 us (2%)
  local copies, waits for them, and re-layouts  2.03 us (2%)
    pallas_call x6, Pallas kernels, call(): pl.pallas_call(kernel, out_shape=out_shape, in_specs=in_specs, out_specs=...  45.8 us
    ppermute x8, waiting for transfers between devices, receive(): return lax.ppermute(shard, AXES, pairs)  35.7 us
    ppermute x8, starting transfers between devices, receive(): return lax.ppermute(shard, AXES, pairs)  20.2 us
    ppermute x7, starting transfers between devices, fetch(): lax.ppermute(value, AXES, [(d, d ^ step) for d in range(lax.axis_size(AXE...  7.95 us
    ppermute x7, waiting for transfers between devices, fetch(): lax.ppermute(value, AXES, [(d, d ^ step) for d in range(lax.axis_size(AXE...  3.84 us
  transfers between devices with their start and end apart: 15, of which 6 were waited for; matrix products, arithmetic and copies ran while one was open for 2% of the time, Pallas kernels for 35%

profile of v14, /device:TPU:0, one launch (start us, length us, event | category | flops | bytes accessed | tf_op | source)
XLA Modules:
  0.0 121.6 jit_solution(11672387096853417931)
XLA Ops:
  0.6 3.4 %shard_map.42 = bf16[81,128,128]{2,1,0:T(8,128)(2,1)} custom-call(bf16[4,20,128,128]{3,2,1,0:T(8,128)(2,1)} %tiles.1, s32[4,20]{1,0:T(4,128)} %columns.3), custom_call_target="tpu_custom_call" | custom-call | bytes 10485760 | tf_op jit(solution)/shard_map/pallas_call | solution.py:373
  4.0 0.5 collective-permute-start.5
  4.5 2.6 %collective-permute-start.3 = (bf16[81,128,128]{2,1,0:T(8,128)(2,1)}, bf16[81,128,128]{2,1,0:T(8,128)(2,1)}, u32[]{:S(2)}, u32[]{:S(2)}) collective-permute-start(bf16[81,128,128]{2,1,0:T(8,128)(2,1)} %shard_map.42), channel_id=1, source_target_pairs={{29,0},{3,1},{0,2},{6,3},{1,4},{7,5},{4,6},{10,7},{5,8},{11,9},{8,... | collective-permute-start | bytes 7962632 | tf_op jit(solution)/shard_map/ppermute | solution.py:48
  7.1 3.1 %collective-permute-start.2 = (bf16[81,128,128]{2,1,0:T(8,128)(2,1)}, bf16[81,128,128]{2,1,0:T(8,128)(2,1)S(1)}, u32[]{:S(2)}, u32[]{:S(2)}) collective-permute-start(bf16[81,128,128]{2,1,0:T(8,128)(2,1)} %shard_map.42), channel_id=1, source_target_pairs={{2,0},{4,1},{31,2},{1,3},{6,4},{8,5},{3,6},{5,7},{10,8},{12,9},{7,... | collective-permute-start | bytes 7962632 | tf_op jit(solution)/shard_map/ppermute | solution.py:48
  10.2 9.7 %shard_map.41 = (f32[4,20,128,128]{3,2,1,0:T(8,128)}, bf16[512,3712]{1,0:T(8,128)(2,1)}, bf16[256,512]{1,0:T(8,128)(2,1)}, s32[4,20]{1,0:T(4,128)S(1)}, f32[1,512]{1,0:T(1,128)}) custom-call(bf16[4,20,128,128]{3,2,1,0:T(8,128)(2,1)} %tiles.1, s32[4,20]{1,0:T(4,128)} %columns.3), custom_call_target="tpu_custom_call" | custom-call | flops 1879048192 | bytes 13107200 | tf_op jit(solution)/shard_map/pallas_call | solution.py:373
  19.9 1.3 %collective-permute-start.4 = (bf16[256,512]{1,0:T(8,128)(2,1)}, bf16[256,512]{1,0:T(8,128)(2,1)S(1)}, u32[]{:S(2)}, u32[]{:S(2)}) collective-permute-start(bf16[256,512]{1,0:T(8,128)(2,1)} %get-tuple-element.76), channel_id=1, source_target_pairs={{1,0},{2,3},{5,4},{6,7},{9,8},{10,11},{13,12},{14,15},{17,16},{18,... | collective-permute-start | bytes 786440 | tf_op jit(solution)/shard_map/ppermute | solution.py:48
  21.2 0.0 collective-permute-done.5.refs_0_
  21.2 9.6 %shard_map.43 = (f32[4,20,128,128]{3,2,1,0:T(8,128)}, f32[1,512]{1,0:T(1,128)S(1)}) custom-call(bf16[512,3712]{1,0:T(8,128)(2,1)} %get-tuple-element.77.left_in, s32[4,20]{1,0:T(4,128)S(1)} %get-tuple-element.75.positions, f32[4,20,128,128]{3,2,1,0:T(8,128)} %get-tuple-element.78.prev, f32[1,512]{1,0:T(1,128)} %get-tuple-element.79.trace_in, ...), custom_call_target="tpu_custom_call" | custom-call | flops 1879048192 | bytes 13107200 | tf_op jit(solution)/shard_map/pallas_call | solution.py:373
  30.9 0.0 collective-permute-done.4
  30.9 34.0 %collective-permute-done.3 = bf16[81,128,128]{2,1,0:T(8,128)(2,1)} collective-permute-done((bf16[81,128,128]{2,1,0:T(8,128)(2,1)}, bf16[81,128,128]{2,1,0:T(8,128)(2,1)}, u32[]{:S(2)}, u32[]{:S(2)}) %collective-permute-start.3) | collective-permute-done | bytes 2654240 | tf_op jit(solution)/shard_map/ppermute | solution.py:48
  64.9 0.6 collective-permute-done.2
  65.5 0.0 copy-start.1
  65.5 1.5 %copy-done.1 = bf16[81,128,128]{2,1,0:T(8,128)(2,1)} copy-done((bf16[81,128,128]{2,1,0:T(8,128)(2,1)}, bf16[81,128,128]{2,1,0:T(8,128)(2,1)S(1)}, u32[]{:S(2)}) %copy-start.1) | copy-done | bytes 2654232
  67.0 0.6 collective-permute-start.6
  67.6 0.5 slice.3
  68.7 25.1 %conditional.1 = (f32[4,20,128,128]{3,2,1,0:T(8,128)}, f32[1,512]{1,0:T(1,128)S(1)}, bf16[512,1024]{1,0:T(8,128)(2,1)}) conditional(s32[]{:T(128)} %bitcast, () %tuple.22, (s32[]{:T(128)}, bf16[81,128,128]{2,1,0:T(8,128)(2,1)}, bf16[81,128,128]{2,1,0:T(8,128)(2,1)}, bf16[512,3712]{1,0:T(8,128)(2,1)}, s32[4,20]{1,0:T(4,128)S(1)}, ...), branch_computations={%region_0.1_spmd, %region_1.2_spmd} | conditional | flops 5638471680 | bytes 74285368 | solution.py:466
  68.8 0.0 copy-start
  68.8 0.0 copy-start.2
  68.8 2.2 %broadcast_select_fusion = bf16[81,128,128]{2,1,0:T(8,128)(2,1)S(1)} fusion(bf16[81,128,128]{2,1,0:T(8,128)(2,1)} %get-tuple-element.43.refs_0_, bf16[81,128,128]{2,1,0:T(8,128)(2,1)} %get-tuple-element.44.refs_1_, pred[]{:T(512)S(6)} %or.2), kind=kLoop, calls=%fused_computation | loop fusion | flops 1327104 | bytes 7962625 | tf_op jit(solution)/shard_map/cond/branch_1_fun/jit(_where)/select_n | solution.py:454
  71.0 1.5 %collective-permute-start = (bf16[81,128,128]{2,1,0:T(8,128)(2,1)S(1)}, bf16[81,128,128]{2,1,0:T(8,128)(2,1)S(1)}, u32[]{:S(2)}, u32[]{:S(2)}) collective-permute-start(bf16[81,128,128]{2,1,0:T(8,128)(2,1)S(1)} %broadcast_select_fusion), channel_id=1, source_target_pairs={{1,0},{0,1},{3,2},{2,3},{5,4},{4,5},{7,6},{6,7},{9,8},{8,9},{11,10... | collective-permute-start | bytes 7962632 | tf_op jit(solution)/shard_map/cond/branch_1_fun/ppermute | solution.py:48
  72.4 6.8 %collective-permute-start.1 = (bf16[256,512]{1,0:T(8,128)(2,1)S(1)}, bf16[256,512]{1,0:T(8,128)(2,1)S(1)}, u32[]{:S(2)}, u32[]{:S(2)}) collective-permute-start(bf16[256,512]{1,0:T(8,128)(2,1)S(1)} %get-tuple-element.47), channel_id=1, source_target_pairs={{31,1},{4,2},{3,5},{8,6},{7,9},{12,10},{11,13},{16,14},{15,17},{20... | collective-permute-start | bytes 786440 | tf_op jit(solution)/shard_map/cond/branch_1_fun/ppermute | solution.py:48
  79.2 0.0 collective-permute-done.refs_2_
  79.2 0.0 copy-done
  79.3 0.0 copy-done.2
  79.3 14.5 %branch_1_fun.2 = (f32[4,20,128,128]{3,2,1,0:T(8,128)}, f32[1,512]{1,0:T(1,128)S(1)}, bf16[512,1024]{1,0:T(8,128)(2,1)}) custom-call(bf16[512,3712]{1,0:T(8,128)(2,1)S(1)} %copy-done, s32[4,20]{1,0:T(4,128)S(1)} %get-tuple-element.40.positions, f32[4,20,128,128]{3,2,1,0:T(8,128)} %get-tuple-element.41.prev, f32[1,512]{1,0:T(1,128)S(1)} %get-tuple-element.42.trace_in, ...), custom_call_target="tpu_custom_call" | custom-call | flops 5637144576 | bytes 18350080 | tf_op jit(solution)/shard_map/cond/branch_1_fun/pallas_call | solution.py:373
  93.8 0.0 collective-permute-done.1.corner
  93.8 0.1 collective-permute-start.7
  93.9 1.1 collective-permute-done.7
  95.0 2.6 %collective-permute-start.10 = (f32[1,512]{1,0:T(1,128)S(1)}, f32[1,512]{1,0:T(1,128)S(1)}, u32[]{:S(2)}, u32[]{:S(2)}) collective-permute-start(f32[1,512]{1,0:T(1,128)S(1)} %add.30), channel_id=1, source_target_pairs={{0,24},{1,25},{2,26},{3,27},{4,28},{5,29},{6,30},{7,31},{8,16},{9,... | collective-permute-start | bytes 6152 | tf_op jit(solution)/shard_map/ppermute | solution.py:52
  97.6 0.0 collective-permute-start.9
  97.6 1.8 %collective-permute-start.8 = (f32[1,512]{1,0:T(1,128)S(1)}, f32[1,512]{1,0:T(1,128)S(1)}, u32[]{:S(2)}, u32[]{:S(2)}) collective-permute-start(f32[1,512]{1,0:T(1,128)S(1)} %add.30), channel_id=1, source_target_pairs={{0,8},{1,9},{2,10},{3,11},{4,12},{5,13},{6,14},{7,15},{8,0},{9,1},... | collective-permute-start | bytes 6152 | tf_op jit(solution)/shard_map/ppermute | solution.py:52
  99.4 1.0 collective-permute-done.10
  100.4 1.7 %collective-permute-done.9 = f32[1,512]{1,0:T(1,128)S(1)} collective-permute-done((f32[1,512]{1,0:T(1,128)S(1)}, f32[1,512]{1,0:T(1,128)S(1)}, u32[]{:S(2)}, u32[]{:S(2)}) %collective-permute-start.9) | collective-permute-done | bytes 2080 | tf_op jit(solution)/shard_map/ppermute | solution.py:52
  102.1 0.0 collective-permute-done.8
  102.1 0.0 collective-permute-done.6.source_a
  102.1 3.9 %collective-permute-start.11 = (bf16[81,128,128]{2,1,0:T(8,128)(2,1)S(1)}, bf16[81,128,128]{2,1,0:T(8,128)(2,1)S(1)}, u32[]{:S(2)}, u32[]{:S(2)}) collective-permute-start(bf16[81,128,128]{2,1,0:T(8,128)(2,1)S(1)} %collective-permute-done.6.source_a), channel_id=1, source_target_pairs={{1,0},{0,1},{3,2},{2,3},{5,4},{4,5},{7,6},{6,7},{9,8},{8,9},{11,10... | collective-permute-start | bytes 7962632 | tf_op jit(solution)/shard_map/ppermute | solution.py:48
  106.0 0.0 collective-permute-start.14
  106.0 2.0 %collective-permute-start.13 = (f32[1,512]{1,0:T(1,128)S(1)}, f32[1,512]{1,0:T(1,128)S(1)}, u32[]{:S(2)}, u32[]{:S(2)}) collective-permute-start(f32[1,512]{1,0:T(1,128)S(1)} %add_add_fusion), channel_id=1, source_target_pairs={{0,4},{1,5},{2,6},{3,7},{4,0},{5,1},{6,2},{7,3},{8,12},{9,13},{10,... | collective-permute-start | bytes 6152 | tf_op jit(solution)/shard_map/ppermute | solution.py:52
  108.1 1.4 %collective-permute-start.12 = (f32[1,512]{1,0:T(1,128)S(1)}, f32[1,512]{1,0:T(1,128)S(1)}, u32[]{:S(2)}, u32[]{:S(2)}) collective-permute-start(f32[1,512]{1,0:T(1,128)S(1)} %add_add_fusion), channel_id=1, source_target_pairs={{0,2},{1,3},{2,0},{3,1},{4,6},{5,7},{6,4},{7,5},{8,10},{9,11},{10,... | collective-permute-start | bytes 6152 | tf_op jit(solution)/shard_map/ppermute | solution.py:52
  109.5 1.1 collective-permute-done.11.source_b
  110.6 8.6 %shard_map.44 = bf16[4,20,128,128]{3,2,1,0:T(8,128)(2,1)} custom-call(bf16[512,1024]{1,0:T(8,128)(2,1)} %get-tuple-element.87.left_in, s32[4,20]{1,0:T(4,128)S(1)} %get-tuple-element.75.positions, f32[4,20,128,128]{3,2,1,0:T(8,128)} %get-tuple-element.90.prev, bf16[81,128,128]{2,1,0:T(8,128)(2,1)S(1)} %collective-permute-done.6.source_a, ...), custom_call_target="tpu_custom_call" | custom-call | flops 3758096384 | bytes 15728640 | tf_op jit(solution)/shard_map/pallas_call | solution.py:373
  119.2 0.0 collective-permute-done.14
  119.2 0.0 collective-permute-done.13
  119.2 0.0 collective-permute-done.12
  119.2 0.6 add_reduce_fusion
  (3 shorter events, 0.0 us)
Async XLA Ops:
  4.0 17.2 %collective-permute-start.5 = (bf16[81,128,128]{2,1,0:T(8,128)(2,1)}, bf16[81,128,128]{2,1,0:T(8,128)(2,1)}, u32[]{:S(2)}, u32[]{:S(2)}) collective-permute-start(bf16[81,128,128]{2,1,0:T(8,128)(2,1)} %shard_map.42), channel_id=1, source_target_pairs={{1,0},{0,1},{3,2},{2,3},{5,4},{4,5},{7,6},{6,7},{9,8},{8,9},{11,10... | collective-permute-start | bytes 7962632 | tf_op jit(solution)/shard_map/ppermute | solution.py:48
  4.5 60.3 %collective-permute-start.3 = (bf16[81,128,128]{2,1,0:T(8,128)(2,1)}, bf16[81,128,128]{2,1,0:T(8,128)(2,1)}, u32[]{:S(2)}, u32[]{:S(2)}) collective-permute-start(bf16[81,128,128]{2,1,0:T(8,128)(2,1)} %shard_map.42), channel_id=1, source_target_pairs={{29,0},{3,1},{0,2},{6,3},{1,4},{7,5},{4,6},{10,7},{5,8},{11,9},{8,... | collective-permute-start | bytes 7962632 | tf_op jit(solution)/shard_map/ppermute | solution.py:48
  7.1 58.4 %collective-permute-start.2 = (bf16[81,128,128]{2,1,0:T(8,128)(2,1)}, bf16[81,128,128]{2,1,0:T(8,128)(2,1)S(1)}, u32[]{:S(2)}, u32[]{:S(2)}) collective-permute-start(bf16[81,128,128]{2,1,0:T(8,128)(2,1)} %shard_map.42), channel_id=1, source_target_pairs={{2,0},{4,1},{31,2},{1,3},{6,4},{8,5},{3,6},{5,7},{10,8},{12,9},{7,... | collective-permute-start | bytes 7962632 | tf_op jit(solution)/shard_map/ppermute | solution.py:48
  19.9 10.9 %collective-permute-start.4 = (bf16[256,512]{1,0:T(8,128)(2,1)}, bf16[256,512]{1,0:T(8,128)(2,1)S(1)}, u32[]{:S(2)}, u32[]{:S(2)}) collective-permute-start(bf16[256,512]{1,0:T(8,128)(2,1)} %get-tuple-element.76), channel_id=1, source_target_pairs={{1,0},{2,3},{5,4},{6,7},{9,8},{10,11},{13,12},{14,15},{17,16},{18,... | collective-permute-start | bytes 786440 | tf_op jit(solution)/shard_map/ppermute | solution.py:48
  65.5 1.5 %copy-start.1 = (bf16[81,128,128]{2,1,0:T(8,128)(2,1)}, bf16[81,128,128]{2,1,0:T(8,128)(2,1)S(1)}, u32[]{:S(2)}) copy-start(bf16[81,128,128]{2,1,0:T(8,128)(2,1)S(1)} %collective-permute-done.2) | copy-start | bytes 7962628
  67.0 35.1 %collective-permute-start.6 = (bf16[81,128,128]{2,1,0:T(8,128)(2,1)}, bf16[81,128,128]{2,1,0:T(8,128)(2,1)S(1)}, u32[]{:S(2)}, u32[]{:S(2)}) collective-permute-start(bf16[81,128,128]{2,1,0:T(8,128)(2,1)} %copy-done.1), channel_id=1, source_target_pairs={{2,0},{28,1},{7,2},{1,3},{6,4},{0,5},{11,6},{5,7},{10,8},{4,9},{15... | collective-permute-start | bytes 7962632 | tf_op jit(solution)/shard_map/ppermute | solution.py:48
  68.8 10.5 %copy-start = (bf16[512,3712]{1,0:T(8,128)(2,1)S(1)}, bf16[512,3712]{1,0:T(8,128)(2,1)}, u32[]{:S(2)}) copy-start(bf16[512,3712]{1,0:T(8,128)(2,1)} %get-tuple-element.39.left_in.left) | copy-start | bytes 11403268 | tf_op jit(solution)/shard_map/cond
  68.8 10.5 %copy-start.2 = (bf16[81,128,128]{2,1,0:T(8,128)(2,1)S(1)}, bf16[81,128,128]{2,1,0:T(8,128)(2,1)}, u32[]{:S(2)}) copy-start(bf16[81,128,128]{2,1,0:T(8,128)(2,1)} %get-tuple-element.43.refs_0_) | copy-start | bytes 7962628 | tf_op jit(solution)/shard_map/cond
  71.0 8.3 %collective-permute-start = (bf16[81,128,128]{2,1,0:T(8,128)(2,1)S(1)}, bf16[81,128,128]{2,1,0:T(8,128)(2,1)S(1)}, u32[]{:S(2)}, u32[]{:S(2)}) collective-permute-start(bf16[81,128,128]{2,1,0:T(8,128)(2,1)S(1)} %broadcast_select_fusion), channel_id=1, source_target_pairs={{1,0},{0,1},{3,2},{2,3},{5,4},{4,5},{7,6},{6,7},{9,8},{8,9},{11,10... | collective-permute-start | bytes 7962632 | tf_op jit(solution)/shard_map/cond/branch_1_fun/ppermute | solution.py:48
  72.4 21.3 %collective-permute-start.1 = (bf16[256,512]{1,0:T(8,128)(2,1)S(1)}, bf16[256,512]{1,0:T(8,128)(2,1)S(1)}, u32[]{:S(2)}, u32[]{:S(2)}) collective-permute-start(bf16[256,512]{1,0:T(8,128)(2,1)S(1)} %get-tuple-element.47), channel_id=1, source_target_pairs={{31,1},{4,2},{3,5},{8,6},{7,9},{12,10},{11,13},{16,14},{15,17},{20... | collective-permute-start | bytes 786440 | tf_op jit(solution)/shard_map/cond/branch_1_fun/ppermute | solution.py:48
  93.8 1.2 %collective-permute-start.7 = (f32[1,512]{1,0:T(1,128)S(1)}, f32[1,512]{1,0:T(1,128)S(1)}, u32[]{:S(2)}, u32[]{:S(2)}) collective-permute-start(f32[1,512]{1,0:T(1,128)S(1)} %get-tuple-element.89), channel_id=1, source_target_pairs={{0,1},{1,0},{2,3},{3,2},{4,5},{5,4},{6,7},{7,6},{8,9},{9,8},{10,11... | collective-permute-start | bytes 6152 | tf_op jit(solution)/shard_map/ppermute | solution.py:52
  95.0 5.4 %collective-permute-start.10 = (f32[1,512]{1,0:T(1,128)S(1)}, f32[1,512]{1,0:T(1,128)S(1)}, u32[]{:S(2)}, u32[]{:S(2)}) collective-permute-start(f32[1,512]{1,0:T(1,128)S(1)} %add.30), channel_id=1, source_target_pairs={{0,24},{1,25},{2,26},{3,27},{4,28},{5,29},{6,30},{7,31},{8,16},{9,... | collective-permute-start | bytes 6152 | tf_op jit(solution)/shard_map/ppermute | solution.py:52
  97.6 4.5 %collective-permute-start.9 = (f32[1,512]{1,0:T(1,128)S(1)}, f32[1,512]{1,0:T(1,128)S(1)}, u32[]{:S(2)}, u32[]{:S(2)}) collective-permute-start(f32[1,512]{1,0:T(1,128)S(1)} %add.30), channel_id=1, source_target_pairs={{0,16},{1,17},{2,18},{3,19},{4,20},{5,21},{6,22},{7,23},{8,24},{9,... | collective-permute-start | bytes 6152 | tf_op jit(solution)/shard_map/ppermute | solution.py:52
  97.6 4.5 %collective-permute-start.8 = (f32[1,512]{1,0:T(1,128)S(1)}, f32[1,512]{1,0:T(1,128)S(1)}, u32[]{:S(2)}, u32[]{:S(2)}) collective-permute-start(f32[1,512]{1,0:T(1,128)S(1)} %add.30), channel_id=1, source_target_pairs={{0,8},{1,9},{2,10},{3,11},{4,12},{5,13},{6,14},{7,15},{8,0},{9,1},... | collective-permute-start | bytes 6152 | tf_op jit(solution)/shard_map/ppermute | solution.py:52
  102.1 8.5 %collective-permute-start.11 = (bf16[81,128,128]{2,1,0:T(8,128)(2,1)S(1)}, bf16[81,128,128]{2,1,0:T(8,128)(2,1)S(1)}, u32[]{:S(2)}, u32[]{:S(2)}) collective-permute-start(bf16[81,128,128]{2,1,0:T(8,128)(2,1)S(1)} %collective-permute-done.6.source_a), channel_id=1, source_target_pairs={{1,0},{0,1},{3,2},{2,3},{5,4},{4,5},{7,6},{6,7},{9,8},{8,9},{11,10... | collective-permute-start | bytes 7962632 | tf_op jit(solution)/shard_map/ppermute | solution.py:48
  106.0 13.1 %collective-permute-start.14 = (f32[1,512]{1,0:T(1,128)S(1)}, f32[1,512]{1,0:T(1,128)S(1)}, u32[]{:S(2)}, u32[]{:S(2)}) collective-permute-start(f32[1,512]{1,0:T(1,128)S(1)} %add_add_fusion), channel_id=1, source_target_pairs={{0,6},{1,7},{2,4},{3,5},{4,2},{5,3},{6,0},{7,1},{8,14},{9,15},{10,... | collective-permute-start | bytes 6152 | tf_op jit(solution)/shard_map/ppermute | solution.py:52
  106.0 13.2 %collective-permute-start.13 = (f32[1,512]{1,0:T(1,128)S(1)}, f32[1,512]{1,0:T(1,128)S(1)}, u32[]{:S(2)}, u32[]{:S(2)}) collective-permute-start(f32[1,512]{1,0:T(1,128)S(1)} %add_add_fusion), channel_id=1, source_target_pairs={{0,4},{1,5},{2,6},{3,7},{4,0},{5,1},{6,2},{7,3},{8,12},{9,13},{10,... | collective-permute-start | bytes 6152 | tf_op jit(solution)/shard_map/ppermute | solution.py:52
  108.1 11.1 %collective-permute-start.12 = (f32[1,512]{1,0:T(1,128)S(1)}, f32[1,512]{1,0:T(1,128)S(1)}, u32[]{:S(2)}, u32[]{:S(2)}) collective-permute-start(f32[1,512]{1,0:T(1,128)S(1)} %add_add_fusion), channel_id=1, source_target_pairs={{0,2},{1,3},{2,0},{3,1},{4,6},{5,7},{6,4},{7,5},{8,10},{9,11},{10,... | collective-permute-start | bytes 6152 | tf_op jit(solution)/shard_map/ppermute | solution.py:52

commit v15 on v14

--- a/solution.py
+++ b/solution.py
@@ -10,7 +10,7 @@
 REACH = 12
 AXES = ("blk", "grp")
 VMEM_LIMIT = 42 * 1024 * 1024
-WHOLE_VMEM = 60 * 1024 * 1024
+WHOLE_VMEM = 62 * 1024 * 1024
 EMPTY = 64
 
 FIRST = (2, 3, -3, -2)

time: 122 us -> 121 us (level)
  local copies, waits for them, and re-layouts: 2.03 us -> 0.52 us
    unnamed x2 -> x0, local copies, waits for them, and re-layouts: 1.51 us -> none
  transfers between devices with their start and end apart: 15 -> 15, of which waited for: 6 -> 6; matrix products, arithmetic and copies ran while one was open for 2% -> 2% of each run, Pallas kernels for 35% -> 36%
where the time goes in v15:
time: 121 us; the launch traced here: 120 us
  Pallas kernels  46.4 us (38%)
  waiting for transfers between devices  39.8 us (33%)
  starting transfers between devices  27.4 us (23%)
  between operations  3.18 us (3%)
  other arithmetic  2.8 us (2%)
    pallas_call x6, Pallas kernels, call(): pl.pallas_call(kernel, out_shape=out_shape, in_specs=in_specs, out_specs=...  46.4 us
    ppermute x8, waiting for transfers between devices, receive(): return lax.ppermute(shard, AXES, pairs)  35.8 us
    ppermute x8, starting transfers between devices, receive(): return lax.ppermute(shard, AXES, pairs)  19.5 us
    ppermute x7, starting transfers between devices, fetch(): lax.ppermute(value, AXES, [(d, d ^ step) for d in range(lax.axis_size(AXE...  7.95 us
    ppermute x7, waiting for transfers between devices, fetch(): lax.ppermute(value, AXES, [(d, d ^ step) for d in range(lax.axis_size(AXE...  3.97 us
  transfers between devices with their start and end apart: 15, of which 6 were waited for; matrix products, arithmetic and copies ran while one was open for 2% of the time, Pallas kernels for 36%

profile of v15, /device:TPU:0, one launch (start us, length us, event | category | flops | bytes accessed | tf_op | source)
XLA Modules:
  0.0 120.2 jit_solution(17499436583490292663)
XLA Ops:
  0.6 3.4 %shard_map.42 = bf16[81,128,128]{2,1,0:T(8,128)(2,1)} custom-call(bf16[4,20,128,128]{3,2,1,0:T(8,128)(2,1)} %tiles.1, s32[4,20]{1,0:T(4,128)} %columns.3), custom_call_target="tpu_custom_call" | custom-call | bytes 10485760 | tf_op jit(solution)/shard_map/pallas_call | solution.py:373
  4.0 0.5 collective-permute-start.5
  4.6 2.6 %collective-permute-start.3 = (bf16[81,128,128]{2,1,0:T(8,128)(2,1)}, bf16[81,128,128]{2,1,0:T(8,128)(2,1)}, u32[]{:S(2)}, u32[]{:S(2)}) collective-permute-start(bf16[81,128,128]{2,1,0:T(8,128)(2,1)} %shard_map.42), channel_id=1, source_target_pairs={{29,0},{3,1},{0,2},{6,3},{1,4},{7,5},{4,6},{10,7},{5,8},{11,9},{8,... | collective-permute-start | bytes 7962632 | tf_op jit(solution)/shard_map/ppermute | solution.py:48
  7.1 3.1 %collective-permute-start.2 = (bf16[81,128,128]{2,1,0:T(8,128)(2,1)}, bf16[81,128,128]{2,1,0:T(8,128)(2,1)}, u32[]{:S(2)}, u32[]{:S(2)}) collective-permute-start(bf16[81,128,128]{2,1,0:T(8,128)(2,1)} %shard_map.42), channel_id=1, source_target_pairs={{2,0},{4,1},{31,2},{1,3},{6,4},{8,5},{3,6},{5,7},{10,8},{12,9},{7,... | collective-permute-start | bytes 7962632 | tf_op jit(solution)/shard_map/ppermute | solution.py:48
  10.2 9.7 %shard_map.41 = (f32[4,20,128,128]{3,2,1,0:T(8,128)}, bf16[512,3712]{1,0:T(8,128)(2,1)}, bf16[256,512]{1,0:T(8,128)(2,1)}, s32[4,20]{1,0:T(4,128)S(1)}, f32[1,512]{1,0:T(1,128)}) custom-call(bf16[4,20,128,128]{3,2,1,0:T(8,128)(2,1)} %tiles.1, s32[4,20]{1,0:T(4,128)} %columns.3), custom_call_target="tpu_custom_call" | custom-call | flops 1879048192 | bytes 13107200 | tf_op jit(solution)/shard_map/pallas_call | solution.py:373
  19.9 1.3 %collective-permute-start.4 = (bf16[256,512]{1,0:T(8,128)(2,1)}, bf16[256,512]{1,0:T(8,128)(2,1)S(1)}, u32[]{:S(2)}, u32[]{:S(2)}) collective-permute-start(bf16[256,512]{1,0:T(8,128)(2,1)} %get-tuple-element.76), channel_id=1, source_target_pairs={{1,0},{2,3},{5,4},{6,7},{9,8},{10,11},{13,12},{14,15},{17,16},{18,... | collective-permute-start | bytes 786440 | tf_op jit(solution)/shard_map/ppermute | solution.py:48
  21.2 0.0 collective-permute-done.5.refs_0_
  21.3 9.6 %shard_map.43 = (f32[4,20,128,128]{3,2,1,0:T(8,128)}, f32[1,512]{1,0:T(1,128)S(1)}) custom-call(bf16[512,3712]{1,0:T(8,128)(2,1)} %get-tuple-element.77.left_in, s32[4,20]{1,0:T(4,128)S(1)} %get-tuple-element.75.positions, f32[4,20,128,128]{3,2,1,0:T(8,128)} %get-tuple-element.78.prev, f32[1,512]{1,0:T(1,128)} %get-tuple-element.79.trace_in, ...), custom_call_target="tpu_custom_call" | custom-call | flops 1879048192 | bytes 13107200 | tf_op jit(solution)/shard_map/pallas_call | solution.py:373
  30.9 0.0 collective-permute-done.4
  30.9 34.0 %collective-permute-done.3 = bf16[81,128,128]{2,1,0:T(8,128)(2,1)} collective-permute-done((bf16[81,128,128]{2,1,0:T(8,128)(2,1)}, bf16[81,128,128]{2,1,0:T(8,128)(2,1)}, u32[]{:S(2)}, u32[]{:S(2)}) %collective-permute-start.3) | collective-permute-done | bytes 2654240 | tf_op jit(solution)/shard_map/ppermute | solution.py:48
  64.9 0.7 collective-permute-done.2
  65.6 0.5 collective-permute-start.6
  66.1 0.5 slice.3
  67.2 25.5 %conditional.1 = (f32[4,20,128,128]{3,2,1,0:T(8,128)}, f32[1,512]{1,0:T(1,128)S(1)}, bf16[512,1024]{1,0:T(8,128)(2,1)}) conditional(s32[]{:T(128)} %bitcast, () %tuple.22, (s32[]{:T(128)}, bf16[81,128,128]{2,1,0:T(8,128)(2,1)}, bf16[81,128,128]{2,1,0:T(8,128)(2,1)}, bf16[512,3712]{1,0:T(8,128)(2,1)}, s32[4,20]{1,0:T(4,128)S(1)}, ...), branch_computations={%region_0.1_spmd, %region_1.2_spmd} | conditional | flops 5638471680 | bytes 63668512 | solution.py:466
  67.3 0.0 copy-start
  67.3 2.2 %broadcast_select_fusion = bf16[81,128,128]{2,1,0:T(8,128)(2,1)S(1)} fusion(bf16[81,128,128]{2,1,0:T(8,128)(2,1)} %get-tuple-element.43.refs_0_, bf16[81,128,128]{2,1,0:T(8,128)(2,1)} %get-tuple-element.44.refs_1_, pred[]{:T(512)S(6)} %or.2), kind=kLoop, calls=%fused_computation | loop fusion | flops 1327104 | bytes 7962625 | tf_op jit(solution)/shard_map/cond/branch_1_fun/jit(_where)/select_n | solution.py:454
  69.5 1.5 %collective-permute-start = (bf16[81,128,128]{2,1,0:T(8,128)(2,1)S(1)}, bf16[81,128,128]{2,1,0:T(8,128)(2,1)S(1)}, u32[]{:S(2)}, u32[]{:S(2)}) collective-permute-start(bf16[81,128,128]{2,1,0:T(8,128)(2,1)S(1)} %broadcast_select_fusion), channel_id=1, source_target_pairs={{1,0},{0,1},{3,2},{2,3},{5,4},{4,5},{7,6},{6,7},{9,8},{8,9},{11,10... | collective-permute-start | bytes 7962632 | tf_op jit(solution)/shard_map/cond/branch_1_fun/ppermute | solution.py:48
  70.9 6.7 %collective-permute-start.1 = (bf16[256,512]{1,0:T(8,128)(2,1)S(1)}, bf16[256,512]{1,0:T(8,128)(2,1)S(1)}, u32[]{:S(2)}, u32[]{:S(2)}) collective-permute-start(bf16[256,512]{1,0:T(8,128)(2,1)S(1)} %get-tuple-element.47), channel_id=1, source_target_pairs={{31,1},{4,2},{3,5},{8,6},{7,9},{12,10},{11,13},{16,14},{15,17},{20... | collective-permute-start | bytes 786440 | tf_op jit(solution)/shard_map/cond/branch_1_fun/ppermute | solution.py:48
  77.6 0.0 collective-permute-done.refs_2_
  77.6 0.0 copy-done
  77.6 15.1 %branch_1_fun.2 = (f32[4,20,128,128]{3,2,1,0:T(8,128)}, f32[1,512]{1,0:T(1,128)S(1)}, bf16[512,1024]{1,0:T(8,128)(2,1)}) custom-call(bf16[512,3712]{1,0:T(8,128)(2,1)S(1)} %copy-done, s32[4,20]{1,0:T(4,128)S(1)} %get-tuple-element.40.positions, f32[4,20,128,128]{3,2,1,0:T(8,128)} %get-tuple-element.41.prev, f32[1,512]{1,0:T(1,128)S(1)} %get-tuple-element.42.trace_in, ...), custom_call_target="tpu_custom_call" | custom-call | flops 5637144576 | bytes 18350080 | tf_op jit(solution)/shard_map/cond/branch_1_fun/pallas_call | solution.py:373
  92.7 0.0 collective-permute-done.1.corner
  92.8 0.1 collective-permute-start.7
  92.9 1.1 collective-permute-done.7
  94.0 2.7 %collective-permute-start.10 = (f32[1,512]{1,0:T(1,128)S(1)}, f32[1,512]{1,0:T(1,128)S(1)}, u32[]{:S(2)}, u32[]{:S(2)}) collective-permute-start(f32[1,512]{1,0:T(1,128)S(1)} %add.30), channel_id=1, source_target_pairs={{0,24},{1,25},{2,26},{3,27},{4,28},{5,29},{6,30},{7,31},{8,16},{9,... | collective-permute-start | bytes 6152 | tf_op jit(solution)/shard_map/ppermute | solution.py:52
  96.7 0.0 collective-permute-start.9
  96.7 1.7 %collective-permute-start.8 = (f32[1,512]{1,0:T(1,128)S(1)}, f32[1,512]{1,0:T(1,128)S(1)}, u32[]{:S(2)}, u32[]{:S(2)}) collective-permute-start(f32[1,512]{1,0:T(1,128)S(1)} %add.30), channel_id=1, source_target_pairs={{0,8},{1,9},{2,10},{3,11},{4,12},{5,13},{6,14},{7,15},{8,0},{9,1},... | collective-permute-start | bytes 6152 | tf_op jit(solution)/shard_map/ppermute | solution.py:52
  98.4 1.0 collective-permute-done.10
  99.4 1.8 %collective-permute-done.9 = f32[1,512]{1,0:T(1,128)S(1)} collective-permute-done((f32[1,512]{1,0:T(1,128)S(1)}, f32[1,512]{1,0:T(1,128)S(1)}, u32[]{:S(2)}, u32[]{:S(2)}) %collective-permute-start.9) | collective-permute-done | bytes 2080 | tf_op jit(solution)/shard_map/ppermute | solution.py:52
  101.2 0.0 collective-permute-done.8
  101.2 0.0 collective-permute-done.6.source_a
  101.2 3.4 %collective-permute-start.11 = (bf16[81,128,128]{2,1,0:T(8,128)(2,1)S(1)}, bf16[81,128,128]{2,1,0:T(8,128)(2,1)S(1)}, u32[]{:S(2)}, u32[]{:S(2)}) collective-permute-start(bf16[81,128,128]{2,1,0:T(8,128)(2,1)S(1)} %collective-permute-done.6.source_a), channel_id=1, source_target_pairs={{1,0},{0,1},{3,2},{2,3},{5,4},{4,5},{7,6},{6,7},{9,8},{8,9},{11,10... | collective-permute-start | bytes 7962632 | tf_op jit(solution)/shard_map/ppermute | solution.py:48
  104.6 0.0 collective-permute-start.14
  104.7 2.0 %collective-permute-start.13 = (f32[1,512]{1,0:T(1,128)S(1)}, f32[1,512]{1,0:T(1,128)S(1)}, u32[]{:S(2)}, u32[]{:S(2)}) collective-permute-start(f32[1,512]{1,0:T(1,128)S(1)} %add_add_fusion), channel_id=1, source_target_pairs={{0,4},{1,5},{2,6},{3,7},{4,0},{5,1},{6,2},{7,3},{8,12},{9,13},{10,... | collective-permute-start | bytes 6152 | tf_op jit(solution)/shard_map/ppermute | solution.py:52
  106.7 1.4 %collective-permute-start.12 = (f32[1,512]{1,0:T(1,128)S(1)}, f32[1,512]{1,0:T(1,128)S(1)}, u32[]{:S(2)}, u32[]{:S(2)}) collective-permute-start(f32[1,512]{1,0:T(1,128)S(1)} %add_add_fusion), channel_id=1, source_target_pairs={{0,2},{1,3},{2,0},{3,1},{4,6},{5,7},{6,4},{7,5},{8,10},{9,11},{10,... | collective-permute-start | bytes 6152 | tf_op jit(solution)/shard_map/ppermute | solution.py:52
  108.1 1.1 collective-permute-done.11.source_b
  109.2 8.5 %shard_map.44 = bf16[4,20,128,128]{3,2,1,0:T(8,128)(2,1)} custom-call(bf16[512,1024]{1,0:T(8,128)(2,1)} %get-tuple-element.87.left_in, s32[4,20]{1,0:T(4,128)S(1)} %get-tuple-element.75.positions, f32[4,20,128,128]{3,2,1,0:T(8,128)} %get-tuple-element.90.prev, bf16[81,128,128]{2,1,0:T(8,128)(2,1)S(1)} %collective-permute-done.6.source_a, ...), custom_call_target="tpu_custom_call" | custom-call | flops 3758096384 | bytes 15728640 | tf_op jit(solution)/shard_map/pallas_call | solution.py:373
  117.8 0.0 collective-permute-done.14
  117.8 0.0 collective-permute-done.13
  117.8 0.0 collective-permute-done.12
  117.8 0.6 add_reduce_fusion
  (3 shorter events, 0.0 us)
Async XLA Ops:
  4.0 17.2 %collective-permute-start.5 = (bf16[81,128,128]{2,1,0:T(8,128)(2,1)}, bf16[81,128,128]{2,1,0:T(8,128)(2,1)}, u32[]{:S(2)}, u32[]{:S(2)}) collective-permute-start(bf16[81,128,128]{2,1,0:T(8,128)(2,1)} %shard_map.42), channel_id=1, source_target_pairs={{1,0},{0,1},{3,2},{2,3},{5,4},{4,5},{7,6},{6,7},{9,8},{8,9},{11,10... | collective-permute-start | bytes 7962632 | tf_op jit(solution)/shard_map/ppermute | solution.py:48
  4.6 60.3 %collective-permute-start.3 = (bf16[81,128,128]{2,1,0:T(8,128)(2,1)}, bf16[81,128,128]{2,1,0:T(8,128)(2,1)}, u32[]{:S(2)}, u32[]{:S(2)}) collective-permute-start(bf16[81,128,128]{2,1,0:T(8,128)(2,1)} %shard_map.42), channel_id=1, source_target_pairs={{29,0},{3,1},{0,2},{6,3},{1,4},{7,5},{4,6},{10,7},{5,8},{11,9},{8,... | collective-permute-start | bytes 7962632 | tf_op jit(solution)/shard_map/ppermute | solution.py:48
  7.1 58.5 %collective-permute-start.2 = (bf16[81,128,128]{2,1,0:T(8,128)(2,1)}, bf16[81,128,128]{2,1,0:T(8,128)(2,1)}, u32[]{:S(2)}, u32[]{:S(2)}) collective-permute-start(bf16[81,128,128]{2,1,0:T(8,128)(2,1)} %shard_map.42), channel_id=1, source_target_pairs={{2,0},{4,1},{31,2},{1,3},{6,4},{8,5},{3,6},{5,7},{10,8},{12,9},{7,... | collective-permute-start | bytes 7962632 | tf_op jit(solution)/shard_map/ppermute | solution.py:48
  19.9 10.9 %collective-permute-start.4 = (bf16[256,512]{1,0:T(8,128)(2,1)}, bf16[256,512]{1,0:T(8,128)(2,1)S(1)}, u32[]{:S(2)}, u32[]{:S(2)}) collective-permute-start(bf16[256,512]{1,0:T(8,128)(2,1)} %get-tuple-element.76), channel_id=1, source_target_pairs={{1,0},{2,3},{5,4},{6,7},{9,8},{10,11},{13,12},{14,15},{17,16},{18,... | collective-permute-start | bytes 786440 | tf_op jit(solution)/shard_map/ppermute | solution.py:48
  65.6 35.6 %collective-permute-start.6 = (bf16[81,128,128]{2,1,0:T(8,128)(2,1)}, bf16[81,128,128]{2,1,0:T(8,128)(2,1)S(1)}, u32[]{:S(2)}, u32[]{:S(2)}) collective-permute-start(bf16[81,128,128]{2,1,0:T(8,128)(2,1)} %collective-permute-done.2), channel_id=1, source_target_pairs={{2,0},{28,1},{7,2},{1,3},{6,4},{0,5},{11,6},{5,7},{10,8},{4,9},{15... | collective-permute-start | bytes 7962632 | tf_op jit(solution)/shard_map/ppermute | solution.py:48
  67.3 10.3 %copy-start = (bf16[512,3712]{1,0:T(8,128)(2,1)S(1)}, bf16[512,3712]{1,0:T(8,128)(2,1)}, u32[]{:S(2)}) copy-start(bf16[512,3712]{1,0:T(8,128)(2,1)} %get-tuple-element.39.left_in.left) | copy-start | bytes 11403268 | tf_op jit(solution)/shard_map/cond
  69.5 8.1 %collective-permute-start = (bf16[81,128,128]{2,1,0:T(8,128)(2,1)S(1)}, bf16[81,128,128]{2,1,0:T(8,128)(2,1)S(1)}, u32[]{:S(2)}, u32[]{:S(2)}) collective-permute-start(bf16[81,128,128]{2,1,0:T(8,128)(2,1)S(1)} %broadcast_select_fusion), channel_id=1, source_target_pairs={{1,0},{0,1},{3,2},{2,3},{5,4},{4,5},{7,6},{6,7},{9,8},{8,9},{11,10... | collective-permute-start | bytes 7962632 | tf_op jit(solution)/shard_map/cond/branch_1_fun/ppermute | solution.py:48
  70.9 21.8 %collective-permute-start.1 = (bf16[256,512]{1,0:T(8,128)(2,1)S(1)}, bf16[256,512]{1,0:T(8,128)(2,1)S(1)}, u32[]{:S(2)}, u32[]{:S(2)}) collective-permute-start(bf16[256,512]{1,0:T(8,128)(2,1)S(1)} %get-tuple-element.47), channel_id=1, source_target_pairs={{31,1},{4,2},{3,5},{8,6},{7,9},{12,10},{11,13},{16,14},{15,17},{20... | collective-permute-start | bytes 786440 | tf_op jit(solution)/shard_map/cond/branch_1_fun/ppermute | solution.py:48
  92.8 1.2 %collective-permute-start.7 = (f32[1,512]{1,0:T(1,128)S(1)}, f32[1,512]{1,0:T(1,128)S(1)}, u32[]{:S(2)}, u32[]{:S(2)}) collective-permute-start(f32[1,512]{1,0:T(1,128)S(1)} %get-tuple-element.89), channel_id=1, source_target_pairs={{0,1},{1,0},{2,3},{3,2},{4,5},{5,4},{6,7},{7,6},{8,9},{9,8},{10,11... | collective-permute-start | bytes 6152 | tf_op jit(solution)/shard_map/ppermute | solution.py:52
  94.0 5.4 %collective-permute-start.10 = (f32[1,512]{1,0:T(1,128)S(1)}, f32[1,512]{1,0:T(1,128)S(1)}, u32[]{:S(2)}, u32[]{:S(2)}) collective-permute-start(f32[1,512]{1,0:T(1,128)S(1)} %add.30), channel_id=1, source_target_pairs={{0,24},{1,25},{2,26},{3,27},{4,28},{5,29},{6,30},{7,31},{8,16},{9,... | collective-permute-start | bytes 6152 | tf_op jit(solution)/shard_map/ppermute | solution.py:52
  96.7 4.5 %collective-permute-start.9 = (f32[1,512]{1,0:T(1,128)S(1)}, f32[1,512]{1,0:T(1,128)S(1)}, u32[]{:S(2)}, u32[]{:S(2)}) collective-permute-start(f32[1,512]{1,0:T(1,128)S(1)} %add.30), channel_id=1, source_target_pairs={{0,16},{1,17},{2,18},{3,19},{4,20},{5,21},{6,22},{7,23},{8,24},{9,... | collective-permute-start | bytes 6152 | tf_op jit(solution)/shard_map/ppermute | solution.py:52
  96.7 4.5 %collective-permute-start.8 = (f32[1,512]{1,0:T(1,128)S(1)}, f32[1,512]{1,0:T(1,128)S(1)}, u32[]{:S(2)}, u32[]{:S(2)}) collective-permute-start(f32[1,512]{1,0:T(1,128)S(1)} %add.30), channel_id=1, source_target_pairs={{0,8},{1,9},{2,10},{3,11},{4,12},{5,13},{6,14},{7,15},{8,0},{9,1},... | collective-permute-start | bytes 6152 | tf_op jit(solution)/shard_map/ppermute | solution.py:52
  101.2 8.0 %collective-permute-start.11 = (bf16[81,128,128]{2,1,0:T(8,128)(2,1)S(1)}, bf16[81,128,128]{2,1,0:T(8,128)(2,1)S(1)}, u32[]{:S(2)}, u32[]{:S(2)}) collective-permute-start(bf16[81,128,128]{2,1,0:T(8,128)(2,1)S(1)} %collective-permute-done.6.source_a), channel_id=1, source_target_pairs={{1,0},{0,1},{3,2},{2,3},{5,4},{4,5},{7,6},{6,7},{9,8},{8,9},{11,10... | collective-permute-start | bytes 7962632 | tf_op jit(solution)/shard_map/ppermute | solution.py:48
  104.6 13.1 %collective-permute-start.14 = (f32[1,512]{1,0:T(1,128)S(1)}, f32[1,512]{1,0:T(1,128)S(1)}, u32[]{:S(2)}, u32[]{:S(2)}) collective-permute-start(f32[1,512]{1,0:T(1,128)S(1)} %add_add_fusion), channel_id=1, source_target_pairs={{0,6},{1,7},{2,4},{3,5},{4,2},{5,3},{6,0},{7,1},{8,14},{9,15},{10,... | collective-permute-start | bytes 6152 | tf_op jit(solution)/shard_map/ppermute | solution.py:52
  104.7 13.1 %collective-permute-start.13 = (f32[1,512]{1,0:T(1,128)S(1)}, f32[1,512]{1,0:T(1,128)S(1)}, u32[]{:S(2)}, u32[]{:S(2)}) collective-permute-start(f32[1,512]{1,0:T(1,128)S(1)} %add_add_fusion), channel_id=1, source_target_pairs={{0,4},{1,5},{2,6},{3,7},{4,0},{5,1},{6,2},{7,3},{8,12},{9,13},{10,... | collective-permute-start | bytes 6152 | tf_op jit(solution)/shard_map/ppermute | solution.py:52
  106.7 11.1 %collective-permute-start.12 = (f32[1,512]{1,0:T(1,128)S(1)}, f32[1,512]{1,0:T(1,128)S(1)}, u32[]{:S(2)}, u32[]{:S(2)}) collective-permute-start(f32[1,512]{1,0:T(1,128)S(1)} %add_add_fusion), channel_id=1, source_target_pairs={{0,2},{1,3},{2,0},{3,1},{4,6},{5,7},{6,4},{7,5},{8,10},{9,11},{10,... | collective-permute-start | bytes 6152 | tf_op jit(solution)/shard_map/ppermute | solution.py:52

commit v16 on v15

--- a/solution.py
+++ b/solution.py
@@ -447,7 +447,8 @@
     total, trace = near(("beside",), [beside], total, trace)
     first, second, corner, total, trace = lax.optimization_barrier((first, second, corner, total, trace))
     relay = receive(first, RELAY_FROM)
-    kind = lax.axis_index(AXES) % 4
+    device = lax.axis_index(AXES)
+    kind = device % 4
 
     def nearby(first, second, corner, total, trace):
         use_first = (kind == 0) | (kind == 3)
@@ -464,7 +465,7 @@
         return jnp.zeros_like(total), jnp.zeros_like(trace), jnp.zeros((z.span, 2 * z.span), dtype)
 
     total, trace, relay_left = lax.cond(
-        positions[0, 0] >= 0, nearby, nothing, first, second, corner, total, trace
+        device < devices, nearby, nothing, first, second, corner, total, trace
     )
     assert devices & (devices - 1) == 0
     steps = [1 << bit for bit in range(devices.bit_length() - 1)]

time: 121 us -> 121 us (level)
  transfers between devices with their start and end apart: 15 -> 15, of which waited for: 6 -> 7; matrix products, arithmetic and copies ran while one was open for 2% -> 2% of each run, Pallas kernels for 36% -> 36%
where the time goes in v16:
time: 121 us; the launch traced here: 120 us
  Pallas kernels  46.4 us (38%)
  waiting for transfers between devices  40.4 us (33%)
  starting transfers between devices  28 us (23%)
  other arithmetic  2.8 us (2%)
  between operations  2.51 us (2%)
    pallas_call x6, Pallas kernels, call(): pl.pallas_call(kernel, out_shape=out_shape, in_specs=in_specs, out_specs=...  46.4 us
    ppermute x8, waiting for transfers between devices, receive(): return lax.ppermute(shard, AXES, pairs)  36.4 us
    ppermute x8, starting transfers between devices, receive(): return lax.ppermute(shard, AXES, pairs)  20.1 us
    ppermute x7, starting transfers between devices, fetch(): lax.ppermute(value, AXES, [(d, d ^ step) for d in range(lax.axis_size(AXE...  7.95 us
    ppermute x7, waiting for transfers between devices, fetch(): lax.ppermute(value, AXES, [(d, d ^ step) for d in range(lax.axis_size(AXE...  3.97 us
  transfers between devices with their start and end apart: 15, of which 7 were waited for; matrix products, arithmetic and copies ran while one was open for 2% of the time, Pallas kernels for 36%

profile of v16, /device:TPU:0, one launch (start us, length us, event | category | flops | bytes accessed | tf_op | source)
XLA Modules:
  0.0 120.2 jit_solution(17263566131706056221)
XLA Ops:
  0.6 3.4 %shard_map.41 = bf16[81,128,128]{2,1,0:T(8,128)(2,1)} custom-call(bf16[4,20,128,128]{3,2,1,0:T(8,128)(2,1)} %own.1, s32[4,20]{1,0:T(4,128)} %columns.3), custom_call_target="tpu_custom_call" | custom-call | bytes 10485760 | tf_op jit(solution)/shard_map/pallas_call | solution.py:373
  4.0 0.5 collective-permute-start.5
  4.6 2.6 %collective-permute-start.3 = (bf16[81,128,128]{2,1,0:T(8,128)(2,1)}, bf16[81,128,128]{2,1,0:T(8,128)(2,1)}, u32[]{:S(2)}, u32[]{:S(2)}) collective-permute-start(bf16[81,128,128]{2,1,0:T(8,128)(2,1)} %shard_map.41), channel_id=1, source_target_pairs={{29,0},{3,1},{0,2},{6,3},{1,4},{7,5},{4,6},{10,7},{5,8},{11,9},{8,... | collective-permute-start | bytes 7962632 | tf_op jit(solution)/shard_map/ppermute | solution.py:48
  7.1 3.1 %collective-permute-start.2 = (bf16[81,128,128]{2,1,0:T(8,128)(2,1)}, bf16[81,128,128]{2,1,0:T(8,128)(2,1)}, u32[]{:S(2)}, u32[]{:S(2)}) collective-permute-start(bf16[81,128,128]{2,1,0:T(8,128)(2,1)} %shard_map.41), channel_id=1, source_target_pairs={{2,0},{4,1},{31,2},{1,3},{6,4},{8,5},{3,6},{5,7},{10,8},{12,9},{7,... | collective-permute-start | bytes 7962632 | tf_op jit(solution)/shard_map/ppermute | solution.py:48
  10.2 9.7 %shard_map.42 = (f32[4,20,128,128]{3,2,1,0:T(8,128)}, bf16[512,3712]{1,0:T(8,128)(2,1)}, bf16[256,512]{1,0:T(8,128)(2,1)}, s32[4,20]{1,0:T(4,128)S(1)}, f32[1,512]{1,0:T(1,128)}) custom-call(bf16[4,20,128,128]{3,2,1,0:T(8,128)(2,1)} %own.1, s32[4,20]{1,0:T(4,128)} %columns.3), custom_call_target="tpu_custom_call" | custom-call | flops 1879048192 | bytes 13107200 | tf_op jit(solution)/shard_map/pallas_call | solution.py:373
  19.9 1.3 %collective-permute-start.4 = (bf16[256,512]{1,0:T(8,128)(2,1)}, bf16[256,512]{1,0:T(8,128)(2,1)S(1)}, u32[]{:S(2)}, u32[]{:S(2)}) collective-permute-start(bf16[256,512]{1,0:T(8,128)(2,1)} %get-tuple-element.75), channel_id=1, source_target_pairs={{1,0},{2,3},{5,4},{6,7},{9,8},{10,11},{13,12},{14,15},{17,16},{18,... | collective-permute-start | bytes 786440 | tf_op jit(solution)/shard_map/ppermute | solution.py:48
  21.2 0.0 collective-permute-done.5.refs_0_
  21.3 9.6 %shard_map.43 = (f32[4,20,128,128]{3,2,1,0:T(8,128)}, f32[1,512]{1,0:T(1,128)S(1)}) custom-call(bf16[512,3712]{1,0:T(8,128)(2,1)} %get-tuple-element.76.left_in, s32[4,20]{1,0:T(4,128)S(1)} %get-tuple-element.77.positions, f32[4,20,128,128]{3,2,1,0:T(8,128)} %get-tuple-element.78.prev, f32[1,512]{1,0:T(1,128)} %get-tuple-element.79.trace_in, ...), custom_call_target="tpu_custom_call" | custom-call | flops 1879048192 | bytes 13107200 | tf_op jit(solution)/shard_map/pallas_call | solution.py:373
  30.9 0.0 collective-permute-done.4
  30.9 34.0 %collective-permute-done.3 = bf16[81,128,128]{2,1,0:T(8,128)(2,1)} collective-permute-done((bf16[81,128,128]{2,1,0:T(8,128)(2,1)}, bf16[81,128,128]{2,1,0:T(8,128)(2,1)}, u32[]{:S(2)}, u32[]{:S(2)}) %collective-permute-start.3) | collective-permute-done | bytes 2654240 | tf_op jit(solution)/shard_map/ppermute | solution.py:48
  64.9 0.7 collective-permute-done.2
  65.6 0.5 collective-permute-start.6
  66.1 25.5 %conditional.1 = (f32[4,20,128,128]{3,2,1,0:T(8,128)}, f32[1,512]{1,0:T(1,128)S(1)}, bf16[512,1024]{1,0:T(8,128)(2,1)}) conditional(s32[]{:T(128)} %convert_element_type.3, () %tuple.22, (s32[]{:T(128)}, bf16[81,128,128]{2,1,0:T(8,128)(2,1)}, bf16[81,128,128]{2,1,0:T(8,128)(2,1)}, bf16[512,3712]{1,0:T(8,128)(2,1)}, s32[4,20]{1,0:T(4,128)S(1)}, ...), branch_computations={%region_0.1_spmd, %region_1.2_spmd} | conditional | flops 5638471680 | bytes 63668488 | solution.py:467
  66.1 0.0 copy-start
  66.1 2.2 %broadcast_select_fusion = bf16[81,128,128]{2,1,0:T(8,128)(2,1)S(1)} fusion(bf16[81,128,128]{2,1,0:T(8,128)(2,1)} %get-tuple-element.43.refs_0_, bf16[81,128,128]{2,1,0:T(8,128)(2,1)} %get-tuple-element.44.refs_1_, pred[]{:T(512)S(6)} %or.2), kind=kLoop, calls=%fused_computation | loop fusion | flops 1327104 | bytes 7962625 | tf_op jit(solution)/shard_map/cond/branch_1_fun/jit(_where)/select_n | solution.py:455
  68.3 1.5 %collective-permute-start = (bf16[81,128,128]{2,1,0:T(8,128)(2,1)S(1)}, bf16[81,128,128]{2,1,0:T(8,128)(2,1)S(1)}, u32[]{:S(2)}, u32[]{:S(2)}) collective-permute-start(bf16[81,128,128]{2,1,0:T(8,128)(2,1)S(1)} %broadcast_select_fusion), channel_id=1, source_target_pairs={{1,0},{0,1},{3,2},{2,3},{5,4},{4,5},{7,6},{6,7},{9,8},{8,9},{11,10... | collective-permute-start | bytes 7962632 | tf_op jit(solution)/shard_map/cond/branch_1_fun/ppermute | solution.py:48
  69.7 6.7 %collective-permute-start.1 = (bf16[256,512]{1,0:T(8,128)(2,1)S(1)}, bf16[256,512]{1,0:T(8,128)(2,1)S(1)}, u32[]{:S(2)}, u32[]{:S(2)}) collective-permute-start(bf16[256,512]{1,0:T(8,128)(2,1)S(1)} %get-tuple-element.47), channel_id=1, source_target_pairs={{31,1},{4,2},{3,5},{8,6},{7,9},{12,10},{11,13},{16,14},{15,17},{20... | collective-permute-start | bytes 786440 | tf_op jit(solution)/shard_map/cond/branch_1_fun/ppermute | solution.py:48
  76.4 0.0 collective-permute-done.refs_2_
  76.4 0.0 copy-done
  76.4 15.1 %branch_1_fun.2 = (f32[4,20,128,128]{3,2,1,0:T(8,128)}, f32[1,512]{1,0:T(1,128)S(1)}, bf16[512,1024]{1,0:T(8,128)(2,1)}) custom-call(bf16[512,3712]{1,0:T(8,128)(2,1)S(1)} %copy-done, s32[4,20]{1,0:T(4,128)S(1)} %get-tuple-element.40.positions, f32[4,20,128,128]{3,2,1,0:T(8,128)} %get-tuple-element.41.prev, f32[1,512]{1,0:T(1,128)S(1)} %get-tuple-element.42.trace_in, ...), custom_call_target="tpu_custom_call" | custom-call | flops 5637144576 | bytes 18350080 | tf_op jit(solution)/shard_map/cond/branch_1_fun/pallas_call | solution.py:373
  91.5 0.0 collective-permute-done.1.corner
  91.6 0.1 collective-permute-start.7
  91.6 1.1 collective-permute-done.7
  92.8 2.7 %collective-permute-start.10 = (f32[1,512]{1,0:T(1,128)S(1)}, f32[1,512]{1,0:T(1,128)S(1)}, u32[]{:S(2)}, u32[]{:S(2)}) collective-permute-start(f32[1,512]{1,0:T(1,128)S(1)} %add.30), channel_id=1, source_target_pairs={{0,24},{1,25},{2,26},{3,27},{4,28},{5,29},{6,30},{7,31},{8,16},{9,... | collective-permute-start | bytes 6152 | tf_op jit(solution)/shard_map/ppermute | solution.py:52
  95.5 0.0 collective-permute-start.9
  95.5 1.7 %collective-permute-start.8 = (f32[1,512]{1,0:T(1,128)S(1)}, f32[1,512]{1,0:T(1,128)S(1)}, u32[]{:S(2)}, u32[]{:S(2)}) collective-permute-start(f32[1,512]{1,0:T(1,128)S(1)} %add.30), channel_id=1, source_target_pairs={{0,8},{1,9},{2,10},{3,11},{4,12},{5,13},{6,14},{7,15},{8,0},{9,1},... | collective-permute-start | bytes 6152 | tf_op jit(solution)/shard_map/ppermute | solution.py:52
  97.2 1.0 collective-permute-done.10
  98.2 1.8 %collective-permute-done.9 = f32[1,512]{1,0:T(1,128)S(1)} collective-permute-done((f32[1,512]{1,0:T(1,128)S(1)}, f32[1,512]{1,0:T(1,128)S(1)}, u32[]{:S(2)}, u32[]{:S(2)}) %collective-permute-start.9) | collective-permute-done | bytes 2080 | tf_op jit(solution)/shard_map/ppermute | solution.py:52
  100.0 0.0 collective-permute-done.8
  100.0 0.6 collective-permute-done.6.source_a
  100.6 4.0 %collective-permute-start.11 = (bf16[81,128,128]{2,1,0:T(8,128)(2,1)S(1)}, bf16[81,128,128]{2,1,0:T(8,128)(2,1)S(1)}, u32[]{:S(2)}, u32[]{:S(2)}) collective-permute-start(bf16[81,128,128]{2,1,0:T(8,128)(2,1)S(1)} %collective-permute-done.6.source_a), channel_id=1, source_target_pairs={{1,0},{0,1},{3,2},{2,3},{5,4},{4,5},{7,6},{6,7},{9,8},{8,9},{11,10... | collective-permute-start | bytes 7962632 | tf_op jit(solution)/shard_map/ppermute | solution.py:48
  104.6 0.0 collective-permute-start.14
  104.7 2.0 %collective-permute-start.13 = (f32[1,512]{1,0:T(1,128)S(1)}, f32[1,512]{1,0:T(1,128)S(1)}, u32[]{:S(2)}, u32[]{:S(2)}) collective-permute-start(f32[1,512]{1,0:T(1,128)S(1)} %add_add_fusion), channel_id=1, source_target_pairs={{0,4},{1,5},{2,6},{3,7},{4,0},{5,1},{6,2},{7,3},{8,12},{9,13},{10,... | collective-permute-start | bytes 6152 | tf_op jit(solution)/shard_map/ppermute | solution.py:52
  106.7 1.4 %collective-permute-start.12 = (f32[1,512]{1,0:T(1,128)S(1)}, f32[1,512]{1,0:T(1,128)S(1)}, u32[]{:S(2)}, u32[]{:S(2)}) collective-permute-start(f32[1,512]{1,0:T(1,128)S(1)} %add_add_fusion), channel_id=1, source_target_pairs={{0,2},{1,3},{2,0},{3,1},{4,6},{5,7},{6,4},{7,5},{8,10},{9,11},{10,... | collective-permute-start | bytes 6152 | tf_op jit(solution)/shard_map/ppermute | solution.py:52
  108.1 1.1 collective-permute-done.11.source_b
  109.2 8.5 %shard_map.44 = bf16[4,20,128,128]{3,2,1,0:T(8,128)(2,1)} custom-call(bf16[512,1024]{1,0:T(8,128)(2,1)} %get-tuple-element.87.left_in, s32[4,20]{1,0:T(4,128)S(1)} %get-tuple-element.77.positions, f32[4,20,128,128]{3,2,1,0:T(8,128)} %get-tuple-element.90.prev, bf16[81,128,128]{2,1,0:T(8,128)(2,1)S(1)} %collective-permute-done.6.source_a, ...), custom_call_target="tpu_custom_call" | custom-call | flops 3758096384 | bytes 15728640 | tf_op jit(solution)/shard_map/pallas_call | solution.py:373
  117.8 0.0 collective-permute-done.14
  117.8 0.0 collective-permute-done.13
  117.8 0.0 collective-permute-done.12
  117.8 0.6 add_reduce_fusion
  (3 shorter events, 0.0 us)
Async XLA Ops:
  4.0 17.2 %collective-permute-start.5 = (bf16[81,128,128]{2,1,0:T(8,128)(2,1)}, bf16[81,128,128]{2,1,0:T(8,128)(2,1)}, u32[]{:S(2)}, u32[]{:S(2)}) collective-permute-start(bf16[81,128,128]{2,1,0:T(8,128)(2,1)} %shard_map.41), channel_id=1, source_target_pairs={{1,0},{0,1},{3,2},{2,3},{5,4},{4,5},{7,6},{6,7},{9,8},{8,9},{11,10... | collective-permute-start | bytes 7962632 | tf_op jit(solution)/shard_map/ppermute | solution.py:48
  4.6 60.3 %collective-permute-start.3 = (bf16[81,128,128]{2,1,0:T(8,128)(2,1)}, bf16[81,128,128]{2,1,0:T(8,128)(2,1)}, u32[]{:S(2)}, u32[]{:S(2)}) collective-permute-start(bf16[81,128,128]{2,1,0:T(8,128)(2,1)} %shard_map.41), channel_id=1, source_target_pairs={{29,0},{3,1},{0,2},{6,3},{1,4},{7,5},{4,6},{10,7},{5,8},{11,9},{8,... | collective-permute-start | bytes 7962632 | tf_op jit(solution)/shard_map/ppermute | solution.py:48
  7.1 58.5 %collective-permute-start.2 = (bf16[81,128,128]{2,1,0:T(8,128)(2,1)}, bf16[81,128,128]{2,1,0:T(8,128)(2,1)}, u32[]{:S(2)}, u32[]{:S(2)}) collective-permute-start(bf16[81,128,128]{2,1,0:T(8,128)(2,1)} %shard_map.41), channel_id=1, source_target_pairs={{2,0},{4,1},{31,2},{1,3},{6,4},{8,5},{3,6},{5,7},{10,8},{12,9},{7,... | collective-permute-start | bytes 7962632 | tf_op jit(solution)/shard_map/ppermute | solution.py:48
  19.9 10.9 %collective-permute-start.4 = (bf16[256,512]{1,0:T(8,128)(2,1)}, bf16[256,512]{1,0:T(8,128)(2,1)S(1)}, u32[]{:S(2)}, u32[]{:S(2)}) collective-permute-start(bf16[256,512]{1,0:T(8,128)(2,1)} %get-tuple-element.75), channel_id=1, source_target_pairs={{1,0},{2,3},{5,4},{6,7},{9,8},{10,11},{13,12},{14,15},{17,16},{18,... | collective-permute-start | bytes 786440 | tf_op jit(solution)/shard_map/ppermute | solution.py:48
  65.6 35.0 %collective-permute-start.6 = (bf16[81,128,128]{2,1,0:T(8,128)(2,1)}, bf16[81,128,128]{2,1,0:T(8,128)(2,1)S(1)}, u32[]{:S(2)}, u32[]{:S(2)}) collective-permute-start(bf16[81,128,128]{2,1,0:T(8,128)(2,1)} %collective-permute-done.2), channel_id=1, source_target_pairs={{2,0},{28,1},{7,2},{1,3},{6,4},{0,5},{11,6},{5,7},{10,8},{4,9},{15... | collective-permute-start | bytes 7962632 | tf_op jit(solution)/shard_map/ppermute | solution.py:48
  66.1 10.3 %copy-start = (bf16[512,3712]{1,0:T(8,128)(2,1)S(1)}, bf16[512,3712]{1,0:T(8,128)(2,1)}, u32[]{:S(2)}) copy-start(bf16[512,3712]{1,0:T(8,128)(2,1)} %get-tuple-element.39.left_in.left) | copy-start | bytes 11403268 | tf_op jit(solution)/shard_map/cond
  68.3 8.1 %collective-permute-start = (bf16[81,128,128]{2,1,0:T(8,128)(2,1)S(1)}, bf16[81,128,128]{2,1,0:T(8,128)(2,1)S(1)}, u32[]{:S(2)}, u32[]{:S(2)}) collective-permute-start(bf16[81,128,128]{2,1,0:T(8,128)(2,1)S(1)} %broadcast_select_fusion), channel_id=1, source_target_pairs={{1,0},{0,1},{3,2},{2,3},{5,4},{4,5},{7,6},{6,7},{9,8},{8,9},{11,10... | collective-permute-start | bytes 7962632 | tf_op jit(solution)/shard_map/cond/branch_1_fun/ppermute | solution.py:48
  69.7 21.8 %collective-permute-start.1 = (bf16[256,512]{1,0:T(8,128)(2,1)S(1)}, bf16[256,512]{1,0:T(8,128)(2,1)S(1)}, u32[]{:S(2)}, u32[]{:S(2)}) collective-permute-start(bf16[256,512]{1,0:T(8,128)(2,1)S(1)} %get-tuple-element.47), channel_id=1, source_target_pairs={{31,1},{4,2},{3,5},{8,6},{7,9},{12,10},{11,13},{16,14},{15,17},{20... | collective-permute-start | bytes 786440 | tf_op jit(solution)/shard_map/cond/branch_1_fun/ppermute | solution.py:48
  91.6 1.2 %collective-permute-start.7 = (f32[1,512]{1,0:T(1,128)S(1)}, f32[1,512]{1,0:T(1,128)S(1)}, u32[]{:S(2)}, u32[]{:S(2)}) collective-permute-start(f32[1,512]{1,0:T(1,128)S(1)} %get-tuple-element.89), channel_id=1, source_target_pairs={{0,1},{1,0},{2,3},{3,2},{4,5},{5,4},{6,7},{7,6},{8,9},{9,8},{10,11... | collective-permute-start | bytes 6152 | tf_op jit(solution)/shard_map/ppermute | solution.py:52
  92.8 5.4 %collective-permute-start.10 = (f32[1,512]{1,0:T(1,128)S(1)}, f32[1,512]{1,0:T(1,128)S(1)}, u32[]{:S(2)}, u32[]{:S(2)}) collective-permute-start(f32[1,512]{1,0:T(1,128)S(1)} %add.30), channel_id=1, source_target_pairs={{0,24},{1,25},{2,26},{3,27},{4,28},{5,29},{6,30},{7,31},{8,16},{9,... | collective-permute-start | bytes 6152 | tf_op jit(solution)/shard_map/ppermute | solution.py:52
  95.5 4.5 %collective-permute-start.9 = (f32[1,512]{1,0:T(1,128)S(1)}, f32[1,512]{1,0:T(1,128)S(1)}, u32[]{:S(2)}, u32[]{:S(2)}) collective-permute-start(f32[1,512]{1,0:T(1,128)S(1)} %add.30), channel_id=1, source_target_pairs={{0,16},{1,17},{2,18},{3,19},{4,20},{5,21},{6,22},{7,23},{8,24},{9,... | collective-permute-start | bytes 6152 | tf_op jit(solution)/shard_map/ppermute | solution.py:52
  95.5 4.5 %collective-permute-start.8 = (f32[1,512]{1,0:T(1,128)S(1)}, f32[1,512]{1,0:T(1,128)S(1)}, u32[]{:S(2)}, u32[]{:S(2)}) collective-permute-start(f32[1,512]{1,0:T(1,128)S(1)} %add.30), channel_id=1, source_target_pairs={{0,8},{1,9},{2,10},{3,11},{4,12},{5,13},{6,14},{7,15},{8,0},{9,1},... | collective-permute-start | bytes 6152 | tf_op jit(solution)/shard_map/ppermute | solution.py:52
  100.6 8.6 %collective-permute-start.11 = (bf16[81,128,128]{2,1,0:T(8,128)(2,1)S(1)}, bf16[81,128,128]{2,1,0:T(8,128)(2,1)S(1)}, u32[]{:S(2)}, u32[]{:S(2)}) collective-permute-start(bf16[81,128,128]{2,1,0:T(8,128)(2,1)S(1)} %collective-permute-done.6.source_a), channel_id=1, source_target_pairs={{1,0},{0,1},{3,2},{2,3},{5,4},{4,5},{7,6},{6,7},{9,8},{8,9},{11,10... | collective-permute-start | bytes 7962632 | tf_op jit(solution)/shard_map/ppermute | solution.py:48
  104.6 13.1 %collective-permute-start.14 = (f32[1,512]{1,0:T(1,128)S(1)}, f32[1,512]{1,0:T(1,128)S(1)}, u32[]{:S(2)}, u32[]{:S(2)}) collective-permute-start(f32[1,512]{1,0:T(1,128)S(1)} %add_add_fusion), channel_id=1, source_target_pairs={{0,6},{1,7},{2,4},{3,5},{4,2},{5,3},{6,0},{7,1},{8,14},{9,15},{10,... | collective-permute-start | bytes 6152 | tf_op jit(solution)/shard_map/ppermute | solution.py:52
  104.7 13.1 %collective-permute-start.13 = (f32[1,512]{1,0:T(1,128)S(1)}, f32[1,512]{1,0:T(1,128)S(1)}, u32[]{:S(2)}, u32[]{:S(2)}) collective-permute-start(f32[1,512]{1,0:T(1,128)S(1)} %add_add_fusion), channel_id=1, source_target_pairs={{0,4},{1,5},{2,6},{3,7},{4,0},{5,1},{6,2},{7,3},{8,12},{9,13},{10,... | collective-permute-start | bytes 6152 | tf_op jit(solution)/shard_map/ppermute | solution.py:52
  106.7 11.1 %collective-permute-start.12 = (f32[1,512]{1,0:T(1,128)S(1)}, f32[1,512]{1,0:T(1,128)S(1)}, u32[]{:S(2)}, u32[]{:S(2)}) collective-permute-start(f32[1,512]{1,0:T(1,128)S(1)} %add_add_fusion), channel_id=1, source_target_pairs={{0,2},{1,3},{2,0},{3,1},{4,6},{5,7},{6,4},{7,5},{8,10},{9,11},{10,... | collective-permute-start | bytes 6152 | tf_op jit(solution)/shard_map/ppermute | solution.py:52

commit v17 on v16

--- a/solution.py
+++ b/solution.py
@@ -453,6 +453,7 @@
     def nearby(first, second, corner, total, trace):
         use_first = (kind == 0) | (kind == 3)
         mixed = receive(jnp.where(use_first, first, second), PARTNER)
+        mixed, corner = lax.optimization_barrier((mixed, corner))
         corner = receive(corner, (0, -2, 2, 0), (LOWER, UPPER))
         total, trace, relay_left = near(("first", "second", "mixed"), [first, second, mixed], total, trace, True)
         trace = call(

time: 121 us -> 121 us (level)
  waiting for transfers between devices: 40.4 us -> 43.1 us
  starting transfers between devices: 28 us -> 25.4 us
    ppermute x8, waiting for transfers between devices: 36.4 us -> 40.4 us  [receive(): return lax.ppermute(shard, AXES, pairs)]
    ppermute x8, starting transfers between devices: 20.1 us -> 17.4 us  [receive(): return lax.ppermute(shard, AXES, pairs)]
    ppermute x7, waiting for transfers between devices: 3.97 us -> 2.71 us  [fetch(): lax.ppermute(value, AXES, [(d, d ^ step) for d in range(lax.axis_size(AXE...]
where the time goes in v17:
time: 121 us; the launch traced here: 120 us
  Pallas kernels  46.3 us (38%)
  waiting for transfers between devices  43.1 us (36%)
  starting transfers between devices  25.4 us (21%)
  other arithmetic  2.8 us (2%)
  between operations  2.51 us (2%)
    pallas_call x6, Pallas kernels, call(): pl.pallas_call(kernel, out_shape=out_shape, in_specs=in_specs, out_specs=...  46.3 us
    ppermute x8, waiting for transfers between devices, receive(): return lax.ppermute(shard, AXES, pairs)  40.4 us
    ppermute x8, starting transfers between devices, receive(): return lax.ppermute(shard, AXES, pairs)  17.4 us
    ppermute x7, starting transfers between devices, fetch(): lax.ppermute(value, AXES, [(d, d ^ step) for d in range(lax.axis_size(AXE...  7.95 us
    ppermute x7, waiting for transfers between devices, fetch(): lax.ppermute(value, AXES, [(d, d ^ step) for d in range(lax.axis_size(AXE...  2.71 us
  transfers between devices with their start and end apart: 15, of which 7 were waited for; matrix products, arithmetic and copies ran while one was open for 2% of the time, Pallas kernels for 36%

profile of v17, /device:TPU:0, one launch (start us, length us, event | category | flops | bytes accessed | tf_op | source)
XLA Modules:
  0.0 120.2 jit_solution(16060204237930947754)
XLA Ops:
  0.6 3.4 %shard_map.41 = bf16[81,128,128]{2,1,0:T(8,128)(2,1)} custom-call(bf16[4,20,128,128]{3,2,1,0:T(8,128)(2,1)} %own.1, s32[4,20]{1,0:T(4,128)} %columns.3), custom_call_target="tpu_custom_call" | custom-call | bytes 10485760 | tf_op jit(solution)/shard_map/pallas_call | solution.py:373
  4.0 0.5 collective-permute-start.5
  4.6 2.6 %collective-permute-start.3 = (bf16[81,128,128]{2,1,0:T(8,128)(2,1)}, bf16[81,128,128]{2,1,0:T(8,128)(2,1)}, u32[]{:S(2)}, u32[]{:S(2)}) collective-permute-start(bf16[81,128,128]{2,1,0:T(8,128)(2,1)} %shard_map.41), channel_id=1, source_target_pairs={{29,0},{3,1},{0,2},{6,3},{1,4},{7,5},{4,6},{10,7},{5,8},{11,9},{8,... | collective-permute-start | bytes 7962632 | tf_op jit(solution)/shard_map/ppermute | solution.py:48
  7.1 3.1 %collective-permute-start.2 = (bf16[81,128,128]{2,1,0:T(8,128)(2,1)}, bf16[81,128,128]{2,1,0:T(8,128)(2,1)}, u32[]{:S(2)}, u32[]{:S(2)}) collective-permute-start(bf16[81,128,128]{2,1,0:T(8,128)(2,1)} %shard_map.41), channel_id=1, source_target_pairs={{2,0},{4,1},{31,2},{1,3},{6,4},{8,5},{3,6},{5,7},{10,8},{12,9},{7,... | collective-permute-start | bytes 7962632 | tf_op jit(solution)/shard_map/ppermute | solution.py:48
  10.2 9.7 %shard_map.42 = (f32[4,20,128,128]{3,2,1,0:T(8,128)}, bf16[512,3712]{1,0:T(8,128)(2,1)}, bf16[256,512]{1,0:T(8,128)(2,1)}, s32[4,20]{1,0:T(4,128)S(1)}, f32[1,512]{1,0:T(1,128)}) custom-call(bf16[4,20,128,128]{3,2,1,0:T(8,128)(2,1)} %own.1, s32[4,20]{1,0:T(4,128)} %columns.3), custom_call_target="tpu_custom_call" | custom-call | flops 1879048192 | bytes 13107200 | tf_op jit(solution)/shard_map/pallas_call | solution.py:373
  19.9 1.3 %collective-permute-start.4 = (bf16[256,512]{1,0:T(8,128)(2,1)}, bf16[256,512]{1,0:T(8,128)(2,1)S(1)}, u32[]{:S(2)}, u32[]{:S(2)}) collective-permute-start(bf16[256,512]{1,0:T(8,128)(2,1)} %get-tuple-element.77), channel_id=1, source_target_pairs={{1,0},{2,3},{5,4},{6,7},{9,8},{10,11},{13,12},{14,15},{17,16},{18,... | collective-permute-start | bytes 786440 | tf_op jit(solution)/shard_map/ppermute | solution.py:48
  21.2 0.0 collective-permute-done.5.refs_0_
  21.3 9.6 %shard_map.43 = (f32[4,20,128,128]{3,2,1,0:T(8,128)}, f32[1,512]{1,0:T(1,128)S(1)}) custom-call(bf16[512,3712]{1,0:T(8,128)(2,1)} %get-tuple-element.78.left_in, s32[4,20]{1,0:T(4,128)S(1)} %get-tuple-element.79.positions, f32[4,20,128,128]{3,2,1,0:T(8,128)} %get-tuple-element.80.prev, f32[1,512]{1,0:T(1,128)} %get-tuple-element.81.trace_in, ...), custom_call_target="tpu_custom_call" | custom-call | flops 1879048192 | bytes 13107200 | tf_op jit(solution)/shard_map/pallas_call | solution.py:373
  30.9 0.0 collective-permute-done.4
  30.9 34.0 %collective-permute-done.3 = bf16[81,128,128]{2,1,0:T(8,128)(2,1)} collective-permute-done((bf16[81,128,128]{2,1,0:T(8,128)(2,1)}, bf16[81,128,128]{2,1,0:T(8,128)(2,1)}, u32[]{:S(2)}, u32[]{:S(2)}) %collective-permute-start.3) | collective-permute-done | bytes 2654240 | tf_op jit(solution)/shard_map/ppermute | solution.py:48
  64.9 0.7 collective-permute-done.2
  65.6 0.5 collective-permute-start.6
  66.1 30.1 %conditional.1 = (f32[4,20,128,128]{3,2,1,0:T(8,128)}, f32[1,512]{1,0:T(1,128)S(1)}, bf16[512,1024]{1,0:T(8,128)(2,1)}) conditional(s32[]{:T(128)} %convert_element_type.3, () %tuple.23, (s32[]{:T(128)}, bf16[81,128,128]{2,1,0:T(8,128)(2,1)}, bf16[81,128,128]{2,1,0:T(8,128)(2,1)}, bf16[256,512]{1,0:T(8,128)(2,1)S(1)}, bf16[512,3712]{1,0:T(8,128)(2,1)}, ...), branch_computations={%region_0.1_spmd, %region_1.2_spmd} | conditional | flops 5638471680 | bytes 63668488 | solution.py:468
  66.1 0.0 copy-start
  66.1 2.2 %broadcast_select_fusion = bf16[81,128,128]{2,1,0:T(8,128)(2,1)S(1)} fusion(bf16[81,128,128]{2,1,0:T(8,128)(2,1)} %get-tuple-element.43.refs_0_, bf16[81,128,128]{2,1,0:T(8,128)(2,1)} %get-tuple-element.44.refs_1_, pred[]{:T(512)S(6)} %or.2), kind=kLoop, calls=%fused_computation | loop fusion | flops 1327104 | bytes 7962625 | tf_op jit(solution)/shard_map/cond/branch_1_fun/jit(_where)/select_n | solution.py:455
  68.3 1.5 %collective-permute-start = (bf16[81,128,128]{2,1,0:T(8,128)(2,1)S(1)}, bf16[81,128,128]{2,1,0:T(8,128)(2,1)S(1)}, u32[]{:S(2)}, u32[]{:S(2)}) collective-permute-start(bf16[81,128,128]{2,1,0:T(8,128)(2,1)S(1)} %broadcast_select_fusion), channel_id=1, source_target_pairs={{1,0},{0,1},{3,2},{2,3},{5,4},{4,5},{7,6},{6,7},{9,8},{8,9},{11,10... | collective-permute-start | bytes 7962632 | tf_op jit(solution)/shard_map/cond/branch_1_fun/ppermute | solution.py:48
  69.7 4.6 %collective-permute-done.refs_2_ = bf16[81,128,128]{2,1,0:T(8,128)(2,1)S(1)} collective-permute-done((bf16[81,128,128]{2,1,0:T(8,128)(2,1)S(1)}, bf16[81,128,128]{2,1,0:T(8,128)(2,1)S(1)}, u32[]{:S(2)}, u32[]{:S(2)}) %collective-permute-start) | collective-permute-done | bytes 2654240 | tf_op jit(solution)/shard_map/cond/branch_1_fun/ppermute | solution.py:48
  74.3 6.7 %collective-permute-start.1 = (bf16[256,512]{1,0:T(8,128)(2,1)S(1)}, bf16[256,512]{1,0:T(8,128)(2,1)S(1)}, u32[]{:S(2)}, u32[]{:S(2)}) collective-permute-start(bf16[256,512]{1,0:T(8,128)(2,1)S(1)} %get-tuple-element.49), channel_id=1, source_target_pairs={{31,1},{4,2},{3,5},{8,6},{7,9},{12,10},{11,13},{16,14},{15,17},{20... | collective-permute-start | bytes 786440 | tf_op jit(solution)/shard_map/cond/branch_1_fun/ppermute | solution.py:48
  81.0 0.0 copy-done
  81.0 15.1 %branch_1_fun.2 = (f32[4,20,128,128]{3,2,1,0:T(8,128)}, f32[1,512]{1,0:T(1,128)S(1)}, bf16[512,1024]{1,0:T(8,128)(2,1)}) custom-call(bf16[512,3712]{1,0:T(8,128)(2,1)S(1)} %copy-done, s32[4,20]{1,0:T(4,128)S(1)} %get-tuple-element.40.positions, f32[4,20,128,128]{3,2,1,0:T(8,128)} %get-tuple-element.41.prev, f32[1,512]{1,0:T(1,128)S(1)} %get-tuple-element.42.trace_in, ...), custom_call_target="tpu_custom_call" | custom-call | flops 5637144576 | bytes 18350080 | tf_op jit(solution)/shard_map/cond/branch_1_fun/pallas_call | solution.py:373
  96.1 0.0 collective-permute-done.1.corner
  96.1 0.1 collective-permute-start.7
  96.2 1.1 collective-permute-done.7
  97.4 0.5 collective-permute-start.10
  97.8 0.0 collective-permute-start.9
  97.8 3.9 %collective-permute-start.8 = (f32[1,512]{1,0:T(1,128)S(1)}, f32[1,512]{1,0:T(1,128)S(1)}, u32[]{:S(2)}, u32[]{:S(2)}) collective-permute-start(f32[1,512]{1,0:T(1,128)S(1)} %add.30), channel_id=1, source_target_pairs={{0,8},{1,9},{2,10},{3,11},{4,12},{5,13},{6,14},{7,15},{8,0},{9,1},... | collective-permute-start | bytes 6152 | tf_op jit(solution)/shard_map/ppermute | solution.py:52
  101.8 1.0 collective-permute-done.10
  102.8 0.0 collective-permute-done.9
  102.8 0.6 collective-permute-done.8
  103.3 0.0 collective-permute-done.6.source_a
  103.3 1.3 %collective-permute-start.11 = (bf16[81,128,128]{2,1,0:T(8,128)(2,1)S(1)}, bf16[81,128,128]{2,1,0:T(8,128)(2,1)S(1)}, u32[]{:S(2)}, u32[]{:S(2)}) collective-permute-start(bf16[81,128,128]{2,1,0:T(8,128)(2,1)S(1)} %collective-permute-done.6.source_a), channel_id=1, source_target_pairs={{1,0},{0,1},{3,2},{2,3},{5,4},{4,5},{7,6},{6,7},{9,8},{8,9},{11,10... | collective-permute-start | bytes 7962632 | tf_op jit(solution)/shard_map/ppermute | solution.py:48
  104.7 0.0 collective-permute-start.14
  104.7 2.0 %collective-permute-start.13 = (f32[1,512]{1,0:T(1,128)S(1)}, f32[1,512]{1,0:T(1,128)S(1)}, u32[]{:S(2)}, u32[]{:S(2)}) collective-permute-start(f32[1,512]{1,0:T(1,128)S(1)} %add_add_fusion), channel_id=1, source_target_pairs={{0,4},{1,5},{2,6},{3,7},{4,0},{5,1},{6,2},{7,3},{8,12},{9,13},{10,... | collective-permute-start | bytes 6152 | tf_op jit(solution)/shard_map/ppermute | solution.py:52
  106.7 1.5 %collective-permute-start.12 = (f32[1,512]{1,0:T(1,128)S(1)}, f32[1,512]{1,0:T(1,128)S(1)}, u32[]{:S(2)}, u32[]{:S(2)}) collective-permute-start(f32[1,512]{1,0:T(1,128)S(1)} %add_add_fusion), channel_id=1, source_target_pairs={{0,2},{1,3},{2,0},{3,1},{4,6},{5,7},{6,4},{7,5},{8,10},{9,11},{10,... | collective-permute-start | bytes 6152 | tf_op jit(solution)/shard_map/ppermute | solution.py:52
  108.1 1.1 collective-permute-done.11.source_b
  109.2 8.5 %shard_map.44 = bf16[4,20,128,128]{3,2,1,0:T(8,128)(2,1)} custom-call(bf16[512,1024]{1,0:T(8,128)(2,1)} %get-tuple-element.89.left_in, s32[4,20]{1,0:T(4,128)S(1)} %get-tuple-element.79.positions, f32[4,20,128,128]{3,2,1,0:T(8,128)} %get-tuple-element.92.prev, bf16[81,128,128]{2,1,0:T(8,128)(2,1)S(1)} %collective-permute-done.6.source_a, ...), custom_call_target="tpu_custom_call" | custom-call | flops 3758096384 | bytes 15728640 | tf_op jit(solution)/shard_map/pallas_call | solution.py:373
  117.8 0.0 collective-permute-done.14
  117.8 0.0 collective-permute-done.13
  117.8 0.0 collective-permute-done.12
  117.8 0.6 add_reduce_fusion
  (3 shorter events, 0.0 us)
Async XLA Ops:
  4.0 17.2 %collective-permute-start.5 = (bf16[81,128,128]{2,1,0:T(8,128)(2,1)}, bf16[81,128,128]{2,1,0:T(8,128)(2,1)}, u32[]{:S(2)}, u32[]{:S(2)}) collective-permute-start(bf16[81,128,128]{2,1,0:T(8,128)(2,1)} %shard_map.41), channel_id=1, source_target_pairs={{1,0},{0,1},{3,2},{2,3},{5,4},{4,5},{7,6},{6,7},{9,8},{8,9},{11,10... | collective-permute-start | bytes 7962632 | tf_op jit(solution)/shard_map/ppermute | solution.py:48
  4.6 60.3 %collective-permute-start.3 = (bf16[81,128,128]{2,1,0:T(8,128)(2,1)}, bf16[81,128,128]{2,1,0:T(8,128)(2,1)}, u32[]{:S(2)}, u32[]{:S(2)}) collective-permute-start(bf16[81,128,128]{2,1,0:T(8,128)(2,1)} %shard_map.41), channel_id=1, source_target_pairs={{29,0},{3,1},{0,2},{6,3},{1,4},{7,5},{4,6},{10,7},{5,8},{11,9},{8,... | collective-permute-start | bytes 7962632 | tf_op jit(solution)/shard_map/ppermute | solution.py:48
  7.1 58.5 %collective-permute-start.2 = (bf16[81,128,128]{2,1,0:T(8,128)(2,1)}, bf16[81,128,128]{2,1,0:T(8,128)(2,1)}, u32[]{:S(2)}, u32[]{:S(2)}) collective-permute-start(bf16[81,128,128]{2,1,0:T(8,128)(2,1)} %shard_map.41), channel_id=1, source_target_pairs={{2,0},{4,1},{31,2},{1,3},{6,4},{8,5},{3,6},{5,7},{10,8},{12,9},{7,... | collective-permute-start | bytes 7962632 | tf_op jit(solution)/shard_map/ppermute | solution.py:48
  19.9 10.9 %collective-permute-start.4 = (bf16[256,512]{1,0:T(8,128)(2,1)}, bf16[256,512]{1,0:T(8,128)(2,1)S(1)}, u32[]{:S(2)}, u32[]{:S(2)}) collective-permute-start(bf16[256,512]{1,0:T(8,128)(2,1)} %get-tuple-element.77), channel_id=1, source_target_pairs={{1,0},{2,3},{5,4},{6,7},{9,8},{10,11},{13,12},{14,15},{17,16},{18,... | collective-permute-start | bytes 786440 | tf_op jit(solution)/shard_map/ppermute | solution.py:48
  65.6 37.7 %collective-permute-start.6 = (bf16[81,128,128]{2,1,0:T(8,128)(2,1)}, bf16[81,128,128]{2,1,0:T(8,128)(2,1)S(1)}, u32[]{:S(2)}, u32[]{:S(2)}) collective-permute-start(bf16[81,128,128]{2,1,0:T(8,128)(2,1)} %collective-permute-done.2), channel_id=1, source_target_pairs={{2,0},{28,1},{7,2},{1,3},{6,4},{0,5},{11,6},{5,7},{10,8},{4,9},{15... | collective-permute-start | bytes 7962632 | tf_op jit(solution)/shard_map/ppermute | solution.py:48
  66.1 14.9 %copy-start = (bf16[512,3712]{1,0:T(8,128)(2,1)S(1)}, bf16[512,3712]{1,0:T(8,128)(2,1)}, u32[]{:S(2)}) copy-start(bf16[512,3712]{1,0:T(8,128)(2,1)} %get-tuple-element.39.left_in.left) | copy-start | bytes 11403268 | tf_op jit(solution)/shard_map/cond
  68.3 6.0 %collective-permute-start = (bf16[81,128,128]{2,1,0:T(8,128)(2,1)S(1)}, bf16[81,128,128]{2,1,0:T(8,128)(2,1)S(1)}, u32[]{:S(2)}, u32[]{:S(2)}) collective-permute-start(bf16[81,128,128]{2,1,0:T(8,128)(2,1)S(1)} %broadcast_select_fusion), channel_id=1, source_target_pairs={{1,0},{0,1},{3,2},{2,3},{5,4},{4,5},{7,6},{6,7},{9,8},{8,9},{11,10... | collective-permute-start | bytes 7962632 | tf_op jit(solution)/shard_map/cond/branch_1_fun/ppermute | solution.py:48
  74.3 21.8 %collective-permute-start.1 = (bf16[256,512]{1,0:T(8,128)(2,1)S(1)}, bf16[256,512]{1,0:T(8,128)(2,1)S(1)}, u32[]{:S(2)}, u32[]{:S(2)}) collective-permute-start(bf16[256,512]{1,0:T(8,128)(2,1)S(1)} %get-tuple-element.49), channel_id=1, source_target_pairs={{31,1},{4,2},{3,5},{8,6},{7,9},{12,10},{11,13},{16,14},{15,17},{20... | collective-permute-start | bytes 786440 | tf_op jit(solution)/shard_map/cond/branch_1_fun/ppermute | solution.py:48
  96.1 1.2 %collective-permute-start.7 = (f32[1,512]{1,0:T(1,128)S(1)}, f32[1,512]{1,0:T(1,128)S(1)}, u32[]{:S(2)}, u32[]{:S(2)}) collective-permute-start(f32[1,512]{1,0:T(1,128)S(1)} %get-tuple-element.91), channel_id=1, source_target_pairs={{0,1},{1,0},{2,3},{3,2},{4,5},{5,4},{6,7},{7,6},{8,9},{9,8},{10,11... | collective-permute-start | bytes 6152 | tf_op jit(solution)/shard_map/ppermute | solution.py:52
  97.4 5.4 %collective-permute-start.10 = (f32[1,512]{1,0:T(1,128)S(1)}, f32[1,512]{1,0:T(1,128)S(1)}, u32[]{:S(2)}, u32[]{:S(2)}) collective-permute-start(f32[1,512]{1,0:T(1,128)S(1)} %add.30), channel_id=1, source_target_pairs={{0,24},{1,25},{2,26},{3,27},{4,28},{5,29},{6,30},{7,31},{8,16},{9,... | collective-permute-start | bytes 6152 | tf_op jit(solution)/shard_map/ppermute | solution.py:52
  97.8 4.9 %collective-permute-start.9 = (f32[1,512]{1,0:T(1,128)S(1)}, f32[1,512]{1,0:T(1,128)S(1)}, u32[]{:S(2)}, u32[]{:S(2)}) collective-permute-start(f32[1,512]{1,0:T(1,128)S(1)} %add.30), channel_id=1, source_target_pairs={{0,16},{1,17},{2,18},{3,19},{4,20},{5,21},{6,22},{7,23},{8,24},{9,... | collective-permute-start | bytes 6152 | tf_op jit(solution)/shard_map/ppermute | solution.py:52
  97.8 5.5 %collective-permute-start.8 = (f32[1,512]{1,0:T(1,128)S(1)}, f32[1,512]{1,0:T(1,128)S(1)}, u32[]{:S(2)}, u32[]{:S(2)}) collective-permute-start(f32[1,512]{1,0:T(1,128)S(1)} %add.30), channel_id=1, source_target_pairs={{0,8},{1,9},{2,10},{3,11},{4,12},{5,13},{6,14},{7,15},{8,0},{9,1},... | collective-permute-start | bytes 6152 | tf_op jit(solution)/shard_map/ppermute | solution.py:52
  103.3 5.9 %collective-permute-start.11 = (bf16[81,128,128]{2,1,0:T(8,128)(2,1)S(1)}, bf16[81,128,128]{2,1,0:T(8,128)(2,1)S(1)}, u32[]{:S(2)}, u32[]{:S(2)}) collective-permute-start(bf16[81,128,128]{2,1,0:T(8,128)(2,1)S(1)} %collective-permute-done.6.source_a), channel_id=1, source_target_pairs={{1,0},{0,1},{3,2},{2,3},{5,4},{4,5},{7,6},{6,7},{9,8},{8,9},{11,10... | collective-permute-start | bytes 7962632 | tf_op jit(solution)/shard_map/ppermute | solution.py:48
  104.7 13.1 %collective-permute-start.14 = (f32[1,512]{1,0:T(1,128)S(1)}, f32[1,512]{1,0:T(1,128)S(1)}, u32[]{:S(2)}, u32[]{:S(2)}) collective-permute-start(f32[1,512]{1,0:T(1,128)S(1)} %add_add_fusion), channel_id=1, source_target_pairs={{0,6},{1,7},{2,4},{3,5},{4,2},{5,3},{6,0},{7,1},{8,14},{9,15},{10,... | collective-permute-start | bytes 6152 | tf_op jit(solution)/shard_map/ppermute | solution.py:52
  104.7 13.1 %collective-permute-start.13 = (f32[1,512]{1,0:T(1,128)S(1)}, f32[1,512]{1,0:T(1,128)S(1)}, u32[]{:S(2)}, u32[]{:S(2)}) collective-permute-start(f32[1,512]{1,0:T(1,128)S(1)} %add_add_fusion), channel_id=1, source_target_pairs={{0,4},{1,5},{2,6},{3,7},{4,0},{5,1},{6,2},{7,3},{8,12},{9,13},{10,... | collective-permute-start | bytes 6152 | tf_op jit(solution)/shard_map/ppermute | solution.py:52
  106.7 11.1 %collective-permute-start.12 = (f32[1,512]{1,0:T(1,128)S(1)}, f32[1,512]{1,0:T(1,128)S(1)}, u32[]{:S(2)}, u32[]{:S(2)}) collective-permute-start(f32[1,512]{1,0:T(1,128)S(1)} %add_add_fusion), channel_id=1, source_target_pairs={{0,2},{1,3},{2,0},{3,1},{4,6},{5,7},{6,4},{7,5},{8,10},{9,11},{10,... | collective-permute-start | bytes 6152 | tf_op jit(solution)/shard_map/ppermute | solution.py:52

commit v18 on v15

--- a/solution.py
+++ b/solution.py
@@ -111,11 +111,13 @@
 
 def pack_body(z, tiles, columns, out, stage, padded, offsets, in_sems, out_sems):
     copies = []
-    for r in range(z.rows):
-        rows = pl.ds(r * z.slots, z.slots)
+    half = z.slots // 2
+    for piece in range(2 * z.rows):
+        source = tiles.at[piece // 2, pl.ds(piece % 2 * half, half)]
+        rows = pl.ds(piece * half, half)
         copies.append((
-            pltpu.make_async_copy(tiles.at[r], stage.at[rows], in_sems.at[r]),
-            pltpu.make_async_copy(stage.at[rows], out.at[rows], out_sems.at[r]),
+            pltpu.make_async_copy(source, stage.at[rows], in_sems.at[piece]),
+            pltpu.make_async_copy(stage.at[rows], out.at[rows], out_sems.at[piece]),
         ))
     for copy, _ in copies:
         copy.start()
@@ -129,7 +131,7 @@
     offset = jnp.where(column < 0, EMPTY, offset)
     offsets[...] = jnp.zeros_like(offsets)
     offsets[0:16, :] = offset.astype(jnp.float32).astype(offsets.dtype)
-    last = pltpu.make_async_copy(offsets, out.at[z.rows * z.slots], out_sems.at[z.rows])
+    last = pltpu.make_async_copy(offsets, out.at[z.rows * z.slots], out_sems.at[2 * z.rows])
     last.start()
     for load, store in copies:
         load.wait()
@@ -322,32 +324,32 @@
         pltpu.make_async_copy(left_in, left, left_sem),
         pltpu.make_async_copy(prev, prev_stage, prev_sem),
     ]
-    for copy in copies:
-        copy.start()
     places = [pick(OFFSETS[name], kind) + z.hops for name in ("relay", "relay_beside")]
-    low = jnp.maximum(0, jnp.minimum(*places) - z.hops)
-    high = jnp.minimum(z.chunks, jnp.maximum(*places) + z.hops + 1)
-
-    def chunk(n):
-        return pl.ds(aligned(n, z.span), z.span)
-
-    def clear_total(n, carry):
-        total[:, chunk(n)] = jnp.zeros((z.span, z.span), jnp.float32)
-        return carry
-
-    def clear_right(n, carry):
-        right[:, chunk(n)] = jnp.zeros((2 * z.span, z.span), right.dtype)
-        return carry
-
-    lax.fori_loop(0, low, clear_total, 0)
-    lax.fori_loop(high, z.chunks, clear_total, 0)
-    total[:, z.window * z.block:] = jnp.zeros((z.span, z.block), jnp.float32)
     decodings = []
     for index in range(2):
         decodings.append(decode(
             z, (source_a, source_b)[index].at[z.rows * z.slots], places[index], vector.at[index], scalars.at[index],
             place_sem.at[index],
         ))
+    for copy in copies:
+        copy.start()
+    low = jnp.maximum(0, jnp.minimum(*places) - z.hops)
+    high = jnp.minimum(z.chunks, jnp.maximum(*places) + z.hops + 1)
+
+    def chunk(n):
+        return pl.ds(aligned(n, z.span), z.span)
+
+    def clear_total(n, carry):
+        total[:, chunk(n)] = jnp.zeros((z.span, z.span), jnp.float32)
+        return carry
+
+    def clear_right(n, carry):
+        right[:, chunk(n)] = jnp.zeros((2 * z.span, z.span), right.dtype)
+        return carry
+
+    lax.fori_loop(0, low, clear_total, 0)
+    lax.fori_loop(high, z.chunks, clear_total, 0)
+    total[:, z.window * z.block:] = jnp.zeros((z.span, z.block), jnp.float32)
     lax.fori_loop(low, high, clear_right, 0)
     for index in range(2):
         decodings[index].wait()
@@ -388,7 +390,7 @@
 def shards(tiles, columns):
     devices = lax.axis_size(AXES)
     z = Sizes(tiles.shape, devices)
-    assert z.hops == 3 and z.rows == 4 and devices % 4 == 0 and devices > 8
+    assert z.hops == 3 and z.rows == 4 and z.slots % 2 == 0 and devices % 4 == 0 and devices > 8
     dtype = tiles.dtype
     shape = jax.ShapeDtypeStruct
     sums = shape(tiles.shape, jnp.float32)
@@ -404,7 +406,7 @@
         shape(payload_shape, dtype), ANY,
         [
             pltpu.VMEM((z.rows * z.slots, z.block, z.block), dtype), pltpu.VMEM((16, z.block), jnp.int32),
-            pltpu.VMEM((z.block, z.block), dtype), DMA((z.rows,)), DMA((z.rows + 1,)),
+            pltpu.VMEM((z.block, z.block), dtype), DMA((2 * z.rows,)), DMA((2 * z.rows + 1,)),
         ],
         0, WHOLE_VMEM,
     )

time: 121 us -> 120 us (level)
  no operation moved by 1% of the time
where the time goes in v18:
time: 120 us
  Pallas kernels  46.2 us (38%)
  waiting for transfers between devices  39.8 us (33%)
  starting transfers between devices  27.4 us (23%)
  between operations  3.18 us (3%)
  other arithmetic  2.8 us (2%)
    pallas_call x6, Pallas kernels, call(): pl.pallas_call(kernel, out_shape=out_shape, in_specs=in_specs, out_specs=...  46.2 us
    ppermute x8, waiting for transfers between devices, receive(): return lax.ppermute(shard, AXES, pairs)  35.8 us
    ppermute x8, starting transfers between devices, receive(): return lax.ppermute(shard, AXES, pairs)  19.5 us
    ppermute x7, starting transfers between devices, fetch(): lax.ppermute(value, AXES, [(d, d ^ step) for d in range(lax.axis_size(AXE...  7.95 us
    ppermute x7, waiting for transfers between devices, fetch(): lax.ppermute(value, AXES, [(d, d ^ step) for d in range(lax.axis_size(AXE...  3.99 us
  transfers between devices with their start and end apart: 15, of which 6 were waited for; matrix products, arithmetic and copies ran while one was open for 2% of the time, Pallas kernels for 36%

profile of v18, /device:TPU:0, one launch (start us, length us, event | category | flops | bytes accessed | tf_op | source)
XLA Modules:
  0.0 120.0 jit_solution(4141205190560284473)
XLA Ops:
  0.6 3.4 %shard_map.42 = bf16[81,128,128]{2,1,0:T(8,128)(2,1)} custom-call(bf16[4,20,128,128]{3,2,1,0:T(8,128)(2,1)} %tiles.1, s32[4,20]{1,0:T(4,128)} %columns.3), custom_call_target="tpu_custom_call" | custom-call | bytes 10485760 | tf_op jit(solution)/shard_map/pallas_call | solution.py:375
  4.0 0.5 collective-permute-start.5
  4.5 2.6 %collective-permute-start.3 = (bf16[81,128,128]{2,1,0:T(8,128)(2,1)}, bf16[81,128,128]{2,1,0:T(8,128)(2,1)}, u32[]{:S(2)}, u32[]{:S(2)}) collective-permute-start(bf16[81,128,128]{2,1,0:T(8,128)(2,1)} %shard_map.42), channel_id=1, source_target_pairs={{29,0},{3,1},{0,2},{6,3},{1,4},{7,5},{4,6},{10,7},{5,8},{11,9},{8,... | collective-permute-start | bytes 7962632 | tf_op jit(solution)/shard_map/ppermute | solution.py:48
  7.1 3.1 %collective-permute-start.2 = (bf16[81,128,128]{2,1,0:T(8,128)(2,1)}, bf16[81,128,128]{2,1,0:T(8,128)(2,1)}, u32[]{:S(2)}, u32[]{:S(2)}) collective-permute-start(bf16[81,128,128]{2,1,0:T(8,128)(2,1)} %shard_map.42), channel_id=1, source_target_pairs={{2,0},{4,1},{31,2},{1,3},{6,4},{8,5},{3,6},{5,7},{10,8},{12,9},{7,... | collective-permute-start | bytes 7962632 | tf_op jit(solution)/shard_map/ppermute | solution.py:48
  10.2 9.7 %shard_map.41 = (f32[4,20,128,128]{3,2,1,0:T(8,128)}, bf16[512,3712]{1,0:T(8,128)(2,1)}, bf16[256,512]{1,0:T(8,128)(2,1)}, s32[4,20]{1,0:T(4,128)S(1)}, f32[1,512]{1,0:T(1,128)}) custom-call(bf16[4,20,128,128]{3,2,1,0:T(8,128)(2,1)} %tiles.1, s32[4,20]{1,0:T(4,128)} %columns.3), custom_call_target="tpu_custom_call" | custom-call | flops 1879048192 | bytes 13107200 | tf_op jit(solution)/shard_map/pallas_call | solution.py:375
  19.9 1.3 %collective-permute-start.4 = (bf16[256,512]{1,0:T(8,128)(2,1)}, bf16[256,512]{1,0:T(8,128)(2,1)S(1)}, u32[]{:S(2)}, u32[]{:S(2)}) collective-permute-start(bf16[256,512]{1,0:T(8,128)(2,1)} %get-tuple-element.76), channel_id=1, source_target_pairs={{1,0},{2,3},{5,4},{6,7},{9,8},{10,11},{13,12},{14,15},{17,16},{18,... | collective-permute-start | bytes 786440 | tf_op jit(solution)/shard_map/ppermute | solution.py:48
  21.2 0.0 collective-permute-done.5.refs_0_
  21.2 9.6 %shard_map.43 = (f32[4,20,128,128]{3,2,1,0:T(8,128)}, f32[1,512]{1,0:T(1,128)S(1)}) custom-call(bf16[512,3712]{1,0:T(8,128)(2,1)} %get-tuple-element.77.left_in, s32[4,20]{1,0:T(4,128)S(1)} %get-tuple-element.75.positions, f32[4,20,128,128]{3,2,1,0:T(8,128)} %get-tuple-element.78.prev, f32[1,512]{1,0:T(1,128)} %get-tuple-element.79.trace_in, ...), custom_call_target="tpu_custom_call" | custom-call | flops 1879048192 | bytes 13107200 | tf_op jit(solution)/shard_map/pallas_call | solution.py:375
  30.8 0.0 collective-permute-done.4
  30.8 34.0 %collective-permute-done.3 = bf16[81,128,128]{2,1,0:T(8,128)(2,1)} collective-permute-done((bf16[81,128,128]{2,1,0:T(8,128)(2,1)}, bf16[81,128,128]{2,1,0:T(8,128)(2,1)}, u32[]{:S(2)}, u32[]{:S(2)}) %collective-permute-start.3) | collective-permute-done | bytes 2654240 | tf_op jit(solution)/shard_map/ppermute | solution.py:48
  64.8 0.7 collective-permute-done.2
  65.6 0.5 collective-permute-start.6
  66.0 0.5 slice.3
  67.2 25.5 %conditional.1 = (f32[4,20,128,128]{3,2,1,0:T(8,128)}, f32[1,512]{1,0:T(1,128)S(1)}, bf16[512,1024]{1,0:T(8,128)(2,1)}) conditional(s32[]{:T(128)} %bitcast, () %tuple.22, (s32[]{:T(128)}, bf16[81,128,128]{2,1,0:T(8,128)(2,1)}, bf16[81,128,128]{2,1,0:T(8,128)(2,1)}, bf16[512,3712]{1,0:T(8,128)(2,1)}, s32[4,20]{1,0:T(4,128)S(1)}, ...), branch_computations={%region_0.1_spmd, %region_1.2_spmd} | conditional | flops 5638471680 | bytes 63668512 | solution.py:468
  67.2 0.0 copy-start
  67.2 2.2 %broadcast_select_fusion = bf16[81,128,128]{2,1,0:T(8,128)(2,1)S(1)} fusion(bf16[81,128,128]{2,1,0:T(8,128)(2,1)} %get-tuple-element.43.refs_0_, bf16[81,128,128]{2,1,0:T(8,128)(2,1)} %get-tuple-element.44.refs_1_, pred[]{:T(512)S(6)} %or.2), kind=kLoop, calls=%fused_computation | loop fusion | flops 1327104 | bytes 7962625 | tf_op jit(solution)/shard_map/cond/branch_1_fun/jit(_where)/select_n | solution.py:456
  69.4 1.5 %collective-permute-start = (bf16[81,128,128]{2,1,0:T(8,128)(2,1)S(1)}, bf16[81,128,128]{2,1,0:T(8,128)(2,1)S(1)}, u32[]{:S(2)}, u32[]{:S(2)}) collective-permute-start(bf16[81,128,128]{2,1,0:T(8,128)(2,1)S(1)} %broadcast_select_fusion), channel_id=1, source_target_pairs={{1,0},{0,1},{3,2},{2,3},{5,4},{4,5},{7,6},{6,7},{9,8},{8,9},{11,10... | collective-permute-start | bytes 7962632 | tf_op jit(solution)/shard_map/cond/branch_1_fun/ppermute | solution.py:48
  70.9 6.7 %collective-permute-start.1 = (bf16[256,512]{1,0:T(8,128)(2,1)S(1)}, bf16[256,512]{1,0:T(8,128)(2,1)S(1)}, u32[]{:S(2)}, u32[]{:S(2)}) collective-permute-start(bf16[256,512]{1,0:T(8,128)(2,1)S(1)} %get-tuple-element.47), channel_id=1, source_target_pairs={{31,1},{4,2},{3,5},{8,6},{7,9},{12,10},{11,13},{16,14},{15,17},{20... | collective-permute-start | bytes 786440 | tf_op jit(solution)/shard_map/cond/branch_1_fun/ppermute | solution.py:48
  77.6 0.0 collective-permute-done.refs_2_
  77.6 0.0 copy-done
  77.6 15.1 %branch_1_fun.2 = (f32[4,20,128,128]{3,2,1,0:T(8,128)}, f32[1,512]{1,0:T(1,128)S(1)}, bf16[512,1024]{1,0:T(8,128)(2,1)}) custom-call(bf16[512,3712]{1,0:T(8,128)(2,1)S(1)} %copy-done, s32[4,20]{1,0:T(4,128)S(1)} %get-tuple-element.40.positions, f32[4,20,128,128]{3,2,1,0:T(8,128)} %get-tuple-element.41.prev, f32[1,512]{1,0:T(1,128)S(1)} %get-tuple-element.42.trace_in, ...), custom_call_target="tpu_custom_call" | custom-call | flops 5637144576 | bytes 18350080 | tf_op jit(solution)/shard_map/cond/branch_1_fun/pallas_call | solution.py:375
  92.7 0.0 collective-permute-done.1.corner
  92.7 0.1 collective-permute-start.7
  92.8 1.1 collective-permute-done.7
  94.0 2.7 %collective-permute-start.10 = (f32[1,512]{1,0:T(1,128)S(1)}, f32[1,512]{1,0:T(1,128)S(1)}, u32[]{:S(2)}, u32[]{:S(2)}) collective-permute-start(f32[1,512]{1,0:T(1,128)S(1)} %add.30), channel_id=1, source_target_pairs={{0,24},{1,25},{2,26},{3,27},{4,28},{5,29},{6,30},{7,31},{8,16},{9,... | collective-permute-start | bytes 6152 | tf_op jit(solution)/shard_map/ppermute | solution.py:52
  96.7 0.0 collective-permute-start.9
  96.7 1.6 %collective-permute-start.8 = (f32[1,512]{1,0:T(1,128)S(1)}, f32[1,512]{1,0:T(1,128)S(1)}, u32[]{:S(2)}, u32[]{:S(2)}) collective-permute-start(f32[1,512]{1,0:T(1,128)S(1)} %add.30), channel_id=1, source_target_pairs={{0,8},{1,9},{2,10},{3,11},{4,12},{5,13},{6,14},{7,15},{8,0},{9,1},... | collective-permute-start | bytes 6152 | tf_op jit(solution)/shard_map/ppermute | solution.py:52
  98.3 1.0 collective-permute-done.10
  99.3 1.8 %collective-permute-done.9 = f32[1,512]{1,0:T(1,128)S(1)} collective-permute-done((f32[1,512]{1,0:T(1,128)S(1)}, f32[1,512]{1,0:T(1,128)S(1)}, u32[]{:S(2)}, u32[]{:S(2)}) %collective-permute-start.9) | collective-permute-done | bytes 2080 | tf_op jit(solution)/shard_map/ppermute | solution.py:52
  101.2 0.0 collective-permute-done.8
  101.2 0.0 collective-permute-done.6.source_a
  101.2 3.4 %collective-permute-start.11 = (bf16[81,128,128]{2,1,0:T(8,128)(2,1)S(1)}, bf16[81,128,128]{2,1,0:T(8,128)(2,1)S(1)}, u32[]{:S(2)}, u32[]{:S(2)}) collective-permute-start(bf16[81,128,128]{2,1,0:T(8,128)(2,1)S(1)} %collective-permute-done.6.source_a), channel_id=1, source_target_pairs={{1,0},{0,1},{3,2},{2,3},{5,4},{4,5},{7,6},{6,7},{9,8},{8,9},{11,10... | collective-permute-start | bytes 7962632 | tf_op jit(solution)/shard_map/ppermute | solution.py:48
  104.6 0.0 collective-permute-start.14
  104.6 2.0 %collective-permute-start.13 = (f32[1,512]{1,0:T(1,128)S(1)}, f32[1,512]{1,0:T(1,128)S(1)}, u32[]{:S(2)}, u32[]{:S(2)}) collective-permute-start(f32[1,512]{1,0:T(1,128)S(1)} %add_add_fusion), channel_id=1, source_target_pairs={{0,4},{1,5},{2,6},{3,7},{4,0},{5,1},{6,2},{7,3},{8,12},{9,13},{10,... | collective-permute-start | bytes 6152 | tf_op jit(solution)/shard_map/ppermute | solution.py:52
  106.6 1.4 %collective-permute-start.12 = (f32[1,512]{1,0:T(1,128)S(1)}, f32[1,512]{1,0:T(1,128)S(1)}, u32[]{:S(2)}, u32[]{:S(2)}) collective-permute-start(f32[1,512]{1,0:T(1,128)S(1)} %add_add_fusion), channel_id=1, source_target_pairs={{0,2},{1,3},{2,0},{3,1},{4,6},{5,7},{6,4},{7,5},{8,10},{9,11},{10,... | collective-permute-start | bytes 6152 | tf_op jit(solution)/shard_map/ppermute | solution.py:52
  108.1 1.1 collective-permute-done.11.source_b
  109.2 8.4 %shard_map.44 = bf16[4,20,128,128]{3,2,1,0:T(8,128)(2,1)} custom-call(bf16[512,1024]{1,0:T(8,128)(2,1)} %get-tuple-element.87.left_in, s32[4,20]{1,0:T(4,128)S(1)} %get-tuple-element.75.positions, f32[4,20,128,128]{3,2,1,0:T(8,128)} %get-tuple-element.90.prev, bf16[81,128,128]{2,1,0:T(8,128)(2,1)S(1)} %collective-permute-done.6.source_a, ...), custom_call_target="tpu_custom_call" | custom-call | flops 3758096384 | bytes 15728640 | tf_op jit(solution)/shard_map/pallas_call | solution.py:375
  117.6 0.0 collective-permute-done.14
  117.6 0.0 collective-permute-done.13
  117.6 0.0 collective-permute-done.12
  117.7 0.6 add_reduce_fusion
  (3 shorter events, 0.0 us)
Async XLA Ops:
  4.0 17.2 %collective-permute-start.5 = (bf16[81,128,128]{2,1,0:T(8,128)(2,1)}, bf16[81,128,128]{2,1,0:T(8,128)(2,1)}, u32[]{:S(2)}, u32[]{:S(2)}) collective-permute-start(bf16[81,128,128]{2,1,0:T(8,128)(2,1)} %shard_map.42), channel_id=1, source_target_pairs={{1,0},{0,1},{3,2},{2,3},{5,4},{4,5},{7,6},{6,7},{9,8},{8,9},{11,10... | collective-permute-start | bytes 7962632 | tf_op jit(solution)/shard_map/ppermute | solution.py:48
  4.5 60.3 %collective-permute-start.3 = (bf16[81,128,128]{2,1,0:T(8,128)(2,1)}, bf16[81,128,128]{2,1,0:T(8,128)(2,1)}, u32[]{:S(2)}, u32[]{:S(2)}) collective-permute-start(bf16[81,128,128]{2,1,0:T(8,128)(2,1)} %shard_map.42), channel_id=1, source_target_pairs={{29,0},{3,1},{0,2},{6,3},{1,4},{7,5},{4,6},{10,7},{5,8},{11,9},{8,... | collective-permute-start | bytes 7962632 | tf_op jit(solution)/shard_map/ppermute | solution.py:48
  7.1 58.5 %collective-permute-start.2 = (bf16[81,128,128]{2,1,0:T(8,128)(2,1)}, bf16[81,128,128]{2,1,0:T(8,128)(2,1)}, u32[]{:S(2)}, u32[]{:S(2)}) collective-permute-start(bf16[81,128,128]{2,1,0:T(8,128)(2,1)} %shard_map.42), channel_id=1, source_target_pairs={{2,0},{4,1},{31,2},{1,3},{6,4},{8,5},{3,6},{5,7},{10,8},{12,9},{7,... | collective-permute-start | bytes 7962632 | tf_op jit(solution)/shard_map/ppermute | solution.py:48
  19.9 10.9 %collective-permute-start.4 = (bf16[256,512]{1,0:T(8,128)(2,1)}, bf16[256,512]{1,0:T(8,128)(2,1)S(1)}, u32[]{:S(2)}, u32[]{:S(2)}) collective-permute-start(bf16[256,512]{1,0:T(8,128)(2,1)} %get-tuple-element.76), channel_id=1, source_target_pairs={{1,0},{2,3},{5,4},{6,7},{9,8},{10,11},{13,12},{14,15},{17,16},{18,... | collective-permute-start | bytes 786440 | tf_op jit(solution)/shard_map/ppermute | solution.py:48
  65.6 35.6 %collective-permute-start.6 = (bf16[81,128,128]{2,1,0:T(8,128)(2,1)}, bf16[81,128,128]{2,1,0:T(8,128)(2,1)S(1)}, u32[]{:S(2)}, u32[]{:S(2)}) collective-permute-start(bf16[81,128,128]{2,1,0:T(8,128)(2,1)} %collective-permute-done.2), channel_id=1, source_target_pairs={{2,0},{28,1},{7,2},{1,3},{6,4},{0,5},{11,6},{5,7},{10,8},{4,9},{15... | collective-permute-start | bytes 7962632 | tf_op jit(solution)/shard_map/ppermute | solution.py:48
  67.2 10.3 %copy-start = (bf16[512,3712]{1,0:T(8,128)(2,1)S(1)}, bf16[512,3712]{1,0:T(8,128)(2,1)}, u32[]{:S(2)}) copy-start(bf16[512,3712]{1,0:T(8,128)(2,1)} %get-tuple-element.39.left_in.left) | copy-start | bytes 11403268 | tf_op jit(solution)/shard_map/cond
  69.4 8.1 %collective-permute-start = (bf16[81,128,128]{2,1,0:T(8,128)(2,1)S(1)}, bf16[81,128,128]{2,1,0:T(8,128)(2,1)S(1)}, u32[]{:S(2)}, u32[]{:S(2)}) collective-permute-start(bf16[81,128,128]{2,1,0:T(8,128)(2,1)S(1)} %broadcast_select_fusion), channel_id=1, source_target_pairs={{1,0},{0,1},{3,2},{2,3},{5,4},{4,5},{7,6},{6,7},{9,8},{8,9},{11,10... | collective-permute-start | bytes 7962632 | tf_op jit(solution)/shard_map/cond/branch_1_fun/ppermute | solution.py:48
  70.9 21.8 %collective-permute-start.1 = (bf16[256,512]{1,0:T(8,128)(2,1)S(1)}, bf16[256,512]{1,0:T(8,128)(2,1)S(1)}, u32[]{:S(2)}, u32[]{:S(2)}) collective-permute-start(bf16[256,512]{1,0:T(8,128)(2,1)S(1)} %get-tuple-element.47), channel_id=1, source_target_pairs={{31,1},{4,2},{3,5},{8,6},{7,9},{12,10},{11,13},{16,14},{15,17},{20... | collective-permute-start | bytes 786440 | tf_op jit(solution)/shard_map/cond/branch_1_fun/ppermute | solution.py:48
  92.7 1.2 %collective-permute-start.7 = (f32[1,512]{1,0:T(1,128)S(1)}, f32[1,512]{1,0:T(1,128)S(1)}, u32[]{:S(2)}, u32[]{:S(2)}) collective-permute-start(f32[1,512]{1,0:T(1,128)S(1)} %get-tuple-element.89), channel_id=1, source_target_pairs={{0,1},{1,0},{2,3},{3,2},{4,5},{5,4},{6,7},{7,6},{8,9},{9,8},{10,11... | collective-permute-start | bytes 6152 | tf_op jit(solution)/shard_map/ppermute | solution.py:52
  94.0 5.4 %collective-permute-start.10 = (f32[1,512]{1,0:T(1,128)S(1)}, f32[1,512]{1,0:T(1,128)S(1)}, u32[]{:S(2)}, u32[]{:S(2)}) collective-permute-start(f32[1,512]{1,0:T(1,128)S(1)} %add.30), channel_id=1, source_target_pairs={{0,24},{1,25},{2,26},{3,27},{4,28},{5,29},{6,30},{7,31},{8,16},{9,... | collective-permute-start | bytes 6152 | tf_op jit(solution)/shard_map/ppermute | solution.py:52
  96.7 4.5 %collective-permute-start.9 = (f32[1,512]{1,0:T(1,128)S(1)}, f32[1,512]{1,0:T(1,128)S(1)}, u32[]{:S(2)}, u32[]{:S(2)}) collective-permute-start(f32[1,512]{1,0:T(1,128)S(1)} %add.30), channel_id=1, source_target_pairs={{0,16},{1,17},{2,18},{3,19},{4,20},{5,21},{6,22},{7,23},{8,24},{9,... | collective-permute-start | bytes 6152 | tf_op jit(solution)/shard_map/ppermute | solution.py:52
  96.7 4.5 %collective-permute-start.8 = (f32[1,512]{1,0:T(1,128)S(1)}, f32[1,512]{1,0:T(1,128)S(1)}, u32[]{:S(2)}, u32[]{:S(2)}) collective-permute-start(f32[1,512]{1,0:T(1,128)S(1)} %add.30), channel_id=1, source_target_pairs={{0,8},{1,9},{2,10},{3,11},{4,12},{5,13},{6,14},{7,15},{8,0},{9,1},... | collective-permute-start | bytes 6152 | tf_op jit(solution)/shard_map/ppermute | solution.py:52
  101.2 8.0 %collective-permute-start.11 = (bf16[81,128,128]{2,1,0:T(8,128)(2,1)S(1)}, bf16[81,128,128]{2,1,0:T(8,128)(2,1)S(1)}, u32[]{:S(2)}, u32[]{:S(2)}) collective-permute-start(bf16[81,128,128]{2,1,0:T(8,128)(2,1)S(1)} %collective-permute-done.6.source_a), channel_id=1, source_target_pairs={{1,0},{0,1},{3,2},{2,3},{5,4},{4,5},{7,6},{6,7},{9,8},{8,9},{11,10... | collective-permute-start | bytes 7962632 | tf_op jit(solution)/shard_map/ppermute | solution.py:48
  104.6 13.0 %collective-permute-start.14 = (f32[1,512]{1,0:T(1,128)S(1)}, f32[1,512]{1,0:T(1,128)S(1)}, u32[]{:S(2)}, u32[]{:S(2)}) collective-permute-start(f32[1,512]{1,0:T(1,128)S(1)} %add_add_fusion), channel_id=1, source_target_pairs={{0,6},{1,7},{2,4},{3,5},{4,2},{5,3},{6,0},{7,1},{8,14},{9,15},{10,... | collective-permute-start | bytes 6152 | tf_op jit(solution)/shard_map/ppermute | solution.py:52
  104.6 13.0 %collective-permute-start.13 = (f32[1,512]{1,0:T(1,128)S(1)}, f32[1,512]{1,0:T(1,128)S(1)}, u32[]{:S(2)}, u32[]{:S(2)}) collective-permute-start(f32[1,512]{1,0:T(1,128)S(1)} %add_add_fusion), channel_id=1, source_target_pairs={{0,4},{1,5},{2,6},{3,7},{4,0},{5,1},{6,2},{7,3},{8,12},{9,13},{10,... | collective-permute-start | bytes 6152 | tf_op jit(solution)/shard_map/ppermute | solution.py:52
  106.6 11.0 %collective-permute-start.12 = (f32[1,512]{1,0:T(1,128)S(1)}, f32[1,512]{1,0:T(1,128)S(1)}, u32[]{:S(2)}, u32[]{:S(2)}) collective-permute-start(f32[1,512]{1,0:T(1,128)S(1)} %add_add_fusion), channel_id=1, source_target_pairs={{0,2},{1,3},{2,0},{3,1},{4,6},{5,7},{6,4},{7,5},{8,10},{9,11},{10,... | collective-permute-start | bytes 6152 | tf_op jit(solution)/shard_map/ppermute | solution.py:52

commit v19 on v18

--- a/solution.py
+++ b/solution.py
@@ -184,13 +184,24 @@
     half = z.span // 2
 
     def corner(start):
-        def go(rows, cols):
-            copy = pltpu.make_async_copy(left.at[rows, cols], corner_out, corner_sem)
+        end = (z.chunks - 1) * z.span
+
+        def go(index, rows, cols, target):
+            copy = pltpu.make_async_copy(left.at[rows, cols], target, corner_sem.at[index])
             copy.start() if start else copy.wait()
-        pl.when(kind == UPPER)(lambda: go(pl.ds(0, half), pl.ds(0, z.span)))
-        pl.when(kind != UPPER)(
-            lambda: go(pl.ds(half, half), pl.ds((z.chunks - 1) * z.span, z.span))
-        )
+
+        @pl.when(kind == UPPER)
+        def _():
+            go(0, pl.ds(0, half), pl.ds(0, half + z.block), corner_out)
+
+        @pl.when(kind != UPPER)
+        def _():
+            go(0, pl.ds(half, half), pl.ds(end + half, half), corner_out.at[:, pl.ds(0, half)])
+            for q in range(2):
+                go(
+                    1 + q, pl.ds(z.span - z.block, z.block), pl.ds(end + q * z.block, z.block),
+                    corner_out.at[pl.ds(q * z.block, z.block), pl.ds(half, z.block)],
+                )
 
     corner(True)
     middle = slice(z.hops * z.span, (z.hops + 1) * z.span)
@@ -296,7 +307,7 @@
         copy.wait()
 
 
-def corner_body(z, left, corner, trace_in, trace, rows, sem):
+def corner_body(z, left, corner, trace_in, trace, square, column, tall, sems):
     kind = lax.axis_index(AXES) % 4
     half = z.span // 2
     end = (z.chunks - 1) * z.span
@@ -304,17 +315,25 @@
 
     @pl.when(kind == UPPER)
     def _():
-        copy = pltpu.make_async_copy(left.at[:, pl.ds(half, half)], rows, sem)
+        copies = [
+            pltpu.make_async_copy(left.at[pl.ds(half, half), pl.ds(half, half)], square, sems.at[0]),
+            pltpu.make_async_copy(left.at[pl.ds(0, half), pl.ds(z.span - z.block, z.block)], column, sems.at[1]),
+        ]
+        for copy in copies:
+            copy.start()
+        for copy in copies:
+            copy.wait()
+        add_trace(trace, jnp.float32(2), square[...], corner[:, :half])
+        for q in range(2):
+            rows = slice(q * z.block, (q + 1) * z.block)
+            add_trace(trace, jnp.float32(2), column[rows], corner[rows, half:])
+
+    @pl.when(kind == LOWER)
+    def _():
+        copy = pltpu.make_async_copy(left.at[pl.ds(0, half + z.block), pl.ds(end, half)], tall, sems.at[0])
         copy.start()
         copy.wait()
-        add_trace(trace, jnp.float32(2), rows[...], corner[...])
-
-    @pl.when(kind == LOWER)
-    def _():
-        copy = pltpu.make_async_copy(left.at[pl.ds(0, half), pl.ds(end, half)], rows.at[pl.ds(0, half)], sem)
-        copy.start()
-        copy.wait()
-        add_trace(trace, jnp.float32(2), rows[:half], corner[:, :half])
+        add_trace(trace, jnp.float32(2), tall[...], corner[...])
 
 
 def last_body(z, left_in, positions, prev, source_a, source_b, out, left, right, total, out_stage,
@@ -417,13 +436,13 @@
     total, left, corner, positions, trace = call(
         z, functools.partial(own_body, z), [tiles, columns], [ANY, SMEM],
         [
-            sums, shape((z.span, z.wide), dtype), shape((z.span // 2, z.span), dtype),
+            sums, shape((z.span, z.wide), dtype), shape((z.span // 2, z.span // 2 + z.block), dtype),
             shape((z.rows, z.slots), jnp.int32), line,
         ],
         [ANY, ANY, ANY, SMEM, VMEM],
         [
             pltpu.VMEM(tiles.shape, dtype), dense, total_buffer, pltpu.VMEM(tiles.shape, jnp.float32),
-            DMA, DMA, DMA, DMA((z.rows,)),
+            DMA, DMA, DMA((3,)), DMA((z.rows,)),
         ],
         1, WHOLE_VMEM,
     )
@@ -449,7 +468,8 @@
     total, trace = near(("beside",), [beside], total, trace)
     first, second, corner, total, trace = lax.optimization_barrier((first, second, corner, total, trace))
     relay = receive(first, RELAY_FROM)
-    kind = lax.axis_index(AXES) % 4
+    device = lax.axis_index(AXES)
+    kind = device % 4
 
     def nearby(first, second, corner, total, trace):
         use_first = (kind == 0) | (kind == 3)
@@ -458,7 +478,11 @@
         total, trace, relay_left = near(("first", "second", "mixed"), [first, second, mixed], total, trace, True)
         trace = call(
             z, functools.partial(corner_body, z), [left, corner, trace], [ANY, VMEM, VMEM], line, VMEM,
-            [pltpu.VMEM((z.span, z.span // 2), dtype), DMA], 0,
+            [
+                pltpu.VMEM((z.span // 2, z.span // 2), dtype), pltpu.VMEM((z.span // 2, z.block), dtype),
+                pltpu.VMEM((z.span // 2 + z.block, z.span // 2), dtype), DMA((2,)),
+            ],
+            0,
         )
         return total, trace, relay_left
 
@@ -466,7 +490,7 @@
         return jnp.zeros_like(total), jnp.zeros_like(trace), jnp.zeros((z.span, 2 * z.span), dtype)
 
     total, trace, relay_left = lax.cond(
-        positions[0, 0] >= 0, nearby, nothing, first, second, corner, total, trace
+        device < devices, nearby, nothing, first, second, corner, total, trace
     )
     assert devices & (devices - 1) == 0
     steps = [1 << bit for bit in range(devices.bit_length() - 1)]

time: 120 us -> 120 us (level)
  no operation moved by 1% of the time
where the time goes in v19:
time: 120 us; the launch traced here: 119 us
  Pallas kernels  46.3 us (39%)
  waiting for transfers between devices  39.7 us (33%)
  starting transfers between devices  28 us (23%)
  other arithmetic  2.8 us (2%)
  between operations  2.52 us (2%)
    pallas_call x6, Pallas kernels, call(): pl.pallas_call(kernel, out_shape=out_shape, in_specs=in_specs, out_specs=...  46.3 us
    ppermute x8, waiting for transfers between devices, receive(): return lax.ppermute(shard, AXES, pairs)  35.8 us
    ppermute x8, starting transfers between devices, receive(): return lax.ppermute(shard, AXES, pairs)  20 us
    ppermute x7, starting transfers between devices, fetch(): lax.ppermute(value, AXES, [(d, d ^ step) for d in range(lax.axis_size(AXE...  7.95 us
    ppermute x7, waiting for transfers between devices, fetch(): lax.ppermute(value, AXES, [(d, d ^ step) for d in range(lax.axis_size(AXE...  3.92 us
  transfers between devices with their start and end apart: 15, of which 6 were waited for; matrix products, arithmetic and copies ran while one was open for 2% of the time, Pallas kernels for 36%

profile of v19, /device:TPU:0, one launch (start us, length us, event | category | flops | bytes accessed | tf_op | source)
XLA Modules:
  0.0 119.3 jit_solution(5780586596028788841)
XLA Ops:
  0.6 3.4 %shard_map.41 = bf16[81,128,128]{2,1,0:T(8,128)(2,1)} custom-call(bf16[4,20,128,128]{3,2,1,0:T(8,128)(2,1)} %own.1, s32[4,20]{1,0:T(4,128)} %columns.3), custom_call_target="tpu_custom_call" | custom-call | bytes 10485760 | tf_op jit(solution)/shard_map/pallas_call | solution.py:394
  4.0 0.5 collective-permute-start.5
  4.5 2.6 %collective-permute-start.3 = (bf16[81,128,128]{2,1,0:T(8,128)(2,1)}, bf16[81,128,128]{2,1,0:T(8,128)(2,1)}, u32[]{:S(2)}, u32[]{:S(2)}) collective-permute-start(bf16[81,128,128]{2,1,0:T(8,128)(2,1)} %shard_map.41), channel_id=1, source_target_pairs={{29,0},{3,1},{0,2},{6,3},{1,4},{7,5},{4,6},{10,7},{5,8},{11,9},{8,... | collective-permute-start | bytes 7962632 | tf_op jit(solution)/shard_map/ppermute | solution.py:48
  7.1 3.1 %collective-permute-start.2 = (bf16[81,128,128]{2,1,0:T(8,128)(2,1)}, bf16[81,128,128]{2,1,0:T(8,128)(2,1)}, u32[]{:S(2)}, u32[]{:S(2)}) collective-permute-start(bf16[81,128,128]{2,1,0:T(8,128)(2,1)} %shard_map.41), channel_id=1, source_target_pairs={{2,0},{4,1},{31,2},{1,3},{6,4},{8,5},{3,6},{5,7},{10,8},{12,9},{7,... | collective-permute-start | bytes 7962632 | tf_op jit(solution)/shard_map/ppermute | solution.py:48
  10.2 9.7 %shard_map.42 = (f32[4,20,128,128]{3,2,1,0:T(8,128)}, bf16[512,3712]{1,0:T(8,128)(2,1)}, bf16[256,384]{1,0:T(8,128)(2,1)}, s32[4,20]{1,0:T(4,128)S(1)}, f32[1,512]{1,0:T(1,128)}) custom-call(bf16[4,20,128,128]{3,2,1,0:T(8,128)(2,1)} %own.1, s32[4,20]{1,0:T(4,128)} %columns.3), custom_call_target="tpu_custom_call" | custom-call | flops 1879048192 | bytes 13107200 | tf_op jit(solution)/shard_map/pallas_call | solution.py:394
  19.9 1.3 %collective-permute-start.4 = (bf16[256,384]{1,0:T(8,128)(2,1)}, bf16[256,384]{1,0:T(8,128)(2,1)S(1)}, u32[]{:S(2)}, u32[]{:S(2)}) collective-permute-start(bf16[256,384]{1,0:T(8,128)(2,1)} %get-tuple-element.75), channel_id=1, source_target_pairs={{1,0},{2,3},{5,4},{6,7},{9,8},{10,11},{13,12},{14,15},{17,16},{18,... | collective-permute-start | bytes 589832 | tf_op jit(solution)/shard_map/ppermute | solution.py:48
  21.2 0.0 collective-permute-done.5.refs_0_
  21.2 9.6 %shard_map.43 = (f32[4,20,128,128]{3,2,1,0:T(8,128)}, f32[1,512]{1,0:T(1,128)S(1)}) custom-call(bf16[512,3712]{1,0:T(8,128)(2,1)} %get-tuple-element.76.left_in, s32[4,20]{1,0:T(4,128)S(1)} %get-tuple-element.77.positions, f32[4,20,128,128]{3,2,1,0:T(8,128)} %get-tuple-element.78.prev, f32[1,512]{1,0:T(1,128)} %get-tuple-element.79.trace_in, ...), custom_call_target="tpu_custom_call" | custom-call | flops 1879048192 | bytes 13107200 | tf_op jit(solution)/shard_map/pallas_call | solution.py:394
  30.8 0.0 collective-permute-done.4
  30.9 34.0 %collective-permute-done.3 = bf16[81,128,128]{2,1,0:T(8,128)(2,1)} collective-permute-done((bf16[81,128,128]{2,1,0:T(8,128)(2,1)}, bf16[81,128,128]{2,1,0:T(8,128)(2,1)}, u32[]{:S(2)}, u32[]{:S(2)}) %collective-permute-start.3) | collective-permute-done | bytes 2654240 | tf_op jit(solution)/shard_map/ppermute | solution.py:48
  64.8 0.7 collective-permute-done.2
  65.6 0.5 collective-permute-start.6
  66.0 25.5 %conditional.1 = (f32[4,20,128,128]{3,2,1,0:T(8,128)}, f32[1,512]{1,0:T(1,128)S(1)}, bf16[512,1024]{1,0:T(8,128)(2,1)}) conditional(s32[]{:T(128)} %convert_element_type.3, () %tuple.22, (s32[]{:T(128)}, bf16[81,128,128]{2,1,0:T(8,128)(2,1)}, bf16[81,128,128]{2,1,0:T(8,128)(2,1)}, bf16[512,3712]{1,0:T(8,128)(2,1)}, s32[4,20]{1,0:T(4,128)S(1)}, ...), branch_computations={%region_0.1_spmd, %region_1.2_spmd} | conditional | flops 5638471680 | bytes 63406344 | solution.py:492
  66.0 0.0 copy-start
  66.0 2.2 %broadcast_select_fusion = bf16[81,128,128]{2,1,0:T(8,128)(2,1)S(1)} fusion(bf16[81,128,128]{2,1,0:T(8,128)(2,1)} %get-tuple-element.43.refs_0_, bf16[81,128,128]{2,1,0:T(8,128)(2,1)} %get-tuple-element.44.refs_1_, pred[]{:T(512)S(6)} %or.2), kind=kLoop, calls=%fused_computation | loop fusion | flops 1327104 | bytes 7962625 | tf_op jit(solution)/shard_map/cond/branch_1_fun/jit(_where)/select_n | solution.py:476
  68.2 1.5 %collective-permute-start = (bf16[81,128,128]{2,1,0:T(8,128)(2,1)S(1)}, bf16[81,128,128]{2,1,0:T(8,128)(2,1)S(1)}, u32[]{:S(2)}, u32[]{:S(2)}) collective-permute-start(bf16[81,128,128]{2,1,0:T(8,128)(2,1)S(1)} %broadcast_select_fusion), channel_id=1, source_target_pairs={{1,0},{0,1},{3,2},{2,3},{5,4},{4,5},{7,6},{6,7},{9,8},{8,9},{11,10... | collective-permute-start | bytes 7962632 | tf_op jit(solution)/shard_map/cond/branch_1_fun/ppermute | solution.py:48
  69.7 6.7 %collective-permute-start.1 = (bf16[256,384]{1,0:T(8,128)(2,1)S(1)}, bf16[256,384]{1,0:T(8,128)(2,1)S(1)}, u32[]{:S(2)}, u32[]{:S(2)}) collective-permute-start(bf16[256,384]{1,0:T(8,128)(2,1)S(1)} %get-tuple-element.47), channel_id=1, source_target_pairs={{31,1},{4,2},{3,5},{8,6},{7,9},{12,10},{11,13},{16,14},{15,17},{20... | collective-permute-start | bytes 589832 | tf_op jit(solution)/shard_map/cond/branch_1_fun/ppermute | solution.py:48
  76.3 0.0 collective-permute-done.refs_2_
  76.3 0.0 copy-done
  76.4 15.1 %branch_1_fun.2 = (f32[4,20,128,128]{3,2,1,0:T(8,128)}, f32[1,512]{1,0:T(1,128)S(1)}, bf16[512,1024]{1,0:T(8,128)(2,1)}) custom-call(bf16[512,3712]{1,0:T(8,128)(2,1)S(1)} %copy-done, s32[4,20]{1,0:T(4,128)S(1)} %get-tuple-element.40.positions, f32[4,20,128,128]{3,2,1,0:T(8,128)} %get-tuple-element.41.prev, f32[1,512]{1,0:T(1,128)S(1)} %get-tuple-element.42.trace_in, ...), custom_call_target="tpu_custom_call" | custom-call | flops 5637144576 | bytes 18350080 | tf_op jit(solution)/shard_map/cond/branch_1_fun/pallas_call | solution.py:394
  91.5 0.0 collective-permute-done.1.corner
  91.5 0.1 collective-permute-start.7
  91.6 1.1 collective-permute-done.7
  92.7 2.7 %collective-permute-start.10 = (f32[1,512]{1,0:T(1,128)S(1)}, f32[1,512]{1,0:T(1,128)S(1)}, u32[]{:S(2)}, u32[]{:S(2)}) collective-permute-start(f32[1,512]{1,0:T(1,128)S(1)} %add.30), channel_id=1, source_target_pairs={{0,24},{1,25},{2,26},{3,27},{4,28},{5,29},{6,30},{7,31},{8,16},{9,... | collective-permute-start | bytes 6152 | tf_op jit(solution)/shard_map/ppermute | solution.py:52
  95.4 0.0 collective-permute-start.9
  95.4 1.7 %collective-permute-start.8 = (f32[1,512]{1,0:T(1,128)S(1)}, f32[1,512]{1,0:T(1,128)S(1)}, u32[]{:S(2)}, u32[]{:S(2)}) collective-permute-start(f32[1,512]{1,0:T(1,128)S(1)} %add.30), channel_id=1, source_target_pairs={{0,8},{1,9},{2,10},{3,11},{4,12},{5,13},{6,14},{7,15},{8,0},{9,1},... | collective-permute-start | bytes 6152 | tf_op jit(solution)/shard_map/ppermute | solution.py:52
  97.1 1.0 collective-permute-done.10
  98.1 1.8 %collective-permute-done.9 = f32[1,512]{1,0:T(1,128)S(1)} collective-permute-done((f32[1,512]{1,0:T(1,128)S(1)}, f32[1,512]{1,0:T(1,128)S(1)}, u32[]{:S(2)}, u32[]{:S(2)}) %collective-permute-start.9) | collective-permute-done | bytes 2080 | tf_op jit(solution)/shard_map/ppermute | solution.py:52
  99.9 0.0 collective-permute-done.8
  99.9 0.0 collective-permute-done.6.source_a
  99.9 4.0 %collective-permute-start.11 = (bf16[81,128,128]{2,1,0:T(8,128)(2,1)S(1)}, bf16[81,128,128]{2,1,0:T(8,128)(2,1)S(1)}, u32[]{:S(2)}, u32[]{:S(2)}) collective-permute-start(bf16[81,128,128]{2,1,0:T(8,128)(2,1)S(1)} %collective-permute-done.6.source_a), channel_id=1, source_target_pairs={{1,0},{0,1},{3,2},{2,3},{5,4},{4,5},{7,6},{6,7},{9,8},{8,9},{11,10... | collective-permute-start | bytes 7962632 | tf_op jit(solution)/shard_map/ppermute | solution.py:48
  103.9 0.0 collective-permute-start.14
  103.9 2.0 %collective-permute-start.13 = (f32[1,512]{1,0:T(1,128)S(1)}, f32[1,512]{1,0:T(1,128)S(1)}, u32[]{:S(2)}, u32[]{:S(2)}) collective-permute-start(f32[1,512]{1,0:T(1,128)S(1)} %add_add_fusion), channel_id=1, source_target_pairs={{0,4},{1,5},{2,6},{3,7},{4,0},{5,1},{6,2},{7,3},{8,12},{9,13},{10,... | collective-permute-start | bytes 6152 | tf_op jit(solution)/shard_map/ppermute | solution.py:52
  105.9 1.4 %collective-permute-start.12 = (f32[1,512]{1,0:T(1,128)S(1)}, f32[1,512]{1,0:T(1,128)S(1)}, u32[]{:S(2)}, u32[]{:S(2)}) collective-permute-start(f32[1,512]{1,0:T(1,128)S(1)} %add_add_fusion), channel_id=1, source_target_pairs={{0,2},{1,3},{2,0},{3,1},{4,6},{5,7},{6,4},{7,5},{8,10},{9,11},{10,... | collective-permute-start | bytes 6152 | tf_op jit(solution)/shard_map/ppermute | solution.py:52
  107.4 1.1 collective-permute-done.11.source_b
  108.5 8.4 %shard_map.44 = bf16[4,20,128,128]{3,2,1,0:T(8,128)(2,1)} custom-call(bf16[512,1024]{1,0:T(8,128)(2,1)} %get-tuple-element.87.left_in, s32[4,20]{1,0:T(4,128)S(1)} %get-tuple-element.77.positions, f32[4,20,128,128]{3,2,1,0:T(8,128)} %get-tuple-element.90.prev, bf16[81,128,128]{2,1,0:T(8,128)(2,1)S(1)} %collective-permute-done.6.source_a, ...), custom_call_target="tpu_custom_call" | custom-call | flops 3758096384 | bytes 15728640 | tf_op jit(solution)/shard_map/pallas_call | solution.py:394
  116.9 0.0 collective-permute-done.14
  116.9 0.0 collective-permute-done.13
  117.0 0.0 collective-permute-done.12
  117.0 0.6 add_reduce_fusion
  (3 shorter events, 0.1 us)
Async XLA Ops:
  4.0 17.2 %collective-permute-start.5 = (bf16[81,128,128]{2,1,0:T(8,128)(2,1)}, bf16[81,128,128]{2,1,0:T(8,128)(2,1)}, u32[]{:S(2)}, u32[]{:S(2)}) collective-permute-start(bf16[81,128,128]{2,1,0:T(8,128)(2,1)} %shard_map.41), channel_id=1, source_target_pairs={{1,0},{0,1},{3,2},{2,3},{5,4},{4,5},{7,6},{6,7},{9,8},{8,9},{11,10... | collective-permute-start | bytes 7962632 | tf_op jit(solution)/shard_map/ppermute | solution.py:48
  4.5 60.3 %collective-permute-start.3 = (bf16[81,128,128]{2,1,0:T(8,128)(2,1)}, bf16[81,128,128]{2,1,0:T(8,128)(2,1)}, u32[]{:S(2)}, u32[]{:S(2)}) collective-permute-start(bf16[81,128,128]{2,1,0:T(8,128)(2,1)} %shard_map.41), channel_id=1, source_target_pairs={{29,0},{3,1},{0,2},{6,3},{1,4},{7,5},{4,6},{10,7},{5,8},{11,9},{8,... | collective-permute-start | bytes 7962632 | tf_op jit(solution)/shard_map/ppermute | solution.py:48
  7.1 58.5 %collective-permute-start.2 = (bf16[81,128,128]{2,1,0:T(8,128)(2,1)}, bf16[81,128,128]{2,1,0:T(8,128)(2,1)}, u32[]{:S(2)}, u32[]{:S(2)}) collective-permute-start(bf16[81,128,128]{2,1,0:T(8,128)(2,1)} %shard_map.41), channel_id=1, source_target_pairs={{2,0},{4,1},{31,2},{1,3},{6,4},{8,5},{3,6},{5,7},{10,8},{12,9},{7,... | collective-permute-start | bytes 7962632 | tf_op jit(solution)/shard_map/ppermute | solution.py:48
  19.9 10.9 %collective-permute-start.4 = (bf16[256,384]{1,0:T(8,128)(2,1)}, bf16[256,384]{1,0:T(8,128)(2,1)S(1)}, u32[]{:S(2)}, u32[]{:S(2)}) collective-permute-start(bf16[256,384]{1,0:T(8,128)(2,1)} %get-tuple-element.75), channel_id=1, source_target_pairs={{1,0},{2,3},{5,4},{6,7},{9,8},{10,11},{13,12},{14,15},{17,16},{18,... | collective-permute-start | bytes 589832 | tf_op jit(solution)/shard_map/ppermute | solution.py:48
  65.6 34.4 %collective-permute-start.6 = (bf16[81,128,128]{2,1,0:T(8,128)(2,1)}, bf16[81,128,128]{2,1,0:T(8,128)(2,1)S(1)}, u32[]{:S(2)}, u32[]{:S(2)}) collective-permute-start(bf16[81,128,128]{2,1,0:T(8,128)(2,1)} %collective-permute-done.2), channel_id=1, source_target_pairs={{2,0},{28,1},{7,2},{1,3},{6,4},{0,5},{11,6},{5,7},{10,8},{4,9},{15... | collective-permute-start | bytes 7962632 | tf_op jit(solution)/shard_map/ppermute | solution.py:48
  66.0 10.3 %copy-start = (bf16[512,3712]{1,0:T(8,128)(2,1)S(1)}, bf16[512,3712]{1,0:T(8,128)(2,1)}, u32[]{:S(2)}) copy-start(bf16[512,3712]{1,0:T(8,128)(2,1)} %get-tuple-element.39.left_in.left) | copy-start | bytes 11403268 | tf_op jit(solution)/shard_map/cond
  68.2 8.1 %collective-permute-start = (bf16[81,128,128]{2,1,0:T(8,128)(2,1)S(1)}, bf16[81,128,128]{2,1,0:T(8,128)(2,1)S(1)}, u32[]{:S(2)}, u32[]{:S(2)}) collective-permute-start(bf16[81,128,128]{2,1,0:T(8,128)(2,1)S(1)} %broadcast_select_fusion), channel_id=1, source_target_pairs={{1,0},{0,1},{3,2},{2,3},{5,4},{4,5},{7,6},{6,7},{9,8},{8,9},{11,10... | collective-permute-start | bytes 7962632 | tf_op jit(solution)/shard_map/cond/branch_1_fun/ppermute | solution.py:48
  69.7 21.8 %collective-permute-start.1 = (bf16[256,384]{1,0:T(8,128)(2,1)S(1)}, bf16[256,384]{1,0:T(8,128)(2,1)S(1)}, u32[]{:S(2)}, u32[]{:S(2)}) collective-permute-start(bf16[256,384]{1,0:T(8,128)(2,1)S(1)} %get-tuple-element.47), channel_id=1, source_target_pairs={{31,1},{4,2},{3,5},{8,6},{7,9},{12,10},{11,13},{16,14},{15,17},{20... | collective-permute-start | bytes 589832 | tf_op jit(solution)/shard_map/cond/branch_1_fun/ppermute | solution.py:48
  91.5 1.2 %collective-permute-start.7 = (f32[1,512]{1,0:T(1,128)S(1)}, f32[1,512]{1,0:T(1,128)S(1)}, u32[]{:S(2)}, u32[]{:S(2)}) collective-permute-start(f32[1,512]{1,0:T(1,128)S(1)} %get-tuple-element.89), channel_id=1, source_target_pairs={{0,1},{1,0},{2,3},{3,2},{4,5},{5,4},{6,7},{7,6},{8,9},{9,8},{10,11... | collective-permute-start | bytes 6152 | tf_op jit(solution)/shard_map/ppermute | solution.py:52
  92.7 5.4 %collective-permute-start.10 = (f32[1,512]{1,0:T(1,128)S(1)}, f32[1,512]{1,0:T(1,128)S(1)}, u32[]{:S(2)}, u32[]{:S(2)}) collective-permute-start(f32[1,512]{1,0:T(1,128)S(1)} %add.30), channel_id=1, source_target_pairs={{0,24},{1,25},{2,26},{3,27},{4,28},{5,29},{6,30},{7,31},{8,16},{9,... | collective-permute-start | bytes 6152 | tf_op jit(solution)/shard_map/ppermute | solution.py:52
  95.4 4.5 %collective-permute-start.9 = (f32[1,512]{1,0:T(1,128)S(1)}, f32[1,512]{1,0:T(1,128)S(1)}, u32[]{:S(2)}, u32[]{:S(2)}) collective-permute-start(f32[1,512]{1,0:T(1,128)S(1)} %add.30), channel_id=1, source_target_pairs={{0,16},{1,17},{2,18},{3,19},{4,20},{5,21},{6,22},{7,23},{8,24},{9,... | collective-permute-start | bytes 6152 | tf_op jit(solution)/shard_map/ppermute | solution.py:52
  95.4 4.5 %collective-permute-start.8 = (f32[1,512]{1,0:T(1,128)S(1)}, f32[1,512]{1,0:T(1,128)S(1)}, u32[]{:S(2)}, u32[]{:S(2)}) collective-permute-start(f32[1,512]{1,0:T(1,128)S(1)} %add.30), channel_id=1, source_target_pairs={{0,8},{1,9},{2,10},{3,11},{4,12},{5,13},{6,14},{7,15},{8,0},{9,1},... | collective-permute-start | bytes 6152 | tf_op jit(solution)/shard_map/ppermute | solution.py:52
  99.9 8.6 %collective-permute-start.11 = (bf16[81,128,128]{2,1,0:T(8,128)(2,1)S(1)}, bf16[81,128,128]{2,1,0:T(8,128)(2,1)S(1)}, u32[]{:S(2)}, u32[]{:S(2)}) collective-permute-start(bf16[81,128,128]{2,1,0:T(8,128)(2,1)S(1)} %collective-permute-done.6.source_a), channel_id=1, source_target_pairs={{1,0},{0,1},{3,2},{2,3},{5,4},{4,5},{7,6},{6,7},{9,8},{8,9},{11,10... | collective-permute-start | bytes 7962632 | tf_op jit(solution)/shard_map/ppermute | solution.py:48
  103.9 13.0 %collective-permute-start.14 = (f32[1,512]{1,0:T(1,128)S(1)}, f32[1,512]{1,0:T(1,128)S(1)}, u32[]{:S(2)}, u32[]{:S(2)}) collective-permute-start(f32[1,512]{1,0:T(1,128)S(1)} %add_add_fusion), channel_id=1, source_target_pairs={{0,6},{1,7},{2,4},{3,5},{4,2},{5,3},{6,0},{7,1},{8,14},{9,15},{10,... | collective-permute-start | bytes 6152 | tf_op jit(solution)/shard_map/ppermute | solution.py:52
  103.9 13.0 %collective-permute-start.13 = (f32[1,512]{1,0:T(1,128)S(1)}, f32[1,512]{1,0:T(1,128)S(1)}, u32[]{:S(2)}, u32[]{:S(2)}) collective-permute-start(f32[1,512]{1,0:T(1,128)S(1)} %add_add_fusion), channel_id=1, source_target_pairs={{0,4},{1,5},{2,6},{3,7},{4,0},{5,1},{6,2},{7,3},{8,12},{9,13},{10,... | collective-permute-start | bytes 6152 | tf_op jit(solution)/shard_map/ppermute | solution.py:52
  105.9 11.0 %collective-permute-start.12 = (f32[1,512]{1,0:T(1,128)S(1)}, f32[1,512]{1,0:T(1,128)S(1)}, u32[]{:S(2)}, u32[]{:S(2)}) collective-permute-start(f32[1,512]{1,0:T(1,128)S(1)} %add_add_fusion), channel_id=1, source_target_pairs={{0,2},{1,3},{2,0},{3,1},{4,6},{5,7},{6,4},{7,5},{8,10},{9,11},{10,... | collective-permute-start | bytes 6152 | tf_op jit(solution)/shard_map/ppermute | solution.py:52

commit v20 on v19

--- a/solution.py
+++ b/solution.py
@@ -162,8 +162,8 @@
     trace[:, :value.shape[1]] += weight.astype(jnp.float32) * diagonal
 
 
-def own_body(z, own, columns, out, left_out, corner_out, positions, trace, stage, left, total, out_stage,
-             in_sem, left_sem, corner_sem, out_sems):
+def own_body(z, own, columns, out, left_out, corner_out, full_out, positions, trace, stage, left, total,
+             out_stage, in_sem, left_sem, corner_sem, out_sems):
     device = lax.axis_index(AXES)
     kind = device % 4
     copy = pltpu.make_async_copy(own, stage, in_sem)
@@ -193,10 +193,12 @@
         @pl.when(kind == UPPER)
         def _():
             go(0, pl.ds(0, half), pl.ds(0, half + z.block), corner_out)
+            go(3, pl.ds(0, z.span), pl.ds(0, z.span), full_out)
 
         @pl.when(kind != UPPER)
         def _():
             go(0, pl.ds(half, half), pl.ds(end + half, half), corner_out.at[:, pl.ds(0, half)])
+            go(3, pl.ds(0, z.span), pl.ds(end, z.span), full_out)
             for q in range(2):
                 go(
                     1 + q, pl.ds(z.span - z.block, z.block), pl.ds(end + q * z.block, z.block),
@@ -307,17 +309,16 @@
         copy.wait()
 
 
-def corner_body(z, left, corner, trace_in, trace, square, column, tall, sems):
+def corner_body(z, full, corner, trace_in, trace, square, column, tall, sems):
     kind = lax.axis_index(AXES) % 4
     half = z.span // 2
-    end = (z.chunks - 1) * z.span
     trace[...] = trace_in[...]
 
-    @pl.when(kind == UPPER)
+    @pl.when(kind == UPPER ^ 1)
     def _():
         copies = [
-            pltpu.make_async_copy(left.at[pl.ds(half, half), pl.ds(half, half)], square, sems.at[0]),
-            pltpu.make_async_copy(left.at[pl.ds(0, half), pl.ds(z.span - z.block, z.block)], column, sems.at[1]),
+            pltpu.make_async_copy(full.at[pl.ds(half, half), pl.ds(half, half)], square, sems.at[0]),
+            pltpu.make_async_copy(full.at[pl.ds(0, half), pl.ds(z.span - z.block, z.block)], column, sems.at[1]),
         ]
         for copy in copies:
             copy.start()
@@ -328,9 +329,9 @@
             rows = slice(q * z.block, (q + 1) * z.block)
             add_trace(trace, jnp.float32(2), column[rows], corner[rows, half:])
 
-    @pl.when(kind == LOWER)
+    @pl.when(kind == LOWER ^ 1)
     def _():
-        copy = pltpu.make_async_copy(left.at[pl.ds(0, half + z.block), pl.ds(end, half)], tall, sems.at[0])
+        copy = pltpu.make_async_copy(full.at[pl.ds(0, half + z.block), pl.ds(0, half)], tall, sems.at[0])
         copy.start()
         copy.wait()
         add_trace(trace, jnp.float32(2), tall[...], corner[...])
@@ -433,20 +434,22 @@
     second = receive(payload, SECOND)
     beside = receive(payload, PARTNER)
 
-    total, left, corner, positions, trace = call(
+    total, left, corner, full, positions, trace = call(
         z, functools.partial(own_body, z), [tiles, columns], [ANY, SMEM],
         [
             sums, shape((z.span, z.wide), dtype), shape((z.span // 2, z.span // 2 + z.block), dtype),
+            shape((z.span, z.span), dtype),
             shape((z.rows, z.slots), jnp.int32), line,
         ],
-        [ANY, ANY, ANY, SMEM, VMEM],
+        [ANY, ANY, ANY, ANY, SMEM, VMEM],
         [
             pltpu.VMEM(tiles.shape, dtype), dense, total_buffer, pltpu.VMEM(tiles.shape, jnp.float32),
-            DMA, DMA, DMA((3,)), DMA((z.rows,)),
+            DMA, DMA, DMA((4,)), DMA((z.rows,)),
         ],
         1, WHOLE_VMEM,
     )
     corner = receive(corner, PARTNER, (0, 3))
+    full = receive(full, PARTNER, (0, 3))
 
     def near(names, arrays, total, trace, final=False):
         extra = [shape((z.span, 2 * z.span), dtype)] * final
@@ -466,18 +469,20 @@
         )
 
     total, trace = near(("beside",), [beside], total, trace)
-    first, second, corner, total, trace = lax.optimization_barrier((first, second, corner, total, trace))
+    first, second, corner, full, total, trace = lax.optimization_barrier(
+        (first, second, corner, full, total, trace)
+    )
     relay = receive(first, RELAY_FROM)
     device = lax.axis_index(AXES)
     kind = device % 4
 
-    def nearby(first, second, corner, total, trace):
+    def nearby(first, second, corner, full, total, trace):
         use_first = (kind == 0) | (kind == 3)
         mixed = receive(jnp.where(use_first, first, second), PARTNER)
-        corner = receive(corner, (0, -2, 2, 0), (LOWER, UPPER))
+        corner = receive(corner, (-1, 0, 0, 1), (0, 3))
         total, trace, relay_left = near(("first", "second", "mixed"), [first, second, mixed], total, trace, True)
         trace = call(
-            z, functools.partial(corner_body, z), [left, corner, trace], [ANY, VMEM, VMEM], line, VMEM,
+            z, functools.partial(corner_body, z), [full, corner, trace], [ANY, VMEM, VMEM], line, VMEM,
             [
                 pltpu.VMEM((z.span // 2, z.span // 2), dtype), pltpu.VMEM((z.span // 2, z.block), dtype),
                 pltpu.VMEM((z.span // 2 + z.block, z.span // 2), dtype), DMA((2,)),
@@ -486,11 +491,11 @@
         )
         return total, trace, relay_left
 
-    def nothing(first, second, corner, total, trace):
+    def nothing(first, second, corner, full, total, trace):
         return jnp.zeros_like(total), jnp.zeros_like(trace), jnp.zeros((z.span, 2 * z.span), dtype)
 
     total, trace, relay_left = lax.cond(
-        device < devices, nearby, nothing, first, second, corner, total, trace
+        device < devices, nearby, nothing, first, second, corner, full, total, trace
     )
     assert devices & (devices - 1) == 0
     steps = [1 << bit for bit in range(devices.bit_length() - 1)]

time: 120 us -> 120 us (level)
  waiting for transfers between devices: 39.7 us -> 38.4 us
    ppermute x8 -> x9, starting transfers between devices: 20 us -> 21.1 us  [receive(): return lax.ppermute(shard, AXES, pairs)]
    ppermute x8 -> x9, waiting for transfers between devices: 35.8 us -> 34.7 us  [receive(): return lax.ppermute(shard, AXES, pairs)]
  transfers between devices with their start and end apart: 15 -> 16, of which waited for: 6 -> 7; matrix products, arithmetic and copies ran while one was open for 2% -> 2% of each run, Pallas kernels for 36% -> 36%
where the time goes in v20:
time: 120 us; the launch traced here: 119 us
  Pallas kernels  46.5 us (39%)
  waiting for transfers between devices  38.4 us (32%)
  starting transfers between devices  29.1 us (24%)
  other arithmetic  2.8 us (2%)
  between operations  2.53 us (2%)
    pallas_call x6, Pallas kernels, call(): pl.pallas_call(kernel, out_shape=out_shape, in_specs=in_specs, out_specs=...  46.5 us
    ppermute x9, waiting for transfers between devices, receive(): return lax.ppermute(shard, AXES, pairs)  34.7 us
    ppermute x9, starting transfers between devices, receive(): return lax.ppermute(shard, AXES, pairs)  21.1 us
    ppermute x7, starting transfers between devices, fetch(): lax.ppermute(value, AXES, [(d, d ^ step) for d in range(lax.axis_size(AXE...  7.95 us
    ppermute x7, waiting for transfers between devices, fetch(): lax.ppermute(value, AXES, [(d, d ^ step) for d in range(lax.axis_size(AXE...  3.62 us
  transfers between devices with their start and end apart: 16, of which 7 were waited for; matrix products, arithmetic and copies ran while one was open for 2% of the time, Pallas kernels for 36%

profile of v20, /device:TPU:0, one launch (start us, length us, event | category | flops | bytes accessed | tf_op | source)
XLA Modules:
  0.0 119.3 jit_solution(17756449519751318876)
XLA Ops:
  0.6 3.4 %shard_map.41 = bf16[81,128,128]{2,1,0:T(8,128)(2,1)} custom-call(bf16[4,20,128,128]{3,2,1,0:T(8,128)(2,1)} %own.1, s32[4,20]{1,0:T(4,128)} %columns.3), custom_call_target="tpu_custom_call" | custom-call | bytes 10485760 | tf_op jit(solution)/shard_map/pallas_call | solution.py:395
  4.0 0.5 collective-permute-start.6
  4.5 2.6 %collective-permute-start.3 = (bf16[81,128,128]{2,1,0:T(8,128)(2,1)}, bf16[81,128,128]{2,1,0:T(8,128)(2,1)}, u32[]{:S(2)}, u32[]{:S(2)}) collective-permute-start(bf16[81,128,128]{2,1,0:T(8,128)(2,1)} %shard_map.41), channel_id=1, source_target_pairs={{29,0},{3,1},{0,2},{6,3},{1,4},{7,5},{4,6},{10,7},{5,8},{11,9},{8,... | collective-permute-start | bytes 7962632 | tf_op jit(solution)/shard_map/ppermute | solution.py:48
  7.1 3.1 %collective-permute-start.2 = (bf16[81,128,128]{2,1,0:T(8,128)(2,1)}, bf16[81,128,128]{2,1,0:T(8,128)(2,1)}, u32[]{:S(2)}, u32[]{:S(2)}) collective-permute-start(bf16[81,128,128]{2,1,0:T(8,128)(2,1)} %shard_map.41), channel_id=1, source_target_pairs={{2,0},{4,1},{31,2},{1,3},{6,4},{8,5},{3,6},{5,7},{10,8},{12,9},{7,... | collective-permute-start | bytes 7962632 | tf_op jit(solution)/shard_map/ppermute | solution.py:48
  10.2 9.7 %shard_map.42 = (f32[4,20,128,128]{3,2,1,0:T(8,128)}, bf16[512,3712]{1,0:T(8,128)(2,1)}, bf16[256,384]{1,0:T(8,128)(2,1)}, bf16[512,512]{1,0:T(8,128)(2,1)}, s32[4,20]{1,0:T(4,128)S(1)}, /*index=5*/f32[1,512]{1,0:T(1,128)}) custom-call(bf16[4,20,128,128]{3,2,1,0:T(8,128)(2,1)} %own.1, s32[4,20]{1,0:T(4,128)} %columns.3), custom_call_target="tpu_custom_call" | custom-call | flops 1879048192 | bytes 13107200 | tf_op jit(solution)/shard_map/pallas_call | solution.py:395
  19.9 1.3 %collective-permute-start.5 = (bf16[512,512]{1,0:T(8,128)(2,1)}, bf16[512,512]{1,0:T(8,128)(2,1)S(1)}, u32[]{:S(2)}, u32[]{:S(2)}) collective-permute-start(bf16[512,512]{1,0:T(8,128)(2,1)} %get-tuple-element.81), channel_id=1, source_target_pairs={{1,0},{2,3},{5,4},{6,7},{9,8},{10,11},{13,12},{14,15},{17,16},{18,... | collective-permute-start | bytes 1572872 | tf_op jit(solution)/shard_map/ppermute | solution.py:48
  21.2 1.3 %collective-permute-start.4 = (bf16[256,384]{1,0:T(8,128)(2,1)}, bf16[256,384]{1,0:T(8,128)(2,1)S(1)}, u32[]{:S(2)}, u32[]{:S(2)}) collective-permute-start(bf16[256,384]{1,0:T(8,128)(2,1)} %get-tuple-element.80), channel_id=1, source_target_pairs={{1,0},{2,3},{5,4},{6,7},{9,8},{10,11},{13,12},{14,15},{17,16},{18,... | collective-permute-start | bytes 589832 | tf_op jit(solution)/shard_map/ppermute | solution.py:48
  22.5 0.0 collective-permute-done.6.refs_0_
  22.5 9.6 %shard_map.43 = (f32[4,20,128,128]{3,2,1,0:T(8,128)}, f32[1,512]{1,0:T(1,128)S(1)}) custom-call(bf16[512,3712]{1,0:T(8,128)(2,1)} %get-tuple-element.82.left_in, s32[4,20]{1,0:T(4,128)S(1)} %get-tuple-element.83.positions, f32[4,20,128,128]{3,2,1,0:T(8,128)} %get-tuple-element.84.prev, f32[1,512]{1,0:T(1,128)} %get-tuple-element.85.trace_in, ...), custom_call_target="tpu_custom_call" | custom-call | flops 1879048192 | bytes 13107200 | tf_op jit(solution)/shard_map/pallas_call | solution.py:395
  32.1 0.0 collective-permute-done.4
  32.1 0.0 collective-permute-done.5
  32.2 32.7 %collective-permute-done.3 = bf16[81,128,128]{2,1,0:T(8,128)(2,1)} collective-permute-done((bf16[81,128,128]{2,1,0:T(8,128)(2,1)}, bf16[81,128,128]{2,1,0:T(8,128)(2,1)}, u32[]{:S(2)}, u32[]{:S(2)}) %collective-permute-start.3) | collective-permute-done | bytes 2654240 | tf_op jit(solution)/shard_map/ppermute | solution.py:48
  64.8 0.7 collective-permute-done.2
  65.6 0.5 collective-permute-start.7
  66.0 25.5 %conditional.1 = (f32[4,20,128,128]{3,2,1,0:T(8,128)}, f32[1,512]{1,0:T(1,128)S(1)}, bf16[512,1024]{1,0:T(8,128)(2,1)}) conditional(s32[]{:T(128)} %convert_element_type.3, () %tuple.22, (s32[]{:T(128)}, bf16[81,128,128]{2,1,0:T(8,128)(2,1)}, bf16[81,128,128]{2,1,0:T(8,128)(2,1)}, bf16[512,3712]{1,0:T(8,128)(2,1)}, s32[4,20]{1,0:T(4,128)S(1)}, ...), branch_computations={%region_0.1_spmd, %region_1.2_spmd} | conditional | flops 5638471680 | bytes 63406344 | solution.py:497
  66.0 0.0 copy-start
  66.0 2.2 %broadcast_select_fusion = bf16[81,128,128]{2,1,0:T(8,128)(2,1)S(1)} fusion(bf16[81,128,128]{2,1,0:T(8,128)(2,1)} %get-tuple-element.45.refs_0_, bf16[81,128,128]{2,1,0:T(8,128)(2,1)} %get-tuple-element.46.refs_1_, pred[]{:T(512)S(6)} %or.2), kind=kLoop, calls=%fused_computation | loop fusion | flops 1327104 | bytes 7962625 | tf_op jit(solution)/shard_map/cond/branch_1_fun/jit(_where)/select_n | solution.py:481
  68.2 1.5 %collective-permute-start = (bf16[81,128,128]{2,1,0:T(8,128)(2,1)S(1)}, bf16[81,128,128]{2,1,0:T(8,128)(2,1)S(1)}, u32[]{:S(2)}, u32[]{:S(2)}) collective-permute-start(bf16[81,128,128]{2,1,0:T(8,128)(2,1)S(1)} %broadcast_select_fusion), channel_id=1, source_target_pairs={{1,0},{0,1},{3,2},{2,3},{5,4},{4,5},{7,6},{6,7},{9,8},{8,9},{11,10... | collective-permute-start | bytes 7962632 | tf_op jit(solution)/shard_map/cond/branch_1_fun/ppermute | solution.py:48
  69.7 6.4 %collective-permute-start.1 = (bf16[256,384]{1,0:T(8,128)(2,1)S(1)}, bf16[256,384]{1,0:T(8,128)(2,1)S(1)}, u32[]{:S(2)}, u32[]{:S(2)}) collective-permute-start(bf16[256,384]{1,0:T(8,128)(2,1)S(1)} %get-tuple-element.50), channel_id=1, source_target_pairs={{31,0},{4,3},{3,4},{8,7},{7,8},{12,11},{11,12},{16,15},{15,16},{20... | collective-permute-start | bytes 589832 | tf_op jit(solution)/shard_map/cond/branch_1_fun/ppermute | solution.py:48
  76.1 0.0 collective-permute-done.refs_2_
  76.1 0.0 copy-done
  76.1 15.1 %branch_1_fun.2 = (f32[4,20,128,128]{3,2,1,0:T(8,128)}, f32[1,512]{1,0:T(1,128)S(1)}, bf16[512,1024]{1,0:T(8,128)(2,1)}) custom-call(bf16[512,3712]{1,0:T(8,128)(2,1)S(1)} %copy-done, s32[4,20]{1,0:T(4,128)S(1)} %get-tuple-element.42.positions, f32[4,20,128,128]{3,2,1,0:T(8,128)} %get-tuple-element.43.prev, f32[1,512]{1,0:T(1,128)S(1)} %get-tuple-element.44.trace_in, ...), custom_call_target="tpu_custom_call" | custom-call | flops 5637144576 | bytes 18350080 | tf_op jit(solution)/shard_map/cond/branch_1_fun/pallas_call | solution.py:395
  91.2 0.0 collective-permute-done.1.corner
  91.2 0.3 branch_1_fun.3
  91.5 0.1 collective-permute-start.8
  91.6 1.1 collective-permute-done.8
  92.8 2.4 %collective-permute-start.11 = (f32[1,512]{1,0:T(1,128)S(1)}, f32[1,512]{1,0:T(1,128)S(1)}, u32[]{:S(2)}, u32[]{:S(2)}) collective-permute-start(f32[1,512]{1,0:T(1,128)S(1)} %add.30), channel_id=1, source_target_pairs={{0,24},{1,25},{2,26},{3,27},{4,28},{5,29},{6,30},{7,31},{8,16},{9,... | collective-permute-start | bytes 6152 | tf_op jit(solution)/shard_map/ppermute | solution.py:52
  95.1 0.0 collective-permute-start.10
  95.1 2.0 %collective-permute-start.9 = (f32[1,512]{1,0:T(1,128)S(1)}, f32[1,512]{1,0:T(1,128)S(1)}, u32[]{:S(2)}, u32[]{:S(2)}) collective-permute-start(f32[1,512]{1,0:T(1,128)S(1)} %add.30), channel_id=1, source_target_pairs={{0,8},{1,9},{2,10},{3,11},{4,12},{5,13},{6,14},{7,15},{8,0},{9,1},... | collective-permute-start | bytes 6152 | tf_op jit(solution)/shard_map/ppermute | solution.py:52
  97.2 1.0 collective-permute-done.11
  98.1 1.5 %collective-permute-done.10 = f32[1,512]{1,0:T(1,128)S(1)} collective-permute-done((f32[1,512]{1,0:T(1,128)S(1)}, f32[1,512]{1,0:T(1,128)S(1)}, u32[]{:S(2)}, u32[]{:S(2)}) %collective-permute-start.10) | collective-permute-done | bytes 2080 | tf_op jit(solution)/shard_map/ppermute | solution.py:52
  99.6 0.0 collective-permute-done.9
  99.6 0.2 collective-permute-done.7.source_a
  99.9 4.0 %collective-permute-start.12 = (bf16[81,128,128]{2,1,0:T(8,128)(2,1)S(1)}, bf16[81,128,128]{2,1,0:T(8,128)(2,1)S(1)}, u32[]{:S(2)}, u32[]{:S(2)}) collective-permute-start(bf16[81,128,128]{2,1,0:T(8,128)(2,1)S(1)} %collective-permute-done.7.source_a), channel_id=1, source_target_pairs={{1,0},{0,1},{3,2},{2,3},{5,4},{4,5},{7,6},{6,7},{9,8},{8,9},{11,10... | collective-permute-start | bytes 7962632 | tf_op jit(solution)/shard_map/ppermute | solution.py:48
  103.9 0.0 collective-permute-start.15
  103.9 2.0 %collective-permute-start.14 = (f32[1,512]{1,0:T(1,128)S(1)}, f32[1,512]{1,0:T(1,128)S(1)}, u32[]{:S(2)}, u32[]{:S(2)}) collective-permute-start(f32[1,512]{1,0:T(1,128)S(1)} %add_add_fusion), channel_id=1, source_target_pairs={{0,4},{1,5},{2,6},{3,7},{4,0},{5,1},{6,2},{7,3},{8,12},{9,13},{10,... | collective-permute-start | bytes 6152 | tf_op jit(solution)/shard_map/ppermute | solution.py:52
  105.9 1.4 %collective-permute-start.13 = (f32[1,512]{1,0:T(1,128)S(1)}, f32[1,512]{1,0:T(1,128)S(1)}, u32[]{:S(2)}, u32[]{:S(2)}) collective-permute-start(f32[1,512]{1,0:T(1,128)S(1)} %add_add_fusion), channel_id=1, source_target_pairs={{0,2},{1,3},{2,0},{3,1},{4,6},{5,7},{6,4},{7,5},{8,10},{9,11},{10,... | collective-permute-start | bytes 6152 | tf_op jit(solution)/shard_map/ppermute | solution.py:52
  107.4 1.1 collective-permute-done.12.source_b
  108.5 8.4 %shard_map.44 = bf16[4,20,128,128]{3,2,1,0:T(8,128)(2,1)} custom-call(bf16[512,1024]{1,0:T(8,128)(2,1)} %get-tuple-element.94.left_in, s32[4,20]{1,0:T(4,128)S(1)} %get-tuple-element.83.positions, f32[4,20,128,128]{3,2,1,0:T(8,128)} %get-tuple-element.97.prev, bf16[81,128,128]{2,1,0:T(8,128)(2,1)S(1)} %collective-permute-done.7.source_a, ...), custom_call_target="tpu_custom_call" | custom-call | flops 3758096384 | bytes 15728640 | tf_op jit(solution)/shard_map/pallas_call | solution.py:395
  116.9 0.0 collective-permute-done.15
  116.9 0.0 collective-permute-done.14
  116.9 0.0 collective-permute-done.13
  117.0 0.6 add_reduce_fusion
  (2 shorter events, 0.0 us)
Async XLA Ops:
  4.0 18.5 %collective-permute-start.6 = (bf16[81,128,128]{2,1,0:T(8,128)(2,1)}, bf16[81,128,128]{2,1,0:T(8,128)(2,1)}, u32[]{:S(2)}, u32[]{:S(2)}) collective-permute-start(bf16[81,128,128]{2,1,0:T(8,128)(2,1)} %shard_map.41), channel_id=1, source_target_pairs={{1,0},{0,1},{3,2},{2,3},{5,4},{4,5},{7,6},{6,7},{9,8},{8,9},{11,10... | collective-permute-start | bytes 7962632 | tf_op jit(solution)/shard_map/ppermute | solution.py:48
  4.5 60.3 %collective-permute-start.3 = (bf16[81,128,128]{2,1,0:T(8,128)(2,1)}, bf16[81,128,128]{2,1,0:T(8,128)(2,1)}, u32[]{:S(2)}, u32[]{:S(2)}) collective-permute-start(bf16[81,128,128]{2,1,0:T(8,128)(2,1)} %shard_map.41), channel_id=1, source_target_pairs={{29,0},{3,1},{0,2},{6,3},{1,4},{7,5},{4,6},{10,7},{5,8},{11,9},{8,... | collective-permute-start | bytes 7962632 | tf_op jit(solution)/shard_map/ppermute | solution.py:48
  7.1 58.5 %collective-permute-start.2 = (bf16[81,128,128]{2,1,0:T(8,128)(2,1)}, bf16[81,128,128]{2,1,0:T(8,128)(2,1)}, u32[]{:S(2)}, u32[]{:S(2)}) collective-permute-start(bf16[81,128,128]{2,1,0:T(8,128)(2,1)} %shard_map.41), channel_id=1, source_target_pairs={{2,0},{4,1},{31,2},{1,3},{6,4},{8,5},{3,6},{5,7},{10,8},{12,9},{7,... | collective-permute-start | bytes 7962632 | tf_op jit(solution)/shard_map/ppermute | solution.py:48
  19.9 12.2 %collective-permute-start.5 = (bf16[512,512]{1,0:T(8,128)(2,1)}, bf16[512,512]{1,0:T(8,128)(2,1)S(1)}, u32[]{:S(2)}, u32[]{:S(2)}) collective-permute-start(bf16[512,512]{1,0:T(8,128)(2,1)} %get-tuple-element.81), channel_id=1, source_target_pairs={{1,0},{2,3},{5,4},{6,7},{9,8},{10,11},{13,12},{14,15},{17,16},{18,... | collective-permute-start | bytes 1572872 | tf_op jit(solution)/shard_map/ppermute | solution.py:48
  21.2 10.9 %collective-permute-start.4 = (bf16[256,384]{1,0:T(8,128)(2,1)}, bf16[256,384]{1,0:T(8,128)(2,1)S(1)}, u32[]{:S(2)}, u32[]{:S(2)}) collective-permute-start(bf16[256,384]{1,0:T(8,128)(2,1)} %get-tuple-element.80), channel_id=1, source_target_pairs={{1,0},{2,3},{5,4},{6,7},{9,8},{10,11},{13,12},{14,15},{17,16},{18,... | collective-permute-start | bytes 589832 | tf_op jit(solution)/shard_map/ppermute | solution.py:48
  65.6 34.3 %collective-permute-start.7 = (bf16[81,128,128]{2,1,0:T(8,128)(2,1)}, bf16[81,128,128]{2,1,0:T(8,128)(2,1)S(1)}, u32[]{:S(2)}, u32[]{:S(2)}) collective-permute-start(bf16[81,128,128]{2,1,0:T(8,128)(2,1)} %collective-permute-done.2), channel_id=1, source_target_pairs={{2,0},{28,1},{7,2},{1,3},{6,4},{0,5},{11,6},{5,7},{10,8},{4,9},{15... | collective-permute-start | bytes 7962632 | tf_op jit(solution)/shard_map/ppermute | solution.py:48
  66.0 10.1 %copy-start = (bf16[512,3712]{1,0:T(8,128)(2,1)S(1)}, bf16[512,3712]{1,0:T(8,128)(2,1)}, u32[]{:S(2)}) copy-start(bf16[512,3712]{1,0:T(8,128)(2,1)} %get-tuple-element.41.left_in) | copy-start | bytes 11403268 | tf_op jit(solution)/shard_map/cond
  68.2 7.9 %collective-permute-start = (bf16[81,128,128]{2,1,0:T(8,128)(2,1)S(1)}, bf16[81,128,128]{2,1,0:T(8,128)(2,1)S(1)}, u32[]{:S(2)}, u32[]{:S(2)}) collective-permute-start(bf16[81,128,128]{2,1,0:T(8,128)(2,1)S(1)} %broadcast_select_fusion), channel_id=1, source_target_pairs={{1,0},{0,1},{3,2},{2,3},{5,4},{4,5},{7,6},{6,7},{9,8},{8,9},{11,10... | collective-permute-start | bytes 7962632 | tf_op jit(solution)/shard_map/cond/branch_1_fun/ppermute | solution.py:48
  69.7 21.5 %collective-permute-start.1 = (bf16[256,384]{1,0:T(8,128)(2,1)S(1)}, bf16[256,384]{1,0:T(8,128)(2,1)S(1)}, u32[]{:S(2)}, u32[]{:S(2)}) collective-permute-start(bf16[256,384]{1,0:T(8,128)(2,1)S(1)} %get-tuple-element.50), channel_id=1, source_target_pairs={{31,0},{4,3},{3,4},{8,7},{7,8},{12,11},{11,12},{16,15},{15,16},{20... | collective-permute-start | bytes 589832 | tf_op jit(solution)/shard_map/cond/branch_1_fun/ppermute | solution.py:48
  91.5 1.2 %collective-permute-start.8 = (f32[1,512]{1,0:T(1,128)S(1)}, f32[1,512]{1,0:T(1,128)S(1)}, u32[]{:S(2)}, u32[]{:S(2)}) collective-permute-start(f32[1,512]{1,0:T(1,128)S(1)} %get-tuple-element.96), channel_id=1, source_target_pairs={{0,1},{1,0},{2,3},{3,2},{4,5},{5,4},{6,7},{7,6},{8,9},{9,8},{10,11... | collective-permute-start | bytes 6152 | tf_op jit(solution)/shard_map/ppermute | solution.py:52
  92.8 5.4 %collective-permute-start.11 = (f32[1,512]{1,0:T(1,128)S(1)}, f32[1,512]{1,0:T(1,128)S(1)}, u32[]{:S(2)}, u32[]{:S(2)}) collective-permute-start(f32[1,512]{1,0:T(1,128)S(1)} %add.30), channel_id=1, source_target_pairs={{0,24},{1,25},{2,26},{3,27},{4,28},{5,29},{6,30},{7,31},{8,16},{9,... | collective-permute-start | bytes 6152 | tf_op jit(solution)/shard_map/ppermute | solution.py:52
  95.1 4.5 %collective-permute-start.10 = (f32[1,512]{1,0:T(1,128)S(1)}, f32[1,512]{1,0:T(1,128)S(1)}, u32[]{:S(2)}, u32[]{:S(2)}) collective-permute-start(f32[1,512]{1,0:T(1,128)S(1)} %add.30), channel_id=1, source_target_pairs={{0,16},{1,17},{2,18},{3,19},{4,20},{5,21},{6,22},{7,23},{8,24},{9,... | collective-permute-start | bytes 6152 | tf_op jit(solution)/shard_map/ppermute | solution.py:52
  95.1 4.5 %collective-permute-start.9 = (f32[1,512]{1,0:T(1,128)S(1)}, f32[1,512]{1,0:T(1,128)S(1)}, u32[]{:S(2)}, u32[]{:S(2)}) collective-permute-start(f32[1,512]{1,0:T(1,128)S(1)} %add.30), channel_id=1, source_target_pairs={{0,8},{1,9},{2,10},{3,11},{4,12},{5,13},{6,14},{7,15},{8,0},{9,1},... | collective-permute-start | bytes 6152 | tf_op jit(solution)/shard_map/ppermute | solution.py:52
  99.9 8.6 %collective-permute-start.12 = (bf16[81,128,128]{2,1,0:T(8,128)(2,1)S(1)}, bf16[81,128,128]{2,1,0:T(8,128)(2,1)S(1)}, u32[]{:S(2)}, u32[]{:S(2)}) collective-permute-start(bf16[81,128,128]{2,1,0:T(8,128)(2,1)S(1)} %collective-permute-done.7.source_a), channel_id=1, source_target_pairs={{1,0},{0,1},{3,2},{2,3},{5,4},{4,5},{7,6},{6,7},{9,8},{8,9},{11,10... | collective-permute-start | bytes 7962632 | tf_op jit(solution)/shard_map/ppermute | solution.py:48
  103.9 13.0 %collective-permute-start.15 = (f32[1,512]{1,0:T(1,128)S(1)}, f32[1,512]{1,0:T(1,128)S(1)}, u32[]{:S(2)}, u32[]{:S(2)}) collective-permute-start(f32[1,512]{1,0:T(1,128)S(1)} %add_add_fusion), channel_id=1, source_target_pairs={{0,6},{1,7},{2,4},{3,5},{4,2},{5,3},{6,0},{7,1},{8,14},{9,15},{10,... | collective-permute-start | bytes 6152 | tf_op jit(solution)/shard_map/ppermute | solution.py:52
  103.9 13.0 %collective-permute-start.14 = (f32[1,512]{1,0:T(1,128)S(1)}, f32[1,512]{1,0:T(1,128)S(1)}, u32[]{:S(2)}, u32[]{:S(2)}) collective-permute-start(f32[1,512]{1,0:T(1,128)S(1)} %add_add_fusion), channel_id=1, source_target_pairs={{0,4},{1,5},{2,6},{3,7},{4,0},{5,1},{6,2},{7,3},{8,12},{9,13},{10,... | collective-permute-start | bytes 6152 | tf_op jit(solution)/shard_map/ppermute | solution.py:52
  105.9 11.0 %collective-permute-start.13 = (f32[1,512]{1,0:T(1,128)S(1)}, f32[1,512]{1,0:T(1,128)S(1)}, u32[]{:S(2)}, u32[]{:S(2)}) collective-permute-start(f32[1,512]{1,0:T(1,128)S(1)} %add_add_fusion), channel_id=1, source_target_pairs={{0,2},{1,3},{2,0},{3,1},{4,6},{5,7},{6,4},{7,5},{8,10},{9,11},{10,... | collective-permute-start | bytes 6152 | tf_op jit(solution)/shard_map/ppermute | solution.py:52

commit v21 on v20

--- a/solution.py
+++ b/solution.py
@@ -97,7 +97,7 @@
             column = pl.ds(aligned(place(r, u), z.block), z.block)
             dense[top + r * z.block:top + (r + 1) * z.block, column] = source[r * z.slots + u]
             return carry
-        lax.fori_loop(0, z.slots, one, 0, unroll=10)
+        lax.fori_loop(0, z.slots, one, 0, unroll=20)
 
 
 def decode(z, offsets, spot, vector, scalars, sem):
@@ -149,7 +149,7 @@
                 value = value + prev[r, s]
             stage[r, s] = value.astype(stage.dtype)
             return carry
-        lax.fori_loop(0, z.slots, one, 0, unroll=10)
+        lax.fori_loop(0, z.slots, one, 0, unroll=20)
         pltpu.make_async_copy(stage.at[r], out.at[r], sems.at[r]).start()
     for r in range(z.rows):
         pltpu.make_async_copy(stage.at[r], out.at[r], sems.at[r]).wait()
@@ -178,7 +178,7 @@
             positions[r, u] = column
             left[r * z.block:(r + 1) * z.block, pl.ds(aligned(column, z.block), z.block)] = stage[r, u]
             return carry
-        lax.fori_loop(0, z.slots, place, 0, unroll=10)
+        lax.fori_loop(0, z.slots, place, 0, unroll=20)
     left_copy = pltpu.make_async_copy(left, left_out, left_sem)
     left_copy.start()
     half = z.span // 2

time: 120 us -> 120 us (level)
  no operation moved by 1% of the time
where the time goes in v21:
time: 120 us; the launch traced here: 119 us
  Pallas kernels  46 us (38%)
  waiting for transfers between devices  38.7 us (32%)
  starting transfers between devices  29.1 us (24%)
  other arithmetic  2.8 us (2%)
  between operations  2.53 us (2%)
    pallas_call x6, Pallas kernels, call(): pl.pallas_call(kernel, out_shape=out_shape, in_specs=in_specs, out_specs=...  46 us
    ppermute x9, waiting for transfers between devices, receive(): return lax.ppermute(shard, AXES, pairs)  35.1 us
    ppermute x9, starting transfers between devices, receive(): return lax.ppermute(shard, AXES, pairs)  21.1 us
    ppermute x7, starting transfers between devices, fetch(): lax.ppermute(value, AXES, [(d, d ^ step) for d in range(lax.axis_size(AXE...  7.95 us
    ppermute x7, waiting for transfers between devices, fetch(): lax.ppermute(value, AXES, [(d, d ^ step) for d in range(lax.axis_size(AXE...  3.64 us
  transfers between devices with their start and end apart: 16, of which 7 were waited for; matrix products, arithmetic and copies ran while one was open for 2% of the time, Pallas kernels for 36%

profile of v21, /device:TPU:0, one launch (start us, length us, event | category | flops | bytes accessed | tf_op | source)
XLA Modules:
  0.0 119.1 jit_solution(4247604510966085954)
XLA Ops:
  0.6 3.4 %shard_map.41 = bf16[81,128,128]{2,1,0:T(8,128)(2,1)} custom-call(bf16[4,20,128,128]{3,2,1,0:T(8,128)(2,1)} %own.1, s32[4,20]{1,0:T(4,128)} %columns.3), custom_call_target="tpu_custom_call" | custom-call | bytes 10485760 | tf_op jit(solution)/shard_map/pallas_call | solution.py:395
  4.0 0.5 collective-permute-start.6
  4.5 2.6 %collective-permute-start.3 = (bf16[81,128,128]{2,1,0:T(8,128)(2,1)}, bf16[81,128,128]{2,1,0:T(8,128)(2,1)}, u32[]{:S(2)}, u32[]{:S(2)}) collective-permute-start(bf16[81,128,128]{2,1,0:T(8,128)(2,1)} %shard_map.41), channel_id=1, source_target_pairs={{29,0},{3,1},{0,2},{6,3},{1,4},{7,5},{4,6},{10,7},{5,8},{11,9},{8,... | collective-permute-start | bytes 7962632 | tf_op jit(solution)/shard_map/ppermute | solution.py:48
  7.1 3.1 %collective-permute-start.2 = (bf16[81,128,128]{2,1,0:T(8,128)(2,1)}, bf16[81,128,128]{2,1,0:T(8,128)(2,1)}, u32[]{:S(2)}, u32[]{:S(2)}) collective-permute-start(bf16[81,128,128]{2,1,0:T(8,128)(2,1)} %shard_map.41), channel_id=1, source_target_pairs={{2,0},{4,1},{31,2},{1,3},{6,4},{8,5},{3,6},{5,7},{10,8},{12,9},{7,... | collective-permute-start | bytes 7962632 | tf_op jit(solution)/shard_map/ppermute | solution.py:48
  10.2 9.5 %shard_map.42 = (f32[4,20,128,128]{3,2,1,0:T(8,128)}, bf16[512,3712]{1,0:T(8,128)(2,1)}, bf16[256,384]{1,0:T(8,128)(2,1)}, bf16[512,512]{1,0:T(8,128)(2,1)}, s32[4,20]{1,0:T(4,128)S(1)}, /*index=5*/f32[1,512]{1,0:T(1,128)}) custom-call(bf16[4,20,128,128]{3,2,1,0:T(8,128)(2,1)} %own.1, s32[4,20]{1,0:T(4,128)} %columns.3), custom_call_target="tpu_custom_call" | custom-call | flops 1879048192 | bytes 13107200 | tf_op jit(solution)/shard_map/pallas_call | solution.py:395
  19.7 1.3 %collective-permute-start.5 = (bf16[512,512]{1,0:T(8,128)(2,1)}, bf16[512,512]{1,0:T(8,128)(2,1)S(1)}, u32[]{:S(2)}, u32[]{:S(2)}) collective-permute-start(bf16[512,512]{1,0:T(8,128)(2,1)} %get-tuple-element.81), channel_id=1, source_target_pairs={{1,0},{2,3},{5,4},{6,7},{9,8},{10,11},{13,12},{14,15},{17,16},{18,... | collective-permute-start | bytes 1572872 | tf_op jit(solution)/shard_map/ppermute | solution.py:48
  21.0 1.3 %collective-permute-start.4 = (bf16[256,384]{1,0:T(8,128)(2,1)}, bf16[256,384]{1,0:T(8,128)(2,1)S(1)}, u32[]{:S(2)}, u32[]{:S(2)}) collective-permute-start(bf16[256,384]{1,0:T(8,128)(2,1)} %get-tuple-element.80), channel_id=1, source_target_pairs={{1,0},{2,3},{5,4},{6,7},{9,8},{10,11},{13,12},{14,15},{17,16},{18,... | collective-permute-start | bytes 589832 | tf_op jit(solution)/shard_map/ppermute | solution.py:48
  22.3 0.0 collective-permute-done.6.refs_0_
  22.3 9.5 %shard_map.43 = (f32[4,20,128,128]{3,2,1,0:T(8,128)}, f32[1,512]{1,0:T(1,128)S(1)}) custom-call(bf16[512,3712]{1,0:T(8,128)(2,1)} %get-tuple-element.82.left_in, s32[4,20]{1,0:T(4,128)S(1)} %get-tuple-element.83.positions, f32[4,20,128,128]{3,2,1,0:T(8,128)} %get-tuple-element.84.prev, f32[1,512]{1,0:T(1,128)} %get-tuple-element.85.trace_in, ...), custom_call_target="tpu_custom_call" | custom-call | flops 1879048192 | bytes 13107200 | tf_op jit(solution)/shard_map/pallas_call | solution.py:395
  31.8 0.0 collective-permute-done.4
  31.9 0.0 collective-permute-done.5
  31.9 33.0 %collective-permute-done.3 = bf16[81,128,128]{2,1,0:T(8,128)(2,1)} collective-permute-done((bf16[81,128,128]{2,1,0:T(8,128)(2,1)}, bf16[81,128,128]{2,1,0:T(8,128)(2,1)}, u32[]{:S(2)}, u32[]{:S(2)}) %collective-permute-start.3) | collective-permute-done | bytes 2654240 | tf_op jit(solution)/shard_map/ppermute | solution.py:48
  64.8 0.7 collective-permute-done.2
  65.6 0.5 collective-permute-start.7
  66.0 25.4 %conditional.1 = (f32[4,20,128,128]{3,2,1,0:T(8,128)}, f32[1,512]{1,0:T(1,128)S(1)}, bf16[512,1024]{1,0:T(8,128)(2,1)}) conditional(s32[]{:T(128)} %convert_element_type.3, () %tuple.22, (s32[]{:T(128)}, bf16[81,128,128]{2,1,0:T(8,128)(2,1)}, bf16[81,128,128]{2,1,0:T(8,128)(2,1)}, bf16[512,3712]{1,0:T(8,128)(2,1)}, s32[4,20]{1,0:T(4,128)S(1)}, ...), branch_computations={%region_0.1_spmd, %region_1.2_spmd} | conditional | flops 5638471680 | bytes 63406344 | solution.py:497
  66.0 0.0 copy-start
  66.0 2.2 %broadcast_select_fusion = bf16[81,128,128]{2,1,0:T(8,128)(2,1)S(1)} fusion(bf16[81,128,128]{2,1,0:T(8,128)(2,1)} %get-tuple-element.45.refs_0_, bf16[81,128,128]{2,1,0:T(8,128)(2,1)} %get-tuple-element.46.refs_1_, pred[]{:T(512)S(6)} %or.2), kind=kLoop, calls=%fused_computation | loop fusion | flops 1327104 | bytes 7962625 | tf_op jit(solution)/shard_map/cond/branch_1_fun/jit(_where)/select_n | solution.py:481
  68.2 1.5 %collective-permute-start = (bf16[81,128,128]{2,1,0:T(8,128)(2,1)S(1)}, bf16[81,128,128]{2,1,0:T(8,128)(2,1)S(1)}, u32[]{:S(2)}, u32[]{:S(2)}) collective-permute-start(bf16[81,128,128]{2,1,0:T(8,128)(2,1)S(1)} %broadcast_select_fusion), channel_id=1, source_target_pairs={{1,0},{0,1},{3,2},{2,3},{5,4},{4,5},{7,6},{6,7},{9,8},{8,9},{11,10... | collective-permute-start | bytes 7962632 | tf_op jit(solution)/shard_map/cond/branch_1_fun/ppermute | solution.py:48
  69.7 6.4 %collective-permute-start.1 = (bf16[256,384]{1,0:T(8,128)(2,1)S(1)}, bf16[256,384]{1,0:T(8,128)(2,1)S(1)}, u32[]{:S(2)}, u32[]{:S(2)}) collective-permute-start(bf16[256,384]{1,0:T(8,128)(2,1)S(1)} %get-tuple-element.50), channel_id=1, source_target_pairs={{31,0},{4,3},{3,4},{8,7},{7,8},{12,11},{11,12},{16,15},{15,16},{20... | collective-permute-start | bytes 589832 | tf_op jit(solution)/shard_map/cond/branch_1_fun/ppermute | solution.py:48
  76.1 0.0 collective-permute-done.refs_2_
  76.1 0.0 copy-done
  76.1 14.9 %branch_1_fun.2 = (f32[4,20,128,128]{3,2,1,0:T(8,128)}, f32[1,512]{1,0:T(1,128)S(1)}, bf16[512,1024]{1,0:T(8,128)(2,1)}) custom-call(bf16[512,3712]{1,0:T(8,128)(2,1)S(1)} %copy-done, s32[4,20]{1,0:T(4,128)S(1)} %get-tuple-element.42.positions, f32[4,20,128,128]{3,2,1,0:T(8,128)} %get-tuple-element.43.prev, f32[1,512]{1,0:T(1,128)S(1)} %get-tuple-element.44.trace_in, ...), custom_call_target="tpu_custom_call" | custom-call | flops 5637144576 | bytes 18350080 | tf_op jit(solution)/shard_map/cond/branch_1_fun/pallas_call | solution.py:395
  91.0 0.0 collective-permute-done.1.corner
  91.0 0.5 branch_1_fun.3
  91.5 0.1 collective-permute-start.8
  91.6 1.1 collective-permute-done.8
  92.7 2.4 %collective-permute-start.11 = (f32[1,512]{1,0:T(1,128)S(1)}, f32[1,512]{1,0:T(1,128)S(1)}, u32[]{:S(2)}, u32[]{:S(2)}) collective-permute-start(f32[1,512]{1,0:T(1,128)S(1)} %add.30), channel_id=1, source_target_pairs={{0,24},{1,25},{2,26},{3,27},{4,28},{5,29},{6,30},{7,31},{8,16},{9,... | collective-permute-start | bytes 6152 | tf_op jit(solution)/shard_map/ppermute | solution.py:52
  95.1 0.0 collective-permute-start.10
  95.1 2.0 %collective-permute-start.9 = (f32[1,512]{1,0:T(1,128)S(1)}, f32[1,512]{1,0:T(1,128)S(1)}, u32[]{:S(2)}, u32[]{:S(2)}) collective-permute-start(f32[1,512]{1,0:T(1,128)S(1)} %add.30), channel_id=1, source_target_pairs={{0,8},{1,9},{2,10},{3,11},{4,12},{5,13},{6,14},{7,15},{8,0},{9,1},... | collective-permute-start | bytes 6152 | tf_op jit(solution)/shard_map/ppermute | solution.py:52
  97.1 1.0 collective-permute-done.11
  98.1 1.5 %collective-permute-done.10 = f32[1,512]{1,0:T(1,128)S(1)} collective-permute-done((f32[1,512]{1,0:T(1,128)S(1)}, f32[1,512]{1,0:T(1,128)S(1)}, u32[]{:S(2)}, u32[]{:S(2)}) %collective-permute-start.10) | collective-permute-done | bytes 2080 | tf_op jit(solution)/shard_map/ppermute | solution.py:52
  99.6 0.0 collective-permute-done.9
  99.6 0.3 collective-permute-done.7.source_a
  99.9 4.0 %collective-permute-start.12 = (bf16[81,128,128]{2,1,0:T(8,128)(2,1)S(1)}, bf16[81,128,128]{2,1,0:T(8,128)(2,1)S(1)}, u32[]{:S(2)}, u32[]{:S(2)}) collective-permute-start(bf16[81,128,128]{2,1,0:T(8,128)(2,1)S(1)} %collective-permute-done.7.source_a), channel_id=1, source_target_pairs={{1,0},{0,1},{3,2},{2,3},{5,4},{4,5},{7,6},{6,7},{9,8},{8,9},{11,10... | collective-permute-start | bytes 7962632 | tf_op jit(solution)/shard_map/ppermute | solution.py:48
  103.9 0.0 collective-permute-start.15
  103.9 2.0 %collective-permute-start.14 = (f32[1,512]{1,0:T(1,128)S(1)}, f32[1,512]{1,0:T(1,128)S(1)}, u32[]{:S(2)}, u32[]{:S(2)}) collective-permute-start(f32[1,512]{1,0:T(1,128)S(1)} %add_add_fusion), channel_id=1, source_target_pairs={{0,4},{1,5},{2,6},{3,7},{4,0},{5,1},{6,2},{7,3},{8,12},{9,13},{10,... | collective-permute-start | bytes 6152 | tf_op jit(solution)/shard_map/ppermute | solution.py:52
  105.9 1.4 %collective-permute-start.13 = (f32[1,512]{1,0:T(1,128)S(1)}, f32[1,512]{1,0:T(1,128)S(1)}, u32[]{:S(2)}, u32[]{:S(2)}) collective-permute-start(f32[1,512]{1,0:T(1,128)S(1)} %add_add_fusion), channel_id=1, source_target_pairs={{0,2},{1,3},{2,0},{3,1},{4,6},{5,7},{6,4},{7,5},{8,10},{9,11},{10,... | collective-permute-start | bytes 6152 | tf_op jit(solution)/shard_map/ppermute | solution.py:52
  107.4 1.1 collective-permute-done.12.source_b
  108.5 8.2 %shard_map.44 = bf16[4,20,128,128]{3,2,1,0:T(8,128)(2,1)} custom-call(bf16[512,1024]{1,0:T(8,128)(2,1)} %get-tuple-element.94.left_in, s32[4,20]{1,0:T(4,128)S(1)} %get-tuple-element.83.positions, f32[4,20,128,128]{3,2,1,0:T(8,128)} %get-tuple-element.97.prev, bf16[81,128,128]{2,1,0:T(8,128)(2,1)S(1)} %collective-permute-done.7.source_a, ...), custom_call_target="tpu_custom_call" | custom-call | flops 3758096384 | bytes 15728640 | tf_op jit(solution)/shard_map/pallas_call | solution.py:395
  116.7 0.0 collective-permute-done.15
  116.7 0.0 collective-permute-done.14
  116.7 0.0 collective-permute-done.13
  116.7 0.6 add_reduce_fusion
  (2 shorter events, 0.0 us)
Async XLA Ops:
  4.0 18.3 %collective-permute-start.6 = (bf16[81,128,128]{2,1,0:T(8,128)(2,1)}, bf16[81,128,128]{2,1,0:T(8,128)(2,1)}, u32[]{:S(2)}, u32[]{:S(2)}) collective-permute-start(bf16[81,128,128]{2,1,0:T(8,128)(2,1)} %shard_map.41), channel_id=1, source_target_pairs={{1,0},{0,1},{3,2},{2,3},{5,4},{4,5},{7,6},{6,7},{9,8},{8,9},{11,10... | collective-permute-start | bytes 7962632 | tf_op jit(solution)/shard_map/ppermute | solution.py:48
  4.5 60.3 %collective-permute-start.3 = (bf16[81,128,128]{2,1,0:T(8,128)(2,1)}, bf16[81,128,128]{2,1,0:T(8,128)(2,1)}, u32[]{:S(2)}, u32[]{:S(2)}) collective-permute-start(bf16[81,128,128]{2,1,0:T(8,128)(2,1)} %shard_map.41), channel_id=1, source_target_pairs={{29,0},{3,1},{0,2},{6,3},{1,4},{7,5},{4,6},{10,7},{5,8},{11,9},{8,... | collective-permute-start | bytes 7962632 | tf_op jit(solution)/shard_map/ppermute | solution.py:48
  7.1 58.5 %collective-permute-start.2 = (bf16[81,128,128]{2,1,0:T(8,128)(2,1)}, bf16[81,128,128]{2,1,0:T(8,128)(2,1)}, u32[]{:S(2)}, u32[]{:S(2)}) collective-permute-start(bf16[81,128,128]{2,1,0:T(8,128)(2,1)} %shard_map.41), channel_id=1, source_target_pairs={{2,0},{4,1},{31,2},{1,3},{6,4},{8,5},{3,6},{5,7},{10,8},{12,9},{7,... | collective-permute-start | bytes 7962632 | tf_op jit(solution)/shard_map/ppermute | solution.py:48
  19.7 12.1 %collective-permute-start.5 = (bf16[512,512]{1,0:T(8,128)(2,1)}, bf16[512,512]{1,0:T(8,128)(2,1)S(1)}, u32[]{:S(2)}, u32[]{:S(2)}) collective-permute-start(bf16[512,512]{1,0:T(8,128)(2,1)} %get-tuple-element.81), channel_id=1, source_target_pairs={{1,0},{2,3},{5,4},{6,7},{9,8},{10,11},{13,12},{14,15},{17,16},{18,... | collective-permute-start | bytes 1572872 | tf_op jit(solution)/shard_map/ppermute | solution.py:48
  21.0 10.8 %collective-permute-start.4 = (bf16[256,384]{1,0:T(8,128)(2,1)}, bf16[256,384]{1,0:T(8,128)(2,1)S(1)}, u32[]{:S(2)}, u32[]{:S(2)}) collective-permute-start(bf16[256,384]{1,0:T(8,128)(2,1)} %get-tuple-element.80), channel_id=1, source_target_pairs={{1,0},{2,3},{5,4},{6,7},{9,8},{10,11},{13,12},{14,15},{17,16},{18,... | collective-permute-start | bytes 589832 | tf_op jit(solution)/shard_map/ppermute | solution.py:48
  65.6 34.3 %collective-permute-start.7 = (bf16[81,128,128]{2,1,0:T(8,128)(2,1)}, bf16[81,128,128]{2,1,0:T(8,128)(2,1)S(1)}, u32[]{:S(2)}, u32[]{:S(2)}) collective-permute-start(bf16[81,128,128]{2,1,0:T(8,128)(2,1)} %collective-permute-done.2), channel_id=1, source_target_pairs={{2,0},{28,1},{7,2},{1,3},{6,4},{0,5},{11,6},{5,7},{10,8},{4,9},{15... | collective-permute-start | bytes 7962632 | tf_op jit(solution)/shard_map/ppermute | solution.py:48
  66.0 10.1 %copy-start = (bf16[512,3712]{1,0:T(8,128)(2,1)S(1)}, bf16[512,3712]{1,0:T(8,128)(2,1)}, u32[]{:S(2)}) copy-start(bf16[512,3712]{1,0:T(8,128)(2,1)} %get-tuple-element.41.left_in) | copy-start | bytes 11403268 | tf_op jit(solution)/shard_map/cond
  68.2 7.9 %collective-permute-start = (bf16[81,128,128]{2,1,0:T(8,128)(2,1)S(1)}, bf16[81,128,128]{2,1,0:T(8,128)(2,1)S(1)}, u32[]{:S(2)}, u32[]{:S(2)}) collective-permute-start(bf16[81,128,128]{2,1,0:T(8,128)(2,1)S(1)} %broadcast_select_fusion), channel_id=1, source_target_pairs={{1,0},{0,1},{3,2},{2,3},{5,4},{4,5},{7,6},{6,7},{9,8},{8,9},{11,10... | collective-permute-start | bytes 7962632 | tf_op jit(solution)/shard_map/cond/branch_1_fun/ppermute | solution.py:48
  69.7 21.3 %collective-permute-start.1 = (bf16[256,384]{1,0:T(8,128)(2,1)S(1)}, bf16[256,384]{1,0:T(8,128)(2,1)S(1)}, u32[]{:S(2)}, u32[]{:S(2)}) collective-permute-start(bf16[256,384]{1,0:T(8,128)(2,1)S(1)} %get-tuple-element.50), channel_id=1, source_target_pairs={{31,0},{4,3},{3,4},{8,7},{7,8},{12,11},{11,12},{16,15},{15,16},{20... | collective-permute-start | bytes 589832 | tf_op jit(solution)/shard_map/cond/branch_1_fun/ppermute | solution.py:48
  91.5 1.2 %collective-permute-start.8 = (f32[1,512]{1,0:T(1,128)S(1)}, f32[1,512]{1,0:T(1,128)S(1)}, u32[]{:S(2)}, u32[]{:S(2)}) collective-permute-start(f32[1,512]{1,0:T(1,128)S(1)} %get-tuple-element.96), channel_id=1, source_target_pairs={{0,1},{1,0},{2,3},{3,2},{4,5},{5,4},{6,7},{7,6},{8,9},{9,8},{10,11... | collective-permute-start | bytes 6152 | tf_op jit(solution)/shard_map/ppermute | solution.py:52
  92.7 5.4 %collective-permute-start.11 = (f32[1,512]{1,0:T(1,128)S(1)}, f32[1,512]{1,0:T(1,128)S(1)}, u32[]{:S(2)}, u32[]{:S(2)}) collective-permute-start(f32[1,512]{1,0:T(1,128)S(1)} %add.30), channel_id=1, source_target_pairs={{0,24},{1,25},{2,26},{3,27},{4,28},{5,29},{6,30},{7,31},{8,16},{9,... | collective-permute-start | bytes 6152 | tf_op jit(solution)/shard_map/ppermute | solution.py:52
  95.1 4.5 %collective-permute-start.10 = (f32[1,512]{1,0:T(1,128)S(1)}, f32[1,512]{1,0:T(1,128)S(1)}, u32[]{:S(2)}, u32[]{:S(2)}) collective-permute-start(f32[1,512]{1,0:T(1,128)S(1)} %add.30), channel_id=1, source_target_pairs={{0,16},{1,17},{2,18},{3,19},{4,20},{5,21},{6,22},{7,23},{8,24},{9,... | collective-permute-start | bytes 6152 | tf_op jit(solution)/shard_map/ppermute | solution.py:52
  95.1 4.5 %collective-permute-start.9 = (f32[1,512]{1,0:T(1,128)S(1)}, f32[1,512]{1,0:T(1,128)S(1)}, u32[]{:S(2)}, u32[]{:S(2)}) collective-permute-start(f32[1,512]{1,0:T(1,128)S(1)} %add.30), channel_id=1, source_target_pairs={{0,8},{1,9},{2,10},{3,11},{4,12},{5,13},{6,14},{7,15},{8,0},{9,1},... | collective-permute-start | bytes 6152 | tf_op jit(solution)/shard_map/ppermute | solution.py:52
  99.9 8.6 %collective-permute-start.12 = (bf16[81,128,128]{2,1,0:T(8,128)(2,1)S(1)}, bf16[81,128,128]{2,1,0:T(8,128)(2,1)S(1)}, u32[]{:S(2)}, u32[]{:S(2)}) collective-permute-start(bf16[81,128,128]{2,1,0:T(8,128)(2,1)S(1)} %collective-permute-done.7.source_a), channel_id=1, source_target_pairs={{1,0},{0,1},{3,2},{2,3},{5,4},{4,5},{7,6},{6,7},{9,8},{8,9},{11,10... | collective-permute-start | bytes 7962632 | tf_op jit(solution)/shard_map/ppermute | solution.py:48
  103.9 12.8 %collective-permute-start.15 = (f32[1,512]{1,0:T(1,128)S(1)}, f32[1,512]{1,0:T(1,128)S(1)}, u32[]{:S(2)}, u32[]{:S(2)}) collective-permute-start(f32[1,512]{1,0:T(1,128)S(1)} %add_add_fusion), channel_id=1, source_target_pairs={{0,6},{1,7},{2,4},{3,5},{4,2},{5,3},{6,0},{7,1},{8,14},{9,15},{10,... | collective-permute-start | bytes 6152 | tf_op jit(solution)/shard_map/ppermute | solution.py:52
  103.9 12.8 %collective-permute-start.14 = (f32[1,512]{1,0:T(1,128)S(1)}, f32[1,512]{1,0:T(1,128)S(1)}, u32[]{:S(2)}, u32[]{:S(2)}) collective-permute-start(f32[1,512]{1,0:T(1,128)S(1)} %add_add_fusion), channel_id=1, source_target_pairs={{0,4},{1,5},{2,6},{3,7},{4,0},{5,1},{6,2},{7,3},{8,12},{9,13},{10,... | collective-permute-start | bytes 6152 | tf_op jit(solution)/shard_map/ppermute | solution.py:52
  105.9 10.8 %collective-permute-start.13 = (f32[1,512]{1,0:T(1,128)S(1)}, f32[1,512]{1,0:T(1,128)S(1)}, u32[]{:S(2)}, u32[]{:S(2)}) collective-permute-start(f32[1,512]{1,0:T(1,128)S(1)} %add_add_fusion), channel_id=1, source_target_pairs={{0,2},{1,3},{2,0},{3,1},{4,6},{5,7},{6,4},{7,5},{8,10},{9,11},{10,... | collective-permute-start | bytes 6152 | tf_op jit(solution)/shard_map/ppermute | solution.py:52
